TPU v7x, 32 devices: a whole 2x2x4 slice. The times are simulated.
32 devices in a mesh: expert: 8 (over z, core), tensor: 4 (over y, x).
Axes of the slice: x: 2, y: 2, z: 4, core: 2. Of those that a mesh axis runs over, the one named last changes fastest.
Arguments:
- layer_input: bfloat16 [1024, 16384], P(None, 'expert'), may hold values from -18 to 18
- gain_one: float32 [1024], replicated, may hold values from 0.1 to 1.9
- attn_in: bfloat16 [3, 1024, 1024], P(None, 'tensor'), may hold values from -0.1875 to 0.1875
- rel_bias: float32 [32, 16], P(None, 'tensor'), may hold values from -4 to 4
- attn_out: bfloat16 [1024, 1024], P('tensor'), may hold values from -0.75 to 0.75
- gain_two: float32 [1024], replicated, may hold values from 0.1 to 1.9
- router: bfloat16 [1024, 16], replicated, may hold values from -0.375 to 0.375
- expert_gate: bfloat16 [16, 2816, 1024], P('expert', 'tensor'), may hold values from -0.1875 to 0.1875
- expert_up: bfloat16 [16, 2816, 1024], P('expert', 'tensor'), may hold values from -0.1875 to 0.1875
- expert_down: bfloat16 [16, 2816, 1024], P('expert', 'tensor'), may hold values from -0.21875 to 0.21875
- routes: int32 [16384, 2], P('expert'), may hold values from 0 to 15, all different within a row
- piece_starts: int32 [16, 2], P('expert'), may hold values from 0 to 768, as said below
- grad_out: bfloat16 [1024, 16384], P(None, 'expert'), may hold values from -6 to 6
Outputs:
- layer_output: bfloat16 [1024, 16384], P(None, 'expert')
- grad_input: float32 [1024, 16384], P(None, 'expert')
- grad_gain_one: float32 [1024], replicated
- grad_attn_in: float32 [3, 1024, 1024], P(None, 'tensor')
- grad_rel_bias: float32 [32, 16], P(None, 'tensor')
- grad_attn_out: float32 [1024, 1024], P('tensor')
- grad_gain_two: float32 [1024], replicated
- grad_router: float32 [1024, 16], replicated
- grad_expert_gate: float32 [16, 2816, 1024], P('expert', 'tensor')
- grad_expert_up: float32 [16, 2816, 1024], P('expert', 'tensor')
- grad_expert_down: float32 [16, 2816, 1024], P('expert', 'tensor')
Inputs may be any that keep to these rules, and one draw needn't show every extreme that they name: `piece_starts`: start i of a sequence lies in [2 * 256 * i, 2 * 256 * i + 256], so the pieces of a sequence never intersect and lie inside it. `routes`: the 2 experts of a token differ.
All inputs are finite; a program needn't handle non-finite values.
Results may differ from a plain program's by a relative error of at most 0.019.
Values may be sent and summed in bfloat16 or wider, within the bound.
A program may use at most 384 MiB of HBM per device.

v0:
```python
from functools import partial

import jax
import jax.numpy as jnp
from jax import lax
from jax.sharding import PartitionSpec as P

EXPERTS = 16
BUCKETS = 32
TOP = 2
PIECE = 256
SEQ = 1024
CAP = 320


EPS = 1e-06
NEG = -1e30
THRESHOLDS = (12, 16, 23, 32, 46, 64, 91)
HIGH = lax.Precision.HIGHEST


def bucket_of(offset):
    magnitude = jnp.abs(offset)
    beyond = sum(((magnitude >= threshold).astype(jnp.int32) for threshold in THRESHOLDS))
    lower_part = jnp.where(magnitude < 8, magnitude, 8 + beyond)
    return lower_part + 16 * (offset > 0).astype(jnp.int32)


def allowed_pairs(seq_starts):
    position = jnp.arange(SEQ, dtype=jnp.int32)
    inside = (position[:, None] >= seq_starts[None, :]) & (
        position[:, None] < seq_starts[None, :] + PIECE
    )
    numbers = jnp.arange(seq_starts.shape[0], dtype=jnp.int32) + 1
    piece_label = jnp.sum(inside.astype(jnp.int32) * numbers[None, :], axis=1)
    causal = position[None, :] <= position[:, None]
    shared = (piece_label[:, None] == piece_label[None, :]) & (piece_label[:, None] > 0)
    return causal | shared


def slot_table(routes):
    flat_routes = routes.reshape(-1)
    onehot = (flat_routes[:, None] == jnp.arange(EXPERTS, dtype=jnp.int32)[None, :]).astype(
        jnp.int32
    )
    before = jnp.cumsum(onehot, axis=0) - onehot
    slot_number = jnp.sum(before * onehot, axis=1)
    kept_pairs = slot_number < CAP
    slot_index = jnp.where(kept_pairs, flat_routes * CAP + slot_number, EXPERTS * CAP)
    return (slot_index.reshape(routes.shape), kept_pairs.reshape(routes.shape))


def bucket_onehot():
    offsets = jnp.arange(2 * SEQ - 1, dtype=jnp.int32) - (SEQ - 1)
    return (bucket_of(offsets)[:, None] == jnp.arange(BUCKETS, dtype=jnp.int32)[None, :]).astype(
        jnp.float32
    )


def expand_line(line):
    head_count = line.shape[0]
    padded = jnp.concatenate([line, jnp.zeros((head_count, 1), line.dtype)], axis=1)
    tiled = jnp.tile(padded, (1, SEQ))[:, : SEQ * (2 * SEQ - 1)].reshape(
        head_count, SEQ, 2 * SEQ - 1
    )
    return tiled[:, :, SEQ - 1 :]


def fold_line(full_grid):
    head_count = full_grid.shape[0]
    padded = jnp.pad(full_grid, ((0, 0), (0, 0), (SEQ - 1, 0))).reshape(
        head_count, SEQ * (2 * SEQ - 1)
    )
    padded = jnp.pad(padded, ((0, 0), (0, SEQ))).reshape(head_count, SEQ, 2 * SEQ)
    return jnp.sum(padded, axis=1)[:, : 2 * SEQ - 1]


def reduce_heads(tensor_value):
    return lax.psum(tensor_value, "tensor")


def spread_slots(tensor_value):
    return lax.all_gather(tensor_value, "tensor", axis=2, tiled=True)


def owner_exchange(tensor_value):
    return lax.all_to_all(tensor_value, "expert", split_axis=0, concat_axis=0, tiled=True)


def expert_sums(tensor_value):
    return lax.psum_scatter(tensor_value, "tensor", scatter_dimension=2, tiled=True)


def norm_forward(resid, gain, model_width):
    scale = lax.rsqrt(jnp.sum(resid * resid, axis=1) / model_width + EPS)[:, None]
    return (scale, (resid * scale * gain).astype(jnp.bfloat16))


def norm_backward(resid, scale, gain, grad_normed, model_width):
    grad_gain = jnp.sum(grad_normed * resid * scale, axis=0)
    scaled = grad_normed * gain
    inner = jnp.sum(scaled * resid, axis=1)[:, None]
    return (grad_gain, scale * scaled - resid * scale**3 * inner / model_width)


def attend_scores(bias_full, queries, key_rows, seq_starts):
    scores = (
        jnp.einsum("qhe,khe->hqk", queries, key_rows, preferred_element_type=jnp.float32) * 0.125
        + bias_full
    )
    return jnp.where(allowed_pairs(seq_starts)[None], scores, NEG)


def attend_forward(bias_full, inputs):
    queries, key_rows, value_rows, seq_starts = inputs
    scores = attend_scores(bias_full, queries, key_rows, seq_starts)
    row_max = jnp.max(scores, axis=2, keepdims=True)
    exponent = jnp.exp(scores - row_max)
    row_sum_exp = jnp.sum(exponent, axis=2, keepdims=True)
    weights = (exponent / row_sum_exp).astype(jnp.bfloat16)
    mixed_heads = jnp.einsum(
        "hqk,khe->qhe", weights, value_rows, preferred_element_type=jnp.float32
    )
    return (mixed_heads.astype(jnp.bfloat16), (row_max + jnp.log(row_sum_exp))[:, :, 0])


def attend_backward(bias_full, running, inputs):
    queries, key_rows, value_rows, grad_heads, seq_starts, log_total = inputs
    scores = attend_scores(bias_full, queries, key_rows, seq_starts)
    probabilities = jnp.exp(scores - log_total[:, :, None])
    grad_probs = jnp.einsum(
        "qhe,khe->hqk", grad_heads, value_rows, preferred_element_type=jnp.float32
    )
    inner = jnp.sum(probabilities * grad_probs, axis=2, keepdims=True)
    grad_scores = (probabilities * (grad_probs - inner)).astype(jnp.bfloat16)
    grad_values = jnp.einsum(
        "hqk,qhe->khe",
        probabilities.astype(jnp.bfloat16),
        grad_heads,
        preferred_element_type=jnp.float32,
    )
    grad_queries = (
        jnp.einsum("hqk,khe->qhe", grad_scores, key_rows, preferred_element_type=jnp.float32)
        * 0.125
    )
    grad_keys = (
        jnp.einsum("hqk,qhe->khe", grad_scores, queries, preferred_element_type=jnp.float32) * 0.125
    )
    return (
        running + grad_scores.astype(jnp.float32),
        jnp.stack([grad_queries, grad_keys, grad_values]),
    )


def gelu_product(left, right):
    return jax.nn.gelu(left, approximate=True) * right


def expert_forward(received, weight_gate, weight_up, weight_down):
    gate_part = jnp.einsum(
        "secd,efd->secf", received, weight_gate, preferred_element_type=jnp.float32
    )
    up_part = jnp.einsum("secd,efd->secf", received, weight_up, preferred_element_type=jnp.float32)
    hidden = gelu_product(gate_part, up_part).astype(jnp.bfloat16)
    partial_out = jnp.einsum(
        "secf,efd->secd", hidden, weight_down, preferred_element_type=jnp.float32
    )
    return (gate_part, up_part, hidden, partial_out)


def expert_backward(
    received, gate_part, up_part, hidden, grad_rows_out, weight_gate, weight_up, weight_down
):
    grad_hidden = jnp.einsum(
        "secd,efd->secf", grad_rows_out, weight_down, preferred_element_type=jnp.float32
    )
    product_value, pullback = jax.vjp(gelu_product, gate_part, up_part)
    grad_gate_part, grad_up_part = pullback(grad_hidden)
    grad_gate_part = grad_gate_part.astype(jnp.bfloat16)
    grad_up_part = grad_up_part.astype(jnp.bfloat16)
    grad_down = jnp.einsum(
        "secf,secd->efd", hidden, grad_rows_out, preferred_element_type=jnp.float32
    )
    grad_gate_w = jnp.einsum(
        "secf,secd->efd", grad_gate_part, received, preferred_element_type=jnp.float32
    )
    grad_up_w = jnp.einsum(
        "secf,secd->efd", grad_up_part, received, preferred_element_type=jnp.float32
    )
    grad_rows_in = jnp.einsum(
        "secf,efd->secd", grad_gate_part, weight_gate, preferred_element_type=jnp.float32
    )
    grad_rows_in = grad_rows_in + jnp.einsum(
        "secf,efd->secd", grad_up_part, weight_up, preferred_element_type=jnp.float32
    )
    return (grad_gate_w, grad_up_w, grad_down, grad_rows_in)


def on_device(
    layer_input,
    gain_one,
    attn_in,
    rel_bias,
    attn_out,
    gain_two,
    router,
    expert_gate,
    expert_up,
    expert_down,
    routes,
    piece_starts,
    grad_out,
):
    tok_count = layer_input.shape[1]
    model_width = layer_input.shape[0]
    heads_here = rel_bias.shape[1]
    head_width = attn_in.shape[1] // heads_here
    seqs_here = piece_starts.shape[0]
    local_experts = expert_gate.shape[0]
    part_rows = CAP // lax.axis_size("tensor")
    share_start = lax.axis_index("tensor") * part_rows
    tokens = layer_input.T.astype(jnp.float32)
    scale_one, normed = norm_forward(tokens, gain_one, model_width)
    project = jnp.einsum("td,chd->cth", normed, attn_in, preferred_element_type=jnp.float32).astype(
        jnp.bfloat16
    )
    by_seq = project.reshape(3, seqs_here, SEQ, heads_here, head_width)
    onehot_line = bucket_onehot()
    bias_full = expand_line(jnp.dot(onehot_line, rel_bias, precision=HIGH).T)
    mixed_heads, log_total = lax.map(
        partial(attend_forward, bias_full), (by_seq[0], by_seq[1], by_seq[2], piece_starts)
    )
    mixed_heads = mixed_heads.reshape(tok_count, heads_here * head_width)
    resid = tokens + reduce_heads(
        jnp.dot(mixed_heads, attn_out, preferred_element_type=jnp.float32)
    )
    scale_two, normed_two = norm_forward(resid, gain_two, model_width)
    logits = jnp.dot(normed_two, router, preferred_element_type=jnp.float32)
    chosen = (routes[:, :, None] == jnp.arange(EXPERTS, dtype=jnp.int32)[None, None, :]).astype(
        jnp.float32
    )
    picked = jnp.sum(chosen * logits[:, None, :], axis=2)
    gate_weights = jax.nn.softmax(picked, axis=1)
    slot_index, kept_pairs = slot_table(routes)
    keep_float = kept_pairs.astype(jnp.float32)
    mix_weight = gate_weights * keep_float
    safe_index = jnp.minimum(slot_index, EXPERTS * CAP - 1)
    token_rows = jnp.repeat(normed_two, TOP, axis=0)
    buffer = (
        jnp.zeros((EXPERTS * CAP + 1, model_width), jnp.bfloat16)
        .at[slot_index.reshape(-1)]
        .set(token_rows)
    )
    buffer = buffer[: EXPERTS * CAP].reshape(-1, local_experts, CAP, model_width)
    received = lax.all_to_all(buffer, "expert", split_axis=0, concat_axis=0, tiled=True)
    gate_part, up_part, hidden, partial_out = expert_forward(
        received, expert_gate, expert_up, expert_down
    )
    returned = spread_slots(owner_exchange(expert_sums(partial_out).astype(jnp.bfloat16)))
    flat_ret = returned.reshape(EXPERTS * CAP, model_width)
    fetched = flat_ret[safe_index].astype(jnp.float32)
    output = resid + jnp.sum(mix_weight[:, :, None] * fetched, axis=1)
    grad_y = grad_out.T.astype(jnp.float32)
    grad_gates = jnp.sum(grad_y[:, None, :] * fetched, axis=2) * keep_float
    grad_picked = gate_weights * (
        grad_gates - jnp.sum(gate_weights * grad_gates, axis=1, keepdims=True)
    )
    grad_logits = jnp.sum(chosen * grad_picked[:, :, None], axis=1)
    grad_router = jnp.dot(normed_two.astype(jnp.float32).T, grad_logits, precision=HIGH)
    grad_normed_two = jnp.dot(grad_logits, router.astype(jnp.float32).T, precision=HIGH)
    slot_grads = (mix_weight[:, :, None] * grad_y[:, None, :]).astype(jnp.bfloat16)
    grad_ret = (
        jnp.zeros((EXPERTS * CAP + 1, model_width), jnp.bfloat16)
        .at[slot_index.reshape(-1)]
        .set(slot_grads.reshape(-1, model_width))
    )
    grad_ret = grad_ret[: EXPERTS * CAP].reshape(-1, local_experts, CAP, model_width)
    grad_share = lax.dynamic_slice_in_dim(grad_ret, share_start, part_rows, 2)
    grad_rows_out = spread_slots(owner_exchange(grad_share))
    grad_expert_gate, grad_expert_up, grad_expert_down, grad_rows_in = expert_backward(
        received, gate_part, up_part, hidden, grad_rows_out, expert_gate, expert_up, expert_down
    )
    grad_back = spread_slots(owner_exchange(expert_sums(grad_rows_in).astype(jnp.bfloat16)))
    flat_back = grad_back.reshape(EXPERTS * CAP, model_width).astype(jnp.float32)
    grad_normed_two = grad_normed_two + jnp.sum(
        flat_back[safe_index] * keep_float[:, :, None], axis=1
    )
    grad_gain_two, grad_resid = norm_backward(
        resid, scale_two, gain_two, grad_normed_two, model_width
    )
    grad_resid = grad_resid + grad_y
    grad_attn = grad_resid.astype(jnp.bfloat16)
    grad_attn_out = jnp.einsum(
        "th,td->hd", mixed_heads, grad_attn, preferred_element_type=jnp.float32
    )
    grad_mixed = jnp.einsum(
        "td,hd->th", grad_attn, attn_out, preferred_element_type=jnp.float32
    ).astype(jnp.bfloat16)
    grad_by_seq = grad_mixed.reshape(seqs_here, SEQ, heads_here, head_width)
    bias_grad_full, grad_project = lax.scan(
        partial(attend_backward, bias_full),
        jnp.zeros_like(bias_full),
        (by_seq[0], by_seq[1], by_seq[2], grad_by_seq, piece_starts, log_total),
    )
    grad_project = (
        jnp.moveaxis(grad_project, 1, 0)
        .reshape(3, tok_count, heads_here * head_width)
        .astype(jnp.bfloat16)
    )
    grad_attn_in = jnp.einsum(
        "cth,td->chd", grad_project, normed, preferred_element_type=jnp.float32
    )
    grad_normed = reduce_heads(
        jnp.einsum("cth,chd->td", grad_project, attn_in, preferred_element_type=jnp.float32)
    )
    grad_gain_one, grad_tokens = norm_backward(
        tokens, scale_one, gain_one, grad_normed, model_width
    )
    grad_tokens = grad_tokens + grad_resid
    grad_rel_bias = jnp.dot(onehot_line.T, fold_line(bias_grad_full).T, precision=HIGH)
    shared = (
        lax.psum(grad_gain_one.astype(jnp.bfloat16), "expert").astype(jnp.float32),
        lax.psum(grad_attn_in.astype(jnp.bfloat16), "expert").astype(jnp.float32),
        lax.psum(grad_rel_bias.astype(jnp.bfloat16), "expert").astype(jnp.float32),
        lax.psum(grad_attn_out.astype(jnp.bfloat16), "expert").astype(jnp.float32),
        lax.psum(grad_gain_two.astype(jnp.bfloat16), "expert").astype(jnp.float32),
        lax.psum(grad_router.astype(jnp.bfloat16), "expert").astype(jnp.float32),
    )
    return (
        output.astype(jnp.bfloat16).T,
        grad_tokens.T,
        shared[0],
        shared[1],
        shared[2],
        shared[3],
        shared[4],
        shared[5],
        grad_expert_gate,
        grad_expert_up,
        grad_expert_down,
    )


def solution(mesh):
    placed = (
        P(None, "expert"),
        P(),
        P(None, "tensor", None),
        P(None, "tensor"),
        P("tensor", None),
        P(),
        P(),
        P("expert", "tensor", None),
        P("expert", "tensor", None),
        P("expert", "tensor", None),
        P("expert", None),
        P("expert", None),
        P(None, "expert"),
    )
    return jax.shard_map(
        on_device,
        mesh=mesh,
        in_specs=placed,
        out_specs=(
            P(None, "expert"),
            P(None, "expert"),
            P(),
            P(None, "tensor", None),
            P(None, "tensor"),
            P("tensor", None),
            P(),
            P(),
            P("expert", "tensor", None),
            P("expert", "tensor", None),
            P("expert", "tensor", None),
        ),
        check_vma=False,
    )
```

profile of v0, /device:TPU:0, one launch (start us, length us, event | category | flops | bytes accessed | tf_op | source)
XLA Modules:
  0.0 2186.2 jit_solution(6676166606946646582)
XLA Ops:
  51.7 11.2 broadcast_bitcast_fusion
  62.9 38.4 %copy.219 = f32[1,4,1024,2048]{3,1,2,0:T(4,128)} copy(f32[1,4,1024,2048]{3,2,1,0:T(8,128)} %broadcast_bitcast_fusion) | data formatting | bytes 67108864
  101.2 22.9 %slice.53 = f32[4,2096128]{1,0:T(4,128)} slice(f32[4,2097152]{1,0:T(4,128)} %bitcast.307), slice={[0:4], [0:2096128]} | slice | bytes 67076096 | tf_op jit(solution)/shard_map/slice | solution.py:63
  124.1 94.0 %reshape.500 = f32[8384512]{0:T(1024)} reshape(f32[4,2096128]{1,0:T(4,128)} %slice.53) | data formatting | bytes 67076096
  218.1 49.6 %reshape.435 = f32[4,1024,2047]{2,1,0:T(8,128)} reshape(f32[8384512]{0:T(1024)} %reshape.500) | data formatting | bytes 67076096 | tf_op jit(solution)/shard_map/reshape | solution.py:63
  267.7 13.2 slice.54
  280.9 16.4 copy.168
  297.3 66.3 %while.25 = (s32[]{:T(128)}, bf16[2,1024,4,64]{1,3,2,0:T(8,128)(2,1)}, f32[2,4,1024]{2,1,0:T(4,128)S(1)}, bf16[2,1024,4,64]{1,3,2,0:T(8,128)(2,1)}, s32[2,2]{1,0...) while((s32[]{:T(128)}, ...), condition=%wide.region_5.6_spmd, body=%wide.region_1.5_spmd.sunk | while | flops 1115953152 | bytes 84033792 | solution.py:230
  298.5 15.4 fusion.188
  313.9 8.2 fusion.189
  331.5 15.4 fusion.188
  346.8 8.2 fusion.189
  402.8 9.3 mul.336
  412.1 20.6 mul.345
  432.7 114.1 %all-reduce.9.cloned.1.call-done = f32[2048,1024]{1,0:T(8,128)} async-done(((f32[2048,1024]{1,0:T(8,128)}), f32[2048,1024]{1,0:T(8,128)}) %all-reduce.9.cloned.1.call-update) | async-done | bytes 8388624 | tf_op jit(solution)/shard_map/psum | solution.py:79
  561.6 27.0 %scatter_custom_fusion.1 = bf16[5121,1024]{1,0:T(8,128)(2,1)} fusion(s32[4096]{0:T(1024)S(1)} %bitcast.317, f32[4096,1024]{1,0:T(8,128)} %mul.345, f32[4096]{0:T(1024)S(1)} %compare_select_fusion.4, bf16[]{:T(256)} %constant.44.clone.1), kind=kCustom, calls=%fused_computation.99 | custom fusion | flops 8388608 | bytes 27281410 | tf_op jit(solution)/shard_map/scatter | solution.py:275
  588.6 9.2 slice.58
  612.8 13.1 reshape.466
  625.9 25.4 %scatter_custom_fusion = bf16[5121,1024]{1,0:T(8,128)(2,1)} fusion(s32[4096]{0:T(1024)S(1)} %bitcast.318, bf16[4096,1024]{1,0:T(8,128)(2,1)} %reshape.466, bf16[]{:T(256)} %constant.44.clone.1), kind=kCustom, calls=%fused_computation.135 | custom fusion | bytes 10488320 | tf_op jit(solution)/shard_map/scatter | solution.py:252
  651.3 9.1 slice.57
  675.4 225.1 %all-to-all-done = bf16[8,2,320,1024]{3,2,1,0:T(8,128)(2,1)} async-done(((bf16[8,2,320,1024]{3,2,1,0:T(8,128)(2,1)}), bf16[8,2,320,1024]{3,2,1,0:T(8,128)(2,1)}, u32[]{:S(2)}, u32[]{:S(2)}) %all-to-all-start) | async-done | bytes 10485792 | tf_op jit(solution)/shard_map/all_to_all | solution.py:255
  900.6 15.2 fusion.75
  915.8 15.2 fusion.77
  931.0 32.3 %fusion.54 = (bf16[8,2,320,704]{3,2,0,1:T(8,128)(2,1)}, bf16[8,2,320,704]{3,2,0,1:T(8,128)(2,1)}, bf16[8,2,320,704]{3,2,0,1:T(8,128)(2,1)}) fusion(f32[2,8,320,704]{3,2,1,0:T(8,128)} %fusion.77, f32[2,8,320,704]{3,2,1,0:T(8,128)} %fusion.75, bf16[8,2,320,1024]{3,2,0,1:T(8,128)(2,1)} %all-gather.6.cloned.1.call-done, bf16[2,704,1024]{2,1,0:T(8,128)(2,1)S(1)} %copy-done), kind=kOutput, calls=%fused_computation.91 | convolution fusion | flops 7475691520 | bytes 63832064 | tf_op jit(solution)/shard_map/secd,efd->secf/dot_general | solution.py:174
  963.3 15.0 fusion.87
  978.3 18.4 add_bitcast_fusion.2
  996.8 15.0 convolution_bitcast_fusion
  1011.8 171.4 %reduce-scatter.5.cloned.1.call-done = f32[8,2,80,1024]{3,2,0,1:T(8,128)} async-done(((f32[8,2,320,1024]{3,2,0,1:T(8,128)}), f32[8,2,80,1024]{3,2,0,1:T(8,128)}) %reduce-scatter.5.cloned.1.call-update) | async-done | bytes 5242896 | tf_op jit(solution)/shard_map/reduce_scatter | solution.py:91
  1186.5 64.8 %all_to_all.20 = bf16[8,2,80,1024]{3,2,1,0:T(8,128)(2,1)} all-to-all(bf16[8,2,80,1024]{3,2,1,0:T(8,128)(2,1)S(1)} %copy.184), channel_id=1, replica_groups=mesh['expert'=8,'tensor'=4] {'expert'}, dimensions={0} | all-to-all | bytes 5242880 | tf_op jit(solution)/shard_map/all_to_all | solution.py:87
  1251.3 122.7 %reduce-scatter.3.cloned.1.call-done = f32[8,2,80,1024]{3,2,0,1:T(8,128)} async-done(((f32[8,2,320,1024]{3,2,0,1:T(8,128)}), f32[8,2,80,1024]{3,2,0,1:T(8,128)}) %reduce-scatter.3.cloned.1.call-update) | async-done | bytes 5242896 | tf_op jit(solution)/shard_map/reduce_scatter | solution.py:91
  1377.3 64.8 %all_to_all.21 = bf16[8,2,80,1024]{3,2,1,0:T(8,128)(2,1)} all-to-all(bf16[8,2,80,1024]{3,2,1,0:T(8,128)(2,1)S(1)} %copy.177), channel_id=1, replica_groups=mesh['expert'=8,'tensor'=4] {'expert'}, dimensions={0} | all-to-all | bytes 5242880 | tf_op jit(solution)/shard_map/all_to_all | solution.py:87
  1443.9 37.1 %all-gather.8.cloned.1.call-done = bf16[8,2,320,1024]{3,2,1,0:T(8,128)(2,1)} async-done(((bf16[8,2,80,1024]{3,2,1,0:T(8,128)(2,1)}), bf16[8,2,320,1024]{3,2,1,0:T(8,128)(2,1)}) %all-gather.8.cloned.1.call-update) | async-done | bytes 10485776 | tf_op jit(solution)/shard_map/all_gather | solution.py:83
  1481.0 16.3 bitcast_convert_fusion
  1497.3 29.5 %gather_fusion.1 = f32[4096,1024]{1,0:T(8,128)} fusion(f32[5120,1024]{1,0:T(8,128)} %bitcast_convert_fusion, s32[4096]{0:T(1024)S(1)} %broadcast_clamp_fusion), kind=kCustom, calls=%fused_computation.1 | custom fusion | bytes 33570816 | tf_op jit(solution)/shard_map/gather | solution.py:286
  1526.8 20.5 reshape.455
  1547.4 40.6 %all-gather.4.cloned.1.call-done = bf16[8,2,320,1024]{3,2,1,0:T(8,128)(2,1)} async-done(((bf16[8,2,80,1024]{3,2,1,0:T(8,128)(2,1)}), bf16[8,2,320,1024]{3,2,1,0:T(8,128)(2,1)}) %all-gather.4.cloned.1.call-update) | async-done | bytes 10485776 | tf_op jit(solution)/shard_map/all_gather | solution.py:83
  1587.9 26.1 %gather_fusion = bf16[4096,1024]{1,0:T(8,128)(2,1)} fusion(bf16[5120,1024]{1,0:T(8,128)(2,1)} %bitcast.305, s32[4096]{0:T(1024)S(1)} %broadcast_clamp_fusion), kind=kCustom, calls=%fused_computation | custom fusion | bytes 16793600 | tf_op jit(solution)/shard_map/gather | solution.py:261
  1614.1 18.2 reshape.482
  1632.2 36.1 %multiply_reduce_fusion.2 = (f32[2048,2]{1,0:T(8,128)}, f32[2048,1024]{1,0:T(8,128)}) fusion(f32[2048,2,1024]{2,1,0:T(2,128)} %reshape.482, f32[2048,1024]{1,0:T(8,128)} %convert_bitcast_fusion, f32[2048,2]{1,0:T(8,128)S(1)} %copy.173), kind=kLoop, calls=%fused_computation.79 | loop fusion | flops 14675968 | bytes 33587200 | tf_op jit(solution)/shard_map/reduce_sum | solution.py:264
  1670.1 25.8 %multiply_reduce_fusion.1 = f32[2048,1024]{1,0:T(8,128)} fusion(f32[2048,2,1024]{2,1,0:T(2,128)} %reshape.455, f32[2048,2]{1,0:T(8,128)S(1)} %copy.185), kind=kLoop, calls=%fused_computation.77 | loop fusion | flops 6291456 | bytes 25182208 | tf_op jit(solution)/shard_map/reduce_sum | solution.py:285
  1696.0 11.6 multiply_reduce_fusion.4
  1707.6 13.2 subtract_add_fusion
  1731.5 130.0 %while.26 = (s32[]{:T(128)}, f32[4,1024,1024]{1,2,0:T(8,128)}, bf16[2,3,1024,4,64]{2,4,3,1,0:T(8,128)(2,1)}, s32[2,2]{1,0:T(2,128)S(1)}, bf16[2,1024,4,64]{1,3,2...) while((s32[]{:T(128)}, f32[4,1024,1024]{1,2,0:T(8,128)}, ...), condition=%wide.region_27.28_spmd.clone, body=%wide.region_24.27_spmd.clone.sunk | while | flops 2748848128 | bytes 216105264 | solution.py:300
  1732.8 9.3 fusion.199
  1742.1 18.8 multiply_reduce_fusion.9
  1760.9 8.6 fusion.203
  1769.5 18.0 select_add_fusion.2
  1794.6 9.3 fusion.199
  1803.9 18.8 multiply_reduce_fusion.9
  1822.7 8.6 fusion.203
  1831.4 23.6 %select_add_fusion.2 = (f32[4,1024,1024]{1,2,0:T(8,128)}, bf16[4,1024,1024]{1,2,0:T(8,128)(2,1)S(1)}) fusion(f32[4,1024,1024]{1,2,0:T(8,128)} %get-tuple-element.536, pred[]{:T(512)S(6)} %compare.6, f32[4,1024,1024]{1,2,0:T(8,128)} %get-tuple-element.492, f32[4,1024,1024]{1,2,0:T(8,128)} %fusion.199, f32[4,1024]{1,0:T(4,128)S(1)} %get-tuple-element.493), kind=kLoop, calls=%fused_computation.30.clone.1 | loop fusion | flops 25165824 | bytes 75513856 | tf_op jit(solution)/shard_map/while/body/eval_jaxpr/add | solution.py:150
  1874.4 7.9 fusion.105
  1882.5 7.8 convolution_bitcast_fusion.1
  1890.3 14.4 fusion.96
  1904.7 14.3 fusion.93
  1919.0 14.7 convolution_bitcast_fusion.2
  1940.2 16.5 copy.218
  1956.6 20.5 pad.9.clone
  1977.2 47.3 %reshape.502 = f32[8384512]{0:T(1024)} reshape(f32[4,1024,2047]{2,1,0:T(8,128)} %pad.9.clone) | data formatting | bytes 67076096
  2024.5 41.2 %reshape.443 = f32[4,2096128]{1,0:T(4,128)} reshape(f32[8384512]{0:T(1024)} %reshape.502) | data formatting | bytes 67076096 | tf_op jit(solution)/shard_map/reshape | solution.py:71
  2065.7 23.8 %pad.10 = f32[4,2097152]{1,0:T(4,128)} pad(f32[4,2096128]{1,0:T(4,128)} %reshape.443, f32[]{:T(128)} %constant.45.clone.1), padding=0_0x0_1024 | pad | bytes 67092484 | tf_op jit(solution)/shard_map/jit(_pad)/pad | solution.py:74
  2089.5 19.3 bitcast_reduce_fusion
  2138.7 9.1 copy.198
  2147.9 28.9 %all-reduce.3 = (bf16[1024]{0:T(1024)(128)(2,1)S(1)}, bf16[32,4]{0,1:T(4,128)(2,1)S(1)}, bf16[1024]{0:T(1024)(128)(2,1)S(1)}, bf16[1024,16]{0,1:T(8,128)(2,1)S(1)}) all-reduce(bf16[1024]{0:T(1024)(128)(2,1)S(1)} %get-tuple-element.293, ...), channel_id=1, replica_groups=mesh['expert'=8,'tensor'=4] {'expert'}, use_global_device_ids=true, to_apply=%region_31.32 | all-reduce | flops 18560 | bytes 74240 | tf_op jit(solution)/shard_map/psum | solution.py:322
  (257 shorter events, 233.4 us)
Async XLA Ops:
  7.2 923.9 %copy-start = (bf16[2,704,1024]{2,1,0:T(8,128)(2,1)S(1)}, bf16[2,704,1024]{2,1,0:T(8,128)(2,1)}, u32[]{:S(2)}) copy-start(bf16[2,704,1024]{2,1,0:T(8,128)(2,1)} %param.26) | copy-start | bytes 8650756
  7.2 10.4 copy-start.44
  7.2 539.7 %all-reduce.9.cloned.1.call-start = ((), (), s32[]{:S(2)}) async-start(), calls=%async_computation.6 | async-start | bytes 16777216 | tf_op jit(solution)/shard_map/psum | solution.py:79
  7.3 43.7 %copy-start.48 = (s32[2047]{0:T(1024)}, s32[2047]{0:T(1024)S(1)}, u32[]{:S(2)}) copy-start(s32[2047]{0:T(1024)S(1)} %fusion.120) | copy-start | bytes 24568
  17.6 6.2 copy-start.33
  30.0 21.0 copy-start.53
  280.9 16.4 copy-start.42
  297.3 69.9 %copy-start.15 = (bf16[256,1024]{1,0:T(8,128)(2,1)S(1)}, bf16[256,1024]{1,0:T(8,128)(2,1)}, u32[]{:S(2)}) copy-start(bf16[256,1024]{1,0:T(8,128)(2,1)} %param.21) | copy-start | bytes 1572868
  313.9 8.2 copy-start.10
  313.9 8.2 copy-start.19
  346.8 8.2 copy-start.10
  346.8 8.2 copy-start.19
  363.6 2.6 copy-start.27
  367.2 4.7 copy-start.23
  385.9 172.0 %copy-start.21 = (s32[2048,2]{0,1:T(2,128)}, s32[2048,2]{0,1:T(2,128)S(1)}, u32[]{:S(2)}) copy-start(s32[2048,2]{0,1:T(2,128)S(1)} %copy.172) | copy-start | bytes 49156
  432.7 120.5 %copy-start.38 = (f32[1024]{0:T(1024)S(1)}, f32[1024]{0:T(1024)}, u32[]{:S(2)}) copy-start(f32[1024]{0:T(1024)} %param.22) | copy-start | bytes 12292
  552.6 5.1 copy-start.3
  552.6 3.9 copy-start.29
  553.2 4.5 copy-start.31
  554.6 2.0 copy-start.4
  558.5 30.0 %copy-start.25 = (f32[2048,2]{0,1:T(2,128)}, f32[2048,2]{0,1:T(2,128)S(1)}, u32[]{:S(2)}) copy-start(f32[2048,2]{0,1:T(2,128)S(1)} %get-tuple-element.340) | copy-start | bytes 49156
  601.3 65.2 %all-to-all-start.2 = ((bf16[8,2,80,1024]{3,2,1,0:T(8,128)(2,1)}), bf16[8,2,80,1024]{3,2,1,0:T(8,128)(2,1)}, u32[]{:S(2)}, u32[]{:S(2)}) async-start(bf16[8,2,80,1024]{3,2,1,0:T(8,128)(2,1)} %constant_dynamic-slice_fusion.2), calls=%async_computation.3 | async-start | bytes 5242880 | tf_op jit(solution)/shard_map/all_to_all | solution.py:87
  666.5 234.0 %all-to-all-start = ((bf16[8,2,320,1024]{3,2,1,0:T(8,128)(2,1)}), bf16[8,2,320,1024]{3,2,1,0:T(8,128)(2,1)}, u32[]{:S(2)}, u32[]{:S(2)}) async-start(bf16[8,2,320,1024]{3,2,1,0:T(8,128)(2,1)} %bitcast.308), calls=%async_computation | async-start | bytes 20971520 | tf_op jit(solution)/shard_map/all_to_all | solution.py:255
  671.7 259.3 %all-gather.6.cloned.1.call-start = ((), (), s32[]{:S(2)}) async-start(), calls=%async_computation.9 | async-start | bytes 13107200 | tf_op jit(solution)/shard_map/all_gather | solution.py:83
  675.4 507.9 %reduce-scatter.5.cloned.1.call-start = ((), (), s32[]{:S(2)}) async-start(), calls=%async_computation.10 | async-start | bytes 26214400 | tf_op jit(solution)/shard_map/reduce_scatter | solution.py:91
  900.6 15.2 copy-start.50
  931.0 32.3 %copy-start.51 = (bf16[2,704,1024]{2,1,0:T(8,128)(2,1)S(1)}, bf16[2,704,1024]{2,1,0:T(8,128)(2,1)}, u32[]{:S(2)}) copy-start(bf16[2,704,1024]{2,1,0:T(8,128)(2,1)} %param.24) | copy-start | bytes 8650756
  996.7 377.4 %reduce-scatter.3.cloned.1.call-start = ((), (), s32[]{:S(2)}) async-start(), calls=%async_computation.7 | async-start | bytes 26214400 | tf_op jit(solution)/shard_map/reduce_scatter | solution.py:91
  1011.8 469.2 %all-gather.8.cloned.1.call-start = ((), (), s32[]{:S(2)}) async-start(), calls=%async_computation.11 | async-start | bytes 13107200 | tf_op jit(solution)/shard_map/all_gather | solution.py:83
  1251.3 336.7 %all-gather.4.cloned.1.call-start = ((), (), s32[]{:S(2)}) async-start(), calls=%async_computation.8 | async-start | bytes 13107200 | tf_op jit(solution)/shard_map/all_gather | solution.py:83
  1377.0 65.2 %copy-start.37 = (s32[2048,2]{0,1:T(2,128)S(1)}, s32[2048,2]{0,1:T(2,128)}, u32[]{:S(2)}) copy-start(s32[2048,2]{0,1:T(2,128)} %get-tuple-element.359) | copy-start | bytes 49156
  1377.0 66.1 %copy-start.22 = (s32[2048,2]{0,1:T(2,128)S(1)}, s32[2048,2]{0,1:T(2,128)}, u32[]{:S(2)}) copy-start(s32[2048,2]{0,1:T(2,128)} %copy-done.21) | copy-start | bytes 49156
  1377.0 66.5 %copy-start.36 = (f32[2048,2]{0,1:T(2,128)S(1)}, f32[2048,2]{0,1:T(2,128)}, u32[]{:S(2)}) copy-start(f32[2048,2]{0,1:T(2,128)} %get-tuple-element.339) | copy-start | bytes 49156
  1442.1 669.1 %all-reduce.13.cloned.1.call-start = ((), (), s32[]{:S(2)}) async-start(), calls=%async_computation.13 | async-start | bytes 4194304 | tf_op jit(solution)/shard_map/psum | solution.py:323
  1632.2 37.7 %copy-start.26 = (f32[2048,2]{0,1:T(2,128)S(1)}, f32[2048,2]{0,1:T(2,128)}, u32[]{:S(2)}) copy-start(f32[2048,2]{0,1:T(2,128)} %copy-done.25) | copy-start | bytes 49156
  1632.2 37.8 %copy-start.24 = (s32[2048,2]{0,1:T(2,128)S(1)}, s32[2048,2]{0,1:T(2,128)}, u32[]{:S(2)}) copy-start(s32[2048,2]{0,1:T(2,128)} %param.27) | copy-start | bytes 49156
  1670.1 25.9 %copy-start.17 = (f32[2048,16]{0,1:T(8,128)}, f32[2048,16]{0,1:T(8,128)S(1)}, u32[]{:S(2)}) copy-start(f32[2048,16]{0,1:T(8,128)S(1)} %select_reduce_fusion) | copy-start | bytes 393220
  1670.1 25.9 %copy-start.30 = (bf16[1024,16]{0,1:T(8,128)(2,1)S(1)}, bf16[1024,16]{0,1:T(8,128)(2,1)}, u32[]{:S(2)}) copy-start(bf16[1024,16]{0,1:T(8,128)(2,1)} %param.23) | copy-start | bytes 98308
  1670.1 25.9 %copy-start.32 = (f32[2048]{0:T(1024)S(1)}, f32[2048]{0:T(1024)}, u32[]{:S(2)}) copy-start(f32[2048]{0:T(1024)} %copy-done.31) | copy-start | bytes 24580
  1670.1 25.9 %copy-start.39 = (f32[1024]{0:T(1024)S(1)}, f32[1024]{0:T(1024)}, u32[]{:S(2)}) copy-start(f32[1024]{0:T(1024)} %param.22) | copy-start | bytes 12292
  1695.9 11.6 copy-start.41
  1707.6 13.3 copy-start.12
  1720.8 3.6 copy-start.2
  1720.8 3.6 copy-start.16
  1724.4 7.2 copy-start.7
  1724.4 7.2 copy-start.28
  1724.4 7.2 copy-start.43
  1787.5 4.3 copy-start.13
  1791.9 1.7 copy-start.14
  1854.9 4.3 copy-start.13
  1861.5 12.9 copy-start.34
  1861.5 12.9 copy-start.45
  1874.4 8.0 copy-start.52
  1882.4 240.8 %all-reduce.11.cloned.1.call-start = ((), (), s32[]{:S(2)}) async-start(), calls=%async_computation.12 | async-start | bytes 16777216 | tf_op jit(solution)/shard_map/psum | solution.py:79
  2089.5 19.3 copy-start.49
  2089.5 20.0 copy-start.5
  2089.5 20.0 copy-start.18
  2108.8 14.4 copy-start.35
  2108.8 14.4 copy-start.46
  2113.3 16.8 copy-start.40
  2123.2 7.0 copy-start.6
  2123.2 8.3 copy-start.9
  2131.5 47.7 %copy-start.1 = (bf16[2,704,1024]{2,1,0:T(8,128)(2,1)S(1)}, bf16[2,704,1024]{2,1,0:T(8,128)(2,1)}, u32[]{:S(2)}) copy-start(bf16[2,704,1024]{2,1,0:T(8,128)(2,1)} %param.26) | copy-start | bytes 8650756
  2138.7 9.1 copy-start.47
  (6 other events, 7.8 us)
Sparse Core Ops, SparseCore 0:
  372.1 174.7 all-reduce.8
  675.5 106.0 all-gather.5
  996.8 186.3 reduce-scatter.4
  1186.2 187.8 reduce-scatter.2
  1375.9 105.0 all-gather.7
  1482.8 105.0 all-gather.3
  1882.5 64.9 all-reduce.12
  1951.5 171.6 all-reduce.10
where the time goes:
time: 2200 us; the launch traced here: 2190 us
  waiting for transfers between devices  724 us (33%)
  local copies, waits for them, and re-layouts  696 us (32%)
  matrix products  329 us (15%)
  other arithmetic  253 us (12%)
  blocking collectives  159 us (7%)
    reduce_scatter x2, waiting for transfers between devices, expert_sums(): lax.psum_scatter(tensor_value, 'tensor', scatter_dimension=2, tiled=True)  294 us
    unnamed x108, local copies, waits for them, and re-layouts  247 us
    all_to_all x1, waiting for transfers between devices, on_device(): lax.all_to_all(buffer, 'expert', split_axis=0, concat_axis=0, tiled=True)  225 us
    all_to_all x2, blocking collectives, owner_exchange(): lax.all_to_all(tensor_value, 'expert', split_axis=0, concat_axis=0, tiled...  130 us
    psum x2, waiting for transfers between devices, reduce_heads(): return lax.psum(tensor_value, 'tensor')  121 us
    all_gather x3, waiting for transfers between devices, spread_slots(): return lax.all_gather(tensor_value, 'tensor', axis=2, tiled=True)  77.7 us
    dot_general x4, matrix products, attend_scores(): jnp.einsum('qhe,khe->hqk', queries, key_rows, preferred_element_type=jnp....  68.4 us
    gather x2, local copies, waits for them, and re-layouts, on_device(): flat_back[safe_index] * keep_float[:, :, None]  50.1 us
  transfers between devices with their start and end apart: 10, of which 8 were waited for; matrix products, arithmetic and copies ran while one was open for 22% of the time, Pallas kernels for 0%

commit v1 on v0

--- a/solution.py
+++ b/solution.py
@@ -3,6 +3,8 @@
 import jax
 import jax.numpy as jnp
 from jax import lax
+from jax.experimental import pallas as pl
+from jax.experimental.pallas import tpu as pltpu
 from jax.sharding import PartitionSpec as P
 
 EXPERTS = 16
@@ -11,12 +13,33 @@
 PIECE = 256
 SEQ = 1024
 CAP = 320
+BLK = 256
 
 
 EPS = 1e-06
 NEG = -1e30
 THRESHOLDS = (12, 16, 23, 32, 46, 64, 91)
 HIGH = lax.Precision.HIGHEST
+F32 = jnp.float32
+BF16 = jnp.bfloat16
+NN = (((1,), (0,)), ((), ()))
+NT = (((1,), (1,)), ((), ()))
+TN = (((0,), (0,)), ((), ()))
+MIB = 1 << 20
+
+
+def mm(left, right, dims=NN):
+    return lax.dot_general(left, right, dims, preferred_element_type=F32)
+
+
+def params(limit=56):
+    return pltpu.CompilerParams(vmem_limit_bytes=limit * MIB)
+
+
+def cost(flops, bytes_accessed, transcendentals=0):
+    return pl.CostEstimate(
+        flops=int(flops), bytes_accessed=int(bytes_accessed), transcendentals=int(transcendentals)
+    )
 
 
 def bucket_of(offset):
@@ -26,6 +49,739 @@
     return lower_part + 16 * (offset > 0).astype(jnp.int32)
 
 
+def project_kernel(x_ref, gain_ref, w_ref, out_ref, scale_ref):
+    x = x_ref[...].astype(F32)
+    scale = lax.rsqrt(jnp.sum(x * x, axis=0, keepdims=True) / x.shape[0] + EPS)
+    normed = (x * scale * gain_ref[...]).astype(BF16)
+    out_ref[...] = mm(w_ref[...], normed).astype(BF16)
+    scale_ref[...] = scale
+
+
+def project(x, gain, weights):
+    width, tokens = x.shape
+    rows = weights.shape[0]
+    tile = 512
+    return pl.pallas_call(
+        project_kernel,
+        grid=(tokens // tile,),
+        in_specs=[
+            pl.BlockSpec((width, tile), lambda i: (0, i)),
+            pl.BlockSpec((width, 1), lambda i: (0, 0)),
+            pl.BlockSpec((rows, width), lambda i: (0, 0)),
+        ],
+        out_specs=[
+            pl.BlockSpec((rows, tile), lambda i: (0, i)),
+            pl.BlockSpec((1, tile), lambda i: (0, i)),
+        ],
+        out_shape=[
+            jax.ShapeDtypeStruct((rows, tokens), BF16),
+            jax.ShapeDtypeStruct((1, tokens), F32),
+        ],
+        compiler_params=params(),
+        cost_estimate=cost(2 * width * tokens * rows, 2 * width * tokens * 2),
+    )(x, gain, weights)
+
+
+def bias_tiles_kernel(table_ref, tiles_ref):
+    key_at = lax.broadcasted_iota(jnp.int32, (BLK, BLK), 0)
+    query_at = lax.broadcasted_iota(jnp.int32, (BLK, BLK), 1)
+    for number, shift in enumerate((-1, 0, 1)):
+        offset = key_at - query_at + shift * BLK
+        bucket = bucket_of(offset)
+        low, high = {-1: (0, 16), 0: (0, 32), 1: (16, 32)}[shift]
+        for head in range(tiles_ref.shape[0]):
+            far = table_ref[15, head]
+            value = jnp.zeros((BLK, BLK), F32)
+            for index in range(low, high):
+                value = jnp.where(bucket == index, table_ref[index, head] - far, value)
+            tiles_ref[head, number] = value
+
+
+def bias_tiles(table):
+    heads = table.shape[1]
+    return pl.pallas_call(
+        bias_tiles_kernel,
+        in_specs=[pl.BlockSpec(memory_space=pltpu.SMEM)],
+        out_specs=pl.BlockSpec(memory_space=pltpu.VMEM),
+        out_shape=jax.ShapeDtypeStruct((heads, 3, BLK, BLK), F32),
+        compiler_params=params(),
+        cost_estimate=cost(heads * 3 * BLK * BLK * 60, heads * 3 * BLK * BLK * 4),
+    )(table)
+
+
+def bias_fold_kernel(near_ref, far_ref, out_ref):
+    heads = near_ref.shape[1]
+    key_at = lax.broadcasted_iota(jnp.int32, (BLK, BLK), 0)
+    query_at = lax.broadcasted_iota(jnp.int32, (BLK, BLK), 1)
+    totals = [[jnp.zeros((8, BLK), F32) for _ in range(BUCKETS)] for _ in range(heads)]
+    for number, shift in enumerate((-1, 0, 1)):
+        bucket = bucket_of(key_at - query_at + shift * BLK)
+        low, high = {-1: (0, 16), 0: (0, 32), 1: (16, 32)}[shift]
+        for head in range(heads):
+            grads = near_ref[0, head, number] + near_ref[1, head, number]
+            for index in range(low, high):
+                kept = jnp.where(bucket == index, grads, 0.0)
+                totals[head][index] = totals[head][index] + jnp.sum(
+                    kept.reshape(BLK // 8, 8, BLK), axis=0
+                )
+    for head in range(heads):
+        totals[head][15] = totals[head][15] + far_ref[0, head] + far_ref[1, head]
+        for index in range(BUCKETS):
+            line = jnp.sum(totals[head][index], axis=0, keepdims=True)
+            out_ref[head, index : index + 1, :] = jnp.broadcast_to(
+                jnp.sum(line, axis=1, keepdims=True), (1, 128)
+            )
+
+
+def bias_fold(near, far):
+    heads = near.shape[1]
+    return pl.pallas_call(
+        bias_fold_kernel,
+        in_specs=[pl.BlockSpec(memory_space=pltpu.VMEM)] * 2,
+        out_specs=pl.BlockSpec(memory_space=pltpu.VMEM),
+        out_shape=jax.ShapeDtypeStruct((heads, BUCKETS, 128), F32),
+        compiler_params=params(),
+        cost_estimate=cost(heads * 3 * BLK * BLK * 60, heads * 6 * BLK * BLK * 4),
+    )(near, far)
+
+
+def key_count(query_block):
+    return 2 * BLK if query_block < 2 else 4 * BLK
+
+
+def block_scores(keys, queries, tiles_ref, limit, block):
+    count = key_count(block)
+    parts = []
+    whole = mm(keys[:, :count], queries, TN)
+    for key_block in range(count // BLK):
+        part = whole[key_block * BLK : (key_block + 1) * BLK]
+        shift = key_block - block
+        if -1 <= shift <= 1:
+            part = part + tiles_ref[0, shift + 1]
+        if shift >= 0:
+            key_at = lax.broadcasted_iota(jnp.int32, (BLK, BLK), 0) + key_block * BLK
+            part = jnp.where(key_at <= limit, part, NEG)
+        parts.append(part)
+    return jnp.concatenate(parts, axis=0)
+
+
+def attend_kernel(q_ref, k_ref, v_ref, tiles_ref, limit_ref, w_ref, out_ref, lse_ref, sent_ref, held):
+    head = pl.program_id(0)
+    width = q_ref.shape[0]
+    queries = q_ref[...] * BF16(0.125)
+    keys, values = k_ref[...], v_ref[...]
+    for block in range(SEQ // BLK):
+        cols = slice(block * BLK, (block + 1) * BLK)
+        scores = block_scores(keys, queries[:, cols], tiles_ref, limit_ref[0, :, cols], block)
+        top = jnp.max(scores, axis=0, keepdims=True)
+        exponent = jnp.exp(scores - top)
+        total = jnp.sum(exponent, axis=0, keepdims=True)
+        mixed = mm(values[:, : key_count(block)], exponent.astype(BF16)) / total
+        mixed = mixed.astype(BF16)
+        out_ref[:, cols] = mixed
+        held[pl.ds(pl.multiple_of(head * width, width), width), cols] = mixed
+        lse_ref[0, :, cols] = top + jnp.log(total)
+
+    @pl.when(head == pl.num_programs(0) - 1)
+    def _():
+        sent_ref[...] = mm(held[...], w_ref[...], TN).astype(BF16)
+
+
+def attend(qkv, tiles, limits, attn_out, seq):
+    heads = tiles.shape[0]
+    width = qkv.shape[0] // (3 * heads)
+    model_width = attn_out.shape[1]
+    return pl.pallas_call(
+        attend_kernel,
+        grid=(heads,),
+        in_specs=[
+            pl.BlockSpec((width, SEQ), lambda h: (h, seq)),
+            pl.BlockSpec((width, SEQ), lambda h: (heads + h, seq)),
+            pl.BlockSpec((width, SEQ), lambda h: (2 * heads + h, seq)),
+            pl.BlockSpec((1, 3, BLK, BLK), lambda h: (h, 0, 0, 0)),
+            pl.BlockSpec((1, 1, SEQ), lambda h: (seq, 0, 0)),
+            pl.BlockSpec((heads * width, model_width), lambda h: (0, 0)),
+        ],
+        out_specs=[
+            pl.BlockSpec((width, SEQ), lambda h: (h, 0)),
+            pl.BlockSpec((1, 1, SEQ), lambda h: (h, 0, 0)),
+            pl.BlockSpec((SEQ, model_width), lambda h: (0, 0)),
+        ],
+        out_shape=[
+            jax.ShapeDtypeStruct((heads * width, SEQ), BF16),
+            jax.ShapeDtypeStruct((heads, 1, SEQ), F32),
+            jax.ShapeDtypeStruct((SEQ, model_width), BF16),
+        ],
+        scratch_shapes=[pltpu.VMEM((heads * width, SEQ), BF16)],
+        compiler_params=params(),
+        cost_estimate=cost(heads * SEQ * SEQ * 512, heads * SEQ * 2048, heads * SEQ * SEQ),
+    )(qkv, qkv, qkv, tiles, limits, attn_out)
+
+
+def attend_back_kernel(
+    q_ref, k_ref, v_ref, tiles_ref, limit_ref, w_ref, grad_ref, lse_ref,
+    dq_ref, dk_ref, dv_ref, near_ref, far_ref, held,
+):
+    head = pl.program_id(0)
+    width = q_ref.shape[0]
+
+    @pl.when(head == 0)
+    def _():
+        held[...] = mm(w_ref[...], grad_ref[...], NT).astype(BF16)
+
+    queries = q_ref[...] * BF16(0.125)
+    keys, values = k_ref[...], v_ref[...]
+    grads = held[pl.ds(pl.multiple_of(head * width, width), width), :]
+    near_ref[...] = jnp.zeros_like(near_ref)
+    far = jnp.zeros((8, BLK), F32)
+    grad_keys = jnp.zeros((width, SEQ), F32)
+    grad_values = jnp.zeros((width, SEQ), F32)
+    for block in range(SEQ // BLK):
+        count = key_count(block)
+        cols = slice(block * BLK, (block + 1) * BLK)
+        scores = block_scores(keys, queries[:, cols], tiles_ref, limit_ref[0, :, cols], block)
+        probs = jnp.exp(scores - lse_ref[0, :, cols])
+        grad_probs = mm(values[:, :count], grads[:, cols], TN)
+        inner = jnp.sum(probs * grad_probs, axis=0, keepdims=True)
+        grad_scores = probs * (grad_probs - inner)
+        for key_block in range(count // BLK):
+            part = grad_scores[key_block * BLK : (key_block + 1) * BLK]
+            shift = key_block - block
+            if -1 <= shift <= 1:
+                near_ref[0, shift + 1] += part
+            elif shift < -1:
+                far = far + jnp.sum(part.reshape(BLK // 8, 8, BLK), axis=0)
+        rounded = grad_scores.astype(BF16)
+        add_values = mm(grads[:, cols], probs.astype(BF16), NT)
+        add_keys = mm(queries[:, cols], rounded, NT)
+        if count == SEQ:
+            grad_values = grad_values + add_values
+            grad_keys = grad_keys + add_keys
+        else:
+            filler = jnp.zeros((width, SEQ - count), F32)
+            grad_values = grad_values + jnp.concatenate([add_values, filler], axis=1)
+            grad_keys = grad_keys + jnp.concatenate([add_keys, filler], axis=1)
+        dq_ref[0, :, cols] = (mm(keys[:, :count], rounded) * 0.125).astype(BF16)
+    dk_ref[0] = grad_keys.astype(BF16)
+    dv_ref[0] = grad_values.astype(BF16)
+    far_ref[0] = far
+
+
+def attend_back(qkv, tiles, limits, attn_out, grad_attn, lse, seq):
+    heads = tiles.shape[0]
+    width = qkv.shape[0] // (3 * heads)
+    model_width = attn_out.shape[1]
+    grad_spec = pl.BlockSpec((1, width, SEQ), lambda h: (h, 0, 0))
+    return pl.pallas_call(
+        attend_back_kernel,
+        grid=(heads,),
+        in_specs=[
+            pl.BlockSpec((width, SEQ), lambda h: (h, seq)),
+            pl.BlockSpec((width, SEQ), lambda h: (heads + h, seq)),
+            pl.BlockSpec((width, SEQ), lambda h: (2 * heads + h, seq)),
+            pl.BlockSpec((1, 3, BLK, BLK), lambda h: (h, 0, 0, 0)),
+            pl.BlockSpec((1, 1, SEQ), lambda h: (seq, 0, 0)),
+            pl.BlockSpec((heads * width, model_width), lambda h: (0, 0)),
+            pl.BlockSpec((SEQ, model_width), lambda h: (0, 0)),
+            pl.BlockSpec((1, 1, SEQ), lambda h: (h, 0, 0)),
+        ],
+        out_specs=[
+            grad_spec,
+            grad_spec,
+            grad_spec,
+            pl.BlockSpec((1, 3, BLK, BLK), lambda h: (h, 0, 0, 0)),
+            pl.BlockSpec((1, 8, BLK), lambda h: (h, 0, 0)),
+        ],
+        out_shape=[jax.ShapeDtypeStruct((heads, width, SEQ), BF16)] * 3
+        + [
+            jax.ShapeDtypeStruct((heads, 3, BLK, BLK), F32),
+            jax.ShapeDtypeStruct((heads, 8, BLK), F32),
+        ],
+        scratch_shapes=[pltpu.VMEM((heads * width, SEQ), BF16)],
+        compiler_params=params(),
+        cost_estimate=cost(heads * SEQ * SEQ * 1280, heads * SEQ * 4096, heads * SEQ * SEQ),
+    )(qkv, qkv, qkv, tiles, limits, attn_out, grad_attn, lse)
+
+
+def project_back_kernel(
+    x_ref, gain_ref, scale_ref, w_ref, *refs
+):
+    grad_refs, (weight_ref, out_ref) = refs[:3], refs[3:]
+    grads = jnp.concatenate([ref[...] for ref in grad_refs], axis=0)
+    normed = (x_ref[...].astype(F32) * scale_ref[...] * gain_ref[...]).astype(BF16)
+    update = mm(grads, normed, NT)
+
+    @pl.when(pl.program_id(0) == 0)
+    def _():
+        weight_ref[...] = update
+
+    @pl.when(pl.program_id(0) > 0)
+    def _():
+        weight_ref[...] += update
+
+    out_ref[0] = mm(w_ref[...], grads).astype(BF16)
+
+
+def project_back(x, gain, scale, weights_t, grads, seq, ranks):
+    width = x.shape[0]
+    rows = weights_t.shape[1]
+    tile = SEQ // ranks
+    return pl.pallas_call(
+        project_back_kernel,
+        grid=(ranks,),
+        in_specs=[
+            pl.BlockSpec((width, tile), lambda i: (0, seq * ranks + i)),
+            pl.BlockSpec((width, 1), lambda i: (0, 0)),
+            pl.BlockSpec((1, tile), lambda i: (0, seq * ranks + i)),
+            pl.BlockSpec((width, rows), lambda i: (0, 0)),
+        ]
+        + [pl.BlockSpec((rows // 3, tile), lambda i: (0, i))] * 3,
+        out_specs=[
+            pl.BlockSpec((rows, width), lambda i: (0, 0)),
+            pl.BlockSpec((1, width, tile), lambda i: (i, 0, 0)),
+        ],
+        out_shape=[
+            jax.ShapeDtypeStruct((rows, width), F32),
+            jax.ShapeDtypeStruct((ranks, width, tile), BF16),
+        ],
+        compiler_params=params(),
+        cost_estimate=cost(4 * width * SEQ * rows, 6 * width * SEQ),
+    )(x, gain, scale, weights_t, *grads)
+
+
+def code_kernel(place_ref, routes_ref, code_ref, half, groups):
+    pair_class, half_index = place_ref[0], place_ref[1]
+    tokens = routes_ref.shape[1]
+    expert = lax.broadcasted_iota(jnp.int32, (EXPERTS, BLK), 0)
+    earlier = (
+        lax.broadcasted_iota(jnp.int32, (BLK, BLK), 0) < lax.broadcasted_iota(jnp.int32, (BLK, BLK), 1)
+    ).astype(F32).astype(BF16)
+    carry = jnp.zeros((EXPERTS, 1), F32)
+    for block in range(tokens // BLK):
+        cols = slice(block * BLK, (block + 1) * BLK)
+        routes = routes_ref[:, cols]
+        hits = [(routes[i : i + 1] == expert) for i in range(TOP)]
+        chosen = sum(hit.astype(F32) for hit in hits)
+        before = mm(chosen.astype(BF16), earlier) + carry
+        carry = carry + jnp.sum(chosen, axis=1, keepdims=True)
+        for i in range(TOP):
+            slot = jnp.sum(jnp.where(hits[i], before, 0.0), axis=0, keepdims=True).astype(jnp.int32)
+            route = routes[i : i + 1]
+            owner = route // 2
+            local = slot - half_index * half
+            mine = (route - 2 * owner == pair_class) & (local >= 0) & (local < half)
+            code_ref[i : i + 1, cols] = jnp.where(mine, owner * half + local, -1)
+
+
+def local_codes(place, routes_t, half, groups):
+    return pl.pallas_call(
+        partial(code_kernel, half=half, groups=groups),
+        in_specs=[
+            pl.BlockSpec(memory_space=pltpu.SMEM),
+            pl.BlockSpec(memory_space=pltpu.VMEM),
+        ],
+        out_specs=pl.BlockSpec(memory_space=pltpu.VMEM),
+        out_shape=jax.ShapeDtypeStruct(routes_t.shape, jnp.int32),
+        compiler_params=params(),
+    )(place, routes_t)
+
+
+def gates_kernel(h0_ref, h1_ref, router_ref, routes_ref, gates_ref):
+    expert = lax.broadcasted_iota(jnp.int32, (EXPERTS, SEQ), 0)
+    for seq, ref in enumerate((h0_ref, h1_ref)):
+        cols = slice(seq * SEQ, (seq + 1) * SEQ)
+        logits = mm(router_ref[...], ref[...], NT)
+        picked = [
+            jnp.sum(jnp.where(routes_ref[i : i + 1, cols] == expert, logits, 0.0), axis=0, keepdims=True)
+            for i in range(TOP)
+        ]
+        top = jnp.maximum(picked[0], picked[1])
+        raised = [jnp.exp(value - top) for value in picked]
+        total = raised[0] + raised[1]
+        for i in range(TOP):
+            gates_ref[i : i + 1, cols] = raised[i] / total
+
+
+def pair_gates(h0, h1, router_t, routes_t):
+    return pl.pallas_call(
+        gates_kernel,
+        in_specs=[pl.BlockSpec(memory_space=pltpu.VMEM)] * 4,
+        out_specs=pl.BlockSpec(memory_space=pltpu.VMEM),
+        out_shape=jax.ShapeDtypeStruct(routes_t.shape, F32),
+        compiler_params=params(),
+        cost_estimate=cost(2 * routes_t.shape[1] * EXPERTS * 1024 * 8, 4 * MIB),
+    )(h0, h1, router_t, routes_t)
+
+
+def dispatch_kernel(code_ref, gates_ref, h0_ref, h1_ref, dy_ref, rows_ref, grads_ref, dy_rows_ref, gate_ref):
+    count = rows_ref.shape[0]
+    slot = lax.broadcasted_iota(jnp.int32, (count, SEQ), 0) + pl.program_id(0) * count
+    rows = jnp.zeros(rows_ref.shape, F32)
+    dy_rows = jnp.zeros(rows_ref.shape, F32)
+    gate = jnp.zeros((count, 1), F32)
+    for seq, ref in enumerate((h0_ref, h1_ref)):
+        cols = slice(seq * SEQ, (seq + 1) * SEQ)
+        hits = [slot == code_ref[i : i + 1, cols] for i in range(TOP)]
+        take = jnp.where(hits[0] | hits[1], 1.0, 0.0).astype(BF16)
+        weighted = jnp.where(hits[0], gates_ref[0:1, cols], jnp.where(hits[1], gates_ref[1:2, cols], 0.0))
+        gate = gate + jnp.sum(weighted, axis=1, keepdims=True)
+        rows = rows + mm(take, ref[...])
+        dy_rows = dy_rows + mm(take, dy_ref[cols, :])
+    rows_ref[...] = rows.astype(BF16)
+    dy_rows_ref[...] = dy_rows.astype(BF16)
+    grads_ref[...] = (dy_rows * gate).astype(BF16)
+    gate_ref[...] = gate
+
+
+def dispatch(code, gates, h0, h1, dy, slots):
+    width = h0.shape[1]
+    tile = slots // 4
+    row_spec = pl.BlockSpec((tile, width), lambda i: (i, 0))
+    whole = lambda shape: pl.BlockSpec(shape, lambda i: (0, 0))
+    return pl.pallas_call(
+        dispatch_kernel,
+        grid=(4,),
+        in_specs=[whole(code.shape), whole(gates.shape), whole(h0.shape), whole(h1.shape), whole(dy.shape)],
+        out_specs=[row_spec, row_spec, row_spec, pl.BlockSpec((tile, 1), lambda i: (i, 0))],
+        out_shape=[jax.ShapeDtypeStruct((slots, width), BF16)] * 3
+        + [jax.ShapeDtypeStruct((slots, 1), F32)],
+        compiler_params=params(),
+        cost_estimate=cost(8 * slots * SEQ * width, 8 * MIB + 6 * slots * width),
+    )(code, gates, h0, h1, dy)
+
+
+def gelu_parts(x):
+    inner = 0.7978845608028654 * (x + 0.044715 * (x * x * x))
+    bend = jnp.tanh(inner)
+    half = 0.5 * (1.0 + bend)
+    slope = half + 0.5 * x * (1.0 - bend * bend) * (
+        0.7978845608028654 * (1.0 + 3.0 * 0.044715 * (x * x))
+    )
+    return x * half, slope
+
+
+def expert_kernel(
+    rows_ref, grads_ref, gate_ref, up_ref, down_ref, ret_ref, back_ref,
+    own_gate, own_up, own_down, far_gate, far_up, far_down,
+    acc_gate, acc_up, acc_down, far_buf, sems,
+):
+    step = pl.program_id(0)
+    rows, grads = rows_ref[...], grads_ref[...]
+    half = gate_ref.shape[1]
+
+    @pl.when(step == 0)
+    def _():
+        for acc in (acc_gate, acc_up, acc_down):
+            acc[...] = jnp.zeros_like(acc)
+
+    ret = jnp.zeros(rows.shape, F32)
+    back = jnp.zeros(rows.shape, F32)
+    for part in range(2):
+        w_gate, w_up, w_down = gate_ref[part], up_ref[part], down_ref[part]
+        gate_part = mm(rows, w_gate, NT)
+        up_part = mm(rows, w_up, NT)
+        grad_hidden = mm(grads, w_down, NT)
+        bent, slope = gelu_parts(gate_part)
+        hidden = (bent * up_part).astype(BF16)
+        grad_gate = (grad_hidden * up_part * slope).astype(BF16)
+        grad_up = (grad_hidden * bent).astype(BF16)
+        ret = ret + mm(hidden, w_down)
+        back = back + mm(grad_gate, w_gate) + mm(grad_up, w_up)
+        acc_down[part] += mm(hidden, grads, TN)
+        acc_gate[part] += mm(grad_gate, rows, TN)
+        acc_up[part] += mm(grad_up, rows, TN)
+    ret_ref[...] = ret.astype(BF16)
+    back_ref[...] = back.astype(BF16)
+
+    @pl.when(step == pl.num_programs(0) - 1)
+    def _():
+        copies = []
+        triples = ((acc_gate, own_gate, far_gate), (acc_up, own_up, far_up), (acc_down, own_down, far_down))
+        for number, (acc, own, far) in enumerate(triples):
+            copies.append(pltpu.make_async_copy(acc.at[0], own, sems.at[2 * number]))
+            copies[-1].start()
+            far_buf[number] = acc[1].astype(BF16)
+            copies.append(pltpu.make_async_copy(far_buf.at[number], far, sems.at[2 * number + 1]))
+            copies[-1].start()
+        for copy in copies:
+            copy.wait()
+
+
+def run_experts(rows, grads, w_gate, w_up, w_down):
+    total, width = rows.shape
+    units = w_gate.shape[1]
+    tile = total // 5
+    weight_spec = pl.BlockSpec((2, units, width), lambda i: (0, 0, 0), pipeline_mode=pl.Buffered(1))
+    row_spec = pl.BlockSpec((tile, width), lambda i: (i, 0))
+    anywhere = pl.BlockSpec(memory_space=pl.ANY)
+    return pl.pallas_call(
+        expert_kernel,
+        grid=(5,),
+        in_specs=[row_spec, row_spec, weight_spec, weight_spec, weight_spec],
+        out_specs=[row_spec, row_spec] + [anywhere] * 6,
+        out_shape=[jax.ShapeDtypeStruct((total, width), BF16)] * 2
+        + [jax.ShapeDtypeStruct((units, width), F32)] * 3
+        + [jax.ShapeDtypeStruct((units, width), BF16)] * 3,
+        scratch_shapes=[pltpu.VMEM((2, units, width), F32)] * 3
+        + [pltpu.VMEM((3, units, width), BF16), pltpu.SemaphoreType.DMA((6,))],
+        compiler_params=params(60),
+        cost_estimate=cost(36 * total * units * width, 8 * total * width + 30 * units * width),
+    )(rows, grads, w_gate, w_up, w_down)
+
+
+def pair_grads_kernel(code_ref, gates_ref, routes_ref, dy_rows_ref, ret_ref, gate_ref, logit_ref, scaled_ref):
+    slots = ret_ref.shape[0]
+    tokens = code_ref.shape[1]
+    found = [jnp.zeros((1, tokens), F32) for _ in range(TOP)]
+    tile = 320
+    for start in range(0, slots, tile):
+        span = slice(start, start + tile)
+        ret = ret_ref[span, :].astype(F32)
+        slot_grad = jnp.sum(dy_rows_ref[span, :].astype(F32) * ret, axis=1, keepdims=True)
+        scaled_ref[span, :] = (ret * gate_ref[span, :]).astype(BF16)
+        slot = lax.broadcasted_iota(jnp.int32, (tile, tokens), 0) + start
+        for i in range(TOP):
+            found[i] = found[i] + jnp.sum(
+                jnp.where(slot == code_ref[i : i + 1, :], slot_grad, 0.0), axis=0, keepdims=True
+            )
+    mean = gates_ref[0:1] * found[0] + gates_ref[1:2] * found[1]
+    expert = lax.broadcasted_iota(jnp.int32, (EXPERTS, tokens), 0)
+    logit_ref[...] = sum(
+        jnp.where(routes_ref[i : i + 1] == expert, gates_ref[i : i + 1] * (found[i] - mean), 0.0)
+        for i in range(TOP)
+    )
+
+
+def pair_grads(code, gates, routes_t, dy_rows, ret, gate_rows):
+    return pl.pallas_call(
+        pair_grads_kernel,
+        in_specs=[pl.BlockSpec(memory_space=pltpu.VMEM)] * 6,
+        out_specs=[pl.BlockSpec(memory_space=pltpu.VMEM)] * 2,
+        out_shape=[
+            jax.ShapeDtypeStruct((EXPERTS, code.shape[1]), F32),
+            jax.ShapeDtypeStruct(ret.shape, BF16),
+        ],
+        compiler_params=params(),
+        cost_estimate=cost(ret.shape[0] * code.shape[1] * 16, 6 * ret.size),
+    )(code, gates, routes_t, dy_rows, ret, gate_rows)
+
+
+def spread_kernel(code_ref, rows_ref, *refs):
+    out_ref = refs[-1]
+    tile = out_ref.shape[0]
+    slot = lax.broadcasted_iota(jnp.int32, (tile, rows_ref.shape[0]), 1)
+    code = code_ref[...]
+    place = jnp.where((slot == code[:, 0:1]) | (slot == code[:, 1:2]), 1.0, 0.0).astype(BF16)
+    value = mm(place, rows_ref[...])
+    if len(refs) == 3:
+        logit, router = refs[0][...], refs[1][...]
+        coarse = logit.astype(BF16)
+        fine = (logit - coarse.astype(F32)).astype(BF16)
+        value = value + mm(coarse, router, NT) + mm(fine, router, NT)
+    out_ref[...] = value.astype(BF16)
+
+
+def spread(code_cols, rows, logit=None, router=None):
+    tokens, width = code_cols.shape[0], rows.shape[1]
+    tile = 512
+    specs = [
+        pl.BlockSpec((tile, TOP), lambda i: (i, 0)),
+        pl.BlockSpec(rows.shape, lambda i: (0, 0)),
+    ]
+    operands = [code_cols, rows]
+    if logit is not None:
+        specs += [
+            pl.BlockSpec((tile, EXPERTS), lambda i: (i, 0)),
+            pl.BlockSpec(router.shape, lambda i: (0, 0)),
+        ]
+        operands += [logit, router]
+    return pl.pallas_call(
+        spread_kernel,
+        grid=(tokens // tile,),
+        in_specs=specs,
+        out_specs=pl.BlockSpec((tile, width), lambda i: (i, 0)),
+        out_shape=jax.ShapeDtypeStruct((tokens, width), BF16),
+        compiler_params=params(),
+        cost_estimate=cost(2 * tokens * width * rows.shape[0], 2 * rows.size + 2 * tokens * width),
+    )(*operands)
+
+
+def assemble_kernel(in_ref, out_ref):
+    out_ref[...] = in_ref[0].astype(out_ref.dtype)
+
+
+def assemble(shards, kind):
+    count, width, tile = shards.shape
+    return pl.pallas_call(
+        assemble_kernel,
+        grid=(count,),
+        in_specs=[pl.BlockSpec((1, width, tile), lambda i: (i, 0, 0))],
+        out_specs=pl.BlockSpec((width, tile), lambda i: (0, i)),
+        out_shape=jax.ShapeDtypeStruct((width, count * tile), kind),
+        compiler_params=params(),
+        cost_estimate=cost(0, 6 * shards.size),
+    )(shards)
+
+
+def on_device(
+    layer_input, gain_one, attn_in, rel_bias, attn_out, gain_two, router,
+    expert_gate, expert_up, expert_down, routes, piece_starts, grad_out,
+):
+    width, tokens = layer_input.shape
+    ranks = lax.axis_size("tensor")
+    groups = lax.axis_size("expert")
+    seqs = piece_starts.shape[0]
+    rank = lax.axis_index("tensor")
+    pair_class, half_index = rank % 2, rank // 2
+    half = CAP // 2
+    share = SEQ // ranks
+    across = [(r, r ^ 1) for r in range(ranks)]
+    along = [(r, r ^ 2) for r in range(ranks)]
+
+    def trade(weights):
+        mine = lax.dynamic_index_in_dim(weights, pair_class, 0, keepdims=True)
+        other = lax.dynamic_index_in_dim(weights, 1 - pair_class, 0, keepdims=True)
+        return jnp.concatenate([mine, lax.ppermute(other, "tensor", across)], axis=0)
+
+    w_gate, w_up, w_down = trade(expert_gate), trade(expert_up), trade(expert_down)
+
+    gain_col = gain_one[:, None]
+    w_in = attn_in.reshape(-1, width)
+    qkv, scale_one = project(layer_input, gain_col, w_in)
+    tiles = bias_tiles(rel_bias)
+    position = jnp.arange(SEQ, dtype=jnp.int32)[None, None, :]
+    starts = piece_starts[:, :, None]
+    inside = (position >= starts) & (position < starts + PIECE)
+    last = jnp.max(jnp.where(inside, starts + (PIECE - 1), -1), axis=1)
+    limits = jnp.maximum(last, position[0])[:, None, :]
+
+    routes_t = routes.T
+    place = jnp.stack([pair_class, half_index]).astype(jnp.int32)
+    code = local_codes(place, routes_t, half, groups)
+    code_cols = code.T
+    dy = grad_out.T
+
+    def own_tokens(array, seq):
+        return lax.dynamic_slice_in_dim(array, seq * SEQ + rank * share, share, 1)
+
+    mixed, lse, resid, scale_two, full_h2 = [], [], [], [], []
+    for seq in range(seqs):
+        mixed_seq, lse_seq, sent = attend(qkv, tiles, limits, attn_out, seq)
+        summed = lax.psum_scatter(sent, "tensor", scatter_dimension=0, tiled=True)
+        resid_seq = own_tokens(layer_input, seq).T.astype(F32) + summed.astype(F32)
+        scale = lax.rsqrt(jnp.sum(resid_seq * resid_seq, axis=1, keepdims=True) / width + EPS)
+        normed = (resid_seq * scale * gain_two).astype(BF16)
+        mixed.append(mixed_seq)
+        lse.append(lse_seq)
+        resid.append(resid_seq)
+        scale_two.append(scale)
+        full_h2.append(lax.all_gather(normed, "tensor", axis=0, tiled=True))
+
+    gates = pair_gates(full_h2[0], full_h2[1], router.T, routes_t)
+    slots = groups * half
+    rows, row_grads, dy_rows, gate_rows = dispatch(code, gates, full_h2[0], full_h2[1], dy, slots)
+
+    def to_owners(array):
+        moved = lax.all_to_all(
+            array.reshape(groups, half, width), "expert", split_axis=0, concat_axis=0, tiled=True
+        )
+        return moved.reshape(slots, width)
+
+    got_rows = to_owners(rows)
+    far_rows = lax.ppermute(got_rows, "tensor", along)
+    got_grads = to_owners(row_grads)
+    far_grads = lax.ppermute(got_grads, "tensor", along)
+    (ret, back, own_gate, own_up, own_down, far_gate, far_up, far_down) = run_experts(
+        jnp.concatenate([got_rows, far_rows]), jnp.concatenate([got_grads, far_grads]), w_gate, w_up, w_down
+    )
+
+    def from_owners(array):
+        other = lax.ppermute(array[slots:], "tensor", along)
+        return to_owners((array[:slots].astype(F32) + other.astype(F32)).astype(BF16))
+
+    ret = from_owners(ret)
+    back = from_owners(back)
+    grad_logit, scaled = pair_grads(code, gates, routes_t, dy_rows, ret, gate_rows)
+    partial_h2 = spread(code_cols, back, grad_logit.T, router)
+    partial_y = spread(code_cols, scaled)
+    grad_router = sum(
+        mm(grad_logit[:, seq * SEQ : (seq + 1) * SEQ], full_h2[seq].astype(F32))
+        for seq in range(seqs)
+    )
+
+    grad_gain_two = jnp.zeros((width,), F32)
+    grad_resid, full_attn, y_shards = [], [], []
+    for seq in range(seqs):
+        span = slice(seq * SEQ, (seq + 1) * SEQ)
+        grad_h2 = lax.psum_scatter(partial_h2[span], "tensor", scatter_dimension=0, tiled=True).astype(F32)
+        own_dy = own_tokens(grad_out, seq).T.astype(F32)
+        grad_gain_two = grad_gain_two + jnp.sum(grad_h2 * resid[seq] * scale_two[seq], axis=0)
+        scaled_h2 = grad_h2 * gain_two
+        inner = jnp.sum(scaled_h2 * resid[seq], axis=1, keepdims=True)
+        grad = scale_two[seq] * scaled_h2 - resid[seq] * scale_two[seq] ** 3 * inner / width + own_dy
+        grad_resid.append(grad)
+        full_attn.append(lax.all_gather(grad.astype(BF16), "tensor", axis=0, tiled=True))
+    for seq in range(seqs):
+        span = slice(seq * SEQ, (seq + 1) * SEQ)
+        y_part = lax.psum_scatter(partial_y[span], "tensor", scatter_dimension=0, tiled=True)
+        y_shards.append((resid[seq] + y_part.astype(F32)).astype(BF16).T)
+    y_all = [lax.all_gather(shard[None], "tensor", axis=0, tiled=True) for shard in y_shards]
+    layer_output = assemble(jnp.concatenate(y_all), BF16)
+
+    grad_attn_out = sum(mm(mixed[seq], full_attn[seq]) for seq in range(seqs))
+    w_in_t = w_in.T
+    grad_in, near, far, shards = [], [], [], []
+    grad_gain_one = jnp.zeros((width,), F32)
+    for seq in range(seqs):
+        dq, dk, dv, near_seq, far_seq = attend_back(
+            qkv, tiles, limits, attn_out, full_attn[seq], lse[seq], seq
+        )
+        near.append(near_seq)
+        far.append(far_seq)
+        grads = [g.reshape(-1, SEQ) for g in (dq, dk, dv)]
+        update, sent = project_back(layer_input, gain_col, scale_one, w_in_t, grads, seq, ranks)
+        grad_in.append(update)
+        grad_h1 = lax.psum_scatter(sent, "tensor", scatter_dimension=0, tiled=True)[0].astype(F32)
+        own_x = own_tokens(layer_input, seq).astype(F32)
+        own_scale = own_tokens(scale_one, seq)
+        grad_gain_one = grad_gain_one + jnp.sum(grad_h1 * own_x * own_scale, axis=1)
+        scaled_h1 = grad_h1 * gain_col
+        inner = jnp.sum(scaled_h1 * own_x, axis=0, keepdims=True)
+        grad = own_scale * scaled_h1 - own_x * own_scale**3 * inner / width + grad_resid[seq].T
+        shards.append(lax.all_gather(grad.astype(BF16)[None], "tensor", axis=0, tiled=True))
+    grad_input = assemble(jnp.concatenate(shards), F32)
+    folded = bias_fold(jnp.stack(near), jnp.stack(far))
+    grad_rel_bias = folded[:, :, 0].T
+
+    def give(own, other):
+        got = lax.ppermute(other, "tensor", across).astype(F32)
+        first = jnp.where(pair_class == 0, own, got)
+        second = jnp.where(pair_class == 0, got, own)
+        return jnp.stack([first, second])
+
+    small = lax.psum(
+        jnp.concatenate([grad_gain_one[None], grad_gain_two[None], grad_router]), ("expert", "tensor")
+    )
+    over_experts = (
+        lax.psum((grad_in[0] + grad_in[1]).astype(BF16), "expert").astype(F32),
+        lax.psum(grad_rel_bias, "expert"),
+        lax.psum(grad_attn_out.astype(BF16), "expert").astype(F32),
+    )
+    return (
+        layer_output,
+        grad_input,
+        small[0],
+        over_experts[0].reshape(attn_in.shape),
+        over_experts[1],
+        over_experts[2],
+        small[1],
+        small[2:].T,
+        give(own_gate, far_gate),
+        give(own_up, far_up),
+        give(own_down, far_down),
+    )
+
+
 def allowed_pairs(seq_starts):
     position = jnp.arange(SEQ, dtype=jnp.int32)
     inside = (position[:, None] >= seq_starts[None, :]) & (
@@ -43,7 +799,12 @@
     onehot = (flat_routes[:, None] == jnp.arange(EXPERTS, dtype=jnp.int32)[None, :]).astype(
         jnp.int32
     )
-    before = jnp.cumsum(onehot, axis=0) - onehot
+    blocks = onehot.reshape(-1, 128, EXPERTS).astype(F32)
+    earlier = jnp.tril(jnp.ones((128, 128), F32), -1)
+    inside = jnp.einsum("ij,bje->bie", earlier, blocks)
+    count = blocks.shape[0]
+    carried = jnp.einsum("ab,be->ae", jnp.tril(jnp.ones((count, count), F32), -1), jnp.sum(blocks, axis=1), precision=HIGH)
+    before = (inside + carried[:, None, :]).astype(jnp.int32).reshape(onehot.shape)
     slot_number = jnp.sum(before * onehot, axis=1)
     kept_pairs = slot_number < CAP
     slot_index = jnp.where(kept_pairs, flat_routes * CAP + slot_number, EXPERTS * CAP)
@@ -196,7 +957,7 @@
     return (grad_gate_w, grad_up_w, grad_down, grad_rows_in)
 
 
-def on_device(
+def on_device_general(
     layer_input,
     gain_one,
     attn_in,
@@ -357,8 +1118,9 @@
         P("expert", None),
         P(None, "expert"),
     )
+    paired = mesh.shape["tensor"] == 4 and mesh.shape["expert"] * 2 == EXPERTS
     return jax.shard_map(
-        on_device,
+        on_device if paired else on_device_general,
         mesh=mesh,
         in_specs=placed,
         out_specs=(

time: 2200 us -> 1470 us (0.67)
  local copies, waits for them, and re-layouts: 696 us -> 58.1 us
  matrix products: 329 us -> 10.2 us
  Pallas kernels: 0 us -> 258 us
  waiting for transfers between devices: 724 us -> 930 us
  other arithmetic: 253 us -> 79.1 us
  blocking collectives: 159 us -> 81.8 us
    dot_general x34 -> x4, matrix products: 329 us -> 10.2 us  [mm(): return lax.dot_general(left, right, dims, preferred_element_type=F32)]
    ppermute x0 -> x10, waiting for transfers between devices: none -> 315 us  [the longest x2 115 us: from_owners(): other = lax.ppermute(array[slots:], 'tensor', along)]
    pallas_call x0 -> x18, Pallas kernels: none -> 258 us  [the longest x1 88.4 us: run_experts(): pl.pallas_call(expert_kernel, grid=(5,), in_specs=[row_spec, row_spec, we...]
    unnamed x108 -> x51, local copies, waits for them, and re-layouts: 247 us -> 10 us
    all_to_all x2 -> x3, waiting for transfers between devices: 231 us -> 107 us  [to_owners(): lax.all_to_all(array.reshape(groups, half, width), 'expert', split_axis=0...]
    reduce_sum x17 -> x5, other arithmetic: 114 us -> 9.45 us  [the longest x2 4.76 us: on_device(): grad_gain_one = grad_gain_one + jnp.sum(grad_h1 * own_x * own_scale, axis=1)]
    reshape x4 -> x1, local copies, waits for them, and re-layouts: 106 us -> 2.58 us  [on_device(): w_in = attn_in.reshape(-1, width)]
    reduce_scatter x2 -> x6, waiting for transfers between devices: 294 us -> 192 us  [the longest x2 75.1 us: on_device(): lax.psum_scatter(partial_y[span], 'tensor', scatter_dimension=0, tiled=True)]
  transfers between devices with their start and end apart: 10 -> 31, of which waited for: 8 -> 24; matrix products, arithmetic and copies ran while one was open for 22% -> 8% of each run, Pallas kernels for 0% -> 7%
where the time goes in v1:
time: 1470 us; the launch traced here: 1460 us
  waiting for transfers between devices  930 us (63%)
  Pallas kernels  258 us (18%)
  blocking collectives  81.8 us (6%)
  other arithmetic  79.1 us (5%)
  local copies, waits for them, and re-layouts  58.1 us (4%)
  starting transfers between devices  25.8 us (2%)
  between operations  15.1 us (1%)
    ppermute x2, waiting for transfers between devices, from_owners(): other = lax.ppermute(array[slots:], 'tensor', along)  115 us
    ppermute x3, waiting for transfers between devices, give(): got = lax.ppermute(other, 'tensor', across).astype(F32)  112 us
    all_to_all x3, waiting for transfers between devices, to_owners(): lax.all_to_all(array.reshape(groups, half, width), 'expert', split_axis=0...  107 us
    psum x1, waiting for transfers between devices, on_device(): lax.psum(jnp.concatenate([grad_gain_one[None], grad_gain_two[None], grad_...  102 us
    pallas_call x1, Pallas kernels, run_experts(): pl.pallas_call(expert_kernel, grid=(5,), in_specs=[row_spec, row_spec, we...  88.4 us
    ppermute x3, waiting for transfers between devices, trade(): lax.ppermute(other, 'tensor', across)  87.4 us
    reduce_scatter x2, waiting for transfers between devices, on_device(): lax.psum_scatter(partial_y[span], 'tensor', scatter_dimension=0, tiled=True)  75.1 us
    all_gather x2, waiting for transfers between devices, on_device(): lax.all_gather(grad.astype(BF16)[None], 'tensor', axis=0, tiled=True)  68.7 us
  transfers between devices with their start and end apart: 31, of which 24 were waited for; matrix products, arithmetic and copies ran while one was open for 8% of the time, Pallas kernels for 7%

profile of v1, /device:TPU:0, one launch (start us, length us, event | category | flops | bytes accessed | tf_op | source)
XLA Modules:
  0.0 1458.4 jit_solution(1239611281169638679)
XLA Ops:
  12.4 6.3 shard_map.213.tiles_ref
  18.7 8.3 shard_map.212
  27.1 13.0 shard_map.214
  40.1 13.0 shard_map.216
  54.9 23.2 %reduce-scatter.13.cloned.1.call-done = bf16[256,1024]{1,0:T(8,128)(2,1)} async-done(((bf16[1024,1024]{1,0:T(8,128)(2,1)}), bf16[256,1024]{1,0:T(8,128)(2,1)}) %reduce-scatter.13.cloned.1.call-update) | async-done | bytes 524304 | tf_op jit(solution)/shard_map/reduce_scatter | solution.py:670
  79.4 37.8 %reduce-scatter.15.cloned.1.call-done = bf16[256,1024]{1,0:T(8,128)(2,1)} async-done(((bf16[1024,1024]{1,0:T(8,128)(2,1)}), bf16[256,1024]{1,0:T(8,128)(2,1)}) %reduce-scatter.15.cloned.1.call-update) | async-done | bytes 524304 | tf_op jit(solution)/shard_map/reduce_scatter | solution.py:670
  121.7 6.4 copy.88
  130.3 26.2 %all-gather.13.cloned.1.call-done.h0_ref = bf16[1024,1024]{1,0:T(8,128)(2,1)} async-done(((bf16[256,1024]{1,0:T(8,128)(2,1)}), bf16[1024,1024]{1,0:T(8,128)(2,1)}) %all-gather.13.cloned.1.call-update) | async-done | bytes 2097168 | tf_op jit(solution)/shard_map/all_gather | solution.py:678
  156.5 37.6 %all-gather.15.cloned.1.call-done.h1_ref = bf16[1024,1024]{1,0:T(8,128)(2,1)} async-done(((bf16[256,1024]{1,0:T(8,128)(2,1)}), bf16[1024,1024]{1,0:T(8,128)(2,1)}) %all-gather.15.cloned.1.call-update) | async-done | bytes 2097168 | tf_op jit(solution)/shard_map/all_gather | solution.py:678
  194.1 4.1 shard_map.217.gates_ref
  198.2 17.2 %shard_map.218 = (bf16[1280,1024]{1,0:T(8,128)(2,1)}, bf16[1280,1024]{1,0:T(8,128)(2,1)}, bf16[1280,1024]{1,0:T(8,128)(2,1)}, f32[1280,1]{1,0:T(8,128)}) custom-call(s32[2,2048]{1,0:T(2,128)} %shard_map.215.code_ref, f32[2,2048]{1,0:T(2,128)} %shard_map.217.gates_ref, bf16[1024,1024]{1,0:T(8,128)(2,1)} %all-gather.13.cloned.1.call-done.h0_ref, ...), custom_call_target="tpu_custom_call" | custom-call | flops 10737418240 | bytes 16252928 | tf_op jit(solution)/shard_map/pallas_call | solution.py:441
  215.4 65.0 %all_to_all.20 = bf16[8,160,1024]{2,1,0:T(8,128)(2,1)} all-to-all(bf16[8,160,1024]{2,1,0:T(8,128)(2,1)} %bitcast.150), channel_id=1, replica_groups=mesh['expert'=8,'tensor'=4] {'expert'}, dimensions={0} | all-to-all | bytes 5242880 | tf_op jit(solution)/shard_map/all_to_all | solution.py:685
  280.4 4.4 all-to-all-start
  286.4 58.8 %all-to-all-done = bf16[8,160,1024]{2,1,0:T(8,128)(2,1)} async-done(((bf16[8,160,1024]{2,1,0:T(8,128)(2,1)}), bf16[8,160,1024]{2,1,0:T(8,128)(2,1)}, u32[]{:S(2)}, u32[]{:S(2)}) %all-to-all-start) | async-done | bytes 2621472 | tf_op jit(solution)/shard_map/all_to_all | solution.py:685
  352.3 30.9 %collective-permute-done.4 = bf16[1,704,1024]{2,1,0:T(8,128)(2,1)S(1)} collective-permute-done((bf16[1,704,1024]{2,1,0:T(8,128)(2,1)S(1)}, bf16[1,704,1024]{2,1,0:T(8,128)(2,1)S(1)}, u32[]{:S(2)}, u32[]{:S(2)}) %collective-permute-start.4) | collective-permute-done | bytes 1441824 | tf_op jit(solution)/shard_map/ppermute | solution.py:644
  385.1 29.1 %collective-permute-done.2 = bf16[1,704,1024]{2,1,0:T(8,128)(2,1)S(1)} collective-permute-done((bf16[1,704,1024]{2,1,0:T(8,128)(2,1)S(1)}, bf16[1,704,1024]{2,1,0:T(8,128)(2,1)S(1)}, u32[]{:S(2)}, u32[]{:S(2)}) %collective-permute-start.2) | collective-permute-done | bytes 1441824 | tf_op jit(solution)/shard_map/ppermute | solution.py:644
  416.0 27.4 %collective-permute-done.3 = bf16[1,704,1024]{2,1,0:T(8,128)(2,1)S(1)} collective-permute-done((bf16[1,704,1024]{2,1,0:T(8,128)(2,1)S(1)}, bf16[1,704,1024]{2,1,0:T(8,128)(2,1)S(1)}, u32[]{:S(2)}, u32[]{:S(2)}) %collective-permute-start.3) | collective-permute-done | bytes 1441824 | tf_op jit(solution)/shard_map/ppermute | solution.py:644
  446.2 4.7 pad_maximum_fusion.5.grads_ref
  450.9 4.7 pad_maximum_fusion.4.rows_ref
  455.5 88.4 %shard_map.219 = (bf16[2560,1024]{1,0:T(8,128)(2,1)}, bf16[2560,1024]{1,0:T(8,128)(2,1)}, f32[704,1024]{1,0:T(8,128)}, f32[704,1024]{1,0:T(8,128)}, f32[704,1024...) custom-call(bf16[2560,1024]{1,0:T(8,128)(2,1)} %pad_maximum_fusion.4.rows_ref, ...), custom_call_target="tpu_custom_call" | custom-call | flops 66437775360 | bytes 42598400 | tf_op jit(solution)/shard_map/pallas_call | solution.py:517
  546.8 56.5 %collective-permute-done.5 = bf16[1280,1024]{1,0:T(8,128)(2,1)S(1)} collective-permute-done((bf16[1280,1024]{1,0:T(8,128)(2,1)S(1)}, bf16[1280,1024]{1,0:T(8,128)(2,1)S(1)}, u32[]{:S(2)}, u32[]{:S(2)}) %collective-permute-start.5) | collective-permute-done | bytes 2621472 | tf_op jit(solution)/shard_map/ppermute | solution.py:699
  606.1 4.4 all-to-all-start.2
  613.2 58.6 %collective-permute-done.6 = bf16[1280,1024]{1,0:T(8,128)(2,1)S(1)} collective-permute-done((bf16[1280,1024]{1,0:T(8,128)(2,1)S(1)}, bf16[1280,1024]{1,0:T(8,128)(2,1)S(1)}, u32[]{:S(2)}, u32[]{:S(2)}) %collective-permute-start.6) | collective-permute-done | bytes 2621472 | tf_op jit(solution)/shard_map/ppermute | solution.py:699
  671.7 4.5 add_convert_fusion
  676.3 4.9 all-to-all-start.3
  683.4 8.2 shard_map.220
  693.8 47.8 %all-to-all-done.3 = bf16[8,160,1024]{2,1,0:T(8,128)(2,1)} async-done(((bf16[8,160,1024]{2,1,0:T(8,128)(2,1)}), bf16[8,160,1024]{2,1,0:T(8,128)(2,1)}, u32[]{:S(2)}, u32[]{:S(2)}) %all-to-all-start.3) | async-done | bytes 2621472 | tf_op jit(solution)/shard_map/all_to_all | solution.py:685
  741.6 11.2 shard_map.223
  752.8 4.7 fusion.49
  758.1 9.5 shard_map.221
  767.6 4.8 fusion.50
  773.3 17.5 %reduce-scatter.21.cloned.1.call-done = bf16[256,1024]{1,0:T(8,128)(2,1)} async-done(((bf16[1024,1024]{1,0:T(8,128)(2,1)}), bf16[256,1024]{1,0:T(8,128)(2,1)}) %reduce-scatter.21.cloned.1.call-update) | async-done | bytes 524304 | tf_op jit(solution)/shard_map/reduce_scatter | solution.py:716
  790.8 38.9 %reduce-scatter.23.cloned.1.call-done = bf16[256,1024]{1,0:T(8,128)(2,1)} async-done(((bf16[1024,1024]{1,0:T(8,128)(2,1)}), bf16[256,1024]{1,0:T(8,128)(2,1)}) %reduce-scatter.23.cloned.1.call-update) | async-done | bytes 524304 | tf_op jit(solution)/shard_map/reduce_scatter | solution.py:716
  831.8 36.6 %reduce-scatter.17.cloned.1.call-done = bf16[256,1024]{1,0:T(8,128)(2,1)} async-done(((bf16[1024,1024]{1,0:T(8,128)(2,1)}), bf16[256,1024]{1,0:T(8,128)(2,1)}) %reduce-scatter.17.cloned.1.call-update) | async-done | bytes 524304 | tf_op jit(solution)/shard_map/reduce_scatter | solution.py:726
  868.4 38.4 %reduce-scatter.19.cloned.1.call-done = bf16[256,1024]{1,0:T(8,128)(2,1)} async-done(((bf16[1024,1024]{1,0:T(8,128)(2,1)}), bf16[256,1024]{1,0:T(8,128)(2,1)}) %reduce-scatter.19.cloned.1.call-update) | async-done | bytes 524304 | tf_op jit(solution)/shard_map/reduce_scatter | solution.py:726
  906.9 3.7 fusion.47
  913.9 32.2 %all-gather.17.cloned.1.call-done.grad_ref = bf16[1024,1024]{1,0:T(8,128)(2,1)} async-done(((bf16[256,1024]{1,0:T(8,128)(2,1)}), bf16[1024,1024]{1,0:T(8,128)(2,1)}) %all-gather.17.cloned.1.call-update) | async-done | bytes 2097168 | tf_op jit(solution)/shard_map/all_gather | solution.py:723
  946.1 16.0 %shard_map.224 = (bf16[4,64,1024]{2,1,0:T(8,128)(2,1)}, bf16[4,64,1024]{2,1,0:T(8,128)(2,1)}, bf16[4,64,1024]{2,1,0:T(8,128)(2,1)}, f32[4,3,256,256]{3,2,1,0:T(8,128)}, f32[4,8,256]{2,1,0:T(8,128)}) custom-call(bf16[768,2048]{1,0:T(8,128)(2,1)} %get-tuple-element.47.q_ref.k_ref.v_ref, bf16[768,2048]{1,0:T(8,128)(2,1)} %get-tuple-element.47.q_ref.k_ref.v_ref, ...), custom_call_target="tpu_custom_call" | custom-call | flops 5368709120 | bytes 16777216 | tf_op jit(solution)/shard_map/pallas_call | solution.py:275
  962.1 10.2 shard_map.225
  972.4 11.3 all-gather.19.cloned.1.call-done.grad_ref
  983.7 16.2 %shard_map.226 = (bf16[4,64,1024]{2,1,0:T(8,128)(2,1)}, bf16[4,64,1024]{2,1,0:T(8,128)(2,1)}, bf16[4,64,1024]{2,1,0:T(8,128)(2,1)}, f32[4,3,256,256]{3,2,1,0:T(8,128)}, f32[4,8,256]{2,1,0:T(8,128)}) custom-call(bf16[768,2048]{1,0:T(8,128)(2,1)} %get-tuple-element.47.q_ref.k_ref.v_ref, bf16[768,2048]{1,0:T(8,128)(2,1)} %get-tuple-element.47.q_ref.k_ref.v_ref, ...), custom_call_target="tpu_custom_call" | custom-call | flops 5368709120 | bytes 16777216 | tf_op jit(solution)/shard_map/pallas_call | solution.py:275
  999.9 10.3 shard_map.227
  1015.3 3.3 fusion.6
  1026.4 35.0 %reduce-scatter.27.cloned.1.call-done = bf16[1,1024,256]{2,1,0:T(8,128)(2,1)} async-done(((bf16[4,1024,256]{2,1,0:T(8,128)(2,1)}), bf16[1,1024,256]{2,1,0:T(8,128)(2,1)}) %reduce-scatter.27.cloned.1.call-update) | async-done | bytes 524304
  1064.8 3.4 fusion.40
  1075.7 46.1 %collective-permute-done.9 = bf16[704,1024]{1,0:T(8,128)(2,1)} collective-permute-done((bf16[704,1024]{1,0:T(8,128)(2,1)}, bf16[704,1024]{1,0:T(8,128)(2,1)}, u32[]{:S(2)}, u32[]{:S(2)}) %collective-permute-start.9) | collective-permute-done | bytes 1441824 | tf_op jit(solution)/shard_map/ppermute | solution.py:757
  1121.8 3.3 fusion.4
  1128.1 41.4 %collective-permute-done.8 = bf16[704,1024]{1,0:T(8,128)(2,1)} collective-permute-done((bf16[704,1024]{1,0:T(8,128)(2,1)}, bf16[704,1024]{1,0:T(8,128)(2,1)}, u32[]{:S(2)}, u32[]{:S(2)}) %collective-permute-start.8) | collective-permute-done | bytes 1441824 | tf_op jit(solution)/shard_map/ppermute | solution.py:757
  1175.0 24.9 %collective-permute-done.7 = bf16[704,1024]{1,0:T(8,128)(2,1)S(1)} collective-permute-done((bf16[704,1024]{1,0:T(8,128)(2,1)}, bf16[704,1024]{1,0:T(8,128)(2,1)S(1)}, u32[]{:S(2)}, u32[]{:S(2)}) %collective-permute-start.7) | collective-permute-done | bytes 1441824 | tf_op jit(solution)/shard_map/ppermute | solution.py:757
  1204.0 3.3 copy.102
  1207.3 4.1 copy.103
  1211.4 4.0 pad_maximum_fusion.6.in_ref
  1215.4 7.9 shard_map.222
  1224.0 3.3 pad_maximum_fusion.near_ref
  1227.3 9.4 shard_map.229
  1237.6 16.8 %psum.30 = f32[32,4]{0,1:T(4,128)} all-reduce(f32[32,4]{0,1:T(4,128)S(1)} %bitcast.171), channel_id=1, replica_groups=mesh['expert'=8,'tensor'=4] {'expert'}, use_global_device_ids=true, to_apply=%region_21.22 | all-reduce | flops 128 | bytes 1024 | tf_op jit(solution)/shard_map/psum | solution.py:767
  1254.5 3.5 reshape.169
  1259.1 101.9 %all-reduce.6.cloned.1.call-done = f32[18,1024]{1,0:T(8,128)} async-done(((f32[18,1024]{1,0:T(8,128)}), f32[18,1024]{1,0:T(8,128)}) %all-reduce.6.cloned.1.call-update) | async-done | bytes 73744 | tf_op jit(solution)/shard_map/psum | solution.py:762
  1363.9 34.9 %all-gather.27.cloned.1.call-done = bf16[4096,256]{0,1:T(8,128)(2,1)} async-done(((bf16[1024,256]{0,1:T(8,128)(2,1)}), bf16[4096,256]{0,1:T(8,128)(2,1)}) %all-gather.27.cloned.1.call-update) | async-done | bytes 2097168 | tf_op jit(solution)/shard_map/all_gather | solution.py:751
  1398.8 3.3 copy.101
  1402.1 33.8 %all-gather.25.cloned.1.call-done = bf16[4096,256]{0,1:T(8,128)(2,1)} async-done(((bf16[1024,256]{0,1:T(8,128)(2,1)}), bf16[4096,256]{0,1:T(8,128)(2,1)}) %all-gather.25.cloned.1.call-update) | async-done | bytes 2097168 | tf_op jit(solution)/shard_map/all_gather | solution.py:751
  1435.9 4.1 copy.97
  1440.0 3.9 pad_maximum_fusion.7.in_ref
  1443.9 7.3 shard_map.228
  (150 shorter events, 91.8 us)
Async XLA Ops:
  7.2 70.9 %reduce-scatter.13.cloned.1.call-start = ((), (), s32[]{:S(2)}) async-start(), calls=%async_computation.12 | async-start | bytes 2621440 | tf_op jit(solution)/shard_map/reduce_scatter | solution.py:670
  40.1 77.1 %reduce-scatter.15.cloned.1.call-start = ((), (), s32[]{:S(2)}) async-start(), calls=%async_computation.14 | async-start | bytes 2621440 | tf_op jit(solution)/shard_map/reduce_scatter | solution.py:670
  53.1 103.4 %all-gather.13.cloned.1.call-start = ((), (), s32[]{:S(2)}) async-start(), calls=%async_computation.13 | async-start | bytes 2621440 | tf_op jit(solution)/shard_map/all_gather | solution.py:678
  53.2 65.3 %copy-start.19 = (f32[1024]{0:T(1024)S(1)}, f32[1024]{0:T(1024)}, u32[]{:S(2)}) copy-start(f32[1024]{0:T(1024)} %param.18) | copy-start | bytes 12292
  121.1 73.1 %all-gather.15.cloned.1.call-start = ((), (), s32[]{:S(2)}) async-start(), calls=%async_computation.15 | async-start | bytes 2621440 | tf_op jit(solution)/shard_map/all_gather | solution.py:678
  280.4 64.7 %all-to-all-start = ((bf16[8,160,1024]{2,1,0:T(8,128)(2,1)}), bf16[8,160,1024]{2,1,0:T(8,128)(2,1)}, u32[]{:S(2)}, u32[]{:S(2)}) async-start(bf16[8,160,1024]{2,1,0:T(8,128)(2,1)} %bitcast.149), calls=%async_computation.2 | async-start | bytes 5242880 | tf_op jit(solution)/shard_map/all_to_all | solution.py:685
  284.8 160.4 %collective-permute-start.1 = (bf16[1280,1024]{1,0:T(8,128)(2,1)}, bf16[1280,1024]{1,0:T(8,128)(2,1)}, u32[]{:S(2)}, u32[]{:S(2)}) collective-permute-start(bf16[1280,1024]{1,0:T(8,128)(2,1)} %bitcast.137), channel_id=1, source_target_pairs={{0,2},{1,3},{2,0},{3,1},{4,6},{5,7},{6,4},{7,5},{8,10},{9,11},{10,... | collective-permute-start | bytes 7864328 | tf_op jit(solution)/shard_map/ppermute | solution.py:693
  345.1 4.4 copy-start.10
  345.1 105.7 %collective-permute-start = (bf16[1280,1024]{1,0:T(8,128)(2,1)}, bf16[1280,1024]{1,0:T(8,128)(2,1)S(1)}, u32[]{:S(2)}, u32[]{:S(2)}) collective-permute-start(bf16[1280,1024]{1,0:T(8,128)(2,1)} %bitcast.11), channel_id=1, source_target_pairs={{0,2},{1,3},{2,0},{3,1},{4,6},{5,7},{6,4},{7,5},{8,10},{9,11},{10,... | collective-permute-start | bytes 7864328 | tf_op jit(solution)/shard_map/ppermute | solution.py:691
  348.7 2.5 copy-start.11
  348.7 34.6 %collective-permute-start.4 = (bf16[1,704,1024]{2,1,0:T(8,128)(2,1)S(1)}, bf16[1,704,1024]{2,1,0:T(8,128)(2,1)S(1)}, u32[]{:S(2)}, u32[]{:S(2)}) collective-permute-start(bf16[1,704,1024]{2,1,0:T(8,128)(2,1)S(1)} %get-tuple-element.112), channel_id=1, source_target_pairs={{0,1},{1,0},{2,3},{3,2},{4,5},{5,4},{6,7},{7,6},{8,9},{9,8},{10,11... | collective-permute-start | bytes 4325384 | tf_op jit(solution)/shard_map/ppermute | solution.py:644
  349.9 64.3 %collective-permute-start.2 = (bf16[1,704,1024]{2,1,0:T(8,128)(2,1)S(1)}, bf16[1,704,1024]{2,1,0:T(8,128)(2,1)S(1)}, u32[]{:S(2)}, u32[]{:S(2)}) collective-permute-start(bf16[1,704,1024]{2,1,0:T(8,128)(2,1)S(1)} %get-tuple-element.116), channel_id=1, source_target_pairs={{0,1},{1,0},{2,3},{3,2},{4,5},{5,4},{6,7},{7,6},{8,9},{9,8},{10,11... | collective-permute-start | bytes 4325384 | tf_op jit(solution)/shard_map/ppermute | solution.py:644
  351.4 92.0 %collective-permute-start.3 = (bf16[1,704,1024]{2,1,0:T(8,128)(2,1)S(1)}, bf16[1,704,1024]{2,1,0:T(8,128)(2,1)S(1)}, u32[]{:S(2)}, u32[]{:S(2)}) collective-permute-start(bf16[1,704,1024]{2,1,0:T(8,128)(2,1)S(1)} %get-tuple-element.114), channel_id=1, source_target_pairs={{0,1},{1,0},{2,3},{3,2},{4,5},{5,4},{6,7},{7,6},{8,9},{9,8},{10,11... | collective-permute-start | bytes 4325384 | tf_op jit(solution)/shard_map/ppermute | solution.py:644
  443.4 2.8 copy-start.2
  543.9 59.4 %copy-start.3 = (bf16[2560,1024]{1,0:T(8,128)(2,1)S(1)}, bf16[2560,1024]{1,0:T(8,128)(2,1)}, u32[]{:S(2)}) copy-start(bf16[2560,1024]{1,0:T(8,128)(2,1)} %get-tuple-element.53) | copy-start | bytes 15728644
  546.0 57.3 %collective-permute-start.5 = (bf16[1280,1024]{1,0:T(8,128)(2,1)S(1)}, bf16[1280,1024]{1,0:T(8,128)(2,1)S(1)}, u32[]{:S(2)}, u32[]{:S(2)}) collective-permute-start(bf16[1280,1024]{1,0:T(8,128)(2,1)S(1)} %slice.43), channel_id=1, source_target_pairs={{0,2},{1,3},{2,0},{3,1},{4,6},{5,7},{6,4},{7,5},{8,10},{9,11},{10,... | collective-permute-start | bytes 7864328 | tf_op jit(solution)/shard_map/ppermute | solution.py:699
  606.1 70.1 %all-to-all-start.2 = ((bf16[8,160,1024]{2,1,0:T(8,128)(2,1)}), bf16[8,160,1024]{2,1,0:T(8,128)(2,1)}, u32[]{:S(2)}, u32[]{:S(2)}) async-start(bf16[8,160,1024]{2,1,0:T(8,128)(2,1)} %bitcast.140), calls=%async_computation.4 | async-start | bytes 5242880 | tf_op jit(solution)/shard_map/all_to_all | solution.py:685
  612.5 59.2 %collective-permute-start.6 = (bf16[1280,1024]{1,0:T(8,128)(2,1)S(1)}, bf16[1280,1024]{1,0:T(8,128)(2,1)S(1)}, u32[]{:S(2)}, u32[]{:S(2)}) collective-permute-start(bf16[1280,1024]{1,0:T(8,128)(2,1)S(1)} %slice.47), channel_id=1, source_target_pairs={{0,2},{1,3},{2,0},{3,1},{4,6},{5,7},{6,4},{7,5},{8,10},{9,11},{10,... | collective-permute-start | bytes 7864328 | tf_op jit(solution)/shard_map/ppermute | solution.py:699
  676.3 5.0 copy-start.17
  676.3 6.3 copy-start.18
  676.3 65.3 %all-to-all-start.3 = ((bf16[8,160,1024]{2,1,0:T(8,128)(2,1)}), bf16[8,160,1024]{2,1,0:T(8,128)(2,1)}, u32[]{:S(2)}, u32[]{:S(2)}) async-start(bf16[8,160,1024]{2,1,0:T(8,128)(2,1)} %bitcast.139), calls=%async_computation.7 | async-start | bytes 5242880 | tf_op jit(solution)/shard_map/all_to_all | solution.py:685
  681.2 109.6 %reduce-scatter.21.cloned.1.call-start = ((), (), s32[]{:S(2)}) async-start(), calls=%async_computation.18 | async-start | bytes 2621440 | tf_op jit(solution)/shard_map/reduce_scatter | solution.py:716
  757.5 72.2 %reduce-scatter.23.cloned.1.call-start = ((), (), s32[]{:S(2)}) async-start(), calls=%async_computation.20 | async-start | bytes 2621440 | tf_op jit(solution)/shard_map/reduce_scatter | solution.py:716
  758.1 110.3 %reduce-scatter.17.cloned.1.call-start = ((), (), s32[]{:S(2)}) async-start(), calls=%async_computation.16 | async-start | bytes 2621440 | tf_op jit(solution)/shard_map/reduce_scatter | solution.py:726
  772.4 57.2 %copy-start = (bf16[256,1024]{1,0:T(8,128)(2,1)S(1)}, bf16[256,1024]{1,0:T(8,128)(2,1)}, u32[]{:S(2)}) copy-start(bf16[256,1024]{1,0:T(8,128)(2,1)} %reduce-scatter.13.cloned.1.call-done) | copy-start | bytes 1572868
  772.4 57.2 %copy-start.1 = (bf16[256,1024]{1,0:T(8,128)(2,1)S(1)}, bf16[256,1024]{1,0:T(8,128)(2,1)}, u32[]{:S(2)}) copy-start(bf16[256,1024]{1,0:T(8,128)(2,1)} %reduce-scatter.15.cloned.1.call-done) | copy-start | bytes 1572868
  772.5 134.4 %reduce-scatter.19.cloned.1.call-start = ((), (), s32[]{:S(2)}) async-start(), calls=%async_computation.17 | async-start | bytes 2621440 | tf_op jit(solution)/shard_map/reduce_scatter | solution.py:726
  773.2 172.9 %all-gather.17.cloned.1.call-start = ((), (), s32[]{:S(2)}) async-start(), calls=%async_computation.19 | async-start | bytes 2621440 | tf_op jit(solution)/shard_map/all_gather | solution.py:723
  790.8 116.1 %copy-start.4 = (bf16[256,1024]{1,0:T(8,128)(2,1)S(1)}, bf16[256,1024]{1,0:T(8,128)(2,1)}, u32[]{:S(2)}) copy-start(bf16[256,1024]{1,0:T(8,128)(2,1)} %reduce-scatter.21.cloned.1.call-done) | copy-start | bytes 1572868
  829.7 77.2 %copy-start.5 = (bf16[256,1024]{1,0:T(8,128)(2,1)S(1)}, bf16[256,1024]{1,0:T(8,128)(2,1)}, u32[]{:S(2)}) copy-start(bf16[256,1024]{1,0:T(8,128)(2,1)} %reduce-scatter.23.cloned.1.call-done) | copy-start | bytes 1572868
  910.6 73.1 %all-gather.19.cloned.1.call-start = ((), (), s32[]{:S(2)}) async-start(), calls=%async_computation.21 | async-start | bytes 2621440 | tf_op jit(solution)/shard_map/all_gather | solution.py:723
  911.2 113.1 %reduce-scatter.25.cloned.1.call-start = ((), (), s32[]{:S(2)}) async-start(), calls=%async_computation.27 | async-start | bytes 2621440
  972.4 89.0 %reduce-scatter.27.cloned.1.call-start = ((), (), s32[]{:S(2)}) async-start(), calls=%async_computation.28 | async-start | bytes 2621440
  1010.2 193.8 %all-gather.21.cloned.1.call-start = ((), (), s32[]{:S(2)}) async-start(), calls=%async_computation.23 | async-start | bytes 2621440 | tf_op jit(solution)/shard_map/all_gather | solution.py:728
  1011.0 196.3 %all-gather.23.cloned.1.call-start = ((), (), s32[]{:S(2)}) async-start(), calls=%async_computation.24 | async-start | bytes 2621440 | tf_op jit(solution)/shard_map/all_gather | solution.py:728
  1011.5 242.9 %all-reduce.8.cloned.1.call-start = ((), (), s32[]{:S(2)}) async-start(), calls=%async_computation.29 | async-start | bytes 4194304 | tf_op jit(solution)/shard_map/psum | solution.py:766
  1011.6 3.7 copy-start.16
  1012.3 6.2 copy-start.9
  1015.3 3.3 copy-start.8
  1018.6 1.8 copy-start.15
  1020.3 43.2 %copy-start.20 = (f32[1024]{0:T(1024)S(1)}, f32[1024]{0:T(1024)}, u32[]{:S(2)}) copy-start(f32[1024]{0:T(1024)} %param.14) | copy-start | bytes 12292
  1020.3 340.7 %all-reduce.6.cloned.1.call-start = ((), (), s32[]{:S(2)}) async-start(), calls=%async_computation.22 | async-start | bytes 196608 | tf_op jit(solution)/shard_map/psum | solution.py:762
  1068.9 330.0 %all-gather.27.cloned.1.call-start = ((), (), s32[]{:S(2)}) async-start(), calls=%async_computation.26 | async-start | bytes 2621440 | tf_op jit(solution)/shard_map/all_gather | solution.py:751
  1071.9 364.0 %all-gather.25.cloned.1.call-start = ((), (), s32[]{:S(2)}) async-start(), calls=%async_computation.25 | async-start | bytes 2621440 | tf_op jit(solution)/shard_map/all_gather | solution.py:751
  1072.2 49.6 %collective-permute-start.9 = (bf16[704,1024]{1,0:T(8,128)(2,1)}, bf16[704,1024]{1,0:T(8,128)(2,1)}, u32[]{:S(2)}, u32[]{:S(2)}) collective-permute-start(bf16[704,1024]{1,0:T(8,128)(2,1)} %get-tuple-element.82), channel_id=1, source_target_pairs={{0,1},{1,0},{2,3},{3,2},{4,5},{5,4},{6,7},{7,6},{8,9},{9,8},{10,11... | collective-permute-start | bytes 4325384 | tf_op jit(solution)/shard_map/ppermute | solution.py:757
  1073.7 95.9 %collective-permute-start.8 = (bf16[704,1024]{1,0:T(8,128)(2,1)}, bf16[704,1024]{1,0:T(8,128)(2,1)}, u32[]{:S(2)}, u32[]{:S(2)}) collective-permute-start(bf16[704,1024]{1,0:T(8,128)(2,1)} %get-tuple-element.80), channel_id=1, source_target_pairs={{0,1},{1,0},{2,3},{3,2},{4,5},{5,4},{6,7},{7,6},{8,9},{9,8},{10,11... | collective-permute-start | bytes 4325384 | tf_op jit(solution)/shard_map/ppermute | solution.py:757
  1074.3 125.6 %collective-permute-start.7 = (bf16[704,1024]{1,0:T(8,128)(2,1)}, bf16[704,1024]{1,0:T(8,128)(2,1)S(1)}, u32[]{:S(2)}, u32[]{:S(2)}) collective-permute-start(bf16[704,1024]{1,0:T(8,128)(2,1)} %get-tuple-element.78), channel_id=1, source_target_pairs={{0,1},{1,0},{2,3},{3,2},{4,5},{5,4},{6,7},{7,6},{8,9},{9,8},{10,11... | collective-permute-start | bytes 4325384 | tf_op jit(solution)/shard_map/ppermute | solution.py:757
  1125.1 44.5 %copy-start.13 = (f32[704,1024]{1,0:T(8,128)S(1)}, f32[704,1024]{1,0:T(8,128)}, u32[]{:S(2)}) copy-start(f32[704,1024]{1,0:T(8,128)} %get-tuple-element.79) | copy-start | bytes 8650756
  1172.0 27.9 %copy-start.12 = (f32[704,1024]{1,0:T(8,128)S(1)}, f32[704,1024]{1,0:T(8,128)}, u32[]{:S(2)}) copy-start(f32[704,1024]{1,0:T(8,128)} %get-tuple-element.77) | copy-start | bytes 8650756
  1215.4 7.9 copy-start.21
  1215.4 7.9 copy-start.22
  1215.4 8.6 copy-start.6
  1215.4 8.6 copy-start.7
  1254.5 3.5 copy-start.14
Sparse Core Ops, SparseCore 0:
  40.2 37.8 reduce-scatter.12
  81.9 35.2 reduce-scatter.14
  121.2 35.2 all-gather.12
  158.8 35.2 all-gather.14
  757.6 33.1 reduce-scatter.20
  794.4 35.1 reduce-scatter.22
  833.2 35.1 reduce-scatter.16
  871.7 35.1 reduce-scatter.18
  910.8 35.2 all-gather.16
  948.4 35.2 all-gather.18
  987.3 35.1 reduce-scatter.24
  1026.2 35.1 reduce-scatter.26
  1063.2 50.7 all-gather.20
  1115.7 52.1 all-gather.22
  1170.2 65.1 all-reduce.7
  1240.8 120.1 all-reduce.5
  1362.7 36.1 all-gather.26
  1400.5 35.2 all-gather.24

commit v2 on v1

--- a/solution.py
+++ b/solution.py
@@ -460,72 +460,202 @@
     return x * half, slope
 
 
+def partner_of(index, step):
+    found = index
+    for bit in (1, 2, 4):
+        found = found + ((step // bit) % 2) * (1 - 2 * ((index // bit) % 2)) * bit
+    return found
+
+
 def expert_kernel(
-    rows_ref, grads_ref, gate_ref, up_ref, down_ref, ret_ref, back_ref,
-    own_gate, own_up, own_down, far_gate, far_up, far_down,
-    acc_gate, acc_up, acc_down, far_buf, sems,
+    rows_in, grads_in, gate_in, up_in, down_in,
+    ret_out, back_out, own_gate, own_up, own_down, far_gate, far_up, far_down,
+    rows, grads, weights, sums, parts, z_send, z_recv, y_send, y_recv, p_send, p_recv, r_send, r_recv, w_send, w_recv, local,
 ):
-    step = pl.program_id(0)
-    rows, grads = rows_ref[...], grads_ref[...]
-    half = gate_ref.shape[1]
-
-    @pl.when(step == 0)
-    def _():
-        for acc in (acc_gate, acc_up, acc_down):
-            acc[...] = jnp.zeros_like(acc)
-
-    ret = jnp.zeros(rows.shape, F32)
-    back = jnp.zeros(rows.shape, F32)
-    for part in range(2):
-        w_gate, w_up, w_down = gate_ref[part], up_ref[part], down_ref[part]
-        gate_part = mm(rows, w_gate, NT)
-        up_part = mm(rows, w_up, NT)
-        grad_hidden = mm(grads, w_down, NT)
-        bent, slope = gelu_parts(gate_part)
-        hidden = (bent * up_part).astype(BF16)
-        grad_gate = (grad_hidden * up_part * slope).astype(BF16)
-        grad_up = (grad_hidden * bent).astype(BF16)
-        ret = ret + mm(hidden, w_down)
-        back = back + mm(grad_gate, w_gate) + mm(grad_up, w_up)
-        acc_down[part] += mm(hidden, grads, TN)
-        acc_gate[part] += mm(grad_gate, rows, TN)
-        acc_up[part] += mm(grad_up, rows, TN)
-    ret_ref[...] = ret.astype(BF16)
-    back_ref[...] = back.astype(BF16)
-
-    @pl.when(step == pl.num_programs(0) - 1)
-    def _():
-        copies = []
-        triples = ((acc_gate, own_gate, far_gate), (acc_up, own_up, far_up), (acc_down, own_down, far_down))
-        for number, (acc, own, far) in enumerate(triples):
-            copies.append(pltpu.make_async_copy(acc.at[0], own, sems.at[2 * number]))
-            copies[-1].start()
-            far_buf[number] = acc[1].astype(BF16)
-            copies.append(pltpu.make_async_copy(far_buf.at[number], far, sems.at[2 * number + 1]))
-            copies[-1].start()
-        for copy in copies:
-            copy.wait()
+    groups, half, width = rows.shape[1:]
+    group, rank = lax.axis_index("expert"), lax.axis_index("tensor")
+    pair_class, half_index = rank % 2, rank // 2
+    across = {"tensor": rank + 1 - 2 * pair_class}
+    along = {"tensor": rank + 2 - 4 * half_index}
+    mesh_ids = pl.DeviceIdType.MESH
+    moved = ((rows_in, rows, ret_out), (grads_in, grads, back_out))
+
+    barrier = pltpu.get_barrier_semaphore()
+    for step in range(1, groups):
+        pl.semaphore_signal(
+            barrier, inc=1, device_id={"expert": partner_of(group, step)}, device_id_type=mesh_ids
+        )
+    pl.semaphore_signal(barrier, inc=1, device_id=across, device_id_type=mesh_ids)
+    pl.semaphore_signal(barrier, inc=1, device_id=along, device_id_type=mesh_ids)
+    pl.semaphore_wait(barrier, groups + 1)
+
+    def remote(source, target, send, recv, device):
+        return pltpu.make_async_remote_copy(
+            src_ref=source, dst_ref=target, send_sem=send, recv_sem=recv,
+            device_id=device, device_id_type=mesh_ids,
+        )
+
+    def block(ref, number):
+        return ref.at[pl.ds(pl.multiple_of(number * half, half), half)]
+
+    def out_of(kind, step):
+        source, held, _ = moved[kind]
+        other = partner_of(group, step)
+        return remote(
+            block(source, other), held.at[0, group], z_send.at[kind, step], z_recv.at[kind, step], {"expert": other}
+        )
+
+    def forward(kind, step):
+        held = moved[kind][1]
+        other = partner_of(group, step)
+        return remote(held.at[0, other], held.at[1, other], y_send.at[kind, step], y_recv.at[kind, step], along)
+
+    def partial_sum(kind, step):
+        held = moved[kind][1]
+        other = partner_of(group, step)
+        return remote(held.at[1, other], parts.at[kind, other], p_send.at[kind, step], p_recv.at[kind, step], along)
+
+    def result(kind, step):
+        other = partner_of(group, step)
+        return remote(
+            parts.at[kind, other], block(moved[kind][2], group), r_send.at[kind, step], r_recv.at[kind, step], {"expert": other}
+        )
+
+    def own_result(kind):
+        return pltpu.make_async_copy(parts.at[kind, group], block(moved[kind][2], group), local.at[kind])
+
+    own = [
+        pltpu.make_async_copy(block(moved[kind][0], group), moved[kind][1].at[0, group], local.at[kind])
+        for kind in range(2)
+    ]
+    for copy in own:
+        copy.start()
+    kept, swapped = [], []
+    for number, ref in enumerate((gate_in, up_in, down_in)):
+        kept.append(pltpu.make_async_copy(ref.at[pair_class], weights.at[number, 0], local.at[2 + number]))
+        swapped.append(
+            remote(ref.at[1 - pair_class], weights.at[number, 1], w_send.at[number], w_recv.at[number], across)
+        )
+    for copy in kept + swapped:
+        copy.start()
+    for step in range(1, groups):
+        for kind in range(2):
+            out_of(kind, step).start()
+    for copy in own:
+        copy.wait()
+    for kind in range(2):
+        forward(kind, 0).start()
+    for number in range(3):
+        for part in range(2):
+            sums[number, part] = jnp.zeros(sums.shape[2:], F32)
+
+    def finish(step):
+        other = partner_of(group, step)
+        for kind in range(2):
+            partial_sum(kind, step).wait()
+            held = moved[kind][1]
+            parts[kind, other] = (parts[kind, other].astype(F32) + held[0, other].astype(F32)).astype(BF16)
+
+        @pl.when(step == 0)
+        def _():
+            for kind in range(2):
+                own_result(kind).start()
+
+        @pl.when(step > 0)
+        def _():
+            for kind in range(2):
+                result(kind, step).start()
+
+    def body(step, carry):
+        @pl.when(step < groups - 1)
+        def _():
+            for kind in range(2):
+                out_of(kind, step + 1).wait()
+                forward(kind, step + 1).start()
+
+        @pl.when(step == 0)
+        def _():
+            for copy in kept + swapped:
+                copy.wait()
+
+        for kind in range(2):
+            forward(kind, step).wait()
+        other = partner_of(group, step)
+        tile = jnp.concatenate([rows[0, other], rows[1, other]], axis=0)
+        grad = jnp.concatenate([grads[0, other], grads[1, other]], axis=0)
+        ret = jnp.zeros(tile.shape, F32)
+        back = jnp.zeros(tile.shape, F32)
+        for part in range(2):
+            w_gate, w_up, w_down = weights[0, part], weights[1, part], weights[2, part]
+            gate_part = mm(tile, w_gate, NT)
+            up_part = mm(tile, w_up, NT)
+            grad_hidden = mm(grad, w_down, NT)
+            bent, slope = gelu_parts(gate_part)
+            hidden = (bent * up_part).astype(BF16)
+            grad_gate = (grad_hidden * up_part * slope).astype(BF16)
+            grad_up = (grad_hidden * bent).astype(BF16)
+            ret = ret + mm(hidden, w_down)
+            back = back + mm(grad_gate, w_gate) + mm(grad_up, w_up)
+            sums[0, part] += mm(grad_gate, tile, TN)
+            sums[1, part] += mm(grad_up, tile, TN)
+            sums[2, part] += mm(hidden, grad, TN)
+        for kind, value in enumerate((ret, back)):
+            held = moved[kind][1]
+            held[0, other] = value[:half].astype(BF16)
+            held[1, other] = value[half:].astype(BF16)
+            partial_sum(kind, step).start()
+
+        @pl.when(step > 0)
+        def _():
+            finish(step - 1)
+
+        return carry
+
+    lax.fori_loop(0, groups, body, 0)
+    copies = []
+    for number, (own_ref, far_ref) in enumerate(((own_gate, far_gate), (own_up, far_up), (own_down, far_down))):
+        copies.append(pltpu.make_async_copy(sums.at[number, 0], own_ref, local.at[2 + number]))
+        copies[-1].start()
+        weights[number, 0] = sums[number, 1].astype(BF16)
+        copies.append(pltpu.make_async_copy(weights.at[number, 0], far_ref, local.at[5 + number]))
+        copies[-1].start()
+    finish(groups - 1)
+    for copy in copies:
+        copy.wait()
+    for kind in range(2):
+        own_result(kind).wait()
+        for step in range(1, groups):
+            result(kind, step).wait()
 
 
 def run_experts(rows, grads, w_gate, w_up, w_down):
-    total, width = rows.shape
+    slots, width = rows.shape
+    half = CAP // 2
+    groups = slots // half
     units = w_gate.shape[1]
-    tile = total // 5
-    weight_spec = pl.BlockSpec((2, units, width), lambda i: (0, 0, 0), pipeline_mode=pl.Buffered(1))
-    row_spec = pl.BlockSpec((tile, width), lambda i: (i, 0))
     anywhere = pl.BlockSpec(memory_space=pl.ANY)
+    pair = pltpu.SemaphoreType.DMA((2, groups))
     return pl.pallas_call(
         expert_kernel,
-        grid=(5,),
-        in_specs=[row_spec, row_spec, weight_spec, weight_spec, weight_spec],
-        out_specs=[row_spec, row_spec] + [anywhere] * 6,
-        out_shape=[jax.ShapeDtypeStruct((total, width), BF16)] * 2
+        in_specs=[anywhere] * 5,
+        out_specs=[anywhere] * 8,
+        out_shape=[jax.ShapeDtypeStruct((slots, width), BF16)] * 2
         + [jax.ShapeDtypeStruct((units, width), F32)] * 3
         + [jax.ShapeDtypeStruct((units, width), BF16)] * 3,
-        scratch_shapes=[pltpu.VMEM((2, units, width), F32)] * 3
-        + [pltpu.VMEM((3, units, width), BF16), pltpu.SemaphoreType.DMA((6,))],
-        compiler_params=params(60),
-        cost_estimate=cost(36 * total * units * width, 8 * total * width + 30 * units * width),
+        scratch_shapes=[
+            pltpu.VMEM((2, groups, half, width), BF16),
+            pltpu.VMEM((2, groups, half, width), BF16),
+            pltpu.VMEM((3, 2, units, width), BF16),
+            pltpu.VMEM((3, 2, units, width), F32),
+            pltpu.VMEM((2, groups, half, width), BF16),
+        ]
+        + [pair] * 8
+        + [pltpu.SemaphoreType.DMA((3,))] * 2
+        + [pltpu.SemaphoreType.DMA((8,))],
+        compiler_params=pltpu.CompilerParams(
+            vmem_limit_bytes=60 * MIB, collective_id=1, has_side_effects=True
+        ),
+        cost_estimate=cost(72 * slots * units * width, 16 * slots * width + 30 * units * width),
     )(rows, grads, w_gate, w_up, w_down)
 
 
@@ -636,14 +766,6 @@
     half = CAP // 2
     share = SEQ // ranks
     across = [(r, r ^ 1) for r in range(ranks)]
-    along = [(r, r ^ 2) for r in range(ranks)]
-
-    def trade(weights):
-        mine = lax.dynamic_index_in_dim(weights, pair_class, 0, keepdims=True)
-        other = lax.dynamic_index_in_dim(weights, 1 - pair_class, 0, keepdims=True)
-        return jnp.concatenate([mine, lax.ppermute(other, "tensor", across)], axis=0)
-
-    w_gate, w_up, w_down = trade(expert_gate), trade(expert_up), trade(expert_down)
 
     gain_col = gain_one[:, None]
     w_in = attn_in.reshape(-1, width)
@@ -681,26 +803,9 @@
     slots = groups * half
     rows, row_grads, dy_rows, gate_rows = dispatch(code, gates, full_h2[0], full_h2[1], dy, slots)
 
-    def to_owners(array):
-        moved = lax.all_to_all(
-            array.reshape(groups, half, width), "expert", split_axis=0, concat_axis=0, tiled=True
-        )
-        return moved.reshape(slots, width)
-
-    got_rows = to_owners(rows)
-    far_rows = lax.ppermute(got_rows, "tensor", along)
-    got_grads = to_owners(row_grads)
-    far_grads = lax.ppermute(got_grads, "tensor", along)
     (ret, back, own_gate, own_up, own_down, far_gate, far_up, far_down) = run_experts(
-        jnp.concatenate([got_rows, far_rows]), jnp.concatenate([got_grads, far_grads]), w_gate, w_up, w_down
-    )
-
-    def from_owners(array):
-        other = lax.ppermute(array[slots:], "tensor", along)
-        return to_owners((array[:slots].astype(F32) + other.astype(F32)).astype(BF16))
-
-    ret = from_owners(ret)
-    back = from_owners(back)
+        rows, row_grads, expert_gate, expert_up, expert_down
+    )
     grad_logit, scaled = pair_grads(code, gates, routes_t, dy_rows, ret, gate_rows)
     partial_h2 = spread(code_cols, back, grad_logit.T, router)
     partial_y = spread(code_cols, scaled)

time: 1470 us -> 1300 us (0.88)
  waiting for transfers between devices: 930 us -> 645 us
  Pallas kernels: 258 us -> 492 us
  blocking collectives: 81.8 us -> 16.9 us
  other arithmetic: 79.1 us -> 57.8 us
  starting transfers between devices: 25.8 us -> 4.74 us
    pallas_call x1, Pallas kernels: 88.4 us -> 323 us  [run_experts(): pl.pallas_call(expert_kernel, in_specs=[anywhere] * 5, out_specs=[anywher...]
    ppermute x7 -> x0, waiting for transfers between devices: 202 us -> none  [the longest x2 115 us: from_owners(): other = lax.ppermute(array[slots:], 'tensor', along)]
    all_to_all x3 -> x0, waiting for transfers between devices: 107 us -> none  [to_owners(): lax.all_to_all(array.reshape(groups, half, width), 'expert', split_axis=0...]
    all_to_all x1 -> x0, blocking collectives: 65 us -> none  [to_owners(): lax.all_to_all(array.reshape(groups, half, width), 'expert', split_axis=0...]
    reduce_scatter x2, waiting for transfers between devices: 56.4 us -> 84.8 us  [on_device(): lax.psum_scatter(partial_h2[span], 'tensor', scatter_dimension=0, tiled=T...]
    concatenate x5 -> x0, other arithmetic: 14.9 us -> none  [the longest x3 5.59 us: trade(): jnp.concatenate([mine, lax.ppermute(other, 'tensor', across)], axis=0)]
  transfers between devices with their start and end apart: 31 -> 21, of which waited for: 24 -> 17; matrix products, arithmetic and copies ran while one was open for 8% -> 7% of each run, Pallas kernels for 7% -> 7%
where the time goes in v2:
time: 1300 us; the launch traced here: 1290 us
  waiting for transfers between devices  645 us (50%)
  Pallas kernels  492 us (38%)
  other arithmetic  57.8 us (4%)
  local copies, waits for them, and re-layouts  51.5 us (4%)
  blocking collectives  16.9 us (1%)
  between operations  14.8 us (1%)
    pallas_call x1, Pallas kernels, run_experts(): pl.pallas_call(expert_kernel, in_specs=[anywhere] * 5, out_specs=[anywher...  323 us
    ppermute x3, waiting for transfers between devices, give(): got = lax.ppermute(other, 'tensor', across).astype(F32)  112 us
    psum x1, waiting for transfers between devices, on_device(): lax.psum(jnp.concatenate([grad_gain_one[None], grad_gain_two[None], grad_...  101 us
    reduce_scatter x2, waiting for transfers between devices, on_device(): lax.psum_scatter(partial_h2[span], 'tensor', scatter_dimension=0, tiled=T...  84.8 us
    reduce_scatter x2, waiting for transfers between devices, on_device(): lax.psum_scatter(partial_y[span], 'tensor', scatter_dimension=0, tiled=True)  75.1 us
    all_gather x2, waiting for transfers between devices, on_device(): lax.all_gather(grad.astype(BF16)[None], 'tensor', axis=0, tiled=True)  68.7 us
    reduce_scatter x2, waiting for transfers between devices, on_device(): summed = lax.psum_scatter(sent, 'tensor', scatter_dimension=0, tiled=True)  60.9 us
    all_gather x2, waiting for transfers between devices, on_device(): full_h2.append(lax.all_gather(normed, 'tensor', axis=0, tiled=True))  60.5 us
  transfers between devices with their start and end apart: 21, of which 17 were waited for; matrix products, arithmetic and copies ran while one was open for 7% of the time, Pallas kernels for 7%

profile of v2, /device:TPU:0, one launch (start us, length us, event | category | flops | bytes accessed | tf_op | source)
XLA Modules:
  0.0 1293.1 jit_solution(15157012504541826265)
XLA Ops:
  12.4 6.4 shard_map.213.tiles_ref
  18.8 8.3 shard_map.212
  27.1 13.0 %shard_map.216 = (bf16[256,1024]{1,0:T(8,128)(2,1)}, f32[4,1,1024]{2,1,0:T(1,128)}, bf16[1024,1024]{1,0:T(8,128)(2,1)}) custom-call(bf16[768,2048]{1,0:T(8,128)(2,1)} %get-tuple-element.47.q_ref.k_ref.v_ref, bf16[768,2048]{1,0:T(8,128)(2,1)} %get-tuple-element.47.q_ref.k_ref.v_ref, bf16[768,2048]{1,0:T(8,128)(2,1)} %get-tuple-element.47.q_ref.k_ref.v_ref, ...), custom_call_target="tpu_custom_call" | custom-call | flops 2147483648 | bytes 8388608 | tf_op jit(solution)/shard_map/pallas_call | solution.py:194
  40.1 13.0 %shard_map.214 = (bf16[256,1024]{1,0:T(8,128)(2,1)}, f32[4,1,1024]{2,1,0:T(1,128)}, bf16[1024,1024]{1,0:T(8,128)(2,1)}) custom-call(bf16[768,2048]{1,0:T(8,128)(2,1)} %get-tuple-element.47.q_ref.k_ref.v_ref, bf16[768,2048]{1,0:T(8,128)(2,1)} %get-tuple-element.47.q_ref.k_ref.v_ref, bf16[768,2048]{1,0:T(8,128)(2,1)} %get-tuple-element.47.q_ref.k_ref.v_ref, ...), custom_call_target="tpu_custom_call" | custom-call | flops 2147483648 | bytes 8388608 | tf_op jit(solution)/shard_map/pallas_call | solution.py:194
  55.0 23.2 %reduce-scatter.15.cloned.1.call-done = bf16[256,1024]{1,0:T(8,128)(2,1)} async-done(((bf16[1024,1024]{1,0:T(8,128)(2,1)}), bf16[256,1024]{1,0:T(8,128)(2,1)}) %reduce-scatter.15.cloned.1.call-update) | async-done | bytes 524304 | tf_op jit(solution)/shard_map/reduce_scatter | solution.py:792
  79.5 37.7 %reduce-scatter.13.cloned.1.call-done = bf16[256,1024]{1,0:T(8,128)(2,1)} async-done(((bf16[1024,1024]{1,0:T(8,128)(2,1)}), bf16[256,1024]{1,0:T(8,128)(2,1)}) %reduce-scatter.13.cloned.1.call-update) | async-done | bytes 524304 | tf_op jit(solution)/shard_map/reduce_scatter | solution.py:792
  118.5 2.6 multiply_convert_fusion
  125.1 2.1 copy.86
  127.2 6.5 copy.88
  133.6 22.9 %all-gather.15.cloned.1.call-done.h1_ref = bf16[1024,1024]{1,0:T(8,128)(2,1)} async-done(((bf16[256,1024]{1,0:T(8,128)(2,1)}), bf16[1024,1024]{1,0:T(8,128)(2,1)}) %all-gather.15.cloned.1.call-update) | async-done | bytes 2097168 | tf_op jit(solution)/shard_map/all_gather | solution.py:800
  156.5 37.6 %all-gather.13.cloned.1.call-done.h0_ref = bf16[1024,1024]{1,0:T(8,128)(2,1)} async-done(((bf16[256,1024]{1,0:T(8,128)(2,1)}), bf16[1024,1024]{1,0:T(8,128)(2,1)}) %all-gather.13.cloned.1.call-update) | async-done | bytes 2097168 | tf_op jit(solution)/shard_map/all_gather | solution.py:800
  194.1 4.1 shard_map.217.gates_ref
  198.2 17.2 %shard_map.218 = (bf16[1280,1024]{1,0:T(8,128)(2,1)}, bf16[1280,1024]{1,0:T(8,128)(2,1)}, bf16[1280,1024]{1,0:T(8,128)(2,1)}, f32[1280,1]{1,0:T(8,128)}) custom-call(s32[2,2048]{1,0:T(2,128)} %shard_map.215.code_ref, f32[2,2048]{1,0:T(2,128)} %shard_map.217.gates_ref, bf16[1024,1024]{1,0:T(8,128)(2,1)} %all-gather.13.cloned.1.call-done.h0_ref, ...), custom_call_target="tpu_custom_call" | custom-call | flops 10737418240 | bytes 16252928 | tf_op jit(solution)/shard_map/pallas_call | solution.py:441
  215.5 322.6 %shard_map.219 = (bf16[1280,1024]{1,0:T(8,128)(2,1)}, bf16[1280,1024]{1,0:T(8,128)(2,1)}, f32[704,1024]{1,0:T(8,128)}, f32[704,1024]{1,0:T(8,128)}, f32[704,1024...) custom-call(bf16[1280,1024]{1,0:T(8,128)(2,1)} %get-tuple-element.51.rows_in, ...), custom_call_target="tpu_custom_call" | custom-call | flops 66437775360 | bytes 42598400 | tf_op jit(solution)/shard_map/pallas_call | solution.py:638
  538.1 8.2 shard_map.220
  546.3 2.2 copy.92
  548.5 11.2 shard_map.223
  559.7 4.7 fusion.49
  565.1 9.4 shard_map.221
  574.4 4.7 fusion.50
  579.9 46.5 %reduce-scatter.21.cloned.1.call-done = bf16[256,1024]{1,0:T(8,128)(2,1)} async-done(((bf16[1024,1024]{1,0:T(8,128)(2,1)}), bf16[256,1024]{1,0:T(8,128)(2,1)}) %reduce-scatter.21.cloned.1.call-update) | async-done | bytes 524304 | tf_op jit(solution)/shard_map/reduce_scatter | solution.py:821
  626.4 38.3 %reduce-scatter.23.cloned.1.call-done = bf16[256,1024]{1,0:T(8,128)(2,1)} async-done(((bf16[1024,1024]{1,0:T(8,128)(2,1)}), bf16[256,1024]{1,0:T(8,128)(2,1)}) %reduce-scatter.23.cloned.1.call-update) | async-done | bytes 524304 | tf_op jit(solution)/shard_map/reduce_scatter | solution.py:821
  664.8 2.1 fusion.26
  666.9 36.6 %reduce-scatter.17.cloned.1.call-done = bf16[256,1024]{1,0:T(8,128)(2,1)} async-done(((bf16[1024,1024]{1,0:T(8,128)(2,1)}), bf16[256,1024]{1,0:T(8,128)(2,1)}) %reduce-scatter.17.cloned.1.call-update) | async-done | bytes 524304 | tf_op jit(solution)/shard_map/reduce_scatter | solution.py:831
  703.5 38.5 %reduce-scatter.19.cloned.1.call-done = bf16[256,1024]{1,0:T(8,128)(2,1)} async-done(((bf16[1024,1024]{1,0:T(8,128)(2,1)}), bf16[256,1024]{1,0:T(8,128)(2,1)}) %reduce-scatter.19.cloned.1.call-update) | async-done | bytes 524304 | tf_op jit(solution)/shard_map/reduce_scatter | solution.py:831
  742.0 3.7 fusion.47
  746.4 3.0 copy.91
  749.4 31.8 %all-gather.19.cloned.1.call-done.grad_ref = bf16[1024,1024]{1,0:T(8,128)(2,1)} async-done(((bf16[256,1024]{1,0:T(8,128)(2,1)}), bf16[1024,1024]{1,0:T(8,128)(2,1)}) %all-gather.19.cloned.1.call-update) | async-done | bytes 2097168 | tf_op jit(solution)/shard_map/all_gather | solution.py:828
  781.2 16.0 %shard_map.226 = (bf16[4,64,1024]{2,1,0:T(8,128)(2,1)}, bf16[4,64,1024]{2,1,0:T(8,128)(2,1)}, bf16[4,64,1024]{2,1,0:T(8,128)(2,1)}, f32[4,3,256,256]{3,2,1,0:T(8,128)}, f32[4,8,256]{2,1,0:T(8,128)}) custom-call(bf16[768,2048]{1,0:T(8,128)(2,1)} %get-tuple-element.47.q_ref.k_ref.v_ref, bf16[768,2048]{1,0:T(8,128)(2,1)} %get-tuple-element.47.q_ref.k_ref.v_ref, ...), custom_call_target="tpu_custom_call" | custom-call | flops 5368709120 | bytes 16777216 | tf_op jit(solution)/shard_map/pallas_call | solution.py:275
  797.2 10.2 shard_map.227
  807.4 11.4 all-gather.17.cloned.1.call-done.grad_ref
  818.8 16.0 %shard_map.224 = (bf16[4,64,1024]{2,1,0:T(8,128)(2,1)}, bf16[4,64,1024]{2,1,0:T(8,128)(2,1)}, bf16[4,64,1024]{2,1,0:T(8,128)(2,1)}, f32[4,3,256,256]{3,2,1,0:T(8,128)}, f32[4,8,256]{2,1,0:T(8,128)}) custom-call(bf16[768,2048]{1,0:T(8,128)(2,1)} %get-tuple-element.47.q_ref.k_ref.v_ref, bf16[768,2048]{1,0:T(8,128)(2,1)} %get-tuple-element.47.q_ref.k_ref.v_ref, ...), custom_call_target="tpu_custom_call" | custom-call | flops 5368709120 | bytes 16777216 | tf_op jit(solution)/shard_map/pallas_call | solution.py:275
  834.8 10.3 shard_map.225
  847.2 2.9 fusion.52
  850.2 3.3 fusion.6
  859.3 2.0 copy.100
  861.4 35.1 %reduce-scatter.25.cloned.1.call-done = bf16[1,1024,256]{2,1,0:T(8,128)(2,1)} async-done(((bf16[4,1024,256]{2,1,0:T(8,128)(2,1)}), bf16[1,1024,256]{2,1,0:T(8,128)(2,1)}) %reduce-scatter.25.cloned.1.call-update) | async-done | bytes 524304
  896.5 2.0 copy.96
  899.9 3.4 fusion.40
  904.0 2.9 fusion.15
  910.7 46.2 %collective-permute-done = bf16[704,1024]{1,0:T(8,128)(2,1)} collective-permute-done((bf16[704,1024]{1,0:T(8,128)(2,1)}, bf16[704,1024]{1,0:T(8,128)(2,1)}, u32[]{:S(2)}, u32[]{:S(2)}) %collective-permute-start) | collective-permute-done | bytes 1441824 | tf_op jit(solution)/shard_map/ppermute | solution.py:862
  956.8 3.3 fusion
  960.2 3.0 pad_maximum_fusion.1
  963.2 41.4 %collective-permute-done.1 = bf16[704,1024]{1,0:T(8,128)(2,1)} collective-permute-done((bf16[704,1024]{1,0:T(8,128)(2,1)}, bf16[704,1024]{1,0:T(8,128)(2,1)}, u32[]{:S(2)}, u32[]{:S(2)}) %collective-permute-start.1) | collective-permute-done | bytes 1441824 | tf_op jit(solution)/shard_map/ppermute | solution.py:862
  1004.6 2.4 fusion.2
  1007.0 3.0 pad_maximum_fusion.2
  1010.1 24.9 %collective-permute-done.2 = bf16[704,1024]{1,0:T(8,128)(2,1)S(1)} collective-permute-done((bf16[704,1024]{1,0:T(8,128)(2,1)}, bf16[704,1024]{1,0:T(8,128)(2,1)S(1)}, u32[]{:S(2)}, u32[]{:S(2)}) %collective-permute-start.2) | collective-permute-done | bytes 1441824 | tf_op jit(solution)/shard_map/ppermute | solution.py:862
  1036.0 3.0 pad_maximum_fusion.3
  1039.0 3.3 copy.103
  1042.4 4.1 copy.102
  1046.5 4.0 pad_maximum_fusion.4.in_ref
  1050.5 7.9 shard_map.222
  1059.0 3.3 pad_maximum_fusion.near_ref
  1062.4 9.4 shard_map.229
  1072.7 16.9 %psum.30 = f32[32,4]{0,1:T(4,128)} all-reduce(f32[32,4]{0,1:T(4,128)S(1)} %bitcast.157), channel_id=1, replica_groups=mesh['expert'=8,'tensor'=4] {'expert'}, use_global_device_ids=true, to_apply=%region_21.22 | all-reduce | flops 128 | bytes 1024 | tf_op jit(solution)/shard_map/psum | solution.py:872
  1089.6 2.1 convert_element_type.135
  1091.7 3.5 reshape.137
  1095.2 100.7 %all-reduce.6.cloned.1.call-done = f32[18,1024]{1,0:T(8,128)} async-done(((f32[18,1024]{1,0:T(8,128)}), f32[18,1024]{1,0:T(8,128)}) %all-reduce.6.cloned.1.call-update) | async-done | bytes 73744 | tf_op jit(solution)/shard_map/psum | solution.py:867
  1198.9 34.9 %all-gather.27.cloned.1.call-done = bf16[4096,256]{0,1:T(8,128)(2,1)} async-done(((bf16[1024,256]{0,1:T(8,128)(2,1)}), bf16[4096,256]{0,1:T(8,128)(2,1)}) %all-gather.27.cloned.1.call-update) | async-done | bytes 2097168 | tf_op jit(solution)/shard_map/all_gather | solution.py:856
  1233.8 3.3 copy.101
  1237.0 33.8 %all-gather.25.cloned.1.call-done = bf16[4096,256]{0,1:T(8,128)(2,1)} async-done(((bf16[1024,256]{0,1:T(8,128)(2,1)}), bf16[4096,256]{0,1:T(8,128)(2,1)}) %all-gather.25.cloned.1.call-update) | async-done | bytes 2097168 | tf_op jit(solution)/shard_map/all_gather | solution.py:856
  1270.8 4.1 copy.97
  1274.9 3.9 pad_maximum_fusion.5.in_ref
  1278.8 7.3 shard_map.228
  (105 shorter events, 35.1 us)
Async XLA Ops:
  7.2 71.0 %reduce-scatter.15.cloned.1.call-start = ((), (), s32[]{:S(2)}) async-start(), calls=%async_computation.10 | async-start | bytes 2621440 | tf_op jit(solution)/shard_map/reduce_scatter | solution.py:792
  40.1 77.1 %reduce-scatter.13.cloned.1.call-start = ((), (), s32[]{:S(2)}) async-start(), calls=%async_computation.8 | async-start | bytes 2621440 | tf_op jit(solution)/shard_map/reduce_scatter | solution.py:792
  53.2 103.4 %all-gather.15.cloned.1.call-start = ((), (), s32[]{:S(2)}) async-start(), calls=%async_computation.11 | async-start | bytes 2621440 | tf_op jit(solution)/shard_map/all_gather | solution.py:800
  53.2 65.3 %copy-start.13 = (f32[1024]{0:T(1024)S(1)}, f32[1024]{0:T(1024)}, u32[]{:S(2)}) copy-start(f32[1024]{0:T(1024)} %param.18) | copy-start | bytes 12292
  79.4 42.6 %copy-start.12 = (bf16[1024,16]{0,1:T(8,128)(2,1)S(1)}, bf16[1024,16]{0,1:T(8,128)(2,1)}, u32[]{:S(2)}) copy-start(bf16[1024,16]{0,1:T(8,128)(2,1)} %param.19) | copy-start | bytes 98308
  121.1 73.1 %all-gather.13.cloned.1.call-start = ((), (), s32[]{:S(2)}) async-start(), calls=%async_computation.9 | async-start | bytes 2621440 | tf_op jit(solution)/shard_map/all_gather | solution.py:800
  121.7 504.8 %reduce-scatter.21.cloned.1.call-start = ((), (), s32[]{:S(2)}) async-start(), calls=%async_computation.14 | async-start | bytes 2621440 | tf_op jit(solution)/shard_map/reduce_scatter | solution.py:821
  564.4 100.3 %reduce-scatter.23.cloned.1.call-start = ((), (), s32[]{:S(2)}) async-start(), calls=%async_computation.16 | async-start | bytes 2621440 | tf_op jit(solution)/shard_map/reduce_scatter | solution.py:821
  565.0 138.5 %reduce-scatter.17.cloned.1.call-start = ((), (), s32[]{:S(2)}) async-start(), calls=%async_computation.12 | async-start | bytes 2621440 | tf_op jit(solution)/shard_map/reduce_scatter | solution.py:831
  579.1 85.7 %copy-start = (bf16[256,1024]{1,0:T(8,128)(2,1)S(1)}, bf16[256,1024]{1,0:T(8,128)(2,1)}, u32[]{:S(2)}) copy-start(bf16[256,1024]{1,0:T(8,128)(2,1)} %reduce-scatter.13.cloned.1.call-done) | copy-start | bytes 1572868
  579.1 85.7 %copy-start.1 = (bf16[256,1024]{1,0:T(8,128)(2,1)S(1)}, bf16[256,1024]{1,0:T(8,128)(2,1)}, u32[]{:S(2)}) copy-start(bf16[256,1024]{1,0:T(8,128)(2,1)} %reduce-scatter.15.cloned.1.call-done) | copy-start | bytes 1572868
  579.1 162.8 %reduce-scatter.19.cloned.1.call-start = ((), (), s32[]{:S(2)}) async-start(), calls=%async_computation.13 | async-start | bytes 2621440 | tf_op jit(solution)/shard_map/reduce_scatter | solution.py:831
  579.9 201.3 %all-gather.19.cloned.1.call-start = ((), (), s32[]{:S(2)}) async-start(), calls=%async_computation.17 | async-start | bytes 2621440 | tf_op jit(solution)/shard_map/all_gather | solution.py:828
  626.4 115.5 %copy-start.2 = (bf16[256,1024]{1,0:T(8,128)(2,1)S(1)}, bf16[256,1024]{1,0:T(8,128)(2,1)}, u32[]{:S(2)}) copy-start(bf16[256,1024]{1,0:T(8,128)(2,1)} %reduce-scatter.21.cloned.1.call-done) | copy-start | bytes 1572868
  664.8 77.2 %copy-start.3 = (bf16[256,1024]{1,0:T(8,128)(2,1)S(1)}, bf16[256,1024]{1,0:T(8,128)(2,1)}, u32[]{:S(2)}) copy-start(bf16[256,1024]{1,0:T(8,128)(2,1)} %reduce-scatter.23.cloned.1.call-done) | copy-start | bytes 1572868
  745.7 73.1 %all-gather.17.cloned.1.call-start = ((), (), s32[]{:S(2)}) async-start(), calls=%async_computation.15 | async-start | bytes 2621440 | tf_op jit(solution)/shard_map/all_gather | solution.py:828
  746.3 113.0 %reduce-scatter.27.cloned.1.call-start = ((), (), s32[]{:S(2)}) async-start(), calls=%async_computation.24 | async-start | bytes 2621440
  807.4 89.1 %reduce-scatter.25.cloned.1.call-start = ((), (), s32[]{:S(2)}) async-start(), calls=%async_computation.23 | async-start | bytes 2621440
  845.2 193.9 %all-gather.23.cloned.1.call-start = ((), (), s32[]{:S(2)}) async-start(), calls=%async_computation.20 | async-start | bytes 2621440 | tf_op jit(solution)/shard_map/all_gather | solution.py:833
  845.9 196.4 %all-gather.21.cloned.1.call-start = ((), (), s32[]{:S(2)}) async-start(), calls=%async_computation.19 | async-start | bytes 2621440 | tf_op jit(solution)/shard_map/all_gather | solution.py:833
  846.5 243.1 %all-reduce.8.cloned.1.call-start = ((), (), s32[]{:S(2)}) async-start(), calls=%async_computation.25 | async-start | bytes 4194304 | tf_op jit(solution)/shard_map/psum | solution.py:871
  846.5 3.6 copy-start.11
  847.2 6.2 copy-start.7
  850.2 3.3 copy-start.6
  853.5 1.8 copy-start.10
  855.2 43.3 %copy-start.14 = (f32[1024]{0:T(1024)S(1)}, f32[1024]{0:T(1024)}, u32[]{:S(2)}) copy-start(f32[1024]{0:T(1024)} %param.14) | copy-start | bytes 12292
  855.2 340.6 %all-reduce.6.cloned.1.call-start = ((), (), s32[]{:S(2)}) async-start(), calls=%async_computation.18 | async-start | bytes 196608 | tf_op jit(solution)/shard_map/psum | solution.py:867
  903.9 329.8 %all-gather.27.cloned.1.call-start = ((), (), s32[]{:S(2)}) async-start(), calls=%async_computation.22 | async-start | bytes 2621440 | tf_op jit(solution)/shard_map/all_gather | solution.py:856
  906.9 363.9 %all-gather.25.cloned.1.call-start = ((), (), s32[]{:S(2)}) async-start(), calls=%async_computation.21 | async-start | bytes 2621440 | tf_op jit(solution)/shard_map/all_gather | solution.py:856
  907.2 49.7 %collective-permute-start = (bf16[704,1024]{1,0:T(8,128)(2,1)}, bf16[704,1024]{1,0:T(8,128)(2,1)}, u32[]{:S(2)}, u32[]{:S(2)}) collective-permute-start(bf16[704,1024]{1,0:T(8,128)(2,1)} %get-tuple-element.78), channel_id=1, source_target_pairs={{0,1},{1,0},{2,3},{3,2},{4,5},{5,4},{6,7},{7,6},{8,9},{9,8},{10,11... | collective-permute-start | bytes 4325384 | tf_op jit(solution)/shard_map/ppermute | solution.py:862
  908.6 96.0 %collective-permute-start.1 = (bf16[704,1024]{1,0:T(8,128)(2,1)}, bf16[704,1024]{1,0:T(8,128)(2,1)}, u32[]{:S(2)}, u32[]{:S(2)}) collective-permute-start(bf16[704,1024]{1,0:T(8,128)(2,1)} %get-tuple-element.80), channel_id=1, source_target_pairs={{0,1},{1,0},{2,3},{3,2},{4,5},{5,4},{6,7},{7,6},{8,9},{9,8},{10,11... | collective-permute-start | bytes 4325384 | tf_op jit(solution)/shard_map/ppermute | solution.py:862
  909.3 125.7 %collective-permute-start.2 = (bf16[704,1024]{1,0:T(8,128)(2,1)}, bf16[704,1024]{1,0:T(8,128)(2,1)S(1)}, u32[]{:S(2)}, u32[]{:S(2)}) collective-permute-start(bf16[704,1024]{1,0:T(8,128)(2,1)} %get-tuple-element.82), channel_id=1, source_target_pairs={{0,1},{1,0},{2,3},{3,2},{4,5},{5,4},{6,7},{7,6},{8,9},{9,8},{10,11... | collective-permute-start | bytes 4325384 | tf_op jit(solution)/shard_map/ppermute | solution.py:862
  960.1 44.4 %copy-start.9 = (f32[704,1024]{1,0:T(8,128)S(1)}, f32[704,1024]{1,0:T(8,128)}, u32[]{:S(2)}) copy-start(f32[704,1024]{1,0:T(8,128)} %get-tuple-element.79) | copy-start | bytes 8650756
  1007.0 27.9 %copy-start.8 = (f32[704,1024]{1,0:T(8,128)S(1)}, f32[704,1024]{1,0:T(8,128)}, u32[]{:S(2)}) copy-start(f32[704,1024]{1,0:T(8,128)} %get-tuple-element.81) | copy-start | bytes 8650756
  1050.5 7.9 copy-start.15
  1050.5 7.9 copy-start.16
  1050.5 8.6 copy-start.4
  1050.5 8.6 copy-start.5
Sparse Core Ops, SparseCore 0:
  40.2 37.8 reduce-scatter.14
  82.0 35.1 reduce-scatter.12
  121.2 35.2 all-gather.14
  158.8 35.2 all-gather.12
  564.6 61.8 reduce-scatter.20
  629.5 35.1 reduce-scatter.22
  668.3 35.1 reduce-scatter.16
  706.7 35.1 reduce-scatter.18
  745.9 35.2 all-gather.18
  783.5 35.2 all-gather.16
  822.4 35.1 reduce-scatter.26
  861.3 35.1 reduce-scatter.24
  898.3 50.7 all-gather.22
  950.8 52.1 all-gather.20
  1005.3 64.9 all-reduce.7
  1075.7 120.1 all-reduce.5
  1197.6 36.1 all-gather.26
  1235.5 35.2 all-gather.24

commit v3 on v2

--- a/solution.py
+++ b/solution.py
@@ -110,7 +110,7 @@
 
 
 def bias_fold_kernel(near_ref, far_ref, out_ref):
-    heads = near_ref.shape[1]
+    heads = out_ref.shape[0]
     key_at = lax.broadcasted_iota(jnp.int32, (BLK, BLK), 0)
     query_at = lax.broadcasted_iota(jnp.int32, (BLK, BLK), 1)
     totals = [[jnp.zeros((8, BLK), F32) for _ in range(BUCKETS)] for _ in range(heads)]
@@ -118,14 +118,14 @@
         bucket = bucket_of(key_at - query_at + shift * BLK)
         low, high = {-1: (0, 16), 0: (0, 32), 1: (16, 32)}[shift]
         for head in range(heads):
-            grads = near_ref[0, head, number] + near_ref[1, head, number]
+            grads = near_ref[head, number] + near_ref[heads + head, number]
             for index in range(low, high):
                 kept = jnp.where(bucket == index, grads, 0.0)
                 totals[head][index] = totals[head][index] + jnp.sum(
                     kept.reshape(BLK // 8, 8, BLK), axis=0
                 )
     for head in range(heads):
-        totals[head][15] = totals[head][15] + far_ref[0, head] + far_ref[1, head]
+        totals[head][15] = totals[head][15] + far_ref[head] + far_ref[heads + head]
         for index in range(BUCKETS):
             line = jnp.sum(totals[head][index], axis=0, keepdims=True)
             out_ref[head, index : index + 1, :] = jnp.broadcast_to(
@@ -134,7 +134,7 @@
 
 
 def bias_fold(near, far):
-    heads = near.shape[1]
+    heads = near.shape[0] // 2
     return pl.pallas_call(
         bias_fold_kernel,
         in_specs=[pl.BlockSpec(memory_space=pltpu.VMEM)] * 2,
@@ -166,7 +166,7 @@
 
 
 def attend_kernel(q_ref, k_ref, v_ref, tiles_ref, limit_ref, w_ref, out_ref, lse_ref, sent_ref, held):
-    head = pl.program_id(0)
+    head = pl.program_id(1)
     width = q_ref.shape[0]
     queries = q_ref[...] * BF16(0.125)
     keys, values = k_ref[...], v_ref[...]
@@ -182,47 +182,61 @@
         held[pl.ds(pl.multiple_of(head * width, width), width), cols] = mixed
         lse_ref[0, :, cols] = top + jnp.log(total)
 
-    @pl.when(head == pl.num_programs(0) - 1)
+    @pl.when(head == pl.num_programs(1) - 1)
     def _():
         sent_ref[...] = mm(held[...], w_ref[...], TN).astype(BF16)
 
 
-def attend(qkv, tiles, limits, attn_out, seq):
+def attend(qkv, tiles, limits, attn_out):
     heads = tiles.shape[0]
+    seqs = limits.shape[0]
     width = qkv.shape[0] // (3 * heads)
     model_width = attn_out.shape[1]
     return pl.pallas_call(
         attend_kernel,
-        grid=(heads,),
+        grid=(seqs, heads),
         in_specs=[
-            pl.BlockSpec((width, SEQ), lambda h: (h, seq)),
-            pl.BlockSpec((width, SEQ), lambda h: (heads + h, seq)),
-            pl.BlockSpec((width, SEQ), lambda h: (2 * heads + h, seq)),
-            pl.BlockSpec((1, 3, BLK, BLK), lambda h: (h, 0, 0, 0)),
-            pl.BlockSpec((1, 1, SEQ), lambda h: (seq, 0, 0)),
-            pl.BlockSpec((heads * width, model_width), lambda h: (0, 0)),
+            pl.BlockSpec((width, SEQ), lambda s, h: (h, s)),
+            pl.BlockSpec((width, SEQ), lambda s, h: (heads + h, s)),
+            pl.BlockSpec((width, SEQ), lambda s, h: (2 * heads + h, s)),
+            pl.BlockSpec((1, 3, BLK, BLK), lambda s, h: (h, 0, 0, 0)),
+            pl.BlockSpec((1, 1, SEQ), lambda s, h: (s, 0, 0)),
+            pl.BlockSpec((heads * width, model_width), lambda s, h: (0, 0)),
         ],
         out_specs=[
-            pl.BlockSpec((width, SEQ), lambda h: (h, 0)),
-            pl.BlockSpec((1, 1, SEQ), lambda h: (h, 0, 0)),
-            pl.BlockSpec((SEQ, model_width), lambda h: (0, 0)),
+            pl.BlockSpec((width, SEQ), lambda s, h: (h, s)),
+            pl.BlockSpec((1, 1, SEQ), lambda s, h: (s * heads + h, 0, 0)),
+            pl.BlockSpec((SEQ, model_width), lambda s, h: (s, 0)),
         ],
         out_shape=[
-            jax.ShapeDtypeStruct((heads * width, SEQ), BF16),
-            jax.ShapeDtypeStruct((heads, 1, SEQ), F32),
-            jax.ShapeDtypeStruct((SEQ, model_width), BF16),
+            jax.ShapeDtypeStruct((heads * width, seqs * SEQ), BF16),
+            jax.ShapeDtypeStruct((seqs * heads, 1, SEQ), F32),
+            jax.ShapeDtypeStruct((seqs * SEQ, model_width), BF16),
         ],
         scratch_shapes=[pltpu.VMEM((heads * width, SEQ), BF16)],
         compiler_params=params(),
-        cost_estimate=cost(heads * SEQ * SEQ * 512, heads * SEQ * 2048, heads * SEQ * SEQ),
+        cost_estimate=cost(seqs * heads * SEQ * SEQ * 512, seqs * heads * SEQ * 2048, seqs * heads * SEQ * SEQ),
     )(qkv, qkv, qkv, tiles, limits, attn_out)
 
 
 def attend_back_kernel(
-    q_ref, k_ref, v_ref, tiles_ref, limit_ref, w_ref, grad_ref, lse_ref,
-    dq_ref, dk_ref, dv_ref, near_ref, far_ref, held,
+    place_ref, q_ref, k_ref, v_ref, tiles_ref, limit_ref, w_ref, grad_ref, lse_ref, *refs
 ):
-    head = pl.program_id(0)
+    own_refs, got_refs = refs[:3], refs[3:6]
+    dq_ref, dk_ref, dv_ref, near_ref, far_ref = refs[6:11]
+    placed_refs, held = refs[11:14], refs[14]
+
+    @pl.when(pl.program_id(0) == 0)
+    def _():
+        for source, target in zip(own_refs, placed_refs):
+            target[0] = source[...]
+
+    @pl.when(pl.program_id(0) == 1)
+    def _():
+        for source, target in zip(got_refs, placed_refs):
+            target[0] = source[...].astype(F32)
+
+    head = pl.program_id(1)
     width = q_ref.shape[0]
 
     @pl.when(head == 0)
@@ -261,92 +275,298 @@
             filler = jnp.zeros((width, SEQ - count), F32)
             grad_values = grad_values + jnp.concatenate([add_values, filler], axis=1)
             grad_keys = grad_keys + jnp.concatenate([add_keys, filler], axis=1)
-        dq_ref[0, :, cols] = (mm(keys[:, :count], rounded) * 0.125).astype(BF16)
-    dk_ref[0] = grad_keys.astype(BF16)
-    dv_ref[0] = grad_values.astype(BF16)
+        dq_ref[:, cols] = (mm(keys[:, :count], rounded) * 0.125).astype(BF16)
+    dk_ref[...] = grad_keys.astype(BF16)
+    dv_ref[...] = grad_values.astype(BF16)
     far_ref[0] = far
 
 
-def attend_back(qkv, tiles, limits, attn_out, grad_attn, lse, seq):
+def attend_back(place, qkv, tiles, limits, attn_out, grad_attn, lse, own_grads, got_grads):
     heads = tiles.shape[0]
+    seqs = limits.shape[0]
     width = qkv.shape[0] // (3 * heads)
     model_width = attn_out.shape[1]
-    grad_spec = pl.BlockSpec((1, width, SEQ), lambda h: (h, 0, 0))
+    units = own_grads[0].shape[0]
+    tile = units // heads
+    grad_spec = pl.BlockSpec((width, SEQ), lambda s, h, p: (h, s))
+    own_spec = pl.BlockSpec((tile, model_width), lambda s, h, p: (jnp.where(s == 0, h, heads - 1), 0))
+    got_spec = pl.BlockSpec((tile, model_width), lambda s, h, p: (jnp.where(s == 0, 0, h), 0))
+    placed_spec = pl.BlockSpec(
+        (1, tile, model_width), lambda s, h, p: (jnp.where(s == 0, p[0], 1 - p[0]), h, 0)
+    )
     return pl.pallas_call(
         attend_back_kernel,
-        grid=(heads,),
-        in_specs=[
-            pl.BlockSpec((width, SEQ), lambda h: (h, seq)),
-            pl.BlockSpec((width, SEQ), lambda h: (heads + h, seq)),
-            pl.BlockSpec((width, SEQ), lambda h: (2 * heads + h, seq)),
-            pl.BlockSpec((1, 3, BLK, BLK), lambda h: (h, 0, 0, 0)),
-            pl.BlockSpec((1, 1, SEQ), lambda h: (seq, 0, 0)),
-            pl.BlockSpec((heads * width, model_width), lambda h: (0, 0)),
-            pl.BlockSpec((SEQ, model_width), lambda h: (0, 0)),
-            pl.BlockSpec((1, 1, SEQ), lambda h: (h, 0, 0)),
-        ],
-        out_specs=[
-            grad_spec,
-            grad_spec,
-            grad_spec,
-            pl.BlockSpec((1, 3, BLK, BLK), lambda h: (h, 0, 0, 0)),
-            pl.BlockSpec((1, 8, BLK), lambda h: (h, 0, 0)),
-        ],
-        out_shape=[jax.ShapeDtypeStruct((heads, width, SEQ), BF16)] * 3
+        grid_spec=pltpu.PrefetchScalarGridSpec(
+            num_scalar_prefetch=1,
+            grid=(seqs, heads),
+            in_specs=[
+                pl.BlockSpec((width, SEQ), lambda s, h, p: (h, s)),
+                pl.BlockSpec((width, SEQ), lambda s, h, p: (heads + h, s)),
+                pl.BlockSpec((width, SEQ), lambda s, h, p: (2 * heads + h, s)),
+                pl.BlockSpec((1, 3, BLK, BLK), lambda s, h, p: (h, 0, 0, 0)),
+                pl.BlockSpec((1, 1, SEQ), lambda s, h, p: (s, 0, 0)),
+                pl.BlockSpec((heads * width, model_width), lambda s, h, p: (0, 0)),
+                pl.BlockSpec((SEQ, model_width), lambda s, h, p: (s, 0)),
+                pl.BlockSpec((1, 1, SEQ), lambda s, h, p: (s * heads + h, 0, 0)),
+            ]
+            + [own_spec] * 3
+            + [got_spec] * 3,
+            out_specs=[
+                grad_spec,
+                grad_spec,
+                grad_spec,
+                pl.BlockSpec((1, 3, BLK, BLK), lambda s, h, p: (s * heads + h, 0, 0, 0)),
+                pl.BlockSpec((1, 8, BLK), lambda s, h, p: (s * heads + h, 0, 0)),
+            ]
+            + [placed_spec] * 3,
+            scratch_shapes=[pltpu.VMEM((heads * width, SEQ), BF16)],
+        ),
+        out_shape=[jax.ShapeDtypeStruct((heads * width, seqs * SEQ), BF16)] * 3
         + [
-            jax.ShapeDtypeStruct((heads, 3, BLK, BLK), F32),
-            jax.ShapeDtypeStruct((heads, 8, BLK), F32),
-        ],
-        scratch_shapes=[pltpu.VMEM((heads * width, SEQ), BF16)],
+            jax.ShapeDtypeStruct((seqs * heads, 3, BLK, BLK), F32),
+            jax.ShapeDtypeStruct((seqs * heads, 8, BLK), F32),
+        ]
+        + [jax.ShapeDtypeStruct((2, units, model_width), F32)] * 3,
         compiler_params=params(),
-        cost_estimate=cost(heads * SEQ * SEQ * 1280, heads * SEQ * 4096, heads * SEQ * SEQ),
-    )(qkv, qkv, qkv, tiles, limits, attn_out, grad_attn, lse)
-
-
-def project_back_kernel(
-    x_ref, gain_ref, scale_ref, w_ref, *refs
-):
-    grad_refs, (weight_ref, out_ref) = refs[:3], refs[3:]
-    grads = jnp.concatenate([ref[...] for ref in grad_refs], axis=0)
-    normed = (x_ref[...].astype(F32) * scale_ref[...] * gain_ref[...]).astype(BF16)
-    update = mm(grads, normed, NT)
+        cost_estimate=cost(seqs * heads * SEQ * SEQ * 1280, seqs * heads * SEQ * 4096, seqs * heads * SEQ * SEQ),
+    )(place, qkv, qkv, qkv, tiles, limits, attn_out, grad_attn, lse, *own_grads, *got_grads)
+
+
+def project_back_kernel(x_ref, gain_ref, scale_ref, w_ref, dq_ref, dk_ref, dv_ref, weight_ref, out_ref, gain_grad_ref):
+    grads = jnp.concatenate([dq_ref[...], dk_ref[...], dv_ref[...]], axis=0)
+    scaled = x_ref[...].astype(F32) * scale_ref[...]
+    update = mm(grads, (scaled * gain_ref[...]).astype(BF16), NT)
+    back = mm(w_ref[...], grads, TN)
+    gain_update = jnp.sum(back * scaled, axis=1, keepdims=True)
 
     @pl.when(pl.program_id(0) == 0)
     def _():
         weight_ref[...] = update
+        gain_grad_ref[...] = gain_update
 
     @pl.when(pl.program_id(0) > 0)
     def _():
         weight_ref[...] += update
-
-    out_ref[0] = mm(w_ref[...], grads).astype(BF16)
-
-
-def project_back(x, gain, scale, weights_t, grads, seq, ranks):
-    width = x.shape[0]
-    rows = weights_t.shape[1]
-    tile = SEQ // ranks
+        gain_grad_ref[...] += gain_update
+
+    out_ref[...] = back.T.astype(BF16)
+
+
+def project_back(x, gain, scale, weights, grads):
+    width, tokens = x.shape
+    rows = weights.shape[0]
+    tile = 512
     return pl.pallas_call(
         project_back_kernel,
-        grid=(ranks,),
+        grid=(tokens // tile,),
         in_specs=[
-            pl.BlockSpec((width, tile), lambda i: (0, seq * ranks + i)),
+            pl.BlockSpec((width, tile), lambda i: (0, i)),
             pl.BlockSpec((width, 1), lambda i: (0, 0)),
-            pl.BlockSpec((1, tile), lambda i: (0, seq * ranks + i)),
-            pl.BlockSpec((width, rows), lambda i: (0, 0)),
+            pl.BlockSpec((1, tile), lambda i: (0, i)),
+            pl.BlockSpec((rows, width), lambda i: (0, 0)),
         ]
         + [pl.BlockSpec((rows // 3, tile), lambda i: (0, i))] * 3,
         out_specs=[
             pl.BlockSpec((rows, width), lambda i: (0, 0)),
-            pl.BlockSpec((1, width, tile), lambda i: (i, 0, 0)),
+            pl.BlockSpec((tile, width), lambda i: (i, 0)),
+            pl.BlockSpec((width, 1), lambda i: (0, 0)),
         ],
         out_shape=[
             jax.ShapeDtypeStruct((rows, width), F32),
-            jax.ShapeDtypeStruct((ranks, width, tile), BF16),
+            jax.ShapeDtypeStruct((tokens, width), BF16),
+            jax.ShapeDtypeStruct((width, 1), F32),
         ],
         compiler_params=params(),
-        cost_estimate=cost(4 * width * SEQ * rows, 6 * width * SEQ),
-    )(x, gain, scale, weights_t, *grads)
+        cost_estimate=cost(4 * width * tokens * rows, 6 * width * tokens),
+    )(x, gain, scale, weights, *grads)
+
+
+def exchange(math, rank, source, full, from_across, from_along, to_across, to_along, turn_across, turn_along, sends, recvs, ready=None, ready_full=None):
+    pair_class, half_index = rank % 2, rank // 2
+    across, along, corner = rank + 1 - 2 * pair_class, rank + 2 - 4 * half_index, 3 - rank
+    mesh_ids = pl.DeviceIdType.MESH
+    rows, width = source.shape[1:]
+    chunks = 4
+    size = rows // chunks
+    low, high = slice(0, width // 2), slice(width // 2, width)
+    barrier = pltpu.get_barrier_semaphore()
+    for other in (across, along):
+        pl.semaphore_signal(barrier, inc=1, device_id={"tensor": other}, device_id_type=mesh_ids)
+    pl.semaphore_wait(barrier, 2)
+
+    def remote(kind, chunk, origin, target, other):
+        return pltpu.make_async_remote_copy(
+            src_ref=origin, dst_ref=target, send_sem=sends.at[kind, chunk], recv_sem=recvs.at[kind, chunk],
+            device_id={"tensor": other}, device_id_type=mesh_ids,
+        )
+
+    spans = [slice(chunk * size, (chunk + 1) * size) for chunk in range(chunks)]
+    first, second, third, fourth = [], [], [], []
+    for chunk, span in enumerate(spans):
+        pair = (
+            remote(0, chunk, source.at[corner, span, low], turn_across.at[span], across),
+            remote(1, chunk, source.at[corner, span, high], turn_along.at[span], along),
+        )
+        for copy in pair:
+            copy.start()
+        first.append(pair)
+    if ready is not None:
+        ready_full[rank] = ready[...]
+        extra = [
+            remote(8, 0, ready, ready_full.at[rank], across),
+            remote(8, 1, ready, ready_full.at[rank], along),
+            remote(8, 2, ready_full.at[along, :, high], ready_full.at[along, :, high], across),
+            remote(8, 3, ready_full.at[across, :, low], ready_full.at[across, :, low], along),
+        ]
+    for chunk, span in enumerate(spans):
+        first[chunk][0].wait()
+        to_along[span, low] = (source[along, span, low].astype(F32) + turn_across[span].astype(F32)).astype(BF16)
+        to_along[span, high] = source[along, span, high]
+        first[chunk][1].wait()
+        to_across[span, low] = source[across, span, low]
+        to_across[span, high] = (source[across, span, high].astype(F32) + turn_along[span].astype(F32)).astype(BF16)
+        pair = (
+            remote(2, chunk, to_across.at[span], from_across.at[span], across),
+            remote(3, chunk, to_along.at[span], from_along.at[span], along),
+        )
+        for copy in pair:
+            copy.start()
+        second.append(pair)
+    if ready is not None:
+        for copy in extra[:2]:
+            copy.start()
+
+    def pass_on(chunk):
+        span = spans[chunk]
+        for copy in third[chunk]:
+            copy.wait()
+        pair = (
+            remote(6, chunk, full.at[along, span, high], full.at[along, span, high], across),
+            remote(7, chunk, full.at[across, span, low], full.at[across, span, low], along),
+        )
+        for copy in pair:
+            copy.start()
+        fourth.append(pair)
+
+    for chunk, span in enumerate(spans):
+        for copy in second[chunk]:
+            copy.wait()
+        total = source[rank, span].astype(F32) + from_across[span].astype(F32) + from_along[span].astype(F32)
+        full[rank, span] = math(span, total).astype(BF16)
+        pair = (
+            remote(4, chunk, full.at[rank, span], full.at[rank, span], across),
+            remote(5, chunk, full.at[rank, span], full.at[rank, span], along),
+        )
+        for copy in pair:
+            copy.start()
+        third.append(pair)
+        if chunk:
+            pass_on(chunk - 1)
+    pass_on(chunks - 1)
+    if ready is not None:
+        for copy in extra[:2]:
+            copy.wait()
+        for copy in extra[2:]:
+            copy.start()
+        for copy in extra[2:]:
+            copy.wait()
+    for pair in fourth:
+        for copy in pair:
+            copy.wait()
+
+
+def exchange_call(kernel, number, source, operands, extra_shapes):
+    tokens, width = source.shape
+    ranks = 4
+    rows = tokens // ranks
+    anywhere = pl.BlockSpec(memory_space=pltpu.VMEM)
+    results = pl.pallas_call(
+        kernel,
+        in_specs=[anywhere] * (1 + len(operands)),
+        out_specs=[anywhere] * (1 + len(extra_shapes)),
+        out_shape=[jax.ShapeDtypeStruct((ranks, rows, width), BF16)]
+        + [jax.ShapeDtypeStruct(shape, kind) for shape, kind in extra_shapes],
+        scratch_shapes=[pltpu.VMEM((rows, width), BF16)] * 4
+        + [pltpu.VMEM((rows, width // 2), BF16)] * 2
+        + [pltpu.SemaphoreType.DMA((9, 4))] * 2,
+        compiler_params=pltpu.CompilerParams(
+            vmem_limit_bytes=48 * MIB, collective_id=number, has_side_effects=True
+        ),
+        cost_estimate=cost(40 * MIB, 200 * MIB),
+    )(source.reshape(ranks, rows, width), *operands)
+    return results[0].reshape(tokens, width), *results[1:]
+
+
+def norm_two_kernel(source, x_ref, gain_ref, full, resid_ref, scale_ref, *rest):
+    def math(span, total):
+        resid = x_ref[span, :].astype(F32) + total
+        scale = lax.rsqrt(jnp.sum(resid * resid, axis=1, keepdims=True) / resid.shape[1] + EPS)
+        resid_ref[span, :] = resid
+        scale_ref[span, :] = scale
+        return resid * scale * gain_ref[...]
+
+    exchange(math, lax.axis_index("tensor"), source, full, *rest)
+
+
+def norm_back(grad, value, scale, gain):
+    scaled = grad * gain
+    inner = jnp.sum(scaled * value, axis=1, keepdims=True)
+    return scale * scaled - value * (scale * scale * scale) * (inner / value.shape[1])
+
+
+def norm_two_back_kernel(source, resid_ref, scale_ref, dy_ref, gain_ref, full, grad_ref, gain_grad_ref, *rest):
+    gain_grad_ref[...] = jnp.zeros_like(gain_grad_ref)
+
+    def math(span, total):
+        resid, scale = resid_ref[span, :], scale_ref[span, :]
+        gain_grad_ref[...] += jnp.sum(total * resid * scale, axis=0, keepdims=True)
+        grad = norm_back(total, resid, scale, gain_ref[...]) + dy_ref[span, :].astype(F32)
+        grad_ref[span, :] = grad
+        return grad
+
+    exchange(math, lax.axis_index("tensor"), source, full, *rest)
+
+
+def norm_one_back_kernel(source, x_ref, scale_ref, grad_ref, gain_ref, ready, full, ready_full, *rest):
+    def math(span, total):
+        x = x_ref[span, :].astype(F32)
+        return norm_back(total, x, scale_ref[span, :], gain_ref[...]) + grad_ref[span, :]
+
+    exchange(math, lax.axis_index("tensor"), source, full, *rest, ready, ready_full)
+
+
+def rank_sum_kernel(in_ref, out_ref, held, sends, recvs):
+    rank = lax.axis_index("tensor")
+    pair_class, half_index = rank % 2, rank // 2
+    others = rank + 1 - 2 * pair_class, rank + 2 - 4 * half_index
+    mesh_ids = pl.DeviceIdType.MESH
+    barrier = pltpu.get_barrier_semaphore()
+    for other in others:
+        pl.semaphore_signal(barrier, inc=1, device_id={"tensor": other}, device_id_type=mesh_ids)
+    pl.semaphore_wait(barrier, 2)
+    held[0] = in_ref[...]
+    for step, other in enumerate(others):
+        copy = pltpu.make_async_remote_copy(
+            src_ref=held.at[step], dst_ref=held.at[2 + step], send_sem=sends.at[step], recv_sem=recvs.at[step],
+            device_id={"tensor": other}, device_id_type=mesh_ids,
+        )
+        copy.start()
+        copy.wait()
+        if step == 0:
+            held[1] = held[0] + held[2]
+        else:
+            out_ref[...] = held[1] + held[3]
+
+
+def rank_sum(part):
+    return pl.pallas_call(
+        rank_sum_kernel,
+        in_specs=[pl.BlockSpec(memory_space=pltpu.VMEM)],
+        out_specs=pl.BlockSpec(memory_space=pltpu.VMEM),
+        out_shape=jax.ShapeDtypeStruct(part.shape, F32),
+        scratch_shapes=[pltpu.VMEM((4, *part.shape), F32)] + [pltpu.SemaphoreType.DMA((2,))] * 2,
+        compiler_params=pltpu.CompilerParams(collective_id=5, has_side_effects=True),
+    )(part)
 
 
 def code_kernel(place_ref, routes_ref, code_ref, half, groups):
@@ -386,68 +606,60 @@
     )(place, routes_t)
 
 
-def gates_kernel(h0_ref, h1_ref, router_ref, routes_ref, gates_ref):
-    expert = lax.broadcasted_iota(jnp.int32, (EXPERTS, SEQ), 0)
-    for seq, ref in enumerate((h0_ref, h1_ref)):
-        cols = slice(seq * SEQ, (seq + 1) * SEQ)
-        logits = mm(router_ref[...], ref[...], NT)
-        picked = [
-            jnp.sum(jnp.where(routes_ref[i : i + 1, cols] == expert, logits, 0.0), axis=0, keepdims=True)
-            for i in range(TOP)
-        ]
-        top = jnp.maximum(picked[0], picked[1])
-        raised = [jnp.exp(value - top) for value in picked]
-        total = raised[0] + raised[1]
-        for i in range(TOP):
-            gates_ref[i : i + 1, cols] = raised[i] / total
-
-
-def pair_gates(h0, h1, router_t, routes_t):
+def gates_kernel(h_ref, router_ref, routes_ref, gates_ref):
+    expert = lax.broadcasted_iota(jnp.int32, (EXPERTS, h_ref.shape[0]), 0)
+    logits = mm(router_ref[...], h_ref[...], NT)
+    picked = [
+        jnp.sum(jnp.where(routes_ref[i : i + 1] == expert, logits, 0.0), axis=0, keepdims=True)
+        for i in range(TOP)
+    ]
+    top = jnp.maximum(picked[0], picked[1])
+    raised = [jnp.exp(value - top) for value in picked]
+    total = raised[0] + raised[1]
+    for i in range(TOP):
+        gates_ref[i : i + 1] = raised[i] / total
+
+
+def pair_gates(h, router_t, routes_t):
     return pl.pallas_call(
         gates_kernel,
-        in_specs=[pl.BlockSpec(memory_space=pltpu.VMEM)] * 4,
+        in_specs=[pl.BlockSpec(memory_space=pltpu.VMEM)] * 3,
         out_specs=pl.BlockSpec(memory_space=pltpu.VMEM),
         out_shape=jax.ShapeDtypeStruct(routes_t.shape, F32),
         compiler_params=params(),
         cost_estimate=cost(2 * routes_t.shape[1] * EXPERTS * 1024 * 8, 4 * MIB),
-    )(h0, h1, router_t, routes_t)
-
-
-def dispatch_kernel(code_ref, gates_ref, h0_ref, h1_ref, dy_ref, rows_ref, grads_ref, dy_rows_ref, gate_ref):
-    count = rows_ref.shape[0]
-    slot = lax.broadcasted_iota(jnp.int32, (count, SEQ), 0) + pl.program_id(0) * count
-    rows = jnp.zeros(rows_ref.shape, F32)
-    dy_rows = jnp.zeros(rows_ref.shape, F32)
-    gate = jnp.zeros((count, 1), F32)
-    for seq, ref in enumerate((h0_ref, h1_ref)):
-        cols = slice(seq * SEQ, (seq + 1) * SEQ)
-        hits = [slot == code_ref[i : i + 1, cols] for i in range(TOP)]
-        take = jnp.where(hits[0] | hits[1], 1.0, 0.0).astype(BF16)
-        weighted = jnp.where(hits[0], gates_ref[0:1, cols], jnp.where(hits[1], gates_ref[1:2, cols], 0.0))
-        gate = gate + jnp.sum(weighted, axis=1, keepdims=True)
-        rows = rows + mm(take, ref[...])
-        dy_rows = dy_rows + mm(take, dy_ref[cols, :])
-    rows_ref[...] = rows.astype(BF16)
+    )(h, router_t, routes_t)
+
+
+def dispatch_kernel(code_ref, gates_ref, h_ref, dy_ref, rows_ref, grads_ref, dy_rows_ref, gate_ref):
+    count, tokens = rows_ref.shape[0], h_ref.shape[0]
+    slot = lax.broadcasted_iota(jnp.int32, (count, tokens), 0) + pl.program_id(0) * count
+    hits = [slot == code_ref[i : i + 1, :] for i in range(TOP)]
+    take = jnp.where(hits[0] | hits[1], 1.0, 0.0).astype(BF16)
+    weighted = jnp.where(hits[0], gates_ref[0:1, :], jnp.where(hits[1], gates_ref[1:2, :], 0.0))
+    gate = jnp.sum(weighted, axis=1, keepdims=True)
+    rows_ref[...] = mm(take, h_ref[...]).astype(BF16)
+    dy_rows = mm(take, dy_ref[...])
     dy_rows_ref[...] = dy_rows.astype(BF16)
     grads_ref[...] = (dy_rows * gate).astype(BF16)
     gate_ref[...] = gate
 
 
-def dispatch(code, gates, h0, h1, dy, slots):
-    width = h0.shape[1]
+def dispatch(code, gates, h, dy, slots):
+    width = h.shape[1]
     tile = slots // 4
     row_spec = pl.BlockSpec((tile, width), lambda i: (i, 0))
     whole = lambda shape: pl.BlockSpec(shape, lambda i: (0, 0))
     return pl.pallas_call(
         dispatch_kernel,
         grid=(4,),
-        in_specs=[whole(code.shape), whole(gates.shape), whole(h0.shape), whole(h1.shape), whole(dy.shape)],
+        in_specs=[whole(code.shape), whole(gates.shape), whole(h.shape), whole(dy.shape)],
         out_specs=[row_spec, row_spec, row_spec, pl.BlockSpec((tile, 1), lambda i: (i, 0))],
         out_shape=[jax.ShapeDtypeStruct((slots, width), BF16)] * 3
         + [jax.ShapeDtypeStruct((slots, 1), F32)],
         compiler_params=params(),
         cost_estimate=cost(8 * slots * SEQ * width, 8 * MIB + 6 * slots * width),
-    )(code, gates, h0, h1, dy)
+    )(code, gates, h, dy)
 
 
 def gelu_parts(x):
@@ -468,9 +680,9 @@
 
 
 def expert_kernel(
-    rows_in, grads_in, gate_in, up_in, down_in,
-    ret_out, back_out, own_gate, own_up, own_down, far_gate, far_up, far_down,
-    rows, grads, weights, sums, parts, z_send, z_recv, y_send, y_recv, p_send, p_recv, r_send, r_recv, w_send, w_recv, local,
+    rows_in, grads_in, gate_in, up_in, down_in, far_gate, far_up,
+    ret_out, back_out, own_gate, own_up, own_down, got_gate, got_up, got_down,
+    rows, grads, weights, sums, parts, z_send, z_recv, y_send, y_recv, p_send, p_recv, r_send, r_recv, w_send, w_recv, g_send, g_recv, local,
 ):
     groups, half, width = rows.shape[1:]
     group, rank = lax.axis_index("expert"), lax.axis_index("tensor")
@@ -530,21 +742,32 @@
     ]
     for copy in own:
         copy.start()
-    kept, swapped = [], []
-    for number, ref in enumerate((gate_in, up_in, down_in)):
-        kept.append(pltpu.make_async_copy(ref.at[pair_class], weights.at[number, 0], local.at[2 + number]))
-        swapped.append(
-            remote(ref.at[1 - pair_class], weights.at[number, 1], w_send.at[number], w_recv.at[number], across)
-        )
-    for copy in kept + swapped:
+    kept = [
+        pltpu.make_async_copy(ref.at[pair_class], weights.at[number, 0], local.at[2 + number])
+        for number, ref in enumerate((gate_in, up_in, down_in))
+    ]
+    kept += [
+        pltpu.make_async_copy(ref, weights.at[number, 1], local.at[5 + number])
+        for number, ref in enumerate((far_gate, far_up))
+    ]
+    kept.append(remote(down_in.at[1 - pair_class], weights.at[2, 1], w_send.at[0], w_recv.at[0], across))
+    for copy in kept:
         copy.start()
     for step in range(1, groups):
         for kind in range(2):
             out_of(kind, step).start()
+    def arrive(step):
+        for kind in range(2):
+            out_of(kind, step).wait()
+            forward(kind, step).start()
+
+    near = groups // 2
     for copy in own:
         copy.wait()
     for kind in range(2):
         forward(kind, 0).start()
+    for step in range(1, near):
+        arrive(step)
     for number in range(3):
         for part in range(2):
             sums[number, part] = jnp.zeros(sums.shape[2:], F32)
@@ -567,15 +790,13 @@
                 result(kind, step).start()
 
     def body(step, carry):
-        @pl.when(step < groups - 1)
+        @pl.when((step >= near) & (step < groups - 1))
         def _():
-            for kind in range(2):
-                out_of(kind, step + 1).wait()
-                forward(kind, step + 1).start()
+            arrive(step + 1)
 
         @pl.when(step == 0)
         def _():
-            for copy in kept + swapped:
+            for copy in kept:
                 copy.wait()
 
         for kind in range(2):
@@ -609,15 +830,19 @@
         def _():
             finish(step - 1)
 
+        @pl.when(step == near - 1)
+        def _():
+            arrive(near)
+
         return carry
 
     lax.fori_loop(0, groups, body, 0)
     copies = []
-    for number, (own_ref, far_ref) in enumerate(((own_gate, far_gate), (own_up, far_up), (own_down, far_down))):
+    for number, (own_ref, got_ref) in enumerate(((own_gate, got_gate), (own_up, got_up), (own_down, got_down))):
+        weights[number, 0] = sums[number, 1].astype(BF16)
+        copies.append(remote(weights.at[number, 0], got_ref, g_send.at[number], g_recv.at[number], across))
+        copies[-1].start()
         copies.append(pltpu.make_async_copy(sums.at[number, 0], own_ref, local.at[2 + number]))
-        copies[-1].start()
-        weights[number, 0] = sums[number, 1].astype(BF16)
-        copies.append(pltpu.make_async_copy(weights.at[number, 0], far_ref, local.at[5 + number]))
         copies[-1].start()
     finish(groups - 1)
     for copy in copies:
@@ -628,7 +853,7 @@
             result(kind, step).wait()
 
 
-def run_experts(rows, grads, w_gate, w_up, w_down):
+def run_experts(rows, grads, w_gate, w_up, w_down, far_gate, far_up):
     slots, width = rows.shape
     half = CAP // 2
     groups = slots // half
@@ -637,7 +862,7 @@
     pair = pltpu.SemaphoreType.DMA((2, groups))
     return pl.pallas_call(
         expert_kernel,
-        in_specs=[anywhere] * 5,
+        in_specs=[anywhere] * 7,
         out_specs=[anywhere] * 8,
         out_shape=[jax.ShapeDtypeStruct((slots, width), BF16)] * 2
         + [jax.ShapeDtypeStruct((units, width), F32)] * 3
@@ -650,13 +875,14 @@
             pltpu.VMEM((2, groups, half, width), BF16),
         ]
         + [pair] * 8
+        + [pltpu.SemaphoreType.DMA((1,))] * 2
         + [pltpu.SemaphoreType.DMA((3,))] * 2
-        + [pltpu.SemaphoreType.DMA((8,))],
+        + [pltpu.SemaphoreType.DMA((7,))],
         compiler_params=pltpu.CompilerParams(
             vmem_limit_bytes=60 * MIB, collective_id=1, has_side_effects=True
         ),
         cost_estimate=cost(72 * slots * units * width, 16 * slots * width + 30 * units * width),
-    )(rows, grads, w_gate, w_up, w_down)
+    )(rows, grads, w_gate, w_up, w_down, far_gate, far_up)
 
 
 def pair_grads_kernel(code_ref, gates_ref, routes_ref, dy_rows_ref, ret_ref, gate_ref, logit_ref, scaled_ref):
@@ -736,21 +962,22 @@
     )(*operands)
 
 
-def assemble_kernel(in_ref, out_ref):
-    out_ref[...] = in_ref[0].astype(out_ref.dtype)
-
-
-def assemble(shards, kind):
-    count, width, tile = shards.shape
+def turn_kernel(in_ref, out_ref):
+    out_ref[...] = in_ref[...].astype(F32).T.astype(out_ref.dtype)
+
+
+def turn(rows, kind):
+    tokens, width = rows.shape
+    tile = 512
     return pl.pallas_call(
-        assemble_kernel,
-        grid=(count,),
-        in_specs=[pl.BlockSpec((1, width, tile), lambda i: (i, 0, 0))],
+        turn_kernel,
+        grid=(tokens // tile,),
+        in_specs=[pl.BlockSpec((tile, width), lambda i: (i, 0))],
         out_specs=pl.BlockSpec((width, tile), lambda i: (0, i)),
-        out_shape=jax.ShapeDtypeStruct((width, count * tile), kind),
+        out_shape=jax.ShapeDtypeStruct((width, tokens), kind),
         compiler_params=params(),
-        cost_estimate=cost(0, 6 * shards.size),
-    )(shards)
+        cost_estimate=cost(0, 6 * rows.size),
+    )(rows)
 
 
 def on_device(
@@ -760,13 +987,15 @@
     width, tokens = layer_input.shape
     ranks = lax.axis_size("tensor")
     groups = lax.axis_size("expert")
-    seqs = piece_starts.shape[0]
     rank = lax.axis_index("tensor")
     pair_class, half_index = rank % 2, rank // 2
     half = CAP // 2
-    share = SEQ // ranks
-    across = [(r, r ^ 1) for r in range(ranks)]
-
+
+    def trade(weights):
+        other = lax.dynamic_index_in_dim(weights, 1 - pair_class, 0, keepdims=False)
+        return lax.ppermute(other, "tensor", [(r, r ^ 1) for r in range(ranks)])
+
+    traded = trade(expert_gate), trade(expert_up)
     gain_col = gain_one[:, None]
     w_in = attn_in.reshape(-1, width)
     qkv, scale_one = project(layer_input, gain_col, w_in)
@@ -783,107 +1012,78 @@
     code_cols = code.T
     dy = grad_out.T
 
-    def own_tokens(array, seq):
-        return lax.dynamic_slice_in_dim(array, seq * SEQ + rank * share, share, 1)
-
-    mixed, lse, resid, scale_two, full_h2 = [], [], [], [], []
-    for seq in range(seqs):
-        mixed_seq, lse_seq, sent = attend(qkv, tiles, limits, attn_out, seq)
-        summed = lax.psum_scatter(sent, "tensor", scatter_dimension=0, tiled=True)
-        resid_seq = own_tokens(layer_input, seq).T.astype(F32) + summed.astype(F32)
-        scale = lax.rsqrt(jnp.sum(resid_seq * resid_seq, axis=1, keepdims=True) / width + EPS)
-        normed = (resid_seq * scale * gain_two).astype(BF16)
-        mixed.append(mixed_seq)
-        lse.append(lse_seq)
-        resid.append(resid_seq)
-        scale_two.append(scale)
-        full_h2.append(lax.all_gather(normed, "tensor", axis=0, tiled=True))
-
-    gates = pair_gates(full_h2[0], full_h2[1], router.T, routes_t)
+    share = tokens // ranks
+
+    def own(rows, axis=0):
+        return lax.dynamic_slice_in_dim(rows, rank * share, share, axis)
+
+    own_x = own(layer_input, 1).T
+    own_scale = own(scale_one, 1).T
+    mixed, lse, sent = attend(qkv, tiles, limits, attn_out)
+    sent, *traded = lax.optimization_barrier((sent, *traded))
+    h2, resid, scale_two = exchange_call(
+        norm_two_kernel, 2, sent, [own_x, gain_two[None]], [((share, width), F32), ((share, 1), F32)]
+    )
+    gates = pair_gates(h2, router.T, routes_t)
     slots = groups * half
-    rows, row_grads, dy_rows, gate_rows = dispatch(code, gates, full_h2[0], full_h2[1], dy, slots)
-
-    (ret, back, own_gate, own_up, own_down, far_gate, far_up, far_down) = run_experts(
-        rows, row_grads, expert_gate, expert_up, expert_down
+    rows, row_grads, dy_rows, gate_rows = dispatch(code, gates, h2, dy, slots)
+    ret, back, *weight_grads = run_experts(
+        rows, row_grads, expert_gate, expert_up, expert_down, *traded
     )
     grad_logit, scaled = pair_grads(code, gates, routes_t, dy_rows, ret, gate_rows)
     partial_h2 = spread(code_cols, back, grad_logit.T, router)
+    grad_router = mm(grad_logit.astype(BF16), h2)
+    grad_attn, grad_resid, grad_gain_two = exchange_call(
+        norm_two_back_kernel, 3, partial_h2, [resid, scale_two, own(dy), gain_two[None]],
+        [((share, width), F32), ((1, width), F32)],
+    )
+
+    scaled, grad_attn = lax.optimization_barrier((scaled, grad_attn))
     partial_y = spread(code_cols, scaled)
-    grad_router = sum(
-        mm(grad_logit[:, seq * SEQ : (seq + 1) * SEQ], full_h2[seq].astype(F32))
-        for seq in range(seqs)
-    )
-
-    grad_gain_two = jnp.zeros((width,), F32)
-    grad_resid, full_attn, y_shards = [], [], []
-    for seq in range(seqs):
-        span = slice(seq * SEQ, (seq + 1) * SEQ)
-        grad_h2 = lax.psum_scatter(partial_h2[span], "tensor", scatter_dimension=0, tiled=True).astype(F32)
-        own_dy = own_tokens(grad_out, seq).T.astype(F32)
-        grad_gain_two = grad_gain_two + jnp.sum(grad_h2 * resid[seq] * scale_two[seq], axis=0)
-        scaled_h2 = grad_h2 * gain_two
-        inner = jnp.sum(scaled_h2 * resid[seq], axis=1, keepdims=True)
-        grad = scale_two[seq] * scaled_h2 - resid[seq] * scale_two[seq] ** 3 * inner / width + own_dy
-        grad_resid.append(grad)
-        full_attn.append(lax.all_gather(grad.astype(BF16), "tensor", axis=0, tiled=True))
-    for seq in range(seqs):
-        span = slice(seq * SEQ, (seq + 1) * SEQ)
-        y_part = lax.psum_scatter(partial_y[span], "tensor", scatter_dimension=0, tiled=True)
-        y_shards.append((resid[seq] + y_part.astype(F32)).astype(BF16).T)
-    y_all = [lax.all_gather(shard[None], "tensor", axis=0, tiled=True) for shard in y_shards]
-    layer_output = assemble(jnp.concatenate(y_all), BF16)
-
-    grad_attn_out = sum(mm(mixed[seq], full_attn[seq]) for seq in range(seqs))
-    w_in_t = w_in.T
-    grad_in, near, far, shards = [], [], [], []
-    grad_gain_one = jnp.zeros((width,), F32)
-    for seq in range(seqs):
-        dq, dk, dv, near_seq, far_seq = attend_back(
-            qkv, tiles, limits, attn_out, full_attn[seq], lse[seq], seq
-        )
-        near.append(near_seq)
-        far.append(far_seq)
-        grads = [g.reshape(-1, SEQ) for g in (dq, dk, dv)]
-        update, sent = project_back(layer_input, gain_col, scale_one, w_in_t, grads, seq, ranks)
-        grad_in.append(update)
-        grad_h1 = lax.psum_scatter(sent, "tensor", scatter_dimension=0, tiled=True)[0].astype(F32)
-        own_x = own_tokens(layer_input, seq).astype(F32)
-        own_scale = own_tokens(scale_one, seq)
-        grad_gain_one = grad_gain_one + jnp.sum(grad_h1 * own_x * own_scale, axis=1)
-        scaled_h1 = grad_h1 * gain_col
-        inner = jnp.sum(scaled_h1 * own_x, axis=0, keepdims=True)
-        grad = own_scale * scaled_h1 - own_x * own_scale**3 * inner / width + grad_resid[seq].T
-        shards.append(lax.all_gather(grad.astype(BF16)[None], "tensor", axis=0, tiled=True))
-    grad_input = assemble(jnp.concatenate(shards), F32)
-    folded = bias_fold(jnp.stack(near), jnp.stack(far))
-    grad_rel_bias = folded[:, :, 0].T
-
-    def give(own, other):
-        got = lax.ppermute(other, "tensor", across).astype(F32)
-        first = jnp.where(pair_class == 0, own, got)
-        second = jnp.where(pair_class == 0, got, own)
-        return jnp.stack([first, second])
-
-    small = lax.psum(
-        jnp.concatenate([grad_gain_one[None], grad_gain_two[None], grad_router]), ("expert", "tensor")
-    )
-    over_experts = (
-        lax.psum((grad_in[0] + grad_in[1]).astype(BF16), "expert").astype(F32),
-        lax.psum(grad_rel_bias, "expert"),
-        lax.psum(grad_attn_out.astype(BF16), "expert").astype(F32),
-    )
+    y_part = lax.psum_scatter(partial_y, "tensor", scatter_dimension=0, tiled=True)
+    partial_y, grad_attn = lax.optimization_barrier((partial_y, grad_attn))
+    dq, dk, dv, near, far, grad_gate, grad_up, grad_down = attend_back(
+        place, qkv, tiles, limits, attn_out, grad_attn, lse, weight_grads[:3], weight_grads[3:]
+    )
+    grad_attn_out = mm(mixed, grad_attn)
+    dq, y_part = lax.optimization_barrier((dq, y_part))
+    grad_in, sent, grad_gain_one = project_back(layer_input, gain_col, scale_one, w_in, (dq, dk, dv))
+    grad_rel_bias = bias_fold(near, far)[:, :, 0].T
+
+    heads = grad_rel_bias.shape[1]
+    small = jnp.concatenate(
+        [
+            grad_gain_one.T,
+            grad_gain_two,
+            grad_router,
+            jnp.pad(grad_rel_bias.reshape(1, -1), ((0, 0), (0, width - grad_rel_bias.size))),
+            jnp.zeros((5, width), F32),
+        ]
+    )
+    sum_in, sum_out, small = lax.psum(
+        (grad_in.astype(BF16), grad_attn_out.astype(BF16), small.astype(BF16)), "expert"
+    )
+    y_own = (resid + y_part.astype(F32)).astype(BF16)
+    grad_rows, y_full = exchange_call(
+        norm_one_back_kernel, 4, sent, [own_x, own_scale, grad_resid, gain_one[None], y_own],
+        [((ranks, share, width), BF16)],
+    )
+    grad_input = turn(grad_rows, F32)
+    layer_output = turn(y_full.reshape(tokens, width), BF16)
+    small, layer_output = lax.optimization_barrier((small.astype(F32), layer_output))
+    over_ranks = rank_sum(small)
     return (
         layer_output,
         grad_input,
-        small[0],
-        over_experts[0].reshape(attn_in.shape),
-        over_experts[1],
-        over_experts[2],
-        small[1],
-        small[2:].T,
-        give(own_gate, far_gate),
-        give(own_up, far_up),
-        give(own_down, far_down),
+        over_ranks[0],
+        sum_in.astype(F32).reshape(attn_in.shape),
+        small[2 + EXPERTS, : BUCKETS * heads].reshape(BUCKETS, heads),
+        sum_out.astype(F32),
+        over_ranks[1],
+        over_ranks[2 : 2 + EXPERTS].T,
+        grad_gate,
+        grad_up,
+        grad_down,
     )
 
 

time: 1300 us -> 863 us (0.66)
  waiting for transfers between devices: 645 us -> 5.04 us
  Pallas kernels: 492 us -> 754 us
  other arithmetic: 57.8 us -> 12.8 us
  local copies, waits for them, and re-layouts: 51.5 us -> 30.2 us
    pallas_call x9 -> x10, Pallas kernels: 416 us -> 677 us  [the longest x1 328 us: run_experts(): pl.pallas_call(expert_kernel, in_specs=[anywhere] * 7, out_specs=[anywher...]
    reduce_scatter x6 -> x1, waiting for transfers between devices: 221 us -> 0.01 us  [on_device(): lax.psum_scatter(partial_y, 'tensor', scatter_dimension=0, tiled=True)]
    all_gather x8 -> x0, waiting for transfers between devices: 172 us -> none  [the longest x2 68.7 us: on_device(): lax.all_gather(grad.astype(BF16)[None], 'tensor', axis=0, tiled=True)]
    ppermute x3 -> x2, waiting for transfers between devices: 112 us -> 5.01 us  [trade(): return lax.ppermute(other, 'tensor', [(r, r ^ 1) for r in range(ranks)])]
    psum x2 -> x1, waiting for transfers between devices: 101 us -> 0.01 us  [on_device(): lax.psum((grad_in.astype(BF16), grad_attn_out.astype(BF16), small.astype(...]
    unnamed x20 -> x2, waiting for transfers between devices: 38.8 us -> 0.03 us
    another operation x8 -> x2, other arithmetic: 19.9 us -> 0.21 us  [the longest x6 15.9 us: give(): return jnp.stack([first, second])]
    all_gather x4 -> x0, local copies, waits for them, and re-layouts: 14.7 us -> none  [the longest x2 7.41 us: on_device(): lax.all_gather(shard[None], 'tensor', axis=0, tiled=True)]
  transfers between devices with their start and end apart: 21 -> 4, of which waited for: 17 -> 1; matrix products, arithmetic and copies ran while one was open for 7% -> 4% of each run, Pallas kernels for 7% -> 25%
where the time goes in v3:
time: 863 us; the launch traced here: 853 us
  Pallas kernels  754 us (87%)
  local copies, waits for them, and re-layouts  30.2 us (3%)
  blocking collectives  26.4 us (3%)
  between operations  14.7 us (2%)
  other arithmetic  12.8 us (1%)
    pallas_call x1, Pallas kernels, run_experts(): pl.pallas_call(expert_kernel, in_specs=[anywhere] * 7, out_specs=[anywher...  328 us
    pallas_call x3, Pallas kernels, exchange_call(): pl.pallas_call(kernel, in_specs=[anywhere] * (1 + len(operands)), out_spe...  256 us
    pallas_call x1, Pallas kernels, attend_back(): pl.pallas_call(attend_back_kernel, grid_spec=pltpu.PrefetchScalarGridSpec...  33.6 us
    psum x1, blocking collectives, on_device(): lax.psum((grad_in.astype(BF16), grad_attn_out.astype(BF16), small.astype(...  26.4 us
    pallas_call x1, Pallas kernels, attend(): pl.pallas_call(attend_kernel, grid=(seqs, heads), in_specs=[pl.BlockSpec(...  23.6 us
    pallas_call x2, Pallas kernels, spread(): pl.pallas_call(spread_kernel, grid=(tokens // tile,), in_specs=specs, out...  20.6 us
  transfers between devices with their start and end apart: 4, of which 1 were waited for; matrix products, arithmetic and copies ran while one was open for 4% of the time, Pallas kernels for 25%

profile of v3, /device:TPU:0, one launch (start us, length us, event | category | flops | bytes accessed | tf_op | source)
XLA Modules:
  0.0 853.0 jit_solution(6317550137772906399)
XLA Ops:
  7.2 0.0 copy-start.5
  7.2 0.0 reduce-scatter.2.cloned.1.call-start
  7.3 0.0 copy-start.9
  7.3 2.7 dynamic-slice_bitcast_fusion
  10.0 2.9 collective-permute-start.1
  13.0 1.2 dynamic-slice_bitcast_fusion.1
  14.2 0.6 pad_add_fusion.place_ref
  14.7 0.7 copy.46.table_ref
  15.4 0.9 copy.51.refs_1_
  16.3 1.0 copy.53.gain_ref
  17.3 1.6 shard_map.214.code_ref
  18.9 2.1 copy.47
  21.0 1.3 constant_dynamic-slice_fusion
  22.3 0.5 copy.57
  22.8 6.4 copy.49
  29.2 6.6 shard_map.213.tiles_ref
  35.8 0.1 fusion.2
  35.9 0.6 iota_maximum_fusion.limit_ref
  36.5 2.3 dynamic-slice_bitcast_fusion.2.dy_ref
  38.8 8.3 shard_map.212
  47.1 23.6 %shard_map.215 = (bf16[256,2048]{1,0:T(8,128)(2,1)}, f32[8,1,1024]{2,1,0:T(1,128)}, bf16[2048,1024]{1,0:T(8,128)(2,1)}) custom-call(bf16[768,2048]{1,0:T(8,128)(2,1)} %get-tuple-element.60.q_ref.k_ref.v_ref, bf16[768,2048]{1,0:T(8,128)(2,1)} %get-tuple-element.60.q_ref.k_ref.v_ref, bf16[768,2048]{1,0:T(8,128)(2,1)} %get-tuple-element.60.q_ref.k_ref.v_ref, ...), custom_call_target="tpu_custom_call" | custom-call | flops 4294967296 | bytes 16777216 | tf_op jit(solution)/shard_map/pallas_call | solution.py:195
  70.7 5.0 collective-permute-done.far_gate
  75.7 75.1 %shard_map.216 = (bf16[4,512,1024]{2,1,0:T(8,128)(2,1)}, f32[512,1024]{1,0:T(8,128)S(1)}, f32[512,1]{1,0:T(8,128)S(1)}) custom-call(bf16[4,512,1024]{2,1,0:T(8,128)(2,1)} %bitcast.49, bf16[512,1024]{1,0:T(8,128)(2,1)S(1)} %bitcast.36, f32[1,1024]{1,0:T(1,128)S(1)} %bitcast.38), custom_call_target="tpu_custom_call" | custom-call | flops 41943040 | bytes 209715200 | tf_op jit(solution)/shard_map/pallas_call | solution.py:483
  150.8 4.0 shard_map.217.gates_ref
  154.9 17.2 %shard_map.218 = (bf16[1280,1024]{1,0:T(8,128)(2,1)}, bf16[1280,1024]{1,0:T(8,128)(2,1)}, bf16[1280,1024]{1,0:T(8,128)(2,1)}, f32[1280,1]{1,0:T(8,128)}) custom-call(s32[2,2048]{1,0:T(2,128)} %shard_map.214.code_ref, f32[2,2048]{1,0:T(2,128)} %shard_map.217.gates_ref, bf16[2048,1024]{1,0:T(8,128)(2,1)} %bitcast.43, bf16[2048,1024]{1,0:T(8,128)(2,1)} %bitcast.45), custom_call_target="tpu_custom_call" | custom-call | flops 10737418240 | bytes 16252928 | tf_op jit(solution)/shard_map/pallas_call | solution.py:653
  172.1 327.8 %shard_map.219 = (bf16[1280,1024]{1,0:T(8,128)(2,1)}, bf16[1280,1024]{1,0:T(8,128)(2,1)}, f32[704,1024]{1,0:T(8,128)}, f32[704,1024]{1,0:T(8,128)}, f32[704,1024...) custom-call(bf16[1280,1024]{1,0:T(8,128)(2,1)} %get-tuple-element.65.rows_in, ...), custom_call_target="tpu_custom_call" | custom-call | flops 66437775360 | bytes 42598400 | tf_op jit(solution)/shard_map/pallas_call | solution.py:863
  499.9 8.2 shard_map.220
  508.1 2.2 copy.50
  510.3 11.3 %shard_map.221 = bf16[2048,1024]{1,0:T(8,128)(2,1)} custom-call(s32[2048,2]{1,0:T(8,128)} %bitcast.53, bf16[1280,1024]{1,0:T(8,128)(2,1)} %get-tuple-element.72.rows_ref, f32[2048,16]{1,0:T(8,128)} %bitcast.52, bf16[1024,16]{1,0:T(8,128)(2,1)} %copy.51.refs_1_), custom_call_target="tpu_custom_call" | custom-call | flops 5368709120 | bytes 6815744 | tf_op jit(solution)/shard_map/pallas_call | solution.py:954
  521.6 73.9 %shard_map.222 = (bf16[4,512,1024]{2,1,0:T(8,128)(2,1)}, f32[512,1024]{1,0:T(8,128)S(1)}, f32[1,1024]{1,0:T(1,128)S(1)}) custom-call(bf16[4,512,1024]{2,1,0:T(8,128)(2,1)} %bitcast.48, f32[512,1024]{1,0:T(8,128)S(1)} %get-tuple-element.74.resid_ref, f32[512,1]{1,0:T(8,128)S(1)} %get-tuple-element.75.scale_ref, bf16[512,1024]{1,0:T(8,128)(2,1)S(1)} %copy-done, ...), custom_call_target="tpu_custom_call" | custom-call | flops 41943040 | bytes 209715200 | tf_op jit(solution)/shard_map/pallas_call | solution.py:483
  595.5 1.3 copy-done.1
  596.8 9.3 %shard_map.223 = bf16[2048,1024]{1,0:T(8,128)(2,1)} custom-call(s32[2048,2]{1,0:T(8,128)} %bitcast.54, bf16[1280,1024]{1,0:T(8,128)(2,1)} %get-tuple-element.77.rows_ref), custom_call_target="tpu_custom_call" | custom-call | flops 5368709120 | bytes 6815744 | tf_op jit(solution)/shard_map/pallas_call | solution.py:954
  606.1 0.0 reduce-scatter.2.cloned.1.call-update
  606.2 0.0 all-reduce.4.cloned.1.call-start
  606.2 0.7 dynamic-slice_bitcast_fusion.3
  606.9 0.1 copy.55.scale_ref
  607.1 33.6 %shard_map.224 = (bf16[256,2048]{1,0:T(8,128)(2,1)}, bf16[256,2048]{1,0:T(8,128)(2,1)}, bf16[256,2048]{1,0:T(8,128)(2,1)}, f32[8,3,256,256]{3,2,1,0:T(8,128)}, f...) custom-call(s32[2]{0:T(128)} %pad_add_fusion.place_ref, ...), custom_call_target="tpu_custom_call" | custom-call | flops 10737418240 | bytes 33554432 | tf_op jit(solution)/shard_map/pallas_call | solution.py:297
  640.7 10.1 %shard_map.226 = f32[4,32,128]{2,1,0:T(8,128)} custom-call(f32[8,3,256,256]{3,2,1,0:T(8,128)} %get-tuple-element.93.near_ref, f32[8,8,256]{2,1,0:T(8,128)} %get-tuple-element.94.far_ref), custom_call_target="tpu_custom_call" | custom-call | flops 47185920 | bytes 6291456 | tf_op jit(solution)/shard_map/pallas_call | solution.py:138
  650.8 1.5 fusion.1
  652.3 0.8 copy.54
  653.0 0.6 reshape.79
  653.7 0.8 pad.5
  654.5 3.7 convolution_convert_fusion.1
  658.2 3.3 convolution_convert_fusion
  661.5 15.2 %shard_map.225 = (f32[768,1024]{1,0:T(8,128)}, bf16[2048,1024]{1,0:T(8,128)(2,1)}, f32[1024,1]{1,0:T(8,128)}) custom-call(bf16[1024,2048]{1,0:T(8,128)(2,1)} %x_ref.3, f32[1024,1]{1,0:T(8,128)} %copy.53.gain_ref, f32[1,2048]{1,0:T(1,128)} %get-tuple-element.59.scale_ref, bf16[768,1024]{1,0:T(8,128)(2,1)} %bitcast.65, ...), custom_call_target="tpu_custom_call" | custom-call | flops 6442450944 | bytes 12582912 | tf_op jit(solution)/shard_map/pallas_call | solution.py:359
  676.7 3.3 convert_element_type.29
  680.0 0.0 all-reduce.4.cloned.1.call-update
  680.1 1.8 add_convert_fusion.ready
  681.8 0.1 copy-done.2
  682.0 106.9 %shard_map.227 = (bf16[4,512,1024]{2,1,0:T(8,128)(2,1)}, bf16[4,512,1024]{2,1,0:T(8,128)(2,1)}) custom-call(bf16[4,512,1024]{2,1,0:T(8,128)(2,1)} %bitcast.51, bf16[512,1024]{1,0:T(8,128)(2,1)S(1)} %bitcast.37, f32[512,1]{1,0:T(8,128)S(1)} %copy.55.scale_ref, f32[512,1024]{1,0:T(8,128)S(1)} %copy-done.2, f32[1,1024]{1,0:T(1,128)S(1)} %bitcast.41, ...), custom_call_target="tpu_custom_call" | custom-call | flops 41943040 | bytes 209715200 | tf_op jit(solution)/shard_map/pallas_call | solution.py:483
  788.9 5.3 shard_map.228
  794.2 0.2 convert_reduce_fusion
  794.4 0.2 concatenate.4
  794.6 26.4 %psum.21 = bf16[24,1024]{1,0:T(8,128)(2,1)S(1)} all-reduce(bf16[24,1024]{1,0:T(8,128)(2,1)S(1)} %concatenate.4), channel_id=1, replica_groups=mesh['expert'=8,'tensor'=4] {'expert'}, use_global_device_ids=true, to_apply=%region_2.3 | all-reduce | flops 24576 | bytes 98304 | tf_op jit(solution)/shard_map/psum | solution.py:1063
  821.0 0.6 convert_element_type.26.in_ref
  821.7 9.3 %shard_map.230 = f32[24,1024]{1,0:T(8,128)} custom-call(f32[24,1024]{1,0:T(8,128)} %convert_element_type.26.in_ref), custom_call_target="tpu_custom_call" | custom-call | tf_op jit(solution)/shard_map/pallas_call | solution.py:562
  831.0 0.7 slice_reduce_fusion
  831.7 0.1 reshape_squeeze.3
  831.8 0.7 copy.56
  832.5 6.5 shard_map.229
  838.9 0.6 fusion.3
  839.5 0.6 slice_bitcast_fusion
  840.2 2.1 convert_element_type.31
  842.3 3.5 reshape.84
  (32 shorter events, 0.1 us)
Async XLA Ops:
  7.2 5.8 copy-start.5
  7.2 654.3 %reduce-scatter.2.cloned.1.call-start = ((), (), s32[]{:S(2)}) async-start(), calls=%async_computation.1 | async-start | bytes 5242880 | tf_op jit(solution)/shard_map/reduce_scatter | solution.py:1043
  7.3 7.5 copy-start.12
  7.3 8.2 copy-start.9
  7.3 9.0 %copy-start.4 = (f32[1024]{0:T(1024)S(1)}, f32[1024]{0:T(1024)}, u32[]{:S(2)}) copy-start(f32[1024]{0:T(1024)} %param.14) | copy-start | bytes 12292
  10.0 60.7 %collective-permute-start.1 = (bf16[704,1024]{1,0:T(8,128)(2,1)}, bf16[704,1024]{1,0:T(8,128)(2,1)}, u32[]{:S(2)}, u32[]{:S(2)}) collective-permute-start(bf16[704,1024]{1,0:T(8,128)(2,1)} %dynamic-slice_bitcast_fusion), channel_id=1, source_target_pairs={{0,1},{1,0},{2,3},{3,2},{4,5},{5,4},{6,7},{7,6},{8,9},{9,8},{10,11... | collective-permute-start | bytes 4325384 | tf_op jit(solution)/shard_map/ppermute | solution.py:996
  14.2 61.6 %collective-permute-start = (bf16[704,1024]{1,0:T(8,128)(2,1)}, bf16[704,1024]{1,0:T(8,128)(2,1)}, u32[]{:S(2)}, u32[]{:S(2)}) collective-permute-start(bf16[704,1024]{1,0:T(8,128)(2,1)} %dynamic-slice_bitcast_fusion.1), channel_id=1, source_target_pairs={{0,1},{1,0},{2,3},{3,2},{4,5},{5,4},{6,7},{7,6},{8,9},{9,8},{10,11... | collective-permute-start | bytes 4325384 | tf_op jit(solution)/shard_map/ppermute | solution.py:996
  29.2 6.6 copy-start.11
  47.1 28.6 %copy-start.3 = (f32[1024]{0:T(1024)S(1)}, f32[1024]{0:T(1024)}, u32[]{:S(2)}) copy-start(f32[1024]{0:T(1024)} %param.18) | copy-start | bytes 12292
  510.3 11.3 %copy-start = (bf16[512,1024]{1,0:T(8,128)(2,1)S(1)}, bf16[512,1024]{1,0:T(8,128)(2,1)}, u32[]{:S(2)}) copy-start(bf16[512,1024]{1,0:T(8,128)(2,1)} %dynamic-slice_bitcast_fusion.2.dy_ref) | copy-start | bytes 3145732
  595.5 1.3 copy-start.1
  606.2 234.0 %all-reduce.4.cloned.1.call-start = ((), (), s32[]{:S(2)}) async-start(), calls=%async_computation.2 | async-start | bytes 4194304 | tf_op jit(solution)/shard_map/psum | solution.py:1063
  640.6 13.8 %copy-start.6 = (f32[16,2048]{1,0:T(8,128)S(1)}, f32[16,2048]{1,0:T(8,128)}, u32[]{:S(2)}) copy-start(f32[16,2048]{1,0:T(8,128)} %get-tuple-element.73) | copy-start | bytes 393220
  653.7 4.5 copy-start.13
  680.1 1.9 copy-start.2
  788.9 5.3 copy-start.7
  788.9 5.5 copy-start.10
  832.4 6.5 copy-start.8
Sparse Core Ops, SparseCore 0:
  606.3 50.6 reduce-scatter.1
  680.2 61.9 all-reduce.3

commit v4 on v3

--- a/solution.py
+++ b/solution.py
@@ -82,19 +82,26 @@
     )(x, gain, weights)
 
 
+def line_offsets(number):
+    column = lax.broadcasted_iota(jnp.int32, (8, BLK), 1)
+    return (number - 1) * BLK - column
+
+
 def bias_tiles_kernel(table_ref, tiles_ref):
-    key_at = lax.broadcasted_iota(jnp.int32, (BLK, BLK), 0)
-    query_at = lax.broadcasted_iota(jnp.int32, (BLK, BLK), 1)
-    for number, shift in enumerate((-1, 0, 1)):
-        offset = key_at - query_at + shift * BLK
-        bucket = bucket_of(offset)
-        low, high = {-1: (0, 16), 0: (0, 32), 1: (16, 32)}[shift]
-        for head in range(tiles_ref.shape[0]):
-            far = table_ref[15, head]
-            value = jnp.zeros((BLK, BLK), F32)
-            for index in range(low, high):
+    row = lax.broadcasted_iota(jnp.int32, (BLK, BLK), 0)
+    column = lax.broadcasted_iota(jnp.int32, (BLK, BLK), 1)
+    buckets = [bucket_of(line_offsets(number)) for number in range(4)]
+    for head in range(tiles_ref.shape[0]):
+        far = table_ref[15, head]
+        rolled = []
+        for number, bucket in enumerate(buckets):
+            value = jnp.zeros((8, BLK), F32)
+            for index in range(BUCKETS):
                 value = jnp.where(bucket == index, table_ref[index, head] - far, value)
-            tiles_ref[head, number] = value
+            whole = jnp.broadcast_to(value[0:1], (BLK, BLK))
+            rolled.append(pltpu.roll(whole, 0, 1, stride=1, stride_axis=0))
+        for number in range(3):
+            tiles_ref[head, number] = jnp.where(column >= row, rolled[number], rolled[number + 1])
 
 
 def bias_tiles(table):
@@ -109,40 +116,34 @@
     )(table)
 
 
-def bias_fold_kernel(near_ref, far_ref, out_ref):
-    heads = out_ref.shape[0]
-    key_at = lax.broadcasted_iota(jnp.int32, (BLK, BLK), 0)
-    query_at = lax.broadcasted_iota(jnp.int32, (BLK, BLK), 1)
-    totals = [[jnp.zeros((8, BLK), F32) for _ in range(BUCKETS)] for _ in range(heads)]
-    for number, shift in enumerate((-1, 0, 1)):
-        bucket = bucket_of(key_at - query_at + shift * BLK)
-        low, high = {-1: (0, 16), 0: (0, 32), 1: (16, 32)}[shift]
-        for head in range(heads):
+def bias_fold(near_ref, far_ref):
+    heads = near_ref.shape[0] // 2
+    columns = []
+    row = lax.broadcasted_iota(jnp.int32, (BLK, BLK), 0)
+    column = lax.broadcasted_iota(jnp.int32, (BLK, BLK), 1)
+    flip = jnp.where(row + column == BLK - 1, 1.0, 0.0).astype(BF16)
+    apart = jnp.where(column == BLK - 1, 0, column + 1)
+    ahead = apart <= row
+    number_at = lax.broadcasted_iota(jnp.int32, (BUCKETS, BLK), 0)
+    for head in range(heads):
+        lines = [jnp.zeros((1, BLK), F32) for _ in range(4)]
+        for number in range(3):
             grads = near_ref[head, number] + near_ref[heads + head, number]
-            for index in range(low, high):
-                kept = jnp.where(bucket == index, grads, 0.0)
-                totals[head][index] = totals[head][index] + jnp.sum(
-                    kept.reshape(BLK // 8, 8, BLK), axis=0
-                )
-    for head in range(heads):
-        totals[head][15] = totals[head][15] + far_ref[head] + far_ref[heads + head]
-        for index in range(BUCKETS):
-            line = jnp.sum(totals[head][index], axis=0, keepdims=True)
-            out_ref[head, index : index + 1, :] = jnp.broadcast_to(
-                jnp.sum(line, axis=1, keepdims=True), (1, 128)
-            )
-
-
-def bias_fold(near, far):
-    heads = near.shape[0] // 2
-    return pl.pallas_call(
-        bias_fold_kernel,
-        in_specs=[pl.BlockSpec(memory_space=pltpu.VMEM)] * 2,
-        out_specs=pl.BlockSpec(memory_space=pltpu.VMEM),
-        out_shape=jax.ShapeDtypeStruct((heads, BUCKETS, 128), F32),
-        compiler_params=params(),
-        cost_estimate=cost(heads * 3 * BLK * BLK * 60, heads * 6 * BLK * BLK * 4),
-    )(near, far)
+            coarse = grads.astype(BF16)
+            fine = (grads - coarse.astype(F32)).astype(BF16)
+            flipped = mm(flip, coarse) + mm(flip, fine)
+            rolled = pltpu.roll(flipped, 0, 1, stride=1, stride_axis=0)
+            lines[number] += jnp.sum(jnp.where(ahead, rolled, 0.0), axis=0, keepdims=True)
+            lines[number + 1] += jnp.sum(jnp.where(ahead, 0.0, rolled), axis=0, keepdims=True)
+        total = jnp.zeros((BUCKETS, 1), F32)
+        for number, line in enumerate(lines):
+            bucket = bucket_of((number - 1) * BLK - apart[:1])
+            total += jnp.sum(jnp.where(bucket == number_at, line, 0.0), axis=1, keepdims=True)
+        distant = jnp.sum(far_ref[head] + far_ref[heads + head], axis=0, keepdims=True)
+        distant = jnp.sum(distant, axis=1, keepdims=True)
+        total += jnp.where(number_at[:, :1] == 15, distant, 0.0)
+        columns.append(total)
+    return columns
 
 
 def key_count(query_block):
@@ -220,21 +221,54 @@
 
 
 def attend_back_kernel(
-    place_ref, q_ref, k_ref, v_ref, tiles_ref, limit_ref, w_ref, grad_ref, lse_ref, *refs
+    q_ref, k_ref, v_ref, tiles_ref, limit_ref, w_ref, grad_ref, lse_ref, part_ref, resid_ref,
+    dq_ref, dk_ref, dv_ref, near_ref, far_ref, y_ref,
+    held, parts, turn_across, turn_along, from_across, from_along, sends, recvs, loads,
 ):
-    own_refs, got_refs = refs[:3], refs[3:6]
-    dq_ref, dk_ref, dv_ref, near_ref, far_ref = refs[6:11]
-    placed_refs, held = refs[11:14], refs[14]
-
-    @pl.when(pl.program_id(0) == 0)
+    rank = lax.axis_index("tensor")
+    pair_class, half_index = rank % 2, rank // 2
+    across, along, corner = rank + 1 - 2 * pair_class, rank + 2 - 4 * half_index, 3 - rank
+    step = pl.program_id(0) * pl.num_programs(1) + pl.program_id(1)
+    mesh_ids = pl.DeviceIdType.MESH
+    middle = parts.shape[2] // 2
+    low, high = slice(0, middle), slice(middle, 2 * middle)
+
+    def remote(number, origin, target, other):
+        return pltpu.make_async_remote_copy(
+            src_ref=origin, dst_ref=target, send_sem=sends.at[number], recv_sem=recvs.at[number],
+            device_id={"tensor": other}, device_id_type=mesh_ids,
+        )
+
+    first = (
+        remote(0, part_ref.at[corner, :, low], turn_across, across),
+        remote(1, part_ref.at[corner, :, high], turn_along, along),
+    )
+    second = remote(2, parts.at[0], from_across, across), remote(3, parts.at[1], from_along, along)
+    local = [
+        pltpu.make_async_copy(part_ref.at[other], parts.at[number], loads.at[number])
+        for number, other in enumerate((across, along, rank))
+    ]
+    local.append(pltpu.make_async_copy(resid_ref, y_ref, loads.at[3]))
+
+    @pl.when(step == 0)
     def _():
-        for source, target in zip(own_refs, placed_refs):
-            target[0] = source[...]
-
-    @pl.when(pl.program_id(0) == 1)
+        barrier = pltpu.get_barrier_semaphore()
+        for other in (across, along):
+            pl.semaphore_signal(barrier, inc=1, device_id={"tensor": other}, device_id_type=mesh_ids)
+        pl.semaphore_wait(barrier, 2)
+        for copy in first:
+            copy.start()
+        for copy in local:
+            copy.start()
+
+    @pl.when(step == 3)
     def _():
-        for source, target in zip(got_refs, placed_refs):
-            target[0] = source[...].astype(F32)
+        for copy in (*first, *local):
+            copy.wait()
+        parts[0, :, high] = (parts[0, :, high].astype(F32) + turn_along[...].astype(F32)).astype(BF16)
+        parts[1, :, low] = (parts[1, :, low].astype(F32) + turn_across[...].astype(F32)).astype(BF16)
+        for copy in second:
+            copy.start()
 
     head = pl.program_id(1)
     width = q_ref.shape[0]
@@ -280,119 +314,153 @@
     dv_ref[...] = grad_values.astype(BF16)
     far_ref[0] = far
 
-
-def attend_back(place, qkv, tiles, limits, attn_out, grad_attn, lse, own_grads, got_grads):
+    @pl.when(step == 7)
+    def _():
+        for copy in second:
+            copy.wait()
+        y_ref[...] += parts[2].astype(F32) + from_across[...].astype(F32) + from_along[...].astype(F32)
+
+
+def attend_back(qkv, tiles, limits, attn_out, grad_attn, lse, part, resid):
     heads = tiles.shape[0]
     seqs = limits.shape[0]
     width = qkv.shape[0] // (3 * heads)
     model_width = attn_out.shape[1]
-    units = own_grads[0].shape[0]
-    tile = units // heads
-    grad_spec = pl.BlockSpec((width, SEQ), lambda s, h, p: (h, s))
-    own_spec = pl.BlockSpec((tile, model_width), lambda s, h, p: (jnp.where(s == 0, h, heads - 1), 0))
-    got_spec = pl.BlockSpec((tile, model_width), lambda s, h, p: (jnp.where(s == 0, 0, h), 0))
-    placed_spec = pl.BlockSpec(
-        (1, tile, model_width), lambda s, h, p: (jnp.where(s == 0, p[0], 1 - p[0]), h, 0)
-    )
+    share = part.shape[1]
+    grad_spec = pl.BlockSpec((width, SEQ), lambda s, h: (h, s))
+    anywhere = pl.BlockSpec(memory_space=pl.ANY)
     return pl.pallas_call(
         attend_back_kernel,
-        grid_spec=pltpu.PrefetchScalarGridSpec(
-            num_scalar_prefetch=1,
-            grid=(seqs, heads),
-            in_specs=[
-                pl.BlockSpec((width, SEQ), lambda s, h, p: (h, s)),
-                pl.BlockSpec((width, SEQ), lambda s, h, p: (heads + h, s)),
-                pl.BlockSpec((width, SEQ), lambda s, h, p: (2 * heads + h, s)),
-                pl.BlockSpec((1, 3, BLK, BLK), lambda s, h, p: (h, 0, 0, 0)),
-                pl.BlockSpec((1, 1, SEQ), lambda s, h, p: (s, 0, 0)),
-                pl.BlockSpec((heads * width, model_width), lambda s, h, p: (0, 0)),
-                pl.BlockSpec((SEQ, model_width), lambda s, h, p: (s, 0)),
-                pl.BlockSpec((1, 1, SEQ), lambda s, h, p: (s * heads + h, 0, 0)),
-            ]
-            + [own_spec] * 3
-            + [got_spec] * 3,
-            out_specs=[
-                grad_spec,
-                grad_spec,
-                grad_spec,
-                pl.BlockSpec((1, 3, BLK, BLK), lambda s, h, p: (s * heads + h, 0, 0, 0)),
-                pl.BlockSpec((1, 8, BLK), lambda s, h, p: (s * heads + h, 0, 0)),
-            ]
-            + [placed_spec] * 3,
-            scratch_shapes=[pltpu.VMEM((heads * width, SEQ), BF16)],
-        ),
+        grid=(seqs, heads),
+        in_specs=[
+            pl.BlockSpec((width, SEQ), lambda s, h: (h, s)),
+            pl.BlockSpec((width, SEQ), lambda s, h: (heads + h, s)),
+            pl.BlockSpec((width, SEQ), lambda s, h: (2 * heads + h, s)),
+            pl.BlockSpec((1, 3, BLK, BLK), lambda s, h: (h, 0, 0, 0)),
+            pl.BlockSpec((1, 1, SEQ), lambda s, h: (s, 0, 0)),
+            pl.BlockSpec((heads * width, model_width), lambda s, h: (0, 0)),
+            pl.BlockSpec((SEQ, model_width), lambda s, h: (s, 0)),
+            pl.BlockSpec((1, 1, SEQ), lambda s, h: (s * heads + h, 0, 0)),
+        ]
+        + [anywhere] * 2,
+        out_specs=[
+            grad_spec,
+            grad_spec,
+            grad_spec,
+            pl.BlockSpec((1, 3, BLK, BLK), lambda s, h: (s * heads + h, 0, 0, 0)),
+            pl.BlockSpec((1, 8, BLK), lambda s, h: (s * heads + h, 0, 0)),
+            pl.BlockSpec((share, model_width), lambda s, h: (0, 0)),
+        ],
         out_shape=[jax.ShapeDtypeStruct((heads * width, seqs * SEQ), BF16)] * 3
         + [
             jax.ShapeDtypeStruct((seqs * heads, 3, BLK, BLK), F32),
             jax.ShapeDtypeStruct((seqs * heads, 8, BLK), F32),
         ]
-        + [jax.ShapeDtypeStruct((2, units, model_width), F32)] * 3,
-        compiler_params=params(),
+        + [jax.ShapeDtypeStruct((share, model_width), F32)],
+        scratch_shapes=[
+            pltpu.VMEM((heads * width, SEQ), BF16),
+            pltpu.VMEM((3, share, model_width), BF16),
+            pltpu.VMEM((share, model_width // 2), BF16),
+            pltpu.VMEM((share, model_width // 2), BF16),
+            pltpu.VMEM((share, model_width), BF16),
+            pltpu.VMEM((share, model_width), BF16),
+            pltpu.SemaphoreType.DMA((4,)),
+            pltpu.SemaphoreType.DMA((4,)),
+            pltpu.SemaphoreType.DMA((4,)),
+        ],
+        compiler_params=pltpu.CompilerParams(
+            vmem_limit_bytes=60 * MIB, collective_id=5, has_side_effects=True
+        ),
         cost_estimate=cost(seqs * heads * SEQ * SEQ * 1280, seqs * heads * SEQ * 4096, seqs * heads * SEQ * SEQ),
-    )(place, qkv, qkv, qkv, tiles, limits, attn_out, grad_attn, lse, *own_grads, *got_grads)
-
-
-def project_back_kernel(x_ref, gain_ref, scale_ref, w_ref, dq_ref, dk_ref, dv_ref, weight_ref, out_ref, gain_grad_ref):
+    )(qkv, qkv, qkv, tiles, limits, attn_out, grad_attn, lse, part, resid)
+
+
+def project_back_kernel(
+    place_ref, x_ref, gain_ref, scale_ref, w_ref, mixed_ref, attn_ref, dq_ref, dk_ref, dv_ref, *refs
+):
+    step = pl.program_id(0)
+    own_refs, got_refs, (weight_ref, out_ref, gain_grad_ref), placed_refs, total = (
+        refs[:2], refs[2:4], refs[4:7], refs[7:9], refs[9]
+    )
+    for own_ref, got_ref, placed_ref in zip(own_refs, got_refs, placed_refs):
+        placed_ref[place_ref[0]] = own_ref[...]
+        placed_ref[1 - place_ref[0]] = got_ref[...].astype(F32)
     grads = jnp.concatenate([dq_ref[...], dk_ref[...], dv_ref[...]], axis=0)
+    rows = grads.shape[0]
     scaled = x_ref[...].astype(F32) * scale_ref[...]
-    update = mm(grads, (scaled * gain_ref[...]).astype(BF16), NT)
+
+    @pl.when(step == 0)
+    def _():
+        total[...] = jnp.zeros_like(total)
+        gain_grad_ref[...] = jnp.zeros_like(gain_grad_ref)
+
+    total[:rows] += mm(grads, (scaled * gain_ref[...]).astype(BF16), NT)
+    total[rows:] += mm(mixed_ref[...], attn_ref[...])
     back = mm(w_ref[...], grads, TN)
-    gain_update = jnp.sum(back * scaled, axis=1, keepdims=True)
-
-    @pl.when(pl.program_id(0) == 0)
+    gain_grad_ref[...] += jnp.sum(back * scaled, axis=1, keepdims=True)
+    out_ref[...] = back.T.astype(BF16)
+
+    @pl.when(step == pl.num_programs(0) - 1)
     def _():
-        weight_ref[...] = update
-        gain_grad_ref[...] = gain_update
-
-    @pl.when(pl.program_id(0) > 0)
-    def _():
-        weight_ref[...] += update
-        gain_grad_ref[...] += gain_update
-
-    out_ref[...] = back.T.astype(BF16)
-
-
-def project_back(x, gain, scale, weights, grads):
+        weight_ref[...] = total[...].astype(BF16)
+
+
+def project_back(place, x, gain, scale, weights, mixed, grad_attn, grads, owns, gots):
     width, tokens = x.shape
     rows = weights.shape[0]
-    tile = 512
+    heads_width = mixed.shape[0]
+    units = owns[0].shape[0]
+    steps = 4
+    tile = tokens // steps
+    part = units // steps
+    column = lambda count: pl.BlockSpec((count, tile), lambda i: (0, i))
     return pl.pallas_call(
         project_back_kernel,
-        grid=(tokens // tile,),
+        grid=(steps,),
         in_specs=[
-            pl.BlockSpec((width, tile), lambda i: (0, i)),
+            pl.BlockSpec(memory_space=pltpu.SMEM),
+            column(width),
             pl.BlockSpec((width, 1), lambda i: (0, 0)),
-            pl.BlockSpec((1, tile), lambda i: (0, i)),
+            column(1),
             pl.BlockSpec((rows, width), lambda i: (0, 0)),
+            column(heads_width),
+            pl.BlockSpec((tile, width), lambda i: (i, 0)),
         ]
-        + [pl.BlockSpec((rows // 3, tile), lambda i: (0, i))] * 3,
+        + [column(rows // 3)] * 3
+        + [pl.BlockSpec((part, width), lambda i: (i, 0))] * 4,
         out_specs=[
-            pl.BlockSpec((rows, width), lambda i: (0, 0)),
+            pl.BlockSpec((rows + heads_width, width), lambda i: (0, 0)),
             pl.BlockSpec((tile, width), lambda i: (i, 0)),
             pl.BlockSpec((width, 1), lambda i: (0, 0)),
-        ],
+        ]
+        + [pl.BlockSpec((2, part, width), lambda i: (0, i, 0))] * 2,
         out_shape=[
-            jax.ShapeDtypeStruct((rows, width), F32),
+            jax.ShapeDtypeStruct((rows + heads_width, width), BF16),
             jax.ShapeDtypeStruct((tokens, width), BF16),
             jax.ShapeDtypeStruct((width, 1), F32),
-        ],
+        ]
+        + [jax.ShapeDtypeStruct((2, units, width), F32)] * 2,
+        scratch_shapes=[pltpu.VMEM((rows + heads_width, width), F32)],
         compiler_params=params(),
-        cost_estimate=cost(4 * width * tokens * rows, 6 * width * tokens),
-    )(x, gain, scale, weights, *grads)
-
-
-def exchange(math, rank, source, full, from_across, from_along, to_across, to_along, turn_across, turn_along, sends, recvs, ready=None, ready_full=None):
+        cost_estimate=cost(5 * width * tokens * rows, 6 * width * tokens + 14 * units * width),
+    )(place, x, gain, scale, weights, mixed, grad_attn, *grads, *owns, *gots)
+
+
+def exchange(math, rank, source, full, from_across, from_along, to_across, to_along, turn_across, turn_along, sends, recvs, ready=None, ready_full=None, side=None, peers=(), fill=None, start=None, cut=None):
     pair_class, half_index = rank % 2, rank // 2
     across, along, corner = rank + 1 - 2 * pair_class, rank + 2 - 4 * half_index, 3 - rank
     mesh_ids = pl.DeviceIdType.MESH
     rows, width = source.shape[1:]
     chunks = 4
     size = rows // chunks
-    low, high = slice(0, width // 2), slice(width // 2, width)
+    cut = cut or width // 2
+    low, high = slice(0, cut), slice(cut, width)
     barrier = pltpu.get_barrier_semaphore()
     for other in (across, along):
         pl.semaphore_signal(barrier, inc=1, device_id={"tensor": other}, device_id_type=mesh_ids)
-    pl.semaphore_wait(barrier, 2)
+    for other in peers:
+        pl.semaphore_signal(barrier, inc=1, device_id={"expert": other}, device_id_type=mesh_ids)
+    pl.semaphore_wait(barrier, 2 + len(peers))
 
     def remote(kind, chunk, origin, target, other):
         return pltpu.make_async_remote_copy(
@@ -400,31 +468,42 @@
             device_id={"tensor": other}, device_id_type=mesh_ids,
         )
 
+    if start:
+        start()
+    if fill:
+        fill(corner)
     spans = [slice(chunk * size, (chunk + 1) * size) for chunk in range(chunks)]
     first, second, third, fourth = [], [], [], []
     for chunk, span in enumerate(spans):
         pair = (
-            remote(0, chunk, source.at[corner, span, low], turn_across.at[span], across),
-            remote(1, chunk, source.at[corner, span, high], turn_along.at[span], along),
+            remote(0, chunk, source.at[corner, span, low], turn_across.at[span, low], across),
+            remote(1, chunk, source.at[corner, span, high], turn_along.at[span, high], along),
         )
         for copy in pair:
             copy.start()
         first.append(pair)
+    if fill:
+        fill(along)
+        fill(across)
     if ready is not None:
         ready_full[rank] = ready[...]
         extra = [
             remote(8, 0, ready, ready_full.at[rank], across),
             remote(8, 1, ready, ready_full.at[rank], along),
-            remote(8, 2, ready_full.at[along, :, high], ready_full.at[along, :, high], across),
-            remote(8, 3, ready_full.at[across, :, low], ready_full.at[across, :, low], along),
+            remote(8, 2, ready_full.at[along, :, low], ready_full.at[along, :, low], across),
+            remote(8, 3, ready_full.at[across, :, high], ready_full.at[across, :, high], along),
         ]
+        for copy in extra[:2]:
+            copy.start()
     for chunk, span in enumerate(spans):
+        if side:
+            side(chunk)
         first[chunk][0].wait()
-        to_along[span, low] = (source[along, span, low].astype(F32) + turn_across[span].astype(F32)).astype(BF16)
+        to_along[span, low] = (source[along, span, low].astype(F32) + turn_across[span, low].astype(F32)).astype(BF16)
         to_along[span, high] = source[along, span, high]
         first[chunk][1].wait()
         to_across[span, low] = source[across, span, low]
-        to_across[span, high] = (source[across, span, high].astype(F32) + turn_along[span].astype(F32)).astype(BF16)
+        to_across[span, high] = (source[across, span, high].astype(F32) + turn_along[span, high].astype(F32)).astype(BF16)
         pair = (
             remote(2, chunk, to_across.at[span], from_across.at[span], across),
             remote(3, chunk, to_along.at[span], from_along.at[span], along),
@@ -434,6 +513,8 @@
         second.append(pair)
     if ready is not None:
         for copy in extra[:2]:
+            copy.wait()
+        for copy in extra[2:]:
             copy.start()
 
     def pass_on(chunk):
@@ -441,14 +522,18 @@
         for copy in third[chunk]:
             copy.wait()
         pair = (
-            remote(6, chunk, full.at[along, span, high], full.at[along, span, high], across),
-            remote(7, chunk, full.at[across, span, low], full.at[across, span, low], along),
+            remote(6, chunk, full.at[along, span, low], full.at[along, span, low], across),
+            remote(7, chunk, full.at[across, span, high], full.at[across, span, high], along),
         )
         for copy in pair:
             copy.start()
         fourth.append(pair)
 
+    if fill:
+        fill(rank)
     for chunk, span in enumerate(spans):
+        if side:
+            side(chunks + chunk)
         for copy in second[chunk]:
             copy.wait()
         total = source[rank, span].astype(F32) + from_across[span].astype(F32) + from_along[span].astype(F32)
@@ -464,40 +549,38 @@
             pass_on(chunk - 1)
     pass_on(chunks - 1)
     if ready is not None:
-        for copy in extra[:2]:
-            copy.wait()
-        for copy in extra[2:]:
-            copy.start()
         for copy in extra[2:]:
             copy.wait()
     for pair in fourth:
         for copy in pair:
             copy.wait()
-
-
-def exchange_call(kernel, number, source, operands, extra_shapes):
-    tokens, width = source.shape
+    if side:
+        side(2 * chunks)
+
+
+def exchange_call(kernel, number, shape, operands, extra_shapes, scratch=(), places=None, out_places=None):
+    tokens, width = shape
     ranks = 4
     rows = tokens // ranks
-    anywhere = pl.BlockSpec(memory_space=pltpu.VMEM)
+    here = pl.BlockSpec(memory_space=pltpu.VMEM)
     results = pl.pallas_call(
         kernel,
-        in_specs=[anywhere] * (1 + len(operands)),
-        out_specs=[anywhere] * (1 + len(extra_shapes)),
+        in_specs=places or [here] * len(operands),
+        out_specs=out_places or [here] * (1 + len(extra_shapes)),
         out_shape=[jax.ShapeDtypeStruct((ranks, rows, width), BF16)]
         + [jax.ShapeDtypeStruct(shape, kind) for shape, kind in extra_shapes],
-        scratch_shapes=[pltpu.VMEM((rows, width), BF16)] * 4
-        + [pltpu.VMEM((rows, width // 2), BF16)] * 2
-        + [pltpu.SemaphoreType.DMA((9, 4))] * 2,
+        scratch_shapes=[pltpu.VMEM((rows, width), BF16)] * 6
+        + [pltpu.SemaphoreType.DMA((9, 4))] * 2
+        + list(scratch),
         compiler_params=pltpu.CompilerParams(
-            vmem_limit_bytes=48 * MIB, collective_id=number, has_side_effects=True
+            vmem_limit_bytes=60 * MIB, collective_id=number, has_side_effects=True
         ),
         cost_estimate=cost(40 * MIB, 200 * MIB),
-    )(source.reshape(ranks, rows, width), *operands)
+    )(*operands)
     return results[0].reshape(tokens, width), *results[1:]
 
 
-def norm_two_kernel(source, x_ref, gain_ref, full, resid_ref, scale_ref, *rest):
+def norm_two_kernel(source, x_ref, gain_ref, grad_out_ref, code_ref, full, resid_ref, scale_ref, dy_ref, dy_rows_ref, *rest):
     def math(span, total):
         resid = x_ref[span, :].astype(F32) + total
         scale = lax.rsqrt(jnp.sum(resid * resid, axis=1, keepdims=True) / resid.shape[1] + EPS)
@@ -505,7 +588,20 @@
         scale_ref[span, :] = scale
         return resid * scale * gain_ref[...]
 
-    exchange(math, lax.axis_index("tensor"), source, full, *rest)
+    ranks, rows, width = source.shape
+    slots = dy_rows_ref.shape[0] // ranks
+
+    def side(number):
+        if number < ranks:
+            span = slice(number * rows, (number + 1) * rows)
+            dy_ref[span, :] = grad_out_ref[:, span].astype(F32).T.astype(BF16)
+        elif number < 2 * ranks:
+            start = (number - ranks) * slots
+            slot = lax.broadcasted_iota(jnp.int32, (slots, dy_ref.shape[0]), 0) + start
+            take = jnp.where((slot == code_ref[0:1]) | (slot == code_ref[1:2]), 1.0, 0.0).astype(BF16)
+            dy_rows_ref[start : start + slots, :] = mm(take, dy_ref[...]).astype(BF16)
+
+    exchange(math, lax.axis_index("tensor"), source, full, *rest, side=side)
 
 
 def norm_back(grad, value, scale, gain):
@@ -514,59 +610,139 @@
     return scale * scaled - value * (scale * scale * scale) * (inner / value.shape[1])
 
 
-def norm_two_back_kernel(source, resid_ref, scale_ref, dy_ref, gain_ref, full, grad_ref, gain_grad_ref, *rest):
+def norm_two_back_kernel(
+    ret_ref, back_ref, code_ref, codes_ref, gates_ref, routes_ref, dy_rows_ref, gate_ref, router_ref, h_ref,
+    resid_ref, scale_ref, dy_ref, gain_ref, up_ref, full, grad_ref, gain_grad_ref, router_grad_ref, y_ref, got_ref,
+    *rest,
+):
+    source, scaled, logit_parts, send, recv = rest[-5:]
+    rank = lax.axis_index("tensor")
+    rows = source.shape[1]
+    slots, tokens = ret_ref.shape[0], code_ref.shape[1]
+    swap = pltpu.make_async_remote_copy(
+        src_ref=up_ref, dst_ref=got_ref, send_sem=send.at[0], recv_sem=recv.at[0],
+        device_id={"tensor": rank + 1 - 2 * (rank % 2)}, device_id_type=pl.DeviceIdType.MESH,
+    )
+
+    def start():
+        swap.start()
+        found = [jnp.zeros((1, tokens), F32) for _ in range(TOP)]
+        tile = slots // 4
+        for begin in range(0, slots, tile):
+            span = slice(begin, begin + tile)
+            ret = ret_ref[span, :].astype(F32)
+            slot_grad = jnp.sum(dy_rows_ref[span, :].astype(F32) * ret, axis=1, keepdims=True)
+            scaled[span, :] = (ret * gate_ref[span, :]).astype(BF16)
+            slot = lax.broadcasted_iota(jnp.int32, (tile, tokens), 0) + begin
+            for i in range(TOP):
+                found[i] = found[i] + jnp.sum(
+                    jnp.where(slot == code_ref[i : i + 1, :], slot_grad, 0.0), axis=0, keepdims=True
+                )
+        mean = gates_ref[0:1] * found[0] + gates_ref[1:2] * found[1]
+        expert = lax.broadcasted_iota(jnp.int32, (EXPERTS, tokens), 0)
+        logit = sum(
+            jnp.where(routes_ref[i : i + 1] == expert, gates_ref[i : i + 1] * (found[i] - mean), 0.0)
+            for i in range(TOP)
+        )
+        coarse = logit.astype(BF16)
+        fine = (logit - coarse.astype(F32)).astype(BF16)
+        for shard in range(tokens // rows):
+            span = slice(shard * rows, (shard + 1) * rows)
+            logit_parts[shard, :EXPERTS] = coarse[:, span]
+            logit_parts[shard, EXPERTS:] = fine[:, span]
+
+    def places(shard):
+        slot = lax.broadcasted_iota(jnp.int32, (rows, slots), 1)
+        codes = codes_ref[pl.ds(pl.multiple_of(shard * rows, rows), rows), :]
+        return jnp.where((slot == codes[:, 0:1]) | (slot == codes[:, 1:2]), 1.0, 0.0).astype(BF16)
+
+    def fill(shard):
+        value = mm(places(shard), back_ref[...])
+        both = jnp.concatenate([router_ref[...], router_ref[...]], axis=0)
+        source[shard] = (value + mm(logit_parts[shard], both, TN)).astype(BF16)
+
+    def side(number):
+        shards = tokens // rows
+        if number < shards:
+            y_ref[number * rows : (number + 1) * rows, :] = mm(places(number), scaled[...]).astype(BF16)
+        elif number == shards:
+            router_grad_ref[...] = sum(
+                mm(logit_parts[shard, :EXPERTS], h_ref[shard * rows : (shard + 1) * rows, :])
+                for shard in range(shards)
+            )
+        elif number == 2 * shards:
+            swap.wait()
+
     gain_grad_ref[...] = jnp.zeros_like(gain_grad_ref)
 
     def math(span, total):
         resid, scale = resid_ref[span, :], scale_ref[span, :]
         gain_grad_ref[...] += jnp.sum(total * resid * scale, axis=0, keepdims=True)
-        grad = norm_back(total, resid, scale, gain_ref[...]) + dy_ref[span, :].astype(F32)
+        own_dy = dy_ref[pl.ds(pl.multiple_of(rank * rows + span.start, 128), span.stop - span.start), :]
+        grad = norm_back(total, resid, scale, gain_ref[...]) + own_dy.astype(F32)
         grad_ref[span, :] = grad
         return grad
 
-    exchange(math, lax.axis_index("tensor"), source, full, *rest)
-
-
-def norm_one_back_kernel(source, x_ref, scale_ref, grad_ref, gain_ref, ready, full, ready_full, *rest):
+    exchange(math, rank, source, full, *rest[:-5], side=side, fill=fill, start=start, cut=source.shape[2] // 4)
+
+
+def norm_one_back_kernel(
+    source, x_ref, scale_ref, grad_ref, gain_ref, ready, gain_one_ref, gain_two_ref, router_ref, near_ref, far_ref,
+    full, ready_full, small_out, *rest
+):
+    held, tensor_sends, tensor_recvs, expert_sends, expert_recvs = rest[-5:]
+    rank, group = lax.axis_index("tensor"), lax.axis_index("expert")
+    pair_class, half_index = rank % 2, rank // 2
+    others = rank + 1 - 2 * pair_class, rank + 2 - 4 * half_index
+    groups = expert_sends.shape[0]
+    mesh_ids = pl.DeviceIdType.MESH
+    peers = [partner_of(group, step) for step in range(1, groups)]
+    summed = slice(0, small_out.shape[0] - BUCKETS)
+
     def math(span, total):
         x = x_ref[span, :].astype(F32)
         return norm_back(total, x, scale_ref[span, :], gain_ref[...]) + grad_ref[span, :]
 
-    exchange(math, lax.axis_index("tensor"), source, full, *rest, ready, ready_full)
-
-
-def rank_sum_kernel(in_ref, out_ref, held, sends, recvs):
-    rank = lax.axis_index("tensor")
-    pair_class, half_index = rank % 2, rank // 2
-    others = rank + 1 - 2 * pair_class, rank + 2 - 4 * half_index
-    mesh_ids = pl.DeviceIdType.MESH
-    barrier = pltpu.get_barrier_semaphore()
-    for other in others:
-        pl.semaphore_signal(barrier, inc=1, device_id={"tensor": other}, device_id_type=mesh_ids)
-    pl.semaphore_wait(barrier, 2)
-    held[0] = in_ref[...]
-    for step, other in enumerate(others):
-        copy = pltpu.make_async_remote_copy(
-            src_ref=held.at[step], dst_ref=held.at[2 + step], send_sem=sends.at[step], recv_sem=recvs.at[step],
-            device_id={"tensor": other}, device_id_type=mesh_ids,
+    def to_rank(step):
+        return pltpu.make_async_remote_copy(
+            src_ref=held.at[groups + step], dst_ref=held.at[groups + 2 + step], send_sem=tensor_sends.at[step],
+            recv_sem=tensor_recvs.at[step], device_id={"tensor": others[step]}, device_id_type=mesh_ids,
         )
-        copy.start()
-        copy.wait()
-        if step == 0:
-            held[1] = held[0] + held[2]
-        else:
-            out_ref[...] = held[1] + held[3]
-
-
-def rank_sum(part):
-    return pl.pallas_call(
-        rank_sum_kernel,
-        in_specs=[pl.BlockSpec(memory_space=pltpu.VMEM)],
-        out_specs=pl.BlockSpec(memory_space=pltpu.VMEM),
-        out_shape=jax.ShapeDtypeStruct(part.shape, F32),
-        scratch_shapes=[pltpu.VMEM((4, *part.shape), F32)] + [pltpu.SemaphoreType.DMA((2,))] * 2,
-        compiler_params=pltpu.CompilerParams(collective_id=5, has_side_effects=True),
-    )(part)
+
+    def to_group(step):
+        return pltpu.make_async_remote_copy(
+            src_ref=held.at[group], dst_ref=held.at[group], send_sem=expert_sends.at[step],
+            recv_sem=expert_recvs.at[step], device_id={"expert": peers[step - 1]}, device_id_type=mesh_ids,
+        )
+
+    def side(number):
+        if number == 0:
+            held[groups] = jnp.zeros(small_out.shape, F32)
+            held[groups, :EXPERTS] = router_ref[...]
+            held[groups, EXPERTS : EXPERTS + 1] = gain_two_ref[...]
+            held[groups, EXPERTS + 1 : EXPERTS + 2] = jnp.broadcast_to(gain_one_ref[...], (gain_one_ref.shape[0], 128)).T[:1]
+            to_rank(0).start()
+        elif number == 1:
+            to_rank(0).wait()
+            held[groups + 1] = held[groups] + held[groups + 2]
+            to_rank(1).start()
+        elif number == 2:
+            to_rank(1).wait()
+            for head, column in enumerate(bias_fold(near_ref, far_ref)):
+                span = slice(summed.stop, summed.stop + BUCKETS)
+                held[group, span, head * 128 : (head + 1) * 128] = jnp.broadcast_to(column, (BUCKETS, 128))
+            held[group, summed] = held[groups + 1, summed] + held[groups + 3, summed]
+            for step in range(1, groups):
+                to_group(step).start()
+        elif number == 8:
+            for step in range(1, groups):
+                to_group(step).wait()
+            total = held[0]
+            for step in range(1, groups):
+                total = total + held[step]
+            small_out[...] = total
+
+    exchange(math, rank, source, full, *rest[:-5], ready, ready_full, side=side, peers=peers)
 
 
 def code_kernel(place_ref, routes_ref, code_ref, half, groups):
@@ -606,60 +782,48 @@
     )(place, routes_t)
 
 
-def gates_kernel(h_ref, router_ref, routes_ref, gates_ref):
-    expert = lax.broadcasted_iota(jnp.int32, (EXPERTS, h_ref.shape[0]), 0)
-    logits = mm(router_ref[...], h_ref[...], NT)
-    picked = [
-        jnp.sum(jnp.where(routes_ref[i : i + 1] == expert, logits, 0.0), axis=0, keepdims=True)
-        for i in range(TOP)
-    ]
-    top = jnp.maximum(picked[0], picked[1])
-    raised = [jnp.exp(value - top) for value in picked]
-    total = raised[0] + raised[1]
-    for i in range(TOP):
-        gates_ref[i : i + 1] = raised[i] / total
-
-
-def pair_gates(h, router_t, routes_t):
-    return pl.pallas_call(
-        gates_kernel,
-        in_specs=[pl.BlockSpec(memory_space=pltpu.VMEM)] * 3,
-        out_specs=pl.BlockSpec(memory_space=pltpu.VMEM),
-        out_shape=jax.ShapeDtypeStruct(routes_t.shape, F32),
-        compiler_params=params(),
-        cost_estimate=cost(2 * routes_t.shape[1] * EXPERTS * 1024 * 8, 4 * MIB),
-    )(h, router_t, routes_t)
-
-
-def dispatch_kernel(code_ref, gates_ref, h_ref, dy_ref, rows_ref, grads_ref, dy_rows_ref, gate_ref):
+def dispatch_kernel(code_ref, routes_ref, router_ref, h_ref, dy_rows_ref, rows_ref, grads_ref, gate_ref, gates_ref):
     count, tokens = rows_ref.shape[0], h_ref.shape[0]
+
+    @pl.when(pl.program_id(0) == 0)
+    def _():
+        expert = lax.broadcasted_iota(jnp.int32, (EXPERTS, tokens), 0)
+        logits = mm(router_ref[...], h_ref[...], NT)
+        picked = [
+            jnp.sum(jnp.where(routes_ref[i : i + 1] == expert, logits, 0.0), axis=0, keepdims=True)
+            for i in range(TOP)
+        ]
+        top = jnp.maximum(picked[0], picked[1])
+        raised = [jnp.exp(value - top) for value in picked]
+        total = raised[0] + raised[1]
+        for i in range(TOP):
+            gates_ref[i : i + 1] = raised[i] / total
+
     slot = lax.broadcasted_iota(jnp.int32, (count, tokens), 0) + pl.program_id(0) * count
     hits = [slot == code_ref[i : i + 1, :] for i in range(TOP)]
     take = jnp.where(hits[0] | hits[1], 1.0, 0.0).astype(BF16)
     weighted = jnp.where(hits[0], gates_ref[0:1, :], jnp.where(hits[1], gates_ref[1:2, :], 0.0))
     gate = jnp.sum(weighted, axis=1, keepdims=True)
     rows_ref[...] = mm(take, h_ref[...]).astype(BF16)
-    dy_rows = mm(take, dy_ref[...])
-    dy_rows_ref[...] = dy_rows.astype(BF16)
-    grads_ref[...] = (dy_rows * gate).astype(BF16)
+    grads_ref[...] = (dy_rows_ref[...].astype(F32) * gate).astype(BF16)
     gate_ref[...] = gate
 
 
-def dispatch(code, gates, h, dy, slots):
-    width = h.shape[1]
+def dispatch(code, routes_t, router_t, h, dy_rows):
+    slots, width = dy_rows.shape
     tile = slots // 4
     row_spec = pl.BlockSpec((tile, width), lambda i: (i, 0))
     whole = lambda shape: pl.BlockSpec(shape, lambda i: (0, 0))
     return pl.pallas_call(
         dispatch_kernel,
         grid=(4,),
-        in_specs=[whole(code.shape), whole(gates.shape), whole(h.shape), whole(dy.shape)],
-        out_specs=[row_spec, row_spec, row_spec, pl.BlockSpec((tile, 1), lambda i: (i, 0))],
-        out_shape=[jax.ShapeDtypeStruct((slots, width), BF16)] * 3
-        + [jax.ShapeDtypeStruct((slots, 1), F32)],
+        in_specs=[whole(code.shape), whole(code.shape), whole(router_t.shape), whole(h.shape), row_spec],
+        out_specs=[row_spec, row_spec, pl.BlockSpec((tile, 1), lambda i: (i, 0)), whole(code.shape)],
+        out_shape=[jax.ShapeDtypeStruct((slots, width), BF16)] * 2
+        + [jax.ShapeDtypeStruct((slots, 1), F32), jax.ShapeDtypeStruct(code.shape, F32)],
         compiler_params=params(),
-        cost_estimate=cost(8 * slots * SEQ * width, 8 * MIB + 6 * slots * width),
-    )(code, gates, h, dy)
+        cost_estimate=cost(4 * slots * SEQ * width, 4 * MIB + 6 * slots * width),
+    )(code, routes_t, router_t, h, dy_rows)
 
 
 def gelu_parts(x):
@@ -680,8 +844,8 @@
 
 
 def expert_kernel(
-    rows_in, grads_in, gate_in, up_in, down_in, far_gate, far_up,
-    ret_out, back_out, own_gate, own_up, own_down, got_gate, got_up, got_down,
+    rows_in, grads_in, gate_in, up_in, down_in, far_gate,
+    ret_out, back_out, own_gate, own_up, own_down, got_gate, sent_up, sent_down,
     rows, grads, weights, sums, parts, z_send, z_recv, y_send, y_recv, p_send, p_recv, r_send, r_recv, w_send, w_recv, g_send, g_recv, local,
 ):
     groups, half, width = rows.shape[1:]
@@ -746,11 +910,11 @@
         pltpu.make_async_copy(ref.at[pair_class], weights.at[number, 0], local.at[2 + number])
         for number, ref in enumerate((gate_in, up_in, down_in))
     ]
+    kept.append(pltpu.make_async_copy(far_gate, weights.at[0, 1], local.at[5]))
     kept += [
-        pltpu.make_async_copy(ref, weights.at[number, 1], local.at[5 + number])
-        for number, ref in enumerate((far_gate, far_up))
+        remote(ref.at[1 - pair_class], weights.at[number, 1], w_send.at[number - 1], w_recv.at[number - 1], across)
+        for number, ref in ((1, up_in), (2, down_in))
     ]
-    kept.append(remote(down_in.at[1 - pair_class], weights.at[2, 1], w_send.at[0], w_recv.at[0], across))
     for copy in kept:
         copy.start()
     for step in range(1, groups):
@@ -838,9 +1002,13 @@
 
     lax.fori_loop(0, groups, body, 0)
     copies = []
-    for number, (own_ref, got_ref) in enumerate(((own_gate, got_gate), (own_up, got_up), (own_down, got_down))):
+    for number, own_ref in enumerate((own_gate, own_up, own_down)):
         weights[number, 0] = sums[number, 1].astype(BF16)
-        copies.append(remote(weights.at[number, 0], got_ref, g_send.at[number], g_recv.at[number], across))
+        if number == 0:
+            copies.append(remote(weights.at[0, 0], got_gate, g_send.at[0], g_recv.at[0], across))
+        else:
+            far_ref = (sent_up, sent_down)[number - 1]
+            copies.append(pltpu.make_async_copy(weights.at[number, 0], far_ref, local.at[4 + number]))
         copies[-1].start()
         copies.append(pltpu.make_async_copy(sums.at[number, 0], own_ref, local.at[2 + number]))
         copies[-1].start()
@@ -853,7 +1021,7 @@
             result(kind, step).wait()
 
 
-def run_experts(rows, grads, w_gate, w_up, w_down, far_gate, far_up):
+def run_experts(rows, grads, w_gate, w_up, w_down, far_gate):
     slots, width = rows.shape
     half = CAP // 2
     groups = slots // half
@@ -862,7 +1030,7 @@
     pair = pltpu.SemaphoreType.DMA((2, groups))
     return pl.pallas_call(
         expert_kernel,
-        in_specs=[anywhere] * 7,
+        in_specs=[anywhere] * 6,
         out_specs=[anywhere] * 8,
         out_shape=[jax.ShapeDtypeStruct((slots, width), BF16)] * 2
         + [jax.ShapeDtypeStruct((units, width), F32)] * 3
@@ -875,91 +1043,14 @@
             pltpu.VMEM((2, groups, half, width), BF16),
         ]
         + [pair] * 8
+        + [pltpu.SemaphoreType.DMA((2,))] * 2
         + [pltpu.SemaphoreType.DMA((1,))] * 2
-        + [pltpu.SemaphoreType.DMA((3,))] * 2
         + [pltpu.SemaphoreType.DMA((7,))],
         compiler_params=pltpu.CompilerParams(
             vmem_limit_bytes=60 * MIB, collective_id=1, has_side_effects=True
         ),
         cost_estimate=cost(72 * slots * units * width, 16 * slots * width + 30 * units * width),
-    )(rows, grads, w_gate, w_up, w_down, far_gate, far_up)
-
-
-def pair_grads_kernel(code_ref, gates_ref, routes_ref, dy_rows_ref, ret_ref, gate_ref, logit_ref, scaled_ref):
-    slots = ret_ref.shape[0]
-    tokens = code_ref.shape[1]
-    found = [jnp.zeros((1, tokens), F32) for _ in range(TOP)]
-    tile = 320
-    for start in range(0, slots, tile):
-        span = slice(start, start + tile)
-        ret = ret_ref[span, :].astype(F32)
-        slot_grad = jnp.sum(dy_rows_ref[span, :].astype(F32) * ret, axis=1, keepdims=True)
-        scaled_ref[span, :] = (ret * gate_ref[span, :]).astype(BF16)
-        slot = lax.broadcasted_iota(jnp.int32, (tile, tokens), 0) + start
-        for i in range(TOP):
-            found[i] = found[i] + jnp.sum(
-                jnp.where(slot == code_ref[i : i + 1, :], slot_grad, 0.0), axis=0, keepdims=True
-            )
-    mean = gates_ref[0:1] * found[0] + gates_ref[1:2] * found[1]
-    expert = lax.broadcasted_iota(jnp.int32, (EXPERTS, tokens), 0)
-    logit_ref[...] = sum(
-        jnp.where(routes_ref[i : i + 1] == expert, gates_ref[i : i + 1] * (found[i] - mean), 0.0)
-        for i in range(TOP)
-    )
-
-
-def pair_grads(code, gates, routes_t, dy_rows, ret, gate_rows):
-    return pl.pallas_call(
-        pair_grads_kernel,
-        in_specs=[pl.BlockSpec(memory_space=pltpu.VMEM)] * 6,
-        out_specs=[pl.BlockSpec(memory_space=pltpu.VMEM)] * 2,
-        out_shape=[
-            jax.ShapeDtypeStruct((EXPERTS, code.shape[1]), F32),
-            jax.ShapeDtypeStruct(ret.shape, BF16),
-        ],
-        compiler_params=params(),
-        cost_estimate=cost(ret.shape[0] * code.shape[1] * 16, 6 * ret.size),
-    )(code, gates, routes_t, dy_rows, ret, gate_rows)
-
-
-def spread_kernel(code_ref, rows_ref, *refs):
-    out_ref = refs[-1]
-    tile = out_ref.shape[0]
-    slot = lax.broadcasted_iota(jnp.int32, (tile, rows_ref.shape[0]), 1)
-    code = code_ref[...]
-    place = jnp.where((slot == code[:, 0:1]) | (slot == code[:, 1:2]), 1.0, 0.0).astype(BF16)
-    value = mm(place, rows_ref[...])
-    if len(refs) == 3:
-        logit, router = refs[0][...], refs[1][...]
-        coarse = logit.astype(BF16)
-        fine = (logit - coarse.astype(F32)).astype(BF16)
-        value = value + mm(coarse, router, NT) + mm(fine, router, NT)
-    out_ref[...] = value.astype(BF16)
-
-
-def spread(code_cols, rows, logit=None, router=None):
-    tokens, width = code_cols.shape[0], rows.shape[1]
-    tile = 512
-    specs = [
-        pl.BlockSpec((tile, TOP), lambda i: (i, 0)),
-        pl.BlockSpec(rows.shape, lambda i: (0, 0)),
-    ]
-    operands = [code_cols, rows]
-    if logit is not None:
-        specs += [
-            pl.BlockSpec((tile, EXPERTS), lambda i: (i, 0)),
-            pl.BlockSpec(router.shape, lambda i: (0, 0)),
-        ]
-        operands += [logit, router]
-    return pl.pallas_call(
-        spread_kernel,
-        grid=(tokens // tile,),
-        in_specs=specs,
-        out_specs=pl.BlockSpec((tile, width), lambda i: (i, 0)),
-        out_shape=jax.ShapeDtypeStruct((tokens, width), BF16),
-        compiler_params=params(),
-        cost_estimate=cost(2 * tokens * width * rows.shape[0], 2 * rows.size + 2 * tokens * width),
-    )(*operands)
+    )(rows, grads, w_gate, w_up, w_down, far_gate)
 
 
 def turn_kernel(in_ref, out_ref):
@@ -980,6 +1071,40 @@
     )(rows)
 
 
+def turn_and_place_kernel(place_ref, in_ref, own_ref, got_ref, out_ref, placed_ref):
+    out_ref[...] = in_ref[...].astype(F32).T.astype(out_ref.dtype)
+    placed_ref[place_ref[0]] = own_ref[...]
+    placed_ref[1 - place_ref[0]] = got_ref[...].astype(F32)
+
+
+def turn_and_place(place, rows, kind, own, got):
+    tokens, width = rows.shape
+    units = own.shape[0]
+    steps = 4
+    tile, part = tokens // steps, units // steps
+    quarter = pl.BlockSpec((part, width), lambda i: (i, 0))
+    return pl.pallas_call(
+        turn_and_place_kernel,
+        grid=(steps,),
+        in_specs=[
+            pl.BlockSpec(memory_space=pltpu.SMEM),
+            pl.BlockSpec((tile, width), lambda i: (i, 0)),
+            quarter,
+            quarter,
+        ],
+        out_specs=[
+            pl.BlockSpec((width, tile), lambda i: (0, i)),
+            pl.BlockSpec((2, part, width), lambda i: (0, i, 0)),
+        ],
+        out_shape=[
+            jax.ShapeDtypeStruct((width, tokens), kind),
+            jax.ShapeDtypeStruct((2, units, width), F32),
+        ],
+        compiler_params=params(),
+        cost_estimate=cost(0, 6 * rows.size + 14 * own.size),
+    )(place, rows, own, got)
+
+
 def on_device(
     layer_input, gain_one, attn_in, rel_bias, attn_out, gain_two, router,
     expert_gate, expert_up, expert_down, routes, piece_starts, grad_out,
@@ -995,7 +1120,7 @@
         other = lax.dynamic_index_in_dim(weights, 1 - pair_class, 0, keepdims=False)
         return lax.ppermute(other, "tensor", [(r, r ^ 1) for r in range(ranks)])
 
-    traded = trade(expert_gate), trade(expert_up)
+    traded = trade(expert_gate)
     gain_col = gain_one[:, None]
     w_in = attn_in.reshape(-1, width)
     qkv, scale_one = project(layer_input, gain_col, w_in)
@@ -1010,77 +1135,81 @@
     place = jnp.stack([pair_class, half_index]).astype(jnp.int32)
     code = local_codes(place, routes_t, half, groups)
     code_cols = code.T
-    dy = grad_out.T
 
     share = tokens // ranks
 
     def own(rows, axis=0):
         return lax.dynamic_slice_in_dim(rows, rank * share, share, axis)
+
+    def by_rank(rows):
+        return rows.reshape(ranks, share, width)
 
     own_x = own(layer_input, 1).T
     own_scale = own(scale_one, 1).T
     mixed, lse, sent = attend(qkv, tiles, limits, attn_out)
-    sent, *traded = lax.optimization_barrier((sent, *traded))
-    h2, resid, scale_two = exchange_call(
-        norm_two_kernel, 2, sent, [own_x, gain_two[None]], [((share, width), F32), ((share, 1), F32)]
-    )
-    gates = pair_gates(h2, router.T, routes_t)
+    sent, traded = lax.optimization_barrier((sent, traded))
     slots = groups * half
-    rows, row_grads, dy_rows, gate_rows = dispatch(code, gates, h2, dy, slots)
-    ret, back, *weight_grads = run_experts(
-        rows, row_grads, expert_gate, expert_up, expert_down, *traded
-    )
-    grad_logit, scaled = pair_grads(code, gates, routes_t, dy_rows, ret, gate_rows)
-    partial_h2 = spread(code_cols, back, grad_logit.T, router)
-    grad_router = mm(grad_logit.astype(BF16), h2)
-    grad_attn, grad_resid, grad_gain_two = exchange_call(
-        norm_two_back_kernel, 3, partial_h2, [resid, scale_two, own(dy), gain_two[None]],
-        [((share, width), F32), ((1, width), F32)],
-    )
-
-    scaled, grad_attn = lax.optimization_barrier((scaled, grad_attn))
-    partial_y = spread(code_cols, scaled)
-    y_part = lax.psum_scatter(partial_y, "tensor", scatter_dimension=0, tiled=True)
-    partial_y, grad_attn = lax.optimization_barrier((partial_y, grad_attn))
-    dq, dk, dv, near, far, grad_gate, grad_up, grad_down = attend_back(
-        place, qkv, tiles, limits, attn_out, grad_attn, lse, weight_grads[:3], weight_grads[3:]
-    )
-    grad_attn_out = mm(mixed, grad_attn)
-    dq, y_part = lax.optimization_barrier((dq, y_part))
-    grad_in, sent, grad_gain_one = project_back(layer_input, gain_col, scale_one, w_in, (dq, dk, dv))
-    grad_rel_bias = bias_fold(near, far)[:, :, 0].T
-
-    heads = grad_rel_bias.shape[1]
-    small = jnp.concatenate(
+    h2, resid, scale_two, dy, dy_rows = exchange_call(
+        norm_two_kernel, 2, sent.shape, [by_rank(sent), own_x, gain_two[None], grad_out, code],
+        [((share, width), F32), ((share, 1), F32), ((tokens, width), BF16), ((slots, width), BF16)],
+    )
+    rows, row_grads, gate_rows, gates = dispatch(code, routes_t, router.T, h2, dy_rows)
+    ret, back, own_gate, own_up, own_down, got_gate, sent_up, sent_down = run_experts(
+        rows, row_grads, expert_gate, expert_up, expert_down, traded
+    )
+    here, anywhere = pl.BlockSpec(memory_space=pltpu.VMEM), pl.BlockSpec(memory_space=pl.ANY)
+    grad_attn, grad_resid, grad_gain_two, grad_router, partial_y, got_up = exchange_call(
+        norm_two_back_kernel, 3, (tokens, width),
+        [ret, back, code, code_cols, gates, routes_t, dy_rows, gate_rows, router.T, h2]
+        + [resid, scale_two, dy, gain_two[None], sent_up],
+        [((share, width), F32), ((1, width), F32), ((EXPERTS, width), F32), ((tokens, width), BF16)]
+        + [(sent_up.shape, BF16)],
         [
-            grad_gain_one.T,
-            grad_gain_two,
-            grad_router,
-            jnp.pad(grad_rel_bias.reshape(1, -1), ((0, 0), (0, width - grad_rel_bias.size))),
-            jnp.zeros((5, width), F32),
+            pltpu.VMEM((ranks, share, width), BF16),
+            pltpu.VMEM((slots, width), BF16),
+            pltpu.VMEM((ranks, 2 * EXPERTS, share), BF16),
         ]
-    )
-    sum_in, sum_out, small = lax.psum(
-        (grad_in.astype(BF16), grad_attn_out.astype(BF16), small.astype(BF16)), "expert"
-    )
-    y_own = (resid + y_part.astype(F32)).astype(BF16)
-    grad_rows, y_full = exchange_call(
-        norm_one_back_kernel, 4, sent, [own_x, own_scale, grad_resid, gain_one[None], y_own],
-        [((ranks, share, width), BF16)],
-    )
+        + [pltpu.SemaphoreType.DMA((1,))] * 2,
+        [here] * 14 + [anywhere],
+        [here] * 5 + [anywhere],
+    )
+
+    dq, dk, dv, near, far, y_own = attend_back(
+        qkv, tiles, limits, attn_out, grad_attn, lse, by_rank(partial_y), resid
+    )
+    sent_down, dq, y_own = lax.optimization_barrier((sent_down, dq, y_own))
+    got_down = lax.ppermute(sent_down, "tensor", [(r, r ^ 1) for r in range(ranks)])
+    weight_rows, sent, grad_gain_one, grad_gate, grad_up = project_back(
+        place, layer_input, gain_col, scale_one, w_in, mixed, grad_attn, (dq, dk, dv),
+        (own_gate, own_up), (got_gate, got_up),
+    )
+    sent, got_down = lax.optimization_barrier((sent, got_down))
+    summed = lax.psum(weight_rows, "expert")
+    y_own = y_own.astype(BF16)
+    small_shape = (EXPERTS + 8 + BUCKETS, width)
+    grad_rows, y_full, small = exchange_call(
+        norm_one_back_kernel, 4, sent.shape,
+        [by_rank(sent), own_x, own_scale, grad_resid, gain_one[None], y_own, grad_gain_one, grad_gain_two, grad_router]
+        + [near, far],
+        [((ranks, share, width), BF16), (small_shape, F32)],
+        [pltpu.VMEM((groups + 4, *small_shape), F32)]
+        + [pltpu.SemaphoreType.DMA((2,))] * 2
+        + [pltpu.SemaphoreType.DMA((groups,))] * 2,
+    )
+    summed, grad_rows = lax.optimization_barrier((summed, grad_rows))
     grad_input = turn(grad_rows, F32)
-    layer_output = turn(y_full.reshape(tokens, width), BF16)
-    small, layer_output = lax.optimization_barrier((small.astype(F32), layer_output))
-    over_ranks = rank_sum(small)
+    layer_output, grad_down = turn_and_place(place, y_full.reshape(tokens, width), BF16, own_down, got_down)
+    in_rows = w_in.shape[0]
+    heads = rel_bias.shape[1]
     return (
         layer_output,
         grad_input,
-        over_ranks[0],
-        sum_in.astype(F32).reshape(attn_in.shape),
-        small[2 + EXPERTS, : BUCKETS * heads].reshape(BUCKETS, heads),
-        sum_out.astype(F32),
-        over_ranks[1],
-        over_ranks[2 : 2 + EXPERTS].T,
+        small[EXPERTS + 1],
+        summed[:in_rows].astype(F32).reshape(attn_in.shape),
+        small[EXPERTS + 8 :, : heads * 128 : 128],
+        summed[in_rows:].astype(F32),
+        small[EXPERTS],
+        small[:EXPERTS].T,
         grad_gate,
         grad_up,
         grad_down,

time: 863 us -> 781 us (0.905)
  blocking collectives: 26.4 us -> 0 us
  Pallas kernels: 754 us -> 731 us
  local copies, waits for them, and re-layouts: 30.2 us -> 15.7 us
    psum x1 -> x0, blocking collectives: 26.4 us -> none  [on_device(): lax.psum((grad_in.astype(BF16), grad_attn_out.astype(BF16), small.astype(...]
    pallas_call x12 -> x7, Pallas kernels: 685 us -> 676 us  [the longest x3 342 us: exchange_call(): pl.pallas_call(kernel, in_specs=places or [here] * len(operands), out_spe...]
  transfers between devices with their start and end apart: 4 -> 3, of which waited for: 1 -> 1; matrix products, arithmetic and copies ran while one was open for 4% -> 2% of each run, Pallas kernels for 25% -> 28%
where the time goes in v4:
time: 781 us; the launch traced here: 775 us
  Pallas kernels  731 us (94%)
  local copies, waits for them, and re-layouts  15.7 us (2%)
  between operations  14.6 us (2%)
    pallas_call x3, Pallas kernels, exchange_call(): pl.pallas_call(kernel, in_specs=places or [here] * len(operands), out_spe...  342 us
    pallas_call x1, Pallas kernels, run_experts(): pl.pallas_call(expert_kernel, in_specs=[anywhere] * 6, out_specs=[anywher...  269 us
    pallas_call x1, Pallas kernels, attend_back(): pl.pallas_call(attend_back_kernel, grid=(seqs, heads), in_specs=[pl.Block...  36.5 us
    pallas_call x1, Pallas kernels, attend(): pl.pallas_call(attend_kernel, grid=(seqs, heads), in_specs=[pl.BlockSpec(...  23.8 us
    pallas_call x1, Pallas kernels, project_back(): pl.pallas_call(project_back_kernel, grid=(steps,), in_specs=[pl.BlockSpec...  21.3 us
  transfers between devices with their start and end apart: 3, of which 1 were waited for; matrix products, arithmetic and copies ran while one was open for 2% of the time, Pallas kernels for 28%

profile of v4, /device:TPU:0, one launch (start us, length us, event | category | flops | bytes accessed | tf_op | source)
XLA Modules:
  0.0 775.4 jit_solution(7186312455182798995)
XLA Ops:
  7.2 0.0 copy-start.3
  7.2 0.0 copy-start.5
  7.2 0.0 all-reduce.2.cloned.1.call-start
  7.3 1.5 dynamic-slice_bitcast_fusion
  8.7 3.0 collective-permute-start
  11.7 0.0 copy-done.3
  11.7 1.0 copy.39.gain_ref
  12.8 0.0 copy-done.5
  12.8 0.7 copy.36.table_ref
  13.5 1.3 constant_dynamic-slice_fusion
  14.8 0.0 copy-start.4
  14.8 1.3 copy.42
  16.1 0.6 pad_add_fusion.place_ref
  16.7 1.6 shard_map.215.code_ref
  18.3 2.1 copy.38
  20.4 3.2 shard_map.213.tiles_ref
  23.6 0.0 copy-done.4
  23.6 0.1 fusion
  23.7 0.6 iota_maximum_fusion.limit_ref
  24.3 8.3 %shard_map.212 = (bf16[768,2048]{1,0:T(8,128)(2,1)}, f32[1,2048]{1,0:T(1,128)}) custom-call(bf16[1024,2048]{1,0:T(8,128)(2,1)} %x_ref.3, f32[1024,1]{1,0:T(8,128)} %copy.39.gain_ref, bf16[768,1024]{1,0:T(8,128)(2,1)} %bitcast.51), custom_call_target="tpu_custom_call" | custom-call | flops 3221225472 | bytes 8388608 | tf_op jit(solution)/shard_map/pallas_call | solution.py:64
  32.6 23.8 %shard_map.214 = (bf16[256,2048]{1,0:T(8,128)(2,1)}, f32[8,1,1024]{2,1,0:T(1,128)}, bf16[2048,1024]{1,0:T(8,128)(2,1)}) custom-call(bf16[768,2048]{1,0:T(8,128)(2,1)} %get-tuple-element.65.q_ref.k_ref.v_ref, bf16[768,2048]{1,0:T(8,128)(2,1)} %get-tuple-element.65.q_ref.k_ref.v_ref, bf16[768,2048]{1,0:T(8,128)(2,1)} %get-tuple-element.65.q_ref.k_ref.v_ref, ...), custom_call_target="tpu_custom_call" | custom-call | flops 4294967296 | bytes 16777216 | tf_op jit(solution)/shard_map/pallas_call | solution.py:196
  56.4 0.0 collective-permute-done.far_gate
  56.5 79.1 %shard_map.216 = (bf16[4,512,1024]{2,1,0:T(8,128)(2,1)}, f32[512,1024]{1,0:T(8,128)}, f32[512,1]{1,0:T(8,128)}, bf16[2048,1024]{1,0:T(8,128)(2,1)}, bf16[1280,1024]{1,0:T(8,128)(2,1)}) custom-call(bf16[4,512,1024]{2,1,0:T(8,128)(2,1)} %bitcast.36, bf16[512,1024]{1,0:T(8,128)(2,1)} %bitcast.27, f32[1,1024]{1,0:T(1,128)} %bitcast.42, ...), custom_call_target="tpu_custom_call" | custom-call | flops 41943040 | bytes 209715200 | tf_op jit(solution)/shard_map/pallas_call | solution.py:566
  135.6 11.5 %shard_map.217 = (bf16[1280,1024]{1,0:T(8,128)(2,1)}, bf16[1280,1024]{1,0:T(8,128)(2,1)}, f32[1280,1]{1,0:T(8,128)}, f32[2,2048]{1,0:T(2,128)}) custom-call(s32[2,2048]{1,0:T(2,128)} %shard_map.215.code_ref, s32[2,2048]{1,0:T(2,128)} %bitcast.38, bf16[16,1024]{1,0:T(8,128)(2,1)} %bitcast.40, bf16[2048,1024]{1,0:T(8,128)(2,1)} %bitcast.31, ...), custom_call_target="tpu_custom_call" | custom-call | flops 5368709120 | bytes 12058624 | tf_op jit(solution)/shard_map/pallas_call | solution.py:817
  147.1 268.8 %shard_map.218 = (bf16[1280,1024]{1,0:T(8,128)(2,1)}, bf16[1280,1024]{1,0:T(8,128)(2,1)}, f32[704,1024]{1,0:T(8,128)}, f32[704,1024]{1,0:T(8,128)}, f32[704,1024...) custom-call(bf16[1280,1024]{1,0:T(8,128)(2,1)} %get-tuple-element.71.rows_in, ...), custom_call_target="tpu_custom_call" | custom-call | flops 66437775360 | bytes 42598400 | tf_op jit(solution)/shard_map/pallas_call | solution.py:1031
  415.9 105.1 %shard_map.219 = (bf16[4,512,1024]{2,1,0:T(8,128)(2,1)}, f32[512,1024]{1,0:T(8,128)}, f32[1,1024]{1,0:T(1,128)}, f32[16,1024]{1,0:T(8,128)}, bf16[2048,1024]{1,0:T(8,128)(2,1)}, /*index=5*/bf16[704,1024]{1,0:T(8,128)(2,1)}) custom-call(bf16[1280,1024]{1,0:T(8,128)(2,1)} %get-tuple-element.74.ret_ref, bf16[1280,1024]{1,0:T(8,128)(2,1)} %get-tuple-element.75.back_ref, ...), custom_call_target="tpu_custom_call" | custom-call | flops 41943040 | bytes 209715200 | tf_op jit(solution)/shard_map/pallas_call | solution.py:566
  521.0 36.5 %shard_map.220 = (bf16[256,2048]{1,0:T(8,128)(2,1)}, bf16[256,2048]{1,0:T(8,128)(2,1)}, bf16[256,2048]{1,0:T(8,128)(2,1)}, f32[8,3,256,256]{3,2,1,0:T(8,128)}, f...) custom-call(bf16[768,2048]{1,0:T(8,128)(2,1)} %get-tuple-element.65.q_ref.k_ref.v_ref, ...), custom_call_target="tpu_custom_call" | custom-call | flops 10737418240 | bytes 33554432 | tf_op jit(solution)/shard_map/pallas_call | solution.py:332
  557.5 0.6 collective-permute-start.1
  558.2 21.3 %shard_map.221 = (bf16[1024,1024]{1,0:T(8,128)(2,1)}, bf16[2048,1024]{1,0:T(8,128)(2,1)}, f32[1024,1]{1,0:T(8,128)}, f32[2,704,1024]{2,1,0:T(8,128)}, f32[2,704,1024]{2,1,0:T(8,128)}) custom-call(s32[2]{0:T(128)} %pad_add_fusion.place_ref, bf16[1024,2048]{1,0:T(8,128)(2,1)} %x_ref.3, f32[1024,1]{1,0:T(8,128)} %copy.39.gain_ref, ...), custom_call_target="tpu_custom_call" | custom-call | flops 8053063680 | bytes 22675456 | tf_op jit(solution)/shard_map/pallas_call | solution.py:417
  579.4 0.0 copy-start.1
  579.4 0.0 all-reduce.2.cloned.1.call-update
  579.5 0.8 dynamic-slice_bitcast_fusion.1
  580.3 0.9 copy.40.scale_ref
  581.1 0.0 copy-done.1
  581.2 1.1 convert_element_type.7.ready
  582.3 4.3 collective-permute-done.1.got_ref
  586.6 0.0 copy-start.2
  586.6 157.9 %shard_map.222 = (bf16[4,512,1024]{2,1,0:T(8,128)(2,1)}, bf16[4,512,1024]{2,1,0:T(8,128)(2,1)}, f32[56,1024]{1,0:T(8,128)}) custom-call(bf16[4,512,1024]{2,1,0:T(8,128)(2,1)} %bitcast.30, bf16[512,1024]{1,0:T(8,128)(2,1)} %bitcast.28, f32[512,1]{1,0:T(8,128)} %copy.40.scale_ref, f32[512,1024]{1,0:T(8,128)} %get-tuple-element.98.grad_ref, ...), custom_call_target="tpu_custom_call" | custom-call | flops 41943040 | bytes 209715200 | tf_op jit(solution)/shard_map/pallas_call | solution.py:566
  744.5 0.0 copy-done.2
  744.5 1.0 slice.20
  745.5 1.4 fusion.1
  746.9 0.0 all-reduce.2.cloned.1.call-done
  746.9 0.0 copy-start
  746.9 1.6 copy-done
  748.5 1.1 slice_convert_fusion
  749.6 1.5 slice_bitcast_fusion
  751.1 0.0 slice-start
  751.1 6.6 shard_map.224
  757.6 0.0 slice-done
  757.6 2.1 convert.1
  759.7 0.7 copy.41
  760.3 7.8 shard_map.223
  (1 shorter events, 0.0 us)
Async XLA Ops:
  7.2 4.6 copy-start.3
  7.2 5.6 copy-start.5
  7.2 739.7 %all-reduce.2.cloned.1.call-start = ((), (), s32[]{:S(2)}) async-start(), calls=%async_computation | async-start | bytes 4194304 | tf_op jit(solution)/shard_map/psum | solution.py:1187
  8.7 47.7 %collective-permute-start = (bf16[704,1024]{1,0:T(8,128)(2,1)S(1)}, bf16[704,1024]{1,0:T(8,128)(2,1)}, u32[]{:S(2)}, u32[]{:S(2)}) collective-permute-start(bf16[704,1024]{1,0:T(8,128)(2,1)S(1)} %dynamic-slice_bitcast_fusion), channel_id=1, source_target_pairs={{0,1},{1,0},{2,3},{3,2},{4,5},{5,4},{6,7},{7,6},{8,9},{9,8},{10,11... | collective-permute-start | bytes 4325384 | tf_op jit(solution)/shard_map/ppermute | solution.py:1121
  14.8 8.8 %copy-start.4 = (s32[2,2]{1,0:T(2,128)S(1)}, s32[2,2]{1,0:T(2,128)}, u32[]{:S(2)}) copy-start(s32[2,2]{1,0:T(2,128)} %param.24) | copy-start | bytes 52
  557.5 29.1 %collective-permute-start.1 = (bf16[704,1024]{1,0:T(8,128)(2,1)}, bf16[704,1024]{1,0:T(8,128)(2,1)S(1)}, u32[]{:S(2)}, u32[]{:S(2)}) collective-permute-start(bf16[704,1024]{1,0:T(8,128)(2,1)} %get-tuple-element.96), channel_id=1, source_target_pairs={{0,1},{1,0},{2,3},{3,2},{4,5},{5,4},{6,7},{7,6},{8,9},{9,8},{10,11... | collective-permute-start | bytes 4325384 | tf_op jit(solution)/shard_map/ppermute | solution.py:1181
  579.4 1.7 copy-start.1
  586.6 157.9 %copy-start.2 = (bf16[704,1024]{1,0:T(8,128)(2,1)}, bf16[704,1024]{1,0:T(8,128)(2,1)S(1)}, u32[]{:S(2)}) copy-start(bf16[704,1024]{1,0:T(8,128)(2,1)S(1)} %collective-permute-done.1.got_ref) | copy-start | bytes 4325380
  746.9 1.6 copy-start
  751.1 6.6 slice-start
Sparse Core Ops, SparseCore 0:
  579.6 98.3 all-reduce.1

commit v5 on v4

--- a/solution.py
+++ b/solution.py
@@ -558,15 +558,15 @@
         side(2 * chunks)
 
 
-def exchange_call(kernel, number, shape, operands, extra_shapes, scratch=(), places=None, out_places=None):
+def exchange_call(kernel, number, shape, operands, extra_shapes, scratch=()):
     tokens, width = shape
     ranks = 4
     rows = tokens // ranks
     here = pl.BlockSpec(memory_space=pltpu.VMEM)
     results = pl.pallas_call(
         kernel,
-        in_specs=places or [here] * len(operands),
-        out_specs=out_places or [here] * (1 + len(extra_shapes)),
+        in_specs=[here] * len(operands),
+        out_specs=[here] * (1 + len(extra_shapes)),
         out_shape=[jax.ShapeDtypeStruct((ranks, rows, width), BF16)]
         + [jax.ShapeDtypeStruct(shape, kind) for shape, kind in extra_shapes],
         scratch_shapes=[pltpu.VMEM((rows, width), BF16)] * 6
@@ -612,20 +612,13 @@
 
 def norm_two_back_kernel(
     ret_ref, back_ref, code_ref, codes_ref, gates_ref, routes_ref, dy_rows_ref, gate_ref, router_ref, h_ref,
-    resid_ref, scale_ref, dy_ref, gain_ref, up_ref, full, grad_ref, gain_grad_ref, router_grad_ref, y_ref, got_ref,
-    *rest,
+    resid_ref, scale_ref, dy_ref, gain_ref, full, grad_ref, gain_grad_ref, router_grad_ref, y_ref, *rest,
 ):
-    source, scaled, logit_parts, send, recv = rest[-5:]
+    source, scaled, logit_parts = rest[-3:]
     rank = lax.axis_index("tensor")
     rows = source.shape[1]
     slots, tokens = ret_ref.shape[0], code_ref.shape[1]
-    swap = pltpu.make_async_remote_copy(
-        src_ref=up_ref, dst_ref=got_ref, send_sem=send.at[0], recv_sem=recv.at[0],
-        device_id={"tensor": rank + 1 - 2 * (rank % 2)}, device_id_type=pl.DeviceIdType.MESH,
-    )
-
     def start():
-        swap.start()
         found = [jnp.zeros((1, tokens), F32) for _ in range(TOP)]
         tile = slots // 4
         for begin in range(0, slots, tile):
@@ -670,8 +663,6 @@
                 mm(logit_parts[shard, :EXPERTS], h_ref[shard * rows : (shard + 1) * rows, :])
                 for shard in range(shards)
             )
-        elif number == 2 * shards:
-            swap.wait()
 
     gain_grad_ref[...] = jnp.zeros_like(gain_grad_ref)
 
@@ -683,7 +674,7 @@
         grad_ref[span, :] = grad
         return grad
 
-    exchange(math, rank, source, full, *rest[:-5], side=side, fill=fill, start=start, cut=source.shape[2] // 4)
+    exchange(math, rank, source, full, *rest[:-3], side=side, fill=fill, start=start)
 
 
 def norm_one_back_kernel(
@@ -845,7 +836,7 @@
 
 def expert_kernel(
     rows_in, grads_in, gate_in, up_in, down_in, far_gate,
-    ret_out, back_out, own_gate, own_up, own_down, got_gate, sent_up, sent_down,
+    ret_out, back_out, own_gate, own_up, own_down, got_gate, got_up, got_down,
     rows, grads, weights, sums, parts, z_send, z_recv, y_send, y_recv, p_send, p_recv, r_send, r_recv, w_send, w_recv, g_send, g_recv, local,
 ):
     groups, half, width = rows.shape[1:]
@@ -920,18 +911,16 @@
     for step in range(1, groups):
         for kind in range(2):
             out_of(kind, step).start()
+
     def arrive(step):
         for kind in range(2):
             out_of(kind, step).wait()
             forward(kind, step).start()
 
-    near = groups // 2
-    for copy in own:
-        copy.wait()
-    for kind in range(2):
-        forward(kind, 0).start()
-    for step in range(1, near):
-        arrive(step)
+    def give(step):
+        for kind in range(2):
+            partial_sum(kind, step).start()
+
     for number in range(3):
         for part in range(2):
             sums[number, part] = jnp.zeros(sums.shape[2:], F32)
@@ -943,26 +932,44 @@
             held = moved[kind][1]
             parts[kind, other] = (parts[kind, other].astype(F32) + held[0, other].astype(F32)).astype(BF16)
 
-        @pl.when(step == 0)
-        def _():
-            for kind in range(2):
+        for kind in range(2):
+            if step == 0:
                 own_result(kind).start()
-
-        @pl.when(step > 0)
-        def _():
-            for kind in range(2):
+            else:
                 result(kind, step).start()
 
-    def body(step, carry):
-        @pl.when((step >= near) & (step < groups - 1))
-        def _():
-            arrive(step + 1)
-
-        @pl.when(step == 0)
+    def act(plan):
+        for action, step in plan:
+            action(step)
+
+    order = (0, 1, 4, 5, 2, 6, 3, 7)
+    before = {
+        0: [(arrive, 1), (arrive, 2), (arrive, 3), (arrive, 4)],
+        1: [(give, 0)],
+        2: [(arrive, 5)],
+        3: [(give, 4), (finish, 0)],
+        4: [(arrive, 6)],
+        5: [(give, 5), (finish, 4)],
+        6: [(arrive, 7)],
+        7: [(give, 6), (finish, 5)],
+    }
+    ahead = [(give, 7)]
+    last = [(give, 2), (finish, 6), (give, 3), (finish, 7), (give, 1), (finish, 2), (finish, 3), (finish, 1)]
+    for copy in own:
+        copy.wait()
+    for kind in range(2):
+        forward(kind, 0).start()
+
+    def body(turn, carry):
+        for number, plan in before.items():
+            pl.when(turn == number)(partial(act, plan))
+
+        @pl.when(turn == 0)
         def _():
             for copy in kept:
                 copy.wait()
 
+        step = sum((turn == number).astype(jnp.int32) * which for number, which in enumerate(order))
         for kind in range(2):
             forward(kind, step).wait()
         other = partner_of(group, step)
@@ -988,31 +995,19 @@
             held = moved[kind][1]
             held[0, other] = value[:half].astype(BF16)
             held[1, other] = value[half:].astype(BF16)
-            partial_sum(kind, step).start()
-
-        @pl.when(step > 0)
-        def _():
-            finish(step - 1)
-
-        @pl.when(step == near - 1)
-        def _():
-            arrive(near)
 
         return carry
 
     lax.fori_loop(0, groups, body, 0)
+    act(ahead)
     copies = []
-    for number, own_ref in enumerate((own_gate, own_up, own_down)):
+    for number, (own_ref, got_ref) in enumerate(((own_gate, got_gate), (own_up, got_up), (own_down, got_down))):
         weights[number, 0] = sums[number, 1].astype(BF16)
-        if number == 0:
-            copies.append(remote(weights.at[0, 0], got_gate, g_send.at[0], g_recv.at[0], across))
-        else:
-            far_ref = (sent_up, sent_down)[number - 1]
-            copies.append(pltpu.make_async_copy(weights.at[number, 0], far_ref, local.at[4 + number]))
+        copies.append(remote(weights.at[number, 0], got_ref, g_send.at[number], g_recv.at[number], across))
         copies[-1].start()
         copies.append(pltpu.make_async_copy(sums.at[number, 0], own_ref, local.at[2 + number]))
         copies[-1].start()
-    finish(groups - 1)
+    act(last)
     for copy in copies:
         copy.wait()
     for kind in range(2):
@@ -1044,8 +1039,8 @@
         ]
         + [pair] * 8
         + [pltpu.SemaphoreType.DMA((2,))] * 2
-        + [pltpu.SemaphoreType.DMA((1,))] * 2
-        + [pltpu.SemaphoreType.DMA((7,))],
+        + [pltpu.SemaphoreType.DMA((3,))] * 2
+        + [pltpu.SemaphoreType.DMA((6,))],
         compiler_params=pltpu.CompilerParams(
             vmem_limit_bytes=60 * MIB, collective_id=1, has_side_effects=True
         ),
@@ -1154,36 +1149,28 @@
         [((share, width), F32), ((share, 1), F32), ((tokens, width), BF16), ((slots, width), BF16)],
     )
     rows, row_grads, gate_rows, gates = dispatch(code, routes_t, router.T, h2, dy_rows)
-    ret, back, own_gate, own_up, own_down, got_gate, sent_up, sent_down = run_experts(
+    ret, back, *weight_grads = run_experts(
         rows, row_grads, expert_gate, expert_up, expert_down, traded
     )
-    here, anywhere = pl.BlockSpec(memory_space=pltpu.VMEM), pl.BlockSpec(memory_space=pl.ANY)
-    grad_attn, grad_resid, grad_gain_two, grad_router, partial_y, got_up = exchange_call(
+    grad_attn, grad_resid, grad_gain_two, grad_router, partial_y = exchange_call(
         norm_two_back_kernel, 3, (tokens, width),
         [ret, back, code, code_cols, gates, routes_t, dy_rows, gate_rows, router.T, h2]
-        + [resid, scale_two, dy, gain_two[None], sent_up],
-        [((share, width), F32), ((1, width), F32), ((EXPERTS, width), F32), ((tokens, width), BF16)]
-        + [(sent_up.shape, BF16)],
+        + [resid, scale_two, dy, gain_two[None]],
+        [((share, width), F32), ((1, width), F32), ((EXPERTS, width), F32), ((tokens, width), BF16)],
         [
             pltpu.VMEM((ranks, share, width), BF16),
             pltpu.VMEM((slots, width), BF16),
             pltpu.VMEM((ranks, 2 * EXPERTS, share), BF16),
-        ]
-        + [pltpu.SemaphoreType.DMA((1,))] * 2,
-        [here] * 14 + [anywhere],
-        [here] * 5 + [anywhere],
+        ],
     )
 
     dq, dk, dv, near, far, y_own = attend_back(
         qkv, tiles, limits, attn_out, grad_attn, lse, by_rank(partial_y), resid
     )
-    sent_down, dq, y_own = lax.optimization_barrier((sent_down, dq, y_own))
-    got_down = lax.ppermute(sent_down, "tensor", [(r, r ^ 1) for r in range(ranks)])
     weight_rows, sent, grad_gain_one, grad_gate, grad_up = project_back(
         place, layer_input, gain_col, scale_one, w_in, mixed, grad_attn, (dq, dk, dv),
-        (own_gate, own_up), (got_gate, got_up),
-    )
-    sent, got_down = lax.optimization_barrier((sent, got_down))
+        weight_grads[:2], weight_grads[3:5],
+    )
     summed = lax.psum(weight_rows, "expert")
     y_own = y_own.astype(BF16)
     small_shape = (EXPERTS + 8 + BUCKETS, width)
@@ -1198,7 +1185,7 @@
     )
     summed, grad_rows = lax.optimization_barrier((summed, grad_rows))
     grad_input = turn(grad_rows, F32)
-    layer_output, grad_down = turn_and_place(place, y_full.reshape(tokens, width), BF16, own_down, got_down)
+    layer_output, grad_down = turn_and_place(place, y_full.reshape(tokens, width), BF16, weight_grads[2], weight_grads[5])
     in_rows = w_in.shape[0]
     heads = rel_bias.shape[1]
     return (

time: 781 us -> 731 us (0.936)
  Pallas kernels: 731 us -> 687 us
    pallas_call x3, Pallas kernels: 342 us -> 286 us  [exchange_call(): pl.pallas_call(kernel, in_specs=[here] * len(operands), out_specs=[here]...]
    pallas_call x1, Pallas kernels: 269 us -> 277 us  [run_experts(): pl.pallas_call(expert_kernel, in_specs=[anywhere] * 6, out_specs=[anywher...]
  transfers between devices with their start and end apart: 3 -> 2, of which waited for: 1 -> 0; matrix products, arithmetic and copies ran while one was open for 2% -> 2% of each run, Pallas kernels for 28% -> 23%
where the time goes in v5:
time: 731 us; the launch traced here: 726 us
  Pallas kernels  687 us (94%)
  local copies, waits for them, and re-layouts  15.7 us (2%)
  between operations  14.6 us (2%)
    pallas_call x3, Pallas kernels, exchange_call(): pl.pallas_call(kernel, in_specs=[here] * len(operands), out_specs=[here]...  286 us
    pallas_call x1, Pallas kernels, run_experts(): pl.pallas_call(expert_kernel, in_specs=[anywhere] * 6, out_specs=[anywher...  277 us
    pallas_call x1, Pallas kernels, attend_back(): pl.pallas_call(attend_back_kernel, grid=(seqs, heads), in_specs=[pl.Block...  39.4 us
    pallas_call x1, Pallas kernels, attend(): pl.pallas_call(attend_kernel, grid=(seqs, heads), in_specs=[pl.BlockSpec(...  23.8 us
    pallas_call x1, Pallas kernels, project_back(): pl.pallas_call(project_back_kernel, grid=(steps,), in_specs=[pl.BlockSpec...  21.3 us
  transfers between devices with their start and end apart: 2, of which 0 were waited for; matrix products, arithmetic and copies ran while one was open for 2% of the time, Pallas kernels for 23%

profile of v5, /device:TPU:0, one launch (start us, length us, event | category | flops | bytes accessed | tf_op | source)
XLA Modules:
  0.0 725.8 jit_solution(10509744982395356488)
XLA Ops:
  7.2 0.0 copy-start.2
  7.2 0.0 copy-start.4
  7.2 0.0 all-reduce.2.cloned.1.call-start
  7.3 1.5 dynamic-slice_bitcast_fusion
  8.7 3.0 collective-permute-start
  11.7 0.0 copy-done.2
  11.7 1.0 copy.39.gain_ref
  12.8 0.0 copy-done.4
  12.8 0.7 copy.36.table_ref
  13.5 1.3 constant_dynamic-slice_fusion
  14.8 0.0 copy-start.3
  14.8 1.3 copy.42
  16.1 0.6 pad_add_fusion.place_ref
  16.7 1.6 shard_map.215.code_ref
  18.3 2.1 copy.38
  20.3 3.2 shard_map.213.tiles_ref
  23.6 0.0 copy-done.3
  23.6 0.1 fusion
  23.7 0.6 iota_maximum_fusion.limit_ref
  24.3 8.3 %shard_map.212 = (bf16[768,2048]{1,0:T(8,128)(2,1)}, f32[1,2048]{1,0:T(1,128)}) custom-call(bf16[1024,2048]{1,0:T(8,128)(2,1)} %x_ref.3, f32[1024,1]{1,0:T(8,128)} %copy.39.gain_ref, bf16[768,1024]{1,0:T(8,128)(2,1)} %bitcast.51), custom_call_target="tpu_custom_call" | custom-call | flops 3221225472 | bytes 8388608 | tf_op jit(solution)/shard_map/pallas_call | solution.py:64
  32.6 23.8 %shard_map.214 = (bf16[256,2048]{1,0:T(8,128)(2,1)}, f32[8,1,1024]{2,1,0:T(1,128)}, bf16[2048,1024]{1,0:T(8,128)(2,1)}) custom-call(bf16[768,2048]{1,0:T(8,128)(2,1)} %get-tuple-element.59.q_ref.k_ref.v_ref, bf16[768,2048]{1,0:T(8,128)(2,1)} %get-tuple-element.59.q_ref.k_ref.v_ref, bf16[768,2048]{1,0:T(8,128)(2,1)} %get-tuple-element.59.q_ref.k_ref.v_ref, ...), custom_call_target="tpu_custom_call" | custom-call | flops 4294967296 | bytes 16777216 | tf_op jit(solution)/shard_map/pallas_call | solution.py:196
  56.4 0.0 collective-permute-done.far_gate
  56.4 79.3 %shard_map.216 = (bf16[4,512,1024]{2,1,0:T(8,128)(2,1)}, f32[512,1024]{1,0:T(8,128)}, f32[512,1]{1,0:T(8,128)}, bf16[2048,1024]{1,0:T(8,128)(2,1)}, bf16[1280,1024]{1,0:T(8,128)(2,1)}) custom-call(bf16[4,512,1024]{2,1,0:T(8,128)(2,1)} %bitcast.36, bf16[512,1024]{1,0:T(8,128)(2,1)} %bitcast.27, f32[1,1024]{1,0:T(1,128)} %bitcast.42, ...), custom_call_target="tpu_custom_call" | custom-call | flops 41943040 | bytes 209715200 | tf_op jit(solution)/shard_map/pallas_call | solution.py:566
  135.7 11.5 %shard_map.217 = (bf16[1280,1024]{1,0:T(8,128)(2,1)}, bf16[1280,1024]{1,0:T(8,128)(2,1)}, f32[1280,1]{1,0:T(8,128)}, f32[2,2048]{1,0:T(2,128)}) custom-call(s32[2,2048]{1,0:T(2,128)} %shard_map.215.code_ref, s32[2,2048]{1,0:T(2,128)} %bitcast.38, bf16[16,1024]{1,0:T(8,128)(2,1)} %bitcast.40, bf16[2048,1024]{1,0:T(8,128)(2,1)} %bitcast.32, ...), custom_call_target="tpu_custom_call" | custom-call | flops 5368709120 | bytes 12058624 | tf_op jit(solution)/shard_map/pallas_call | solution.py:808
  147.2 277.2 %shard_map.218 = (bf16[1280,1024]{1,0:T(8,128)(2,1)}, bf16[1280,1024]{1,0:T(8,128)(2,1)}, f32[704,1024]{1,0:T(8,128)}, f32[704,1024]{1,0:T(8,128)}, f32[704,1024...) custom-call(bf16[1280,1024]{1,0:T(8,128)(2,1)} %get-tuple-element.65.rows_in, ...), custom_call_target="tpu_custom_call" | custom-call | flops 66437775360 | bytes 42598400 | tf_op jit(solution)/shard_map/pallas_call | solution.py:1026
  424.5 86.2 %shard_map.219 = (bf16[4,512,1024]{2,1,0:T(8,128)(2,1)}, f32[512,1024]{1,0:T(8,128)}, f32[1,1024]{1,0:T(1,128)}, f32[16,1024]{1,0:T(8,128)}, bf16[2048,1024]{1,0:T(8,128)(2,1)}) custom-call(bf16[1280,1024]{1,0:T(8,128)(2,1)} %get-tuple-element.68.ret_ref, bf16[1280,1024]{1,0:T(8,128)(2,1)} %get-tuple-element.69.back_ref, s32[2,2048]{1,0:T(2,128)} %shard_map.215.code_ref, ...), custom_call_target="tpu_custom_call" | custom-call | flops 41943040 | bytes 209715200 | tf_op jit(solution)/shard_map/pallas_call | solution.py:566
  510.7 39.4 %shard_map.220 = (bf16[256,2048]{1,0:T(8,128)(2,1)}, bf16[256,2048]{1,0:T(8,128)(2,1)}, bf16[256,2048]{1,0:T(8,128)(2,1)}, f32[8,3,256,256]{3,2,1,0:T(8,128)}, f...) custom-call(bf16[768,2048]{1,0:T(8,128)(2,1)} %get-tuple-element.59.q_ref.k_ref.v_ref, ...), custom_call_target="tpu_custom_call" | custom-call | flops 10737418240 | bytes 33554432 | tf_op jit(solution)/shard_map/pallas_call | solution.py:332
  550.1 21.3 %shard_map.221 = (bf16[1024,1024]{1,0:T(8,128)(2,1)}, bf16[2048,1024]{1,0:T(8,128)(2,1)}, f32[1024,1]{1,0:T(8,128)}, f32[2,704,1024]{2,1,0:T(8,128)}, f32[2,704,1024]{2,1,0:T(8,128)}) custom-call(s32[2]{0:T(128)} %pad_add_fusion.place_ref, bf16[1024,2048]{1,0:T(8,128)(2,1)} %x_ref.3, f32[1024,1]{1,0:T(8,128)} %copy.39.gain_ref, ...), custom_call_target="tpu_custom_call" | custom-call | flops 8053063680 | bytes 22675456 | tf_op jit(solution)/shard_map/pallas_call | solution.py:417
  571.3 0.0 copy-start.1
  571.4 0.0 all-reduce.2.cloned.1.call-update
  571.4 0.8 dynamic-slice_bitcast_fusion.1
  572.2 0.9 copy.40.scale_ref
  573.1 0.0 copy-done.1
  573.1 1.1 convert_element_type.7.ready
  574.2 120.7 %shard_map.222 = (bf16[4,512,1024]{2,1,0:T(8,128)(2,1)}, bf16[4,512,1024]{2,1,0:T(8,128)(2,1)}, f32[56,1024]{1,0:T(8,128)}) custom-call(bf16[4,512,1024]{2,1,0:T(8,128)(2,1)} %bitcast.30, bf16[512,1024]{1,0:T(8,128)(2,1)} %bitcast.28, f32[512,1]{1,0:T(8,128)} %copy.40.scale_ref, f32[512,1024]{1,0:T(8,128)} %get-tuple-element.86.grad_ref, ...), custom_call_target="tpu_custom_call" | custom-call | flops 41943040 | bytes 209715200 | tf_op jit(solution)/shard_map/pallas_call | solution.py:566
  694.9 1.0 slice.20
  695.9 0.7 copy.41
  696.6 7.8 %shard_map.223 = (bf16[1024,2048]{1,0:T(8,128)(2,1)}, f32[2,704,1024]{2,1,0:T(8,128)}) custom-call(s32[2]{0:T(128)} %pad_add_fusion.place_ref, bf16[2048,1024]{1,0:T(8,128)(2,1)} %bitcast.35, f32[704,1024]{1,0:T(8,128)} %get-tuple-element.94.own_ref, bf16[704,1024]{1,0:T(8,128)(2,1)} %get-tuple-element.95.got_ref), custom_call_target="tpu_custom_call" | custom-call | bytes 22675456 | tf_op jit(solution)/shard_map/pallas_call | solution.py:1081
  704.3 1.4 fusion.1
  705.8 1.5 slice_bitcast_fusion
  707.2 0.0 all-reduce.2.cloned.1.call-done
  707.2 0.0 copy-start
  707.2 1.6 copy-done
  708.8 1.1 slice_convert_fusion
  709.9 0.0 slice-start
  709.9 6.6 shard_map.224
  716.5 0.0 slice-done
  716.5 2.1 convert.1
  (1 shorter events, 0.0 us)
Async XLA Ops:
  7.2 4.6 copy-start.2
  7.2 5.6 copy-start.4
  7.2 700.0 %all-reduce.2.cloned.1.call-start = ((), (), s32[]{:S(2)}) async-start(), calls=%async_computation | async-start | bytes 4194304 | tf_op jit(solution)/shard_map/psum | solution.py:1174
  8.7 47.7 %collective-permute-start = (bf16[704,1024]{1,0:T(8,128)(2,1)S(1)}, bf16[704,1024]{1,0:T(8,128)(2,1)}, u32[]{:S(2)}, u32[]{:S(2)}) collective-permute-start(bf16[704,1024]{1,0:T(8,128)(2,1)S(1)} %dynamic-slice_bitcast_fusion), channel_id=1, source_target_pairs={{0,1},{1,0},{2,3},{3,2},{4,5},{5,4},{6,7},{7,6},{8,9},{9,8},{10,11... | collective-permute-start | bytes 4325384 | tf_op jit(solution)/shard_map/ppermute | solution.py:1116
  14.8 8.8 %copy-start.3 = (s32[2,2]{1,0:T(2,128)S(1)}, s32[2,2]{1,0:T(2,128)}, u32[]{:S(2)}) copy-start(s32[2,2]{1,0:T(2,128)} %param.24) | copy-start | bytes 52
  571.3 1.8 copy-start.1
  707.2 1.6 copy-start
  709.9 6.6 slice-start
Sparse Core Ops, SparseCore 0:
  571.5 73.4 all-reduce.1

commit v6 on v5

--- a/solution.py
+++ b/solution.py
@@ -118,7 +118,8 @@
 
 def bias_fold(near_ref, far_ref):
     heads = near_ref.shape[0] // 2
-    columns = []
+    sums = jnp.zeros((BUCKETS, 128), F32)
+    lane = lax.broadcasted_iota(jnp.int32, (BUCKETS, 128), 1)
     row = lax.broadcasted_iota(jnp.int32, (BLK, BLK), 0)
     column = lax.broadcasted_iota(jnp.int32, (BLK, BLK), 1)
     flip = jnp.where(row + column == BLK - 1, 1.0, 0.0).astype(BF16)
@@ -142,8 +143,8 @@
         distant = jnp.sum(far_ref[head] + far_ref[heads + head], axis=0, keepdims=True)
         distant = jnp.sum(distant, axis=1, keepdims=True)
         total += jnp.where(number_at[:, :1] == 15, distant, 0.0)
-        columns.append(total)
-    return columns
+        sums = jnp.where(lane == head, total, sums)
+    return sums
 
 
 def key_count(query_block):
@@ -223,7 +224,7 @@
 def attend_back_kernel(
     q_ref, k_ref, v_ref, tiles_ref, limit_ref, w_ref, grad_ref, lse_ref, part_ref, resid_ref,
     dq_ref, dk_ref, dv_ref, near_ref, far_ref, y_ref,
-    held, parts, turn_across, turn_along, from_across, from_along, sends, recvs, loads,
+    held, parts, total, turn_across, turn_along, from_across, from_along, sends, recvs, loads,
 ):
     rank = lax.axis_index("tensor")
     pair_class, half_index = rank % 2, rank // 2
@@ -248,7 +249,7 @@
         pltpu.make_async_copy(part_ref.at[other], parts.at[number], loads.at[number])
         for number, other in enumerate((across, along, rank))
     ]
-    local.append(pltpu.make_async_copy(resid_ref, y_ref, loads.at[3]))
+    local.append(pltpu.make_async_copy(resid_ref, total, loads.at[3]))
 
     @pl.when(step == 0)
     def _():
@@ -318,7 +319,8 @@
     def _():
         for copy in second:
             copy.wait()
-        y_ref[...] += parts[2].astype(F32) + from_across[...].astype(F32) + from_along[...].astype(F32)
+        summed = parts[2].astype(F32) + from_across[...].astype(F32) + from_along[...].astype(F32)
+        y_ref[...] = (total[...] + summed).astype(BF16)
 
 
 def attend_back(qkv, tiles, limits, attn_out, grad_attn, lse, part, resid):
@@ -356,10 +358,11 @@
             jax.ShapeDtypeStruct((seqs * heads, 3, BLK, BLK), F32),
             jax.ShapeDtypeStruct((seqs * heads, 8, BLK), F32),
         ]
-        + [jax.ShapeDtypeStruct((share, model_width), F32)],
+        + [jax.ShapeDtypeStruct((share, model_width), BF16)],
         scratch_shapes=[
             pltpu.VMEM((heads * width, SEQ), BF16),
             pltpu.VMEM((3, share, model_width), BF16),
+            pltpu.VMEM((share, model_width), F32),
             pltpu.VMEM((share, model_width // 2), BF16),
             pltpu.VMEM((share, model_width // 2), BF16),
             pltpu.VMEM((share, model_width), BF16),
@@ -486,14 +489,12 @@
         fill(along)
         fill(across)
     if ready is not None:
-        ready_full[rank] = ready[...]
+        _, near_across, near_along = ready
         extra = [
-            remote(8, 0, ready, ready_full.at[rank], across),
-            remote(8, 1, ready, ready_full.at[rank], along),
-            remote(8, 2, ready_full.at[along, :, low], ready_full.at[along, :, low], across),
-            remote(8, 3, ready_full.at[across, :, high], ready_full.at[across, :, high], along),
+            remote(8, 0, near_along.at[:, low], ready_full.at[along, :, low], across),
+            remote(8, 1, near_across.at[:, high], ready_full.at[across, :, high], along),
         ]
-        for copy in extra[:2]:
+        for copy in extra:
             copy.start()
     for chunk, span in enumerate(spans):
         if side:
@@ -512,10 +513,8 @@
             copy.start()
         second.append(pair)
     if ready is not None:
-        for copy in extra[:2]:
-            copy.wait()
-        for copy in extra[2:]:
-            copy.start()
+        for other, piece in zip((rank, across, along), ready):
+            ready_full[other] = piece[...]
 
     def pass_on(chunk):
         span = spans[chunk]
@@ -549,7 +548,7 @@
             pass_on(chunk - 1)
     pass_on(chunks - 1)
     if ready is not None:
-        for copy in extra[2:]:
+        for copy in extra:
             copy.wait()
     for pair in fourth:
         for copy in pair:
@@ -558,14 +557,14 @@
         side(2 * chunks)
 
 
-def exchange_call(kernel, number, shape, operands, extra_shapes, scratch=()):
+def exchange_call(kernel, number, shape, operands, extra_shapes, scratch=(), in_hbm=()):
     tokens, width = shape
     ranks = 4
     rows = tokens // ranks
     here = pl.BlockSpec(memory_space=pltpu.VMEM)
     results = pl.pallas_call(
         kernel,
-        in_specs=[here] * len(operands),
+        in_specs=[pl.BlockSpec(memory_space=pl.ANY) if k in in_hbm else here for k in range(len(operands))],
         out_specs=[here] * (1 + len(extra_shapes)),
         out_shape=[jax.ShapeDtypeStruct((ranks, rows, width), BF16)]
         + [jax.ShapeDtypeStruct(shape, kind) for shape, kind in extra_shapes],
@@ -580,18 +579,29 @@
     return results[0].reshape(tokens, width), *results[1:]
 
 
-def norm_two_kernel(source, x_ref, gain_ref, grad_out_ref, code_ref, full, resid_ref, scale_ref, dy_ref, dy_rows_ref, *rest):
+def norm_two_kernel(
+    source, x_ref, gain_ref, grad_out_ref, routes_ref,
+    full, resid_ref, scale_ref, dy_ref, dy_rows_ref, code_ref, codes_ref, own_ref, *rest,
+):
+    held, load = rest[-2:]
+    rank = lax.axis_index("tensor")
+    ranks, rows, width = source.shape
+    slots = dy_rows_ref.shape[0] // ranks
+    own = pltpu.make_async_copy(x_ref.at[:, pl.ds(pl.multiple_of(rank * rows, rows), rows)], held, load.at[0])
+
     def math(span, total):
-        resid = x_ref[span, :].astype(F32) + total
+        resid = own_ref[span, :].astype(F32) + total
         scale = lax.rsqrt(jnp.sum(resid * resid, axis=1, keepdims=True) / resid.shape[1] + EPS)
         resid_ref[span, :] = resid
         scale_ref[span, :] = scale
         return resid * scale * gain_ref[...]
 
-    ranks, rows, width = source.shape
-    slots = dy_rows_ref.shape[0] // ranks
-
     def side(number):
+        if number == 0:
+            own.wait()
+            own_ref[...] = held[...].astype(F32).T.astype(BF16)
+            local_codes(routes_ref, code_ref, rank % 2, rank // 2, CAP // 2)
+            codes_ref[...] = jnp.concatenate([code_ref[...].astype(F32)] * 4, axis=0).T[:, :TOP].astype(jnp.int32)
         if number < ranks:
             span = slice(number * rows, (number + 1) * rows)
             dy_ref[span, :] = grad_out_ref[:, span].astype(F32).T.astype(BF16)
@@ -601,7 +611,7 @@
             take = jnp.where((slot == code_ref[0:1]) | (slot == code_ref[1:2]), 1.0, 0.0).astype(BF16)
             dy_rows_ref[start : start + slots, :] = mm(take, dy_ref[...]).astype(BF16)
 
-    exchange(math, lax.axis_index("tensor"), source, full, *rest, side=side)
+    exchange(math, rank, source, full, *rest[:-2], side=side, start=own.start)
 
 
 def norm_back(grad, value, scale, gain):
@@ -678,10 +688,10 @@
 
 
 def norm_one_back_kernel(
-    source, x_ref, scale_ref, grad_ref, gain_ref, ready, gain_one_ref, gain_two_ref, router_ref, near_ref, far_ref,
-    full, ready_full, small_out, *rest
+    source, x_ref, scale_ref, grad_ref, gain_ref, y_own, y_across, y_along, gain_one_ref, gain_two_ref, router_ref,
+    near_ref, far_ref, full, ready_full, small_out, *rest,
 ):
-    held, tensor_sends, tensor_recvs, expert_sends, expert_recvs = rest[-5:]
+    held, near, scale, load, tensor_sends, tensor_recvs, expert_sends, expert_recvs = rest[-8:]
     rank, group = lax.axis_index("tensor"), lax.axis_index("expert")
     pair_class, half_index = rank % 2, rank // 2
     others = rank + 1 - 2 * pair_class, rank + 2 - 4 * half_index
@@ -689,10 +699,12 @@
     mesh_ids = pl.DeviceIdType.MESH
     peers = [partner_of(group, step) for step in range(1, groups)]
     summed = slice(0, small_out.shape[0] - BUCKETS)
+    rows = source.shape[1]
+    loading = pltpu.make_async_copy(near_ref, near, load.at[0])
 
     def math(span, total):
         x = x_ref[span, :].astype(F32)
-        return norm_back(total, x, scale_ref[span, :], gain_ref[...]) + grad_ref[span, :]
+        return norm_back(total, x, scale[span, :], gain_ref[...]) + grad_ref[span, :]
 
     def to_rank(step):
         return pltpu.make_async_remote_copy(
@@ -706,22 +718,27 @@
             recv_sem=expert_recvs.at[step], device_id={"expert": peers[step - 1]}, device_id_type=mesh_ids,
         )
 
+    def start():
+        loading.start()
+        held[groups] = jnp.zeros(small_out.shape, F32)
+        held[groups, :EXPERTS] = router_ref[...]
+        held[groups, EXPERTS : EXPERTS + 1] = gain_two_ref[...]
+        held[groups, EXPERTS + 1 : EXPERTS + 2] = jnp.broadcast_to(gain_one_ref[...], (gain_one_ref.shape[0], 128)).T[:1]
+        to_rank(0).start()
+
     def side(number):
         if number == 0:
-            held[groups] = jnp.zeros(small_out.shape, F32)
-            held[groups, :EXPERTS] = router_ref[...]
-            held[groups, EXPERTS : EXPERTS + 1] = gain_two_ref[...]
-            held[groups, EXPERTS + 1 : EXPERTS + 2] = jnp.broadcast_to(gain_one_ref[...], (gain_one_ref.shape[0], 128)).T[:1]
-            to_rank(0).start()
+            own_scale = scale_ref[:, pl.ds(pl.multiple_of(rank * rows, rows), rows)]
+            scale[...] = jnp.broadcast_to(own_scale, (8, rows)).T[:, :1]
+            loading.wait()
+            held[group] = jnp.zeros(small_out.shape, F32)
+            held[group, summed.stop :, :128] = bias_fold(near, far_ref)
         elif number == 1:
             to_rank(0).wait()
             held[groups + 1] = held[groups] + held[groups + 2]
             to_rank(1).start()
-        elif number == 2:
+        elif number == 5:
             to_rank(1).wait()
-            for head, column in enumerate(bias_fold(near_ref, far_ref)):
-                span = slice(summed.stop, summed.stop + BUCKETS)
-                held[group, span, head * 128 : (head + 1) * 128] = jnp.broadcast_to(column, (BUCKETS, 128))
             held[group, summed] = held[groups + 1, summed] + held[groups + 3, summed]
             for step in range(1, groups):
                 to_group(step).start()
@@ -733,11 +750,12 @@
                 total = total + held[step]
             small_out[...] = total
 
-    exchange(math, rank, source, full, *rest[:-5], ready, ready_full, side=side, peers=peers)
-
-
-def code_kernel(place_ref, routes_ref, code_ref, half, groups):
-    pair_class, half_index = place_ref[0], place_ref[1]
+    exchange(
+        math, rank, source, full, *rest[:-8], (y_own, y_across, y_along), ready_full, side=side, peers=peers, start=start
+    )
+
+
+def local_codes(routes_ref, code_ref, pair_class, half_index, half):
     tokens = routes_ref.shape[1]
     expert = lax.broadcasted_iota(jnp.int32, (EXPERTS, BLK), 0)
     earlier = (
@@ -758,19 +776,6 @@
             local = slot - half_index * half
             mine = (route - 2 * owner == pair_class) & (local >= 0) & (local < half)
             code_ref[i : i + 1, cols] = jnp.where(mine, owner * half + local, -1)
-
-
-def local_codes(place, routes_t, half, groups):
-    return pl.pallas_call(
-        partial(code_kernel, half=half, groups=groups),
-        in_specs=[
-            pl.BlockSpec(memory_space=pltpu.SMEM),
-            pl.BlockSpec(memory_space=pltpu.VMEM),
-        ],
-        out_specs=pl.BlockSpec(memory_space=pltpu.VMEM),
-        out_shape=jax.ShapeDtypeStruct(routes_t.shape, jnp.int32),
-        compiler_params=params(),
-    )(place, routes_t)
 
 
 def dispatch_kernel(code_ref, routes_ref, router_ref, h_ref, dy_rows_ref, rows_ref, grads_ref, gate_ref, gates_ref):
@@ -1048,56 +1053,75 @@
     )(rows, grads, w_gate, w_up, w_down, far_gate)
 
 
-def turn_kernel(in_ref, out_ref):
-    out_ref[...] = in_ref[...].astype(F32).T.astype(out_ref.dtype)
-
-
-def turn(rows, kind):
-    tokens, width = rows.shape
-    tile = 512
-    return pl.pallas_call(
-        turn_kernel,
-        grid=(tokens // tile,),
-        in_specs=[pl.BlockSpec((tile, width), lambda i: (i, 0))],
-        out_specs=pl.BlockSpec((width, tile), lambda i: (0, i)),
-        out_shape=jax.ShapeDtypeStruct((width, tokens), kind),
-        compiler_params=params(),
-        cost_estimate=cost(0, 6 * rows.size),
-    )(rows)
-
-
-def turn_and_place_kernel(place_ref, in_ref, own_ref, got_ref, out_ref, placed_ref):
-    out_ref[...] = in_ref[...].astype(F32).T.astype(out_ref.dtype)
+def finish_kernel(
+    place_ref, rows_ref, y_ref, own_ref, got_ref, summed_ref, small_ref,
+    output_ref, grad_ref, placed_ref, in_ref, out_ref, one_ref, two_ref, router_ref, bias_ref,
+):
+    step = pl.program_id(0)
+    output_ref[...] = y_ref[...].astype(F32).T.astype(BF16)
+    grad_ref[...] = rows_ref[...].astype(F32).T
     placed_ref[place_ref[0]] = own_ref[...]
     placed_ref[1 - place_ref[0]] = got_ref[...].astype(F32)
 
-
-def turn_and_place(place, rows, kind, own, got):
+    @pl.when(step < 3)
+    def _():
+        in_ref[...] = summed_ref[...].astype(F32)
+
+    @pl.when(step == 3)
+    def _():
+        out_ref[...] = summed_ref[...].astype(F32)
+        router_ref[...] = small_ref[:EXPERTS]
+        two_ref[...] = small_ref[EXPERTS : EXPERTS + 1]
+        one_ref[...] = small_ref[EXPERTS + 1 : EXPERTS + 2]
+        bias_ref[...] = small_ref[EXPERTS + 8 :, :128].T[: bias_ref.shape[0]]
+
+
+def finish_outputs(place, rows, y_rows, own, got, summed, small, heads):
     tokens, width = rows.shape
     units = own.shape[0]
     steps = 4
-    tile, part = tokens // steps, units // steps
+    tile, part, block = tokens // steps, units // steps, summed.shape[0] // steps
     quarter = pl.BlockSpec((part, width), lambda i: (i, 0))
+    token_spec = pl.BlockSpec((tile, width), lambda i: (i, 0))
+    feature_spec = pl.BlockSpec((width, tile), lambda i: (0, i))
+    whole = lambda *shape: pl.BlockSpec(shape, lambda i: (0, 0))
     return pl.pallas_call(
-        turn_and_place_kernel,
+        finish_kernel,
         grid=(steps,),
         in_specs=[
             pl.BlockSpec(memory_space=pltpu.SMEM),
-            pl.BlockSpec((tile, width), lambda i: (i, 0)),
+            token_spec,
+            token_spec,
             quarter,
             quarter,
+            pl.BlockSpec((block, width), lambda i: (i, 0)),
+            whole(*small.shape),
         ],
         out_specs=[
-            pl.BlockSpec((width, tile), lambda i: (0, i)),
+            feature_spec,
+            feature_spec,
             pl.BlockSpec((2, part, width), lambda i: (0, i, 0)),
+            pl.BlockSpec((block, width), lambda i: (jnp.minimum(i, 2), 0)),
+            whole(block, width),
+            whole(1, width),
+            whole(1, width),
+            whole(EXPERTS, width),
+            whole(heads, BUCKETS),
         ],
         out_shape=[
-            jax.ShapeDtypeStruct((width, tokens), kind),
+            jax.ShapeDtypeStruct((width, tokens), BF16),
+            jax.ShapeDtypeStruct((width, tokens), F32),
             jax.ShapeDtypeStruct((2, units, width), F32),
+            jax.ShapeDtypeStruct((3 * block, width), F32),
+            jax.ShapeDtypeStruct((block, width), F32),
+            jax.ShapeDtypeStruct((1, width), F32),
+            jax.ShapeDtypeStruct((1, width), F32),
+            jax.ShapeDtypeStruct((EXPERTS, width), F32),
+            jax.ShapeDtypeStruct((heads, BUCKETS), F32),
         ],
         compiler_params=params(),
-        cost_estimate=cost(0, 6 * rows.size + 14 * own.size),
-    )(place, rows, own, got)
+        cost_estimate=cost(0, 10 * rows.size + 14 * own.size + 6 * summed.size),
+    )(place, rows, y_rows, own, got, summed, small)
 
 
 def on_device(
@@ -1128,25 +1152,20 @@
 
     routes_t = routes.T
     place = jnp.stack([pair_class, half_index]).astype(jnp.int32)
-    code = local_codes(place, routes_t, half, groups)
-    code_cols = code.T
-
     share = tokens // ranks
-
-    def own(rows, axis=0):
-        return lax.dynamic_slice_in_dim(rows, rank * share, share, axis)
 
     def by_rank(rows):
         return rows.reshape(ranks, share, width)
 
-    own_x = own(layer_input, 1).T
-    own_scale = own(scale_one, 1).T
     mixed, lse, sent = attend(qkv, tiles, limits, attn_out)
     sent, traded = lax.optimization_barrier((sent, traded))
     slots = groups * half
-    h2, resid, scale_two, dy, dy_rows = exchange_call(
-        norm_two_kernel, 2, sent.shape, [by_rank(sent), own_x, gain_two[None], grad_out, code],
-        [((share, width), F32), ((share, 1), F32), ((tokens, width), BF16), ((slots, width), BF16)],
+    h2, resid, scale_two, dy, dy_rows, code, code_cols, own_x = exchange_call(
+        norm_two_kernel, 2, sent.shape, [by_rank(sent), layer_input, gain_two[None], grad_out, routes_t],
+        [((share, width), F32), ((share, 1), F32), ((tokens, width), BF16), ((slots, width), BF16)]
+        + [((TOP, tokens), jnp.int32), ((tokens, TOP), jnp.int32), ((share, width), BF16)],
+        [pltpu.VMEM((width, share), BF16), pltpu.SemaphoreType.DMA((1,))],
+        (1,),
     )
     rows, row_grads, gate_rows, gates = dispatch(code, routes_t, router.T, h2, dy_rows)
     ret, back, *weight_grads = run_experts(
@@ -1167,36 +1186,40 @@
     dq, dk, dv, near, far, y_own = attend_back(
         qkv, tiles, limits, attn_out, grad_attn, lse, by_rank(partial_y), resid
     )
+    dq, y_own = lax.optimization_barrier((dq, y_own))
+    y_across = lax.ppermute(y_own, "tensor", [(r, r ^ 1) for r in range(ranks)])
+    y_along = lax.ppermute(y_own, "tensor", [(r, r ^ 2) for r in range(ranks)])
     weight_rows, sent, grad_gain_one, grad_gate, grad_up = project_back(
         place, layer_input, gain_col, scale_one, w_in, mixed, grad_attn, (dq, dk, dv),
         weight_grads[:2], weight_grads[3:5],
     )
+    sent, y_across, y_along = lax.optimization_barrier((sent, y_across, y_along))
     summed = lax.psum(weight_rows, "expert")
-    y_own = y_own.astype(BF16)
     small_shape = (EXPERTS + 8 + BUCKETS, width)
     grad_rows, y_full, small = exchange_call(
         norm_one_back_kernel, 4, sent.shape,
-        [by_rank(sent), own_x, own_scale, grad_resid, gain_one[None], y_own, grad_gain_one, grad_gain_two, grad_router]
-        + [near, far],
+        [by_rank(sent), own_x, scale_one, grad_resid, gain_one[None], y_own, y_across, y_along]
+        + [grad_gain_one, grad_gain_two, grad_router, near, far],
         [((ranks, share, width), BF16), (small_shape, F32)],
-        [pltpu.VMEM((groups + 4, *small_shape), F32)]
+        [pltpu.VMEM((groups + 4, *small_shape), F32), pltpu.VMEM(near.shape, F32), pltpu.VMEM((share, 1), F32)]
+        + [pltpu.SemaphoreType.DMA((1,))]
         + [pltpu.SemaphoreType.DMA((2,))] * 2
         + [pltpu.SemaphoreType.DMA((groups,))] * 2,
+        (11,),
     )
     summed, grad_rows = lax.optimization_barrier((summed, grad_rows))
-    grad_input = turn(grad_rows, F32)
-    layer_output, grad_down = turn_and_place(place, y_full.reshape(tokens, width), BF16, weight_grads[2], weight_grads[5])
-    in_rows = w_in.shape[0]
-    heads = rel_bias.shape[1]
+    layer_output, grad_input, grad_down, grad_in, grad_attn_out, grad_one, grad_two, grad_router, grad_bias = finish_outputs(
+        place, grad_rows, y_full.reshape(tokens, width), weight_grads[2], weight_grads[5], summed, small, rel_bias.shape[1]
+    )
     return (
         layer_output,
         grad_input,
-        small[EXPERTS + 1],
-        summed[:in_rows].astype(F32).reshape(attn_in.shape),
-        small[EXPERTS + 8 :, : heads * 128 : 128],
-        summed[in_rows:].astype(F32),
-        small[EXPERTS],
-        small[:EXPERTS].T,
+        grad_one[0],
+        grad_in.reshape(attn_in.shape),
+        grad_bias.T,
+        grad_attn_out,
+        grad_two[0],
+        grad_router.T,
         grad_gate,
         grad_up,
         grad_down,

time: 731 us -> 702 us (0.960); the launches traced: 726 us -> 689 us
  Pallas kernels: 687 us -> 663 us
  local copies, waits for them, and re-layouts: 15.7 us -> 4.51 us
    pallas_call x6 -> x4, Pallas kernels: 302 us -> 278 us  [the longest x3 263 us: exchange_call(): pl.pallas_call(kernel, in_specs=[pl.BlockSpec(memory_space=pl.ANY) if k i...]
  transfers between devices with their start and end apart: 2 -> 4, of which waited for: 0 -> 0; matrix products, arithmetic and copies ran while one was open for 2% -> 0% of each run, Pallas kernels for 23% -> 22%
where the time goes in v6:
time: 702 us; the launch traced here: 689 us
  Pallas kernels  663 us (94%)
  between operations  14.7 us (2%)
    pallas_call x1, Pallas kernels, run_experts(): pl.pallas_call(expert_kernel, in_specs=[anywhere] * 6, out_specs=[anywher...  277 us
    pallas_call x3, Pallas kernels, exchange_call(): pl.pallas_call(kernel, in_specs=[pl.BlockSpec(memory_space=pl.ANY) if k i...  263 us
    pallas_call x1, Pallas kernels, attend_back(): pl.pallas_call(attend_back_kernel, grid=(seqs, heads), in_specs=[pl.Block...  39.1 us
    pallas_call x1, Pallas kernels, attend(): pl.pallas_call(attend_kernel, grid=(seqs, heads), in_specs=[pl.BlockSpec(...  23.6 us
    pallas_call x1, Pallas kernels, project_back(): pl.pallas_call(project_back_kernel, grid=(steps,), in_specs=[pl.BlockSpec...  21.3 us
    pallas_call x1, Pallas kernels, finish_outputs(): pl.pallas_call(finish_kernel, grid=(steps,), in_specs=[pl.BlockSpec(memor...  15.7 us
  transfers between devices with their start and end apart: 4, of which 0 were waited for; matrix products, arithmetic and copies ran while one was open for 0% of the time, Pallas kernels for 22%

profile of v6, /device:TPU:0, one launch (start us, length us, event | category | flops | bytes accessed | tf_op | source)
XLA Modules:
  0.0 688.6 jit_solution(8727146332438426843)
XLA Ops:
  7.2 0.0 copy-start.4
  7.2 0.0 copy-start.2
  7.2 0.0 all-reduce.2.cloned.1.call-start
  7.3 0.0 copy-start.3
  7.3 1.5 dynamic-slice_bitcast_fusion
  8.8 3.0 collective-permute-start
  11.8 0.0 copy-done.4
  11.8 0.7 copy.29.table_ref
  12.4 0.0 copy-done.2
  12.5 1.0 copy.30.gain_ref
  13.5 3.2 shard_map.213.tiles_ref
  16.7 0.6 pad_add_fusion.place_ref
  17.3 0.0 copy-done.3
  17.3 0.1 fusion
  17.4 0.6 iota_maximum_fusion.limit_ref
  18.0 8.3 %shard_map.212 = (bf16[768,2048]{1,0:T(8,128)(2,1)}, f32[1,2048]{1,0:T(1,128)}) custom-call(bf16[1024,2048]{1,0:T(8,128)(2,1)} %x_ref.5, f32[1024,1]{1,0:T(8,128)} %copy.30.gain_ref, bf16[768,1024]{1,0:T(8,128)(2,1)} %bitcast.41), custom_call_target="tpu_custom_call" | custom-call | flops 3221225472 | bytes 8388608 | tf_op jit(solution)/shard_map/pallas_call | solution.py:64
  26.3 23.6 %shard_map.214 = (bf16[256,2048]{1,0:T(8,128)(2,1)}, f32[8,1,1024]{2,1,0:T(1,128)}, bf16[2048,1024]{1,0:T(8,128)(2,1)}) custom-call(bf16[768,2048]{1,0:T(8,128)(2,1)} %get-tuple-element.74.q_ref.k_ref.v_ref, bf16[768,2048]{1,0:T(8,128)(2,1)} %get-tuple-element.74.q_ref.k_ref.v_ref, bf16[768,2048]{1,0:T(8,128)(2,1)} %get-tuple-element.74.q_ref.k_ref.v_ref, ...), custom_call_target="tpu_custom_call" | custom-call | flops 4294967296 | bytes 16777216 | tf_op jit(solution)/shard_map/pallas_call | solution.py:197
  49.9 0.0 collective-permute-done.far_gate
  49.9 0.0 copy-start.5
  50.0 80.1 %shard_map.215 = (bf16[4,512,1024]{2,1,0:T(8,128)(2,1)}, f32[512,1024]{1,0:T(8,128)}, f32[512,1]{1,0:T(8,128)}, bf16[2048,1024]{1,0:T(8,128)(2,1)}, bf16[1280,10...) custom-call(bf16[4,512,1024]{2,1,0:T(8,128)(2,1)} %bitcast.27, ...), custom_call_target="tpu_custom_call" | custom-call | flops 41943040 | bytes 209715200 | tf_op jit(solution)/shard_map/pallas_call | solution.py:565
  130.1 0.0 copy-done.5
  130.1 11.9 %shard_map.216 = (bf16[1280,1024]{1,0:T(8,128)(2,1)}, bf16[1280,1024]{1,0:T(8,128)(2,1)}, f32[1280,1]{1,0:T(8,128)}, f32[2,2048]{1,0:T(2,128)}) custom-call(s32[2,2048]{1,0:T(2,128)} %get-tuple-element.78.code_ref, s32[2,2048]{1,0:T(2,128)} %bitcast.29, bf16[16,1024]{1,0:T(8,128)(2,1)} %bitcast.31, bf16[2048,1024]{1,0:T(8,128)(2,1)} %bitcast.25, ...), custom_call_target="tpu_custom_call" | custom-call | flops 5368709120 | bytes 12058624 | tf_op jit(solution)/shard_map/pallas_call | solution.py:813
  141.9 277.2 %shard_map.217 = (bf16[1280,1024]{1,0:T(8,128)(2,1)}, bf16[1280,1024]{1,0:T(8,128)(2,1)}, f32[704,1024]{1,0:T(8,128)}, f32[704,1024]{1,0:T(8,128)}, f32[704,1024...) custom-call(bf16[1280,1024]{1,0:T(8,128)(2,1)} %get-tuple-element.81.rows_in, ...), custom_call_target="tpu_custom_call" | custom-call | flops 66437775360 | bytes 42598400 | tf_op jit(solution)/shard_map/pallas_call | solution.py:1031
  419.2 86.2 %shard_map.218 = (bf16[4,512,1024]{2,1,0:T(8,128)(2,1)}, f32[512,1024]{1,0:T(8,128)}, f32[1,1024]{1,0:T(1,128)}, f32[16,1024]{1,0:T(8,128)}, bf16[2048,1024]{1,0:T(8,128)(2,1)}) custom-call(bf16[1280,1024]{1,0:T(8,128)(2,1)} %get-tuple-element.84.ret_ref, bf16[1280,1024]{1,0:T(8,128)(2,1)} %get-tuple-element.85.back_ref, ...), custom_call_target="tpu_custom_call" | custom-call | flops 41943040 | bytes 209715200 | tf_op jit(solution)/shard_map/pallas_call | solution.py:565
  505.4 39.1 %shard_map.219 = (bf16[256,2048]{1,0:T(8,128)(2,1)}, bf16[256,2048]{1,0:T(8,128)(2,1)}, bf16[256,2048]{1,0:T(8,128)(2,1)}, f32[8,3,256,256]{3,2,1,0:T(8,128)}, f...) custom-call(bf16[768,2048]{1,0:T(8,128)(2,1)} %get-tuple-element.74.q_ref.k_ref.v_ref, ...), custom_call_target="tpu_custom_call" | custom-call | flops 10737418240 | bytes 33554432 | tf_op jit(solution)/shard_map/pallas_call | solution.py:334
  544.5 0.4 collective-permute-start.2
  545.0 1.6 collective-permute-start.1
  546.6 21.3 %shard_map.220 = (bf16[1024,1024]{1,0:T(8,128)(2,1)}, bf16[2048,1024]{1,0:T(8,128)(2,1)}, f32[1024,1]{1,0:T(8,128)}, f32[2,704,1024]{2,1,0:T(8,128)}, f32[2,704,1024]{2,1,0:T(8,128)}) custom-call(s32[2]{0:T(128)} %pad_add_fusion.place_ref, bf16[1024,2048]{1,0:T(8,128)(2,1)} %x_ref.5, f32[1024,1]{1,0:T(8,128)} %copy.30.gain_ref, ...), custom_call_target="tpu_custom_call" | custom-call | flops 8053063680 | bytes 22675456 | tf_op jit(solution)/shard_map/pallas_call | solution.py:420
  568.0 0.0 all-reduce.2.cloned.1.call-update
  568.0 0.0 collective-permute-done.2.y_along
  568.0 0.0 copy-start
  568.0 0.0 collective-permute-done.1.y_across
  568.0 0.0 copy-start.1
  568.0 0.9 copy-done
  569.0 0.3 copy-done.1
  569.3 96.3 %shard_map.221 = (bf16[4,512,1024]{2,1,0:T(8,128)(2,1)}, bf16[4,512,1024]{2,1,0:T(8,128)(2,1)}, f32[56,1024]{1,0:T(8,128)}) custom-call(bf16[4,512,1024]{2,1,0:T(8,128)(2,1)} %bitcast.22, bf16[512,1024]{1,0:T(8,128)(2,1)} %get-tuple-element.108.x_ref, f32[1,2048]{1,0:T(1,128)} %get-tuple-element.73.scale_ref, f32[512,1024]{1,0:T(8,128)} %get-tuple-element.109.grad_ref, ...), custom_call_target="tpu_custom_call" | custom-call | flops 41943040 | bytes 209715200 | tf_op jit(solution)/shard_map/pallas_call | solution.py:565
  665.6 0.0 all-reduce.2.cloned.1.call-done.summed_ref
  665.6 15.7 %shard_map.222 = (bf16[1024,2048]{1,0:T(8,128)(2,1)}, f32[1024,2048]{1,0:T(8,128)}, f32[2,704,1024]{2,1,0:T(8,128)}, f32[768,1024]{1,0:T(8,128)}, f32[256,1024]{...) custom-call(s32[2]{0:T(128)} %pad_add_fusion.place_ref, ...), custom_call_target="tpu_custom_call" | custom-call | bytes 37355520 | tf_op jit(solution)/shard_map/pallas_call | solution.py:1088
  (1 shorter events, 0.0 us)
Async XLA Ops:
  7.2 4.6 copy-start.4
  7.2 5.3 copy-start.2
  7.2 658.4 %all-reduce.2.cloned.1.call-start = ((), (), s32[]{:S(2)}) async-start(), calls=%async_computation | async-start | bytes 4194304 | tf_op jit(solution)/shard_map/psum | solution.py:1197
  7.3 10.0 %copy-start.3 = (s32[2,2]{1,0:T(2,128)S(1)}, s32[2,2]{1,0:T(2,128)}, u32[]{:S(2)}) copy-start(s32[2,2]{1,0:T(2,128)} %param.24) | copy-start | bytes 52
  8.8 41.2 %collective-permute-start = (bf16[704,1024]{1,0:T(8,128)(2,1)S(1)}, bf16[704,1024]{1,0:T(8,128)(2,1)S(1)}, u32[]{:S(2)}, u32[]{:S(2)}) collective-permute-start(bf16[704,1024]{1,0:T(8,128)(2,1)S(1)} %dynamic-slice_bitcast_fusion), channel_id=1, source_target_pairs={{0,1},{1,0},{2,3},{3,2},{4,5},{5,4},{6,7},{7,6},{8,9},{9,8},{10,11... | collective-permute-start | bytes 4325384 | tf_op jit(solution)/shard_map/ppermute | solution.py:1140
  49.9 80.1 %copy-start.5 = (bf16[704,1024]{1,0:T(8,128)(2,1)}, bf16[704,1024]{1,0:T(8,128)(2,1)S(1)}, u32[]{:S(2)}) copy-start(bf16[704,1024]{1,0:T(8,128)(2,1)S(1)} %collective-permute-done.far_gate) | copy-start | bytes 4325380
  544.5 23.5 %collective-permute-start.2 = (bf16[512,1024]{1,0:T(8,128)(2,1)}, bf16[512,1024]{1,0:T(8,128)(2,1)S(1)}, u32[]{:S(2)}, u32[]{:S(2)}) collective-permute-start(bf16[512,1024]{1,0:T(8,128)(2,1)} %get-tuple-element.106.y_own), channel_id=1, source_target_pairs={{0,2},{1,3},{2,0},{3,1},{4,6},{5,7},{6,4},{7,5},{8,10},{9,11},{10,... | collective-permute-start | bytes 3145736 | tf_op jit(solution)/shard_map/ppermute | solution.py:1191
  545.0 23.0 %collective-permute-start.1 = (bf16[512,1024]{1,0:T(8,128)(2,1)}, bf16[512,1024]{1,0:T(8,128)(2,1)S(1)}, u32[]{:S(2)}, u32[]{:S(2)}) collective-permute-start(bf16[512,1024]{1,0:T(8,128)(2,1)} %get-tuple-element.106.y_own), channel_id=1, source_target_pairs={{0,1},{1,0},{2,3},{3,2},{4,5},{5,4},{6,7},{7,6},{8,9},{9,8},{10,11... | collective-permute-start | bytes 3145736 | tf_op jit(solution)/shard_map/ppermute | solution.py:1190
  568.0 1.0 copy-start
  568.0 1.3 copy-start.1
Sparse Core Ops, SparseCore 0:
  568.1 94.2 all-reduce.1

commit v7 on v6

--- a/solution.py
+++ b/solution.py
@@ -379,7 +379,7 @@
 
 
 def project_back_kernel(
-    place_ref, x_ref, gain_ref, scale_ref, w_ref, mixed_ref, attn_ref, dq_ref, dk_ref, dv_ref, *refs
+    place_ref, x_ref, gain_ref, gain_row_ref, scale_ref, w_ref, mixed_ref, attn_ref, dq_ref, dk_ref, dv_ref, *refs
 ):
     step = pl.program_id(0)
     own_refs, got_refs, (weight_ref, out_ref, gain_grad_ref), placed_refs, total = (
@@ -390,25 +390,24 @@
         placed_ref[1 - place_ref[0]] = got_ref[...].astype(F32)
     grads = jnp.concatenate([dq_ref[...], dk_ref[...], dv_ref[...]], axis=0)
     rows = grads.shape[0]
-    scaled = x_ref[...].astype(F32) * scale_ref[...]
+    normed = (x_ref[...].astype(F32) * scale_ref[...] * gain_ref[...]).astype(BF16)
 
     @pl.when(step == 0)
     def _():
         total[...] = jnp.zeros_like(total)
-        gain_grad_ref[...] = jnp.zeros_like(gain_grad_ref)
-
-    total[:rows] += mm(grads, (scaled * gain_ref[...]).astype(BF16), NT)
+
+    total[:rows] += mm(grads, normed, NT)
     total[rows:] += mm(mixed_ref[...], attn_ref[...])
-    back = mm(w_ref[...], grads, TN)
-    gain_grad_ref[...] += jnp.sum(back * scaled, axis=1, keepdims=True)
-    out_ref[...] = back.T.astype(BF16)
+    out_ref[...] = mm(grads, w_ref[...], TN).astype(BF16)
 
     @pl.when(step == pl.num_programs(0) - 1)
     def _():
         weight_ref[...] = total[...].astype(BF16)
-
-
-def project_back(place, x, gain, scale, weights, mixed, grad_attn, grads, owns, gots):
+        through = jnp.sum(total[:rows] * w_ref[...].astype(F32), axis=0, keepdims=True)
+        gain_grad_ref[...] = through / gain_row_ref[...]
+
+
+def project_back(place, x, gain, gain_row, scale, weights, mixed, grad_attn, grads, owns, gots):
     width, tokens = x.shape
     rows = weights.shape[0]
     heads_width = mixed.shape[0]
@@ -424,6 +423,7 @@
             pl.BlockSpec(memory_space=pltpu.SMEM),
             column(width),
             pl.BlockSpec((width, 1), lambda i: (0, 0)),
+            pl.BlockSpec((1, width), lambda i: (0, 0)),
             column(1),
             pl.BlockSpec((rows, width), lambda i: (0, 0)),
             column(heads_width),
@@ -434,22 +434,22 @@
         out_specs=[
             pl.BlockSpec((rows + heads_width, width), lambda i: (0, 0)),
             pl.BlockSpec((tile, width), lambda i: (i, 0)),
-            pl.BlockSpec((width, 1), lambda i: (0, 0)),
+            pl.BlockSpec((1, width), lambda i: (0, 0)),
         ]
         + [pl.BlockSpec((2, part, width), lambda i: (0, i, 0))] * 2,
         out_shape=[
             jax.ShapeDtypeStruct((rows + heads_width, width), BF16),
             jax.ShapeDtypeStruct((tokens, width), BF16),
-            jax.ShapeDtypeStruct((width, 1), F32),
+            jax.ShapeDtypeStruct((1, width), F32),
         ]
         + [jax.ShapeDtypeStruct((2, units, width), F32)] * 2,
         scratch_shapes=[pltpu.VMEM((rows + heads_width, width), F32)],
         compiler_params=params(),
         cost_estimate=cost(5 * width * tokens * rows, 6 * width * tokens + 14 * units * width),
-    )(place, x, gain, scale, weights, mixed, grad_attn, *grads, *owns, *gots)
-
-
-def exchange(math, rank, source, full, from_across, from_along, to_across, to_along, turn_across, turn_along, sends, recvs, ready=None, ready_full=None, side=None, peers=(), fill=None, start=None, cut=None):
+    )(place, x, gain, gain_row, scale, weights, mixed, grad_attn, *grads, *owns, *gots)
+
+
+def exchange(math, rank, source, full, from_across, from_along, to_across, to_along, turn_across, turn_along, sends, recvs, ready=None, ready_full=None, side=None, peers=(), fill=None, start=None, cut=None, later=None):
     pair_class, half_index = rank % 2, rank // 2
     across, along, corner = rank + 1 - 2 * pair_class, rank + 2 - 4 * half_index, 3 - rank
     mesh_ids = pl.DeviceIdType.MESH
@@ -459,11 +459,12 @@
     cut = cut or width // 2
     low, high = slice(0, cut), slice(cut, width)
     barrier = pltpu.get_barrier_semaphore()
-    for other in (across, along):
+    near = (across, along, corner) if later else (across, along)
+    for other in near:
         pl.semaphore_signal(barrier, inc=1, device_id={"tensor": other}, device_id_type=mesh_ids)
     for other in peers:
         pl.semaphore_signal(barrier, inc=1, device_id={"expert": other}, device_id_type=mesh_ids)
-    pl.semaphore_wait(barrier, 2 + len(peers))
+    pl.semaphore_wait(barrier, len(near) + len(peers))
 
     def remote(kind, chunk, origin, target, other):
         return pltpu.make_async_remote_copy(
@@ -530,6 +531,8 @@
 
     if fill:
         fill(rank)
+    if later:
+        later((across, along, corner))
     for chunk, span in enumerate(spans):
         if side:
             side(chunks + chunk)
@@ -550,10 +553,12 @@
     if ready is not None:
         for copy in extra:
             copy.wait()
+    if side and later:
+        side(2 * chunks)
     for pair in fourth:
         for copy in pair:
             copy.wait()
-    if side:
+    if side and not later:
         side(2 * chunks)
 
 
@@ -624,11 +629,14 @@
     ret_ref, back_ref, code_ref, codes_ref, gates_ref, routes_ref, dy_rows_ref, gate_ref, router_ref, h_ref,
     resid_ref, scale_ref, dy_ref, gain_ref, full, grad_ref, gain_grad_ref, router_grad_ref, y_ref, *rest,
 ):
-    source, scaled, logit_parts = rest[-3:]
+    source, scaled, logit_parts, logit_own, send, recv = rest[-6:]
     rank = lax.axis_index("tensor")
     rows = source.shape[1]
     slots, tokens = ret_ref.shape[0], code_ref.shape[1]
-    def start():
+    ranks = tokens // rows
+    copies = []
+
+    def later(others):
         found = [jnp.zeros((1, tokens), F32) for _ in range(TOP)]
         tile = slots // 4
         for begin in range(0, slots, tile):
@@ -647,12 +655,16 @@
             jnp.where(routes_ref[i : i + 1] == expert, gates_ref[i : i + 1] * (found[i] - mean), 0.0)
             for i in range(TOP)
         )
-        coarse = logit.astype(BF16)
-        fine = (logit - coarse.astype(F32)).astype(BF16)
-        for shard in range(tokens // rows):
-            span = slice(shard * rows, (shard + 1) * rows)
-            logit_parts[shard, :EXPERTS] = coarse[:, span]
-            logit_parts[shard, EXPERTS:] = fine[:, span]
+        for shard in range(ranks):
+            logit_parts[shard] = logit[:, shard * rows : (shard + 1) * rows]
+        for number, other in enumerate(others):
+            copies.append(
+                pltpu.make_async_remote_copy(
+                    src_ref=logit_parts.at[other], dst_ref=logit_parts.at[ranks + number], send_sem=send.at[number],
+                    recv_sem=recv.at[number], device_id={"tensor": other}, device_id_type=pl.DeviceIdType.MESH,
+                )
+            )
+            copies[-1].start()
 
     def places(shard):
         slot = lax.broadcasted_iota(jnp.int32, (rows, slots), 1)
@@ -660,45 +672,51 @@
         return jnp.where((slot == codes[:, 0:1]) | (slot == codes[:, 1:2]), 1.0, 0.0).astype(BF16)
 
     def fill(shard):
-        value = mm(places(shard), back_ref[...])
-        both = jnp.concatenate([router_ref[...], router_ref[...]], axis=0)
-        source[shard] = (value + mm(logit_parts[shard], both, TN)).astype(BF16)
+        source[shard] = mm(places(shard), back_ref[...]).astype(BF16)
 
     def side(number):
-        shards = tokens // rows
-        if number < shards:
-            y_ref[number * rows : (number + 1) * rows, :] = mm(places(number), scaled[...]).astype(BF16)
-        elif number == shards:
+        if number == ranks:
             router_grad_ref[...] = sum(
-                mm(logit_parts[shard, :EXPERTS], h_ref[shard * rows : (shard + 1) * rows, :])
-                for shard in range(shards)
+                mm(logit_parts[shard].astype(BF16), h_ref[shard * rows : (shard + 1) * rows, :])
+                for shard in range(ranks)
             )
+            for copy in copies:
+                copy.wait()
+            logit = logit_parts[rank] + logit_parts[ranks] + logit_parts[ranks + 1] + logit_parts[ranks + 2]
+            coarse = logit.astype(BF16)
+            logit_own[:EXPERTS] = coarse
+            logit_own[EXPERTS:] = (logit - coarse.astype(F32)).astype(BF16)
+        elif number > ranks:
+            shard = number - ranks - 1
+            y_ref[shard * rows : (shard + 1) * rows, :] = mm(places(shard), scaled[...]).astype(BF16)
 
     gain_grad_ref[...] = jnp.zeros_like(gain_grad_ref)
 
     def math(span, total):
         resid, scale = resid_ref[span, :], scale_ref[span, :]
+        both = jnp.concatenate([router_ref[...], router_ref[...]], axis=0)
+        total = total + mm(logit_own[:, span], both, TN)
         gain_grad_ref[...] += jnp.sum(total * resid * scale, axis=0, keepdims=True)
         own_dy = dy_ref[pl.ds(pl.multiple_of(rank * rows + span.start, 128), span.stop - span.start), :]
         grad = norm_back(total, resid, scale, gain_ref[...]) + own_dy.astype(F32)
         grad_ref[span, :] = grad
         return grad
 
-    exchange(math, rank, source, full, *rest[:-3], side=side, fill=fill, start=start)
+    exchange(math, rank, source, full, *rest[:-6], side=side, fill=fill, later=later)
 
 
 def norm_one_back_kernel(
     source, x_ref, scale_ref, grad_ref, gain_ref, y_own, y_across, y_along, gain_one_ref, gain_two_ref, router_ref,
     near_ref, far_ref, full, ready_full, small_out, *rest,
 ):
-    held, near, scale, load, tensor_sends, tensor_recvs, expert_sends, expert_recvs = rest[-8:]
+    held, gathered, near, scale, load, tensor_sends, tensor_recvs, expert_sends, expert_recvs = rest[-9:]
     rank, group = lax.axis_index("tensor"), lax.axis_index("expert")
     pair_class, half_index = rank % 2, rank // 2
     others = rank + 1 - 2 * pair_class, rank + 2 - 4 * half_index
     groups = expert_sends.shape[0]
     mesh_ids = pl.DeviceIdType.MESH
     peers = [partner_of(group, step) for step in range(1, groups)]
-    summed = slice(0, small_out.shape[0] - BUCKETS)
+    heads = near_ref.shape[0] // 2
     rows = source.shape[1]
     loading = pltpu.make_async_copy(near_ref, near, load.at[0])
 
@@ -708,22 +726,22 @@
 
     def to_rank(step):
         return pltpu.make_async_remote_copy(
-            src_ref=held.at[groups + step], dst_ref=held.at[groups + 2 + step], send_sem=tensor_sends.at[step],
+            src_ref=held.at[step], dst_ref=held.at[2 + step], send_sem=tensor_sends.at[step],
             recv_sem=tensor_recvs.at[step], device_id={"tensor": others[step]}, device_id_type=mesh_ids,
         )
 
     def to_group(step):
         return pltpu.make_async_remote_copy(
-            src_ref=held.at[group], dst_ref=held.at[group], send_sem=expert_sends.at[step],
+            src_ref=gathered.at[group], dst_ref=gathered.at[group], send_sem=expert_sends.at[step],
             recv_sem=expert_recvs.at[step], device_id={"expert": peers[step - 1]}, device_id_type=mesh_ids,
         )
 
     def start():
         loading.start()
-        held[groups] = jnp.zeros(small_out.shape, F32)
-        held[groups, :EXPERTS] = router_ref[...]
-        held[groups, EXPERTS : EXPERTS + 1] = gain_two_ref[...]
-        held[groups, EXPERTS + 1 : EXPERTS + 2] = jnp.broadcast_to(gain_one_ref[...], (gain_one_ref.shape[0], 128)).T[:1]
+        held[0] = jnp.zeros(small_out.shape, F32)
+        held[0, :EXPERTS] = router_ref[...]
+        held[0, EXPERTS : EXPERTS + 1] = gain_two_ref[...]
+        held[0, EXPERTS + 1 : EXPERTS + 2] = gain_one_ref[...]
         to_rank(0).start()
 
     def side(number):
@@ -731,27 +749,29 @@
             own_scale = scale_ref[:, pl.ds(pl.multiple_of(rank * rows, rows), rows)]
             scale[...] = jnp.broadcast_to(own_scale, (8, rows)).T[:, :1]
             loading.wait()
-            held[group] = jnp.zeros(small_out.shape, F32)
-            held[group, summed.stop :, :128] = bias_fold(near, far_ref)
+            small_out[:BUCKETS, :128] = bias_fold(near, far_ref)
         elif number == 1:
             to_rank(0).wait()
-            held[groups + 1] = held[groups] + held[groups + 2]
+            held[1] = held[0] + held[2]
             to_rank(1).start()
         elif number == 5:
             to_rank(1).wait()
-            held[group, summed] = held[groups + 1, summed] + held[groups + 3, summed]
+            turned = small_out[:BUCKETS, :128].T
+            held[0] = held[1] + held[3]
+            held[0, EXPERTS + 2 : EXPERTS + 2 + heads, :BUCKETS] = turned[:heads]
+            gathered[group] = held[0].astype(BF16)
             for step in range(1, groups):
                 to_group(step).start()
         elif number == 8:
             for step in range(1, groups):
                 to_group(step).wait()
-            total = held[0]
+            total = gathered[0].astype(F32)
             for step in range(1, groups):
-                total = total + held[step]
+                total = total + gathered[step].astype(F32)
             small_out[...] = total
 
     exchange(
-        math, rank, source, full, *rest[:-8], (y_own, y_across, y_along), ready_full, side=side, peers=peers, start=start
+        math, rank, source, full, *rest[:-9], (y_own, y_across, y_along), ready_full, side=side, peers=peers, start=start
     )
 
 
@@ -1073,7 +1093,7 @@
         router_ref[...] = small_ref[:EXPERTS]
         two_ref[...] = small_ref[EXPERTS : EXPERTS + 1]
         one_ref[...] = small_ref[EXPERTS + 1 : EXPERTS + 2]
-        bias_ref[...] = small_ref[EXPERTS + 8 :, :128].T[: bias_ref.shape[0]]
+        bias_ref[...] = small_ref[EXPERTS + 2 : EXPERTS + 2 + bias_ref.shape[0], :BUCKETS]
 
 
 def finish_outputs(place, rows, y_rows, own, got, summed, small, heads):
@@ -1179,8 +1199,10 @@
         [
             pltpu.VMEM((ranks, share, width), BF16),
             pltpu.VMEM((slots, width), BF16),
-            pltpu.VMEM((ranks, 2 * EXPERTS, share), BF16),
-        ],
+            pltpu.VMEM((ranks + 3, EXPERTS, share), F32),
+            pltpu.VMEM((2 * EXPERTS, share), BF16),
+        ]
+        + [pltpu.SemaphoreType.DMA((3,))] * 2,
     )
 
     dq, dk, dv, near, far, y_own = attend_back(
@@ -1190,18 +1212,18 @@
     y_across = lax.ppermute(y_own, "tensor", [(r, r ^ 1) for r in range(ranks)])
     y_along = lax.ppermute(y_own, "tensor", [(r, r ^ 2) for r in range(ranks)])
     weight_rows, sent, grad_gain_one, grad_gate, grad_up = project_back(
-        place, layer_input, gain_col, scale_one, w_in, mixed, grad_attn, (dq, dk, dv),
+        place, layer_input, gain_col, gain_one[None], scale_one, w_in, mixed, grad_attn, (dq, dk, dv),
         weight_grads[:2], weight_grads[3:5],
     )
     sent, y_across, y_along = lax.optimization_barrier((sent, y_across, y_along))
     summed = lax.psum(weight_rows, "expert")
-    small_shape = (EXPERTS + 8 + BUCKETS, width)
+    small_shape = (BUCKETS, width)
     grad_rows, y_full, small = exchange_call(
         norm_one_back_kernel, 4, sent.shape,
         [by_rank(sent), own_x, scale_one, grad_resid, gain_one[None], y_own, y_across, y_along]
         + [grad_gain_one, grad_gain_two, grad_router, near, far],
         [((ranks, share, width), BF16), (small_shape, F32)],
-        [pltpu.VMEM((groups + 4, *small_shape), F32), pltpu.VMEM(near.shape, F32), pltpu.VMEM((share, 1), F32)]
+        [pltpu.VMEM((4, *small_shape), F32), pltpu.VMEM((groups, *small_shape), BF16), pltpu.VMEM(near.shape, F32), pltpu.VMEM((share, 1), F32)]
         + [pltpu.SemaphoreType.DMA((1,))]
         + [pltpu.SemaphoreType.DMA((2,))] * 2
         + [pltpu.SemaphoreType.DMA((groups,))] * 2,

time: 702 us -> 694 us (0.989)
  transfers between devices with their start and end apart: 4 -> 4, of which waited for: 0 -> 1; matrix products, arithmetic and copies ran while one was open for 0% -> 0% of each run, Pallas kernels for 22% -> 22%
where the time goes in v7:
time: 694 us; the launch traced here: 684 us
  Pallas kernels  658 us (95%)
  between operations  14.6 us (2%)
    pallas_call x1, Pallas kernels, run_experts(): pl.pallas_call(expert_kernel, in_specs=[anywhere] * 6, out_specs=[anywher...  277 us
    pallas_call x3, Pallas kernels, exchange_call(): pl.pallas_call(kernel, in_specs=[pl.BlockSpec(memory_space=pl.ANY) if k i...  262 us
    pallas_call x1, Pallas kernels, attend_back(): pl.pallas_call(attend_back_kernel, grid=(seqs, heads), in_specs=[pl.Block...  36.6 us
    pallas_call x1, Pallas kernels, attend(): pl.pallas_call(attend_kernel, grid=(seqs, heads), in_specs=[pl.BlockSpec(...  23.6 us
    pallas_call x1, Pallas kernels, project_back(): pl.pallas_call(project_back_kernel, grid=(steps,), in_specs=[pl.BlockSpec...  20.4 us
    pallas_call x1, Pallas kernels, finish_outputs(): pl.pallas_call(finish_kernel, grid=(steps,), in_specs=[pl.BlockSpec(memor...  15.7 us
  transfers between devices with their start and end apart: 4, of which 1 were waited for; matrix products, arithmetic and copies ran while one was open for 0% of the time, Pallas kernels for 22%

profile of v7, /device:TPU:0, one launch (start us, length us, event | category | flops | bytes accessed | tf_op | source)
XLA Modules:
  0.0 684.2 jit_solution(10878461753772942198)
XLA Ops:
  7.2 0.0 copy-start.4
  7.2 0.0 copy-start.2
  7.2 0.0 all-reduce.2.cloned.1.call-start
  7.3 0.0 copy-start.3
  7.3 1.5 dynamic-slice_bitcast_fusion
  8.8 3.0 collective-permute-start
  11.8 0.0 copy-done.4
  11.8 0.7 copy.29.table_ref
  12.4 0.0 copy-done.2
  12.5 1.0 copy.30.gain_ref
  13.5 3.2 shard_map.213.tiles_ref
  16.7 0.6 pad_add_fusion.place_ref
  17.3 0.0 copy-done.3
  17.3 0.1 fusion
  17.4 0.6 iota_maximum_fusion.limit_ref
  18.0 8.3 %shard_map.212 = (bf16[768,2048]{1,0:T(8,128)(2,1)}, f32[1,2048]{1,0:T(1,128)}) custom-call(bf16[1024,2048]{1,0:T(8,128)(2,1)} %x_ref.5, f32[1024,1]{1,0:T(8,128)} %copy.30.gain_ref, bf16[768,1024]{1,0:T(8,128)(2,1)} %bitcast.42), custom_call_target="tpu_custom_call" | custom-call | flops 3221225472 | bytes 8388608 | tf_op jit(solution)/shard_map/pallas_call | solution.py:64
  26.3 23.6 %shard_map.214 = (bf16[256,2048]{1,0:T(8,128)(2,1)}, f32[8,1,1024]{2,1,0:T(1,128)}, bf16[2048,1024]{1,0:T(8,128)(2,1)}) custom-call(bf16[768,2048]{1,0:T(8,128)(2,1)} %get-tuple-element.74.q_ref.k_ref.v_ref, bf16[768,2048]{1,0:T(8,128)(2,1)} %get-tuple-element.74.q_ref.k_ref.v_ref, bf16[768,2048]{1,0:T(8,128)(2,1)} %get-tuple-element.74.q_ref.k_ref.v_ref, ...), custom_call_target="tpu_custom_call" | custom-call | flops 4294967296 | bytes 16777216 | tf_op jit(solution)/shard_map/pallas_call | solution.py:197
  49.9 0.0 collective-permute-done.far_gate
  49.9 0.0 copy-start.5
  50.0 80.1 %shard_map.215 = (bf16[4,512,1024]{2,1,0:T(8,128)(2,1)}, f32[512,1024]{1,0:T(8,128)}, f32[512,1]{1,0:T(8,128)}, bf16[2048,1024]{1,0:T(8,128)(2,1)}, bf16[1280,10...) custom-call(bf16[4,512,1024]{2,1,0:T(8,128)(2,1)} %bitcast.26, ...), custom_call_target="tpu_custom_call" | custom-call | flops 41943040 | bytes 209715200 | tf_op jit(solution)/shard_map/pallas_call | solution.py:570
  130.1 0.0 copy-done.5
  130.1 11.9 %shard_map.216 = (bf16[1280,1024]{1,0:T(8,128)(2,1)}, bf16[1280,1024]{1,0:T(8,128)(2,1)}, f32[1280,1]{1,0:T(8,128)}, f32[2,2048]{1,0:T(2,128)}) custom-call(s32[2,2048]{1,0:T(2,128)} %get-tuple-element.78.code_ref, s32[2,2048]{1,0:T(2,128)} %bitcast.29, bf16[16,1024]{1,0:T(8,128)(2,1)} %bitcast.31, bf16[2048,1024]{1,0:T(8,128)(2,1)} %bitcast.24, ...), custom_call_target="tpu_custom_call" | custom-call | flops 5368709120 | bytes 12058624 | tf_op jit(solution)/shard_map/pallas_call | solution.py:833
  141.9 277.2 %shard_map.217 = (bf16[1280,1024]{1,0:T(8,128)(2,1)}, bf16[1280,1024]{1,0:T(8,128)(2,1)}, f32[704,1024]{1,0:T(8,128)}, f32[704,1024]{1,0:T(8,128)}, f32[704,1024...) custom-call(bf16[1280,1024]{1,0:T(8,128)(2,1)} %get-tuple-element.81.rows_in, ...), custom_call_target="tpu_custom_call" | custom-call | flops 66437775360 | bytes 42598400 | tf_op jit(solution)/shard_map/pallas_call | solution.py:1051
  419.2 86.3 %shard_map.218 = (bf16[4,512,1024]{2,1,0:T(8,128)(2,1)}, f32[512,1024]{1,0:T(8,128)}, f32[1,1024]{1,0:T(1,128)}, f32[16,1024]{1,0:T(8,128)}, bf16[2048,1024]{1,0:T(8,128)(2,1)}) custom-call(bf16[1280,1024]{1,0:T(8,128)(2,1)} %get-tuple-element.84.ret_ref, bf16[1280,1024]{1,0:T(8,128)(2,1)} %get-tuple-element.85.back_ref, ...), custom_call_target="tpu_custom_call" | custom-call | flops 41943040 | bytes 209715200 | tf_op jit(solution)/shard_map/pallas_call | solution.py:570
  505.4 36.6 %shard_map.219 = (bf16[256,2048]{1,0:T(8,128)(2,1)}, bf16[256,2048]{1,0:T(8,128)(2,1)}, bf16[256,2048]{1,0:T(8,128)(2,1)}, f32[8,3,256,256]{3,2,1,0:T(8,128)}, f...) custom-call(bf16[768,2048]{1,0:T(8,128)(2,1)} %get-tuple-element.74.q_ref.k_ref.v_ref, ...), custom_call_target="tpu_custom_call" | custom-call | flops 10737418240 | bytes 33554432 | tf_op jit(solution)/shard_map/pallas_call | solution.py:334
  542.0 1.5 collective-permute-start.2
  543.6 0.6 collective-permute-start.1
  544.1 20.4 %shard_map.220 = (bf16[1024,1024]{1,0:T(8,128)(2,1)}, bf16[2048,1024]{1,0:T(8,128)(2,1)}, f32[1,1024]{1,0:T(1,128)}, f32[2,704,1024]{2,1,0:T(8,128)}, f32[2,704,1024]{2,1,0:T(8,128)}) custom-call(s32[2]{0:T(128)} %pad_add_fusion.place_ref, bf16[1024,2048]{1,0:T(8,128)(2,1)} %x_ref.5, f32[1024,1]{1,0:T(8,128)} %copy.30.gain_ref, f32[1,1024]{1,0:T(1,128)} %bitcast.35, ...), custom_call_target="tpu_custom_call" | custom-call | flops 8053063680 | bytes 22675456 | tf_op jit(solution)/shard_map/pallas_call | solution.py:419
  564.6 0.0 all-reduce.2.cloned.1.call-update
  564.6 0.0 collective-permute-done.2.y_along
  564.6 0.0 copy-start
  564.6 0.5 collective-permute-done.1.y_across
  565.1 0.0 copy-start.1
  565.1 0.5 copy-done
  565.6 0.5 copy-done.1
  566.1 95.2 %shard_map.221 = (bf16[4,512,1024]{2,1,0:T(8,128)(2,1)}, bf16[4,512,1024]{2,1,0:T(8,128)(2,1)}, f32[32,1024]{1,0:T(8,128)}) custom-call(bf16[4,512,1024]{2,1,0:T(8,128)(2,1)} %bitcast.27, bf16[512,1024]{1,0:T(8,128)(2,1)} %get-tuple-element.108.x_ref, f32[1,2048]{1,0:T(1,128)} %get-tuple-element.73.scale_ref, f32[512,1024]{1,0:T(8,128)} %get-tuple-element.109.grad_ref, ...), custom_call_target="tpu_custom_call" | custom-call | flops 41943040 | bytes 209715200 | tf_op jit(solution)/shard_map/pallas_call | solution.py:570
  661.3 0.0 all-reduce.2.cloned.1.call-done.summed_ref
  661.3 15.7 %shard_map.222 = (bf16[1024,2048]{1,0:T(8,128)(2,1)}, f32[1024,2048]{1,0:T(8,128)}, f32[2,704,1024]{2,1,0:T(8,128)}, f32[768,1024]{1,0:T(8,128)}, f32[256,1024]{...) custom-call(s32[2]{0:T(128)} %pad_add_fusion.place_ref, ...), custom_call_target="tpu_custom_call" | custom-call | bytes 37355520 | tf_op jit(solution)/shard_map/pallas_call | solution.py:1108
  (1 shorter events, 0.0 us)
Async XLA Ops:
  7.2 4.6 copy-start.4
  7.2 5.3 copy-start.2
  7.2 654.1 %all-reduce.2.cloned.1.call-start = ((), (), s32[]{:S(2)}) async-start(), calls=%async_computation | async-start | bytes 4194304 | tf_op jit(solution)/shard_map/psum | solution.py:1219
  7.3 10.0 %copy-start.3 = (s32[2,2]{1,0:T(2,128)S(1)}, s32[2,2]{1,0:T(2,128)}, u32[]{:S(2)}) copy-start(s32[2,2]{1,0:T(2,128)} %param.24) | copy-start | bytes 52
  8.8 41.2 %collective-permute-start = (bf16[704,1024]{1,0:T(8,128)(2,1)S(1)}, bf16[704,1024]{1,0:T(8,128)(2,1)S(1)}, u32[]{:S(2)}, u32[]{:S(2)}) collective-permute-start(bf16[704,1024]{1,0:T(8,128)(2,1)S(1)} %dynamic-slice_bitcast_fusion), channel_id=1, source_target_pairs={{0,1},{1,0},{2,3},{3,2},{4,5},{5,4},{6,7},{7,6},{8,9},{9,8},{10,11... | collective-permute-start | bytes 4325384 | tf_op jit(solution)/shard_map/ppermute | solution.py:1160
  49.9 80.1 %copy-start.5 = (bf16[704,1024]{1,0:T(8,128)(2,1)}, bf16[704,1024]{1,0:T(8,128)(2,1)S(1)}, u32[]{:S(2)}) copy-start(bf16[704,1024]{1,0:T(8,128)(2,1)S(1)} %collective-permute-done.far_gate) | copy-start | bytes 4325380
  542.0 22.6 %collective-permute-start.2 = (bf16[512,1024]{1,0:T(8,128)(2,1)}, bf16[512,1024]{1,0:T(8,128)(2,1)S(1)}, u32[]{:S(2)}, u32[]{:S(2)}) collective-permute-start(bf16[512,1024]{1,0:T(8,128)(2,1)} %get-tuple-element.106.y_own), channel_id=1, source_target_pairs={{0,2},{1,3},{2,0},{3,1},{4,6},{5,7},{6,4},{7,5},{8,10},{9,11},{10,... | collective-permute-start | bytes 3145736 | tf_op jit(solution)/shard_map/ppermute | solution.py:1213
  543.6 21.5 %collective-permute-start.1 = (bf16[512,1024]{1,0:T(8,128)(2,1)}, bf16[512,1024]{1,0:T(8,128)(2,1)S(1)}, u32[]{:S(2)}, u32[]{:S(2)}) collective-permute-start(bf16[512,1024]{1,0:T(8,128)(2,1)} %get-tuple-element.106.y_own), channel_id=1, source_target_pairs={{0,1},{1,0},{2,3},{3,2},{4,5},{5,4},{6,7},{7,6},{8,9},{9,8},{10,11... | collective-permute-start | bytes 3145736 | tf_op jit(solution)/shard_map/ppermute | solution.py:1212
  564.6 1.0 copy-start
  565.1 1.0 copy-start.1
Sparse Core Ops, SparseCore 0:
  564.7 74.4 all-reduce.1

commit v8 on v7

--- a/solution.py
+++ b/solution.py
@@ -449,7 +449,8 @@
     )(place, x, gain, gain_row, scale, weights, mixed, grad_attn, *grads, *owns, *gots)
 
 
-def exchange(math, rank, source, full, from_across, from_along, to_across, to_along, turn_across, turn_along, sends, recvs, ready=None, ready_full=None, side=None, peers=(), fill=None, start=None, cut=None, later=None):
+def exchange(
+    math, rank, source, full_out, full, from_across, from_along, to_across, to_along, turn_across, turn_along, sends, recvs, outs, ready=None, ready_full=None, side=None, peers=(), fill=None, start=None, cut=None, later=None):
     pair_class, half_index = rank % 2, rank // 2
     across, along, corner = rank + 1 - 2 * pair_class, rank + 2 - 4 * half_index, 3 - rank
     mesh_ids = pl.DeviceIdType.MESH
@@ -489,11 +490,21 @@
     if fill:
         fill(along)
         fill(across)
+    leaving = []
+
+    def leave(number, other):
+        leaving.append(pltpu.make_async_copy(full.at[other], full_out.at[other], outs.at[number]))
+        leaving[-1].start()
+
     if ready is not None:
         _, near_across, near_along = ready
         extra = [
             remote(8, 0, near_along.at[:, low], ready_full.at[along, :, low], across),
             remote(8, 1, near_across.at[:, high], ready_full.at[across, :, high], along),
+        ]
+        extra += [
+            pltpu.make_async_copy(piece, ready_full.at[other], outs.at[4 + number])
+            for number, (other, piece) in enumerate(zip((rank, across, along), ready))
         ]
         for copy in extra:
             copy.start()
@@ -513,10 +524,6 @@
         for copy in pair:
             copy.start()
         second.append(pair)
-    if ready is not None:
-        for other, piece in zip((rank, across, along), ready):
-            ready_full[other] = piece[...]
-
     def pass_on(chunk):
         span = spans[chunk]
         for copy in third[chunk]:
@@ -549,7 +556,10 @@
         third.append(pair)
         if chunk:
             pass_on(chunk - 1)
+    leave(0, rank)
     pass_on(chunks - 1)
+    leave(1, across)
+    leave(2, along)
     if ready is not None:
         for copy in extra:
             copy.wait()
@@ -558,11 +568,14 @@
     for pair in fourth:
         for copy in pair:
             copy.wait()
+    leave(3, corner)
     if side and not later:
         side(2 * chunks)
-
-
-def exchange_call(kernel, number, shape, operands, extra_shapes, scratch=(), in_hbm=()):
+    for copy in leaving:
+        copy.wait()
+
+
+def exchange_call(kernel, number, shape, operands, extra_shapes, scratch=(), in_hbm=(), out_hbm=()):
     tokens, width = shape
     ranks = 4
     rows = tokens // ranks
@@ -570,11 +583,14 @@
     results = pl.pallas_call(
         kernel,
         in_specs=[pl.BlockSpec(memory_space=pl.ANY) if k in in_hbm else here for k in range(len(operands))],
-        out_specs=[here] * (1 + len(extra_shapes)),
+        out_specs=[pl.BlockSpec(memory_space=pl.ANY)]
+        + [pl.BlockSpec(memory_space=pl.ANY) if k in out_hbm else here for k in range(len(extra_shapes))],
         out_shape=[jax.ShapeDtypeStruct((ranks, rows, width), BF16)]
         + [jax.ShapeDtypeStruct(shape, kind) for shape, kind in extra_shapes],
-        scratch_shapes=[pltpu.VMEM((rows, width), BF16)] * 6
+        scratch_shapes=[pltpu.VMEM((ranks, rows, width), BF16)]
+        + [pltpu.VMEM((rows, width), BF16)] * 6
         + [pltpu.SemaphoreType.DMA((9, 4))] * 2
+        + [pltpu.SemaphoreType.DMA((7,))]
         + list(scratch),
         compiler_params=pltpu.CompilerParams(
             vmem_limit_bytes=60 * MIB, collective_id=number, has_side_effects=True
@@ -586,11 +602,21 @@
 
 def norm_two_kernel(
     source, x_ref, gain_ref, grad_out_ref, routes_ref,
-    full, resid_ref, scale_ref, dy_ref, dy_rows_ref, code_ref, codes_ref, own_ref, *rest,
+    full, resid_ref, scale_ref, dy_out, dy_rows_out, code_ref, codes_ref, own_ref, *rest,
 ):
-    held, load = rest[-2:]
+    held, grad_out, dy_ref, dy_rows_ref, load = rest[-5:]
     rank = lax.axis_index("tensor")
     ranks, rows, width = source.shape
+    loading = pltpu.make_async_copy(grad_out_ref, grad_out, load.at[1])
+    storing = [
+        pltpu.make_async_copy(dy_ref, dy_out, load.at[2]),
+        pltpu.make_async_copy(dy_rows_ref, dy_rows_out, load.at[3]),
+    ]
+
+    def start():
+        own.start()
+        loading.start()
+
     slots = dy_rows_ref.shape[0] // ranks
     own = pltpu.make_async_copy(x_ref.at[:, pl.ds(pl.multiple_of(rank * rows, rows), rows)], held, load.at[0])
 
@@ -607,16 +633,24 @@
             own_ref[...] = held[...].astype(F32).T.astype(BF16)
             local_codes(routes_ref, code_ref, rank % 2, rank // 2, CAP // 2)
             codes_ref[...] = jnp.concatenate([code_ref[...].astype(F32)] * 4, axis=0).T[:, :TOP].astype(jnp.int32)
+            loading.wait()
         if number < ranks:
             span = slice(number * rows, (number + 1) * rows)
-            dy_ref[span, :] = grad_out_ref[:, span].astype(F32).T.astype(BF16)
+            dy_ref[span, :] = grad_out[:, span].astype(F32).T.astype(BF16)
         elif number < 2 * ranks:
             start = (number - ranks) * slots
             slot = lax.broadcasted_iota(jnp.int32, (slots, dy_ref.shape[0]), 0) + start
             take = jnp.where((slot == code_ref[0:1]) | (slot == code_ref[1:2]), 1.0, 0.0).astype(BF16)
             dy_rows_ref[start : start + slots, :] = mm(take, dy_ref[...]).astype(BF16)
-
-    exchange(math, rank, source, full, *rest[:-2], side=side, start=own.start)
+        if number == ranks - 1:
+            storing[0].start()
+        elif number == 2 * ranks - 1:
+            storing[1].start()
+        elif number == 2 * ranks:
+            for copy in storing:
+                copy.wait()
+
+    exchange(math, rank, source, full, *rest[:-5], side=side, start=start)
 
 
 def norm_back(grad, value, scale, gain):
@@ -626,17 +660,30 @@
 
 
 def norm_two_back_kernel(
-    ret_ref, back_ref, code_ref, codes_ref, gates_ref, routes_ref, dy_rows_ref, gate_ref, router_ref, h_ref,
-    resid_ref, scale_ref, dy_ref, gain_ref, full, grad_ref, gain_grad_ref, router_grad_ref, y_ref, *rest,
+    ret_in, back_ref, code_ref, codes_ref, gates_ref, routes_ref, dy_rows_in, gate_ref, router_ref, h_in,
+    resid_in, scale_ref, dy_in, gain_ref, full, grad_ref, gain_grad_ref, router_grad_ref, y_out, *rest,
 ):
-    source, scaled, logit_parts, logit_own, send, recv = rest[-6:]
+    source, scaled, logit_parts, logit_own, send, recv, ret_ref, dy_rows_ref, h_ref, resid_ref, dy_ref, y_ref, load = rest[-13:]
     rank = lax.axis_index("tensor")
     rows = source.shape[1]
     slots, tokens = ret_ref.shape[0], code_ref.shape[1]
     ranks = tokens // rows
     copies = []
+    own_dy = dy_in.at[pl.ds(pl.multiple_of(rank * rows, rows), rows)]
+    pairs = ((ret_in, ret_ref), (dy_rows_in, dy_rows_ref), (resid_in, resid_ref), (own_dy, dy_ref), (h_in, h_ref))
+    loading = [pltpu.make_async_copy(*pair, load.at[number]) for number, pair in enumerate(pairs)]
+    storing = [
+        pltpu.make_async_copy(y_ref.at[shard], y_out.at[pl.ds(shard * rows, rows)], load.at[5 + shard])
+        for shard in range(ranks)
+    ]
+
+    def start():
+        for copy in loading:
+            copy.start()
 
     def later(others):
+        for copy in loading:
+            copy.wait()
         found = [jnp.zeros((1, tokens), F32) for _ in range(TOP)]
         tile = slots // 4
         for begin in range(0, slots, tile):
@@ -688,7 +735,11 @@
             logit_own[EXPERTS:] = (logit - coarse.astype(F32)).astype(BF16)
         elif number > ranks:
             shard = number - ranks - 1
-            y_ref[shard * rows : (shard + 1) * rows, :] = mm(places(shard), scaled[...]).astype(BF16)
+            y_ref[shard] = mm(places(shard), scaled[...]).astype(BF16)
+            storing[shard].start()
+            if shard == ranks - 1:
+                for copy in storing:
+                    copy.wait()
 
     gain_grad_ref[...] = jnp.zeros_like(gain_grad_ref)
 
@@ -697,19 +748,18 @@
         both = jnp.concatenate([router_ref[...], router_ref[...]], axis=0)
         total = total + mm(logit_own[:, span], both, TN)
         gain_grad_ref[...] += jnp.sum(total * resid * scale, axis=0, keepdims=True)
-        own_dy = dy_ref[pl.ds(pl.multiple_of(rank * rows + span.start, 128), span.stop - span.start), :]
-        grad = norm_back(total, resid, scale, gain_ref[...]) + own_dy.astype(F32)
+        grad = norm_back(total, resid, scale, gain_ref[...]) + dy_ref[span, :].astype(F32)
         grad_ref[span, :] = grad
         return grad
 
-    exchange(math, rank, source, full, *rest[:-6], side=side, fill=fill, later=later)
+    exchange(math, rank, source, full, *rest[:-13], side=side, fill=fill, start=start, later=later)
 
 
 def norm_one_back_kernel(
-    source, x_ref, scale_ref, grad_ref, gain_ref, y_own, y_across, y_along, gain_one_ref, gain_two_ref, router_ref,
+    source, x_in, scale_ref, grad_in, gain_ref, y_own, y_across, y_along, gain_one_ref, gain_two_ref, router_ref,
     near_ref, far_ref, full, ready_full, small_out, *rest,
 ):
-    held, gathered, near, scale, load, tensor_sends, tensor_recvs, expert_sends, expert_recvs = rest[-9:]
+    x_ref, grad_ref, held, gathered, near, scale, load, tensor_sends, tensor_recvs, expert_sends, expert_recvs = rest[-11:]
     rank, group = lax.axis_index("tensor"), lax.axis_index("expert")
     pair_class, half_index = rank % 2, rank // 2
     others = rank + 1 - 2 * pair_class, rank + 2 - 4 * half_index
@@ -718,7 +768,8 @@
     peers = [partner_of(group, step) for step in range(1, groups)]
     heads = near_ref.shape[0] // 2
     rows = source.shape[1]
-    loading = pltpu.make_async_copy(near_ref, near, load.at[0])
+    pairs = ((near_ref, near), (x_in, x_ref), (grad_in, grad_ref))
+    loading = [pltpu.make_async_copy(*pair, load.at[number]) for number, pair in enumerate(pairs)]
 
     def math(span, total):
         x = x_ref[span, :].astype(F32)
@@ -737,7 +788,8 @@
         )
 
     def start():
-        loading.start()
+        for copy in loading:
+            copy.start()
         held[0] = jnp.zeros(small_out.shape, F32)
         held[0, :EXPERTS] = router_ref[...]
         held[0, EXPERTS : EXPERTS + 1] = gain_two_ref[...]
@@ -748,7 +800,8 @@
         if number == 0:
             own_scale = scale_ref[:, pl.ds(pl.multiple_of(rank * rows, rows), rows)]
             scale[...] = jnp.broadcast_to(own_scale, (8, rows)).T[:, :1]
-            loading.wait()
+            for copy in loading:
+                copy.wait()
             small_out[:BUCKETS, :128] = bias_fold(near, far_ref)
         elif number == 1:
             to_rank(0).wait()
@@ -771,7 +824,7 @@
             small_out[...] = total
 
     exchange(
-        math, rank, source, full, *rest[:-9], (y_own, y_across, y_along), ready_full, side=side, peers=peers, start=start
+        math, rank, source, full, *rest[:-11], (y_own, y_across, y_along), ready_full, side=side, peers=peers, start=start
     )
 
 
@@ -1184,8 +1237,10 @@
         norm_two_kernel, 2, sent.shape, [by_rank(sent), layer_input, gain_two[None], grad_out, routes_t],
         [((share, width), F32), ((share, 1), F32), ((tokens, width), BF16), ((slots, width), BF16)]
         + [((TOP, tokens), jnp.int32), ((tokens, TOP), jnp.int32), ((share, width), BF16)],
-        [pltpu.VMEM((width, share), BF16), pltpu.SemaphoreType.DMA((1,))],
-        (1,),
+        [pltpu.VMEM((width, share), BF16), pltpu.VMEM((width, tokens), BF16), pltpu.VMEM((tokens, width), BF16)]
+        + [pltpu.VMEM((slots, width), BF16), pltpu.SemaphoreType.DMA((4,))],
+        (1, 3),
+        (2, 3),
     )
     rows, row_grads, gate_rows, gates = dispatch(code, routes_t, router.T, h2, dy_rows)
     ret, back, *weight_grads = run_experts(
@@ -1202,7 +1257,12 @@
             pltpu.VMEM((ranks + 3, EXPERTS, share), F32),
             pltpu.VMEM((2 * EXPERTS, share), BF16),
         ]
-        + [pltpu.SemaphoreType.DMA((3,))] * 2,
+        + [pltpu.SemaphoreType.DMA((3,))] * 2
+        + [pltpu.VMEM((slots, width), BF16)] * 2
+        + [pltpu.VMEM((tokens, width), BF16), pltpu.VMEM((share, width), F32), pltpu.VMEM((share, width), BF16)]
+        + [pltpu.VMEM((ranks, share, width), BF16), pltpu.SemaphoreType.DMA((9,))],
+        (0, 6, 9, 10, 12),
+        (3,),
     )
 
     dq, dk, dv, near, far, y_own = attend_back(
@@ -1223,11 +1283,13 @@
         [by_rank(sent), own_x, scale_one, grad_resid, gain_one[None], y_own, y_across, y_along]
         + [grad_gain_one, grad_gain_two, grad_router, near, far],
         [((ranks, share, width), BF16), (small_shape, F32)],
-        [pltpu.VMEM((4, *small_shape), F32), pltpu.VMEM((groups, *small_shape), BF16), pltpu.VMEM(near.shape, F32), pltpu.VMEM((share, 1), F32)]
-        + [pltpu.SemaphoreType.DMA((1,))]
+        [pltpu.VMEM((share, width), BF16), pltpu.VMEM((share, width), F32)]
+        + [pltpu.VMEM((4, *small_shape), F32), pltpu.VMEM((groups, *small_shape), BF16), pltpu.VMEM(near.shape, F32), pltpu.VMEM((share, 1), F32)]
+        + [pltpu.SemaphoreType.DMA((3,))]
         + [pltpu.SemaphoreType.DMA((2,))] * 2
         + [pltpu.SemaphoreType.DMA((groups,))] * 2,
-        (11,),
+        (1, 3, 5, 6, 7, 11),
+        (0,),
     )
     summed, grad_rows = lax.optimization_barrier((summed, grad_rows))
     layer_output, grad_input, grad_down, grad_in, grad_attn_out, grad_one, grad_two, grad_router, grad_bias = finish_outputs(

time: 694 us -> 693 us (level)
  transfers between devices with their start and end apart: 4 -> 4, of which waited for: 1 -> 1; matrix products, arithmetic and copies ran while one was open for 0% -> 0% of each run, Pallas kernels for 22% -> 23%
where the time goes in v8:
time: 693 us; the launch traced here: 684 us
  Pallas kernels  658 us (95%)
  between operations  14.6 us (2%)
    pallas_call x1, Pallas kernels, run_experts(): pl.pallas_call(expert_kernel, in_specs=[anywhere] * 6, out_specs=[anywher...  277 us
    pallas_call x3, Pallas kernels, exchange_call(): pl.pallas_call(kernel, in_specs=[pl.BlockSpec(memory_space=pl.ANY) if k i...  261 us
    pallas_call x1, Pallas kernels, attend_back(): pl.pallas_call(attend_back_kernel, grid=(seqs, heads), in_specs=[pl.Block...  36.6 us
    pallas_call x1, Pallas kernels, attend(): pl.pallas_call(attend_kernel, grid=(seqs, heads), in_specs=[pl.BlockSpec(...  23.6 us
    pallas_call x1, Pallas kernels, project_back(): pl.pallas_call(project_back_kernel, grid=(steps,), in_specs=[pl.BlockSpec...  20.4 us
    pallas_call x1, Pallas kernels, finish_outputs(): pl.pallas_call(finish_kernel, grid=(steps,), in_specs=[pl.BlockSpec(memor...  15.7 us
  transfers between devices with their start and end apart: 4, of which 1 were waited for; matrix products, arithmetic and copies ran while one was open for 0% of the time, Pallas kernels for 23%

profile of v8, /device:TPU:0, one launch (start us, length us, event | category | flops | bytes accessed | tf_op | source)
XLA Modules:
  0.0 683.8 jit_solution(1932303606489924112)
XLA Ops:
  7.2 0.0 copy-start.4
  7.2 0.0 copy-start.2
  7.2 0.0 all-reduce.2.cloned.1.call-start
  7.3 0.0 copy-start.3
  7.3 1.5 dynamic-slice_bitcast_fusion
  8.8 3.0 collective-permute-start
  11.8 0.0 copy-done.4
  11.8 0.7 copy.29.table_ref
  12.4 0.0 copy-done.2
  12.5 1.0 copy.30.gain_ref
  13.5 3.2 shard_map.213.tiles_ref
  16.7 0.6 pad_add_fusion.place_ref
  17.3 0.0 copy-done.3
  17.3 0.1 fusion
  17.4 0.6 iota_maximum_fusion.limit_ref
  18.0 8.3 %shard_map.212 = (bf16[768,2048]{1,0:T(8,128)(2,1)}, f32[1,2048]{1,0:T(1,128)}) custom-call(bf16[1024,2048]{1,0:T(8,128)(2,1)} %x_ref.5, f32[1024,1]{1,0:T(8,128)} %copy.30.gain_ref, bf16[768,1024]{1,0:T(8,128)(2,1)} %bitcast.42), custom_call_target="tpu_custom_call" | custom-call | flops 3221225472 | bytes 8388608 | tf_op jit(solution)/shard_map/pallas_call | solution.py:64
  26.3 23.6 %shard_map.214 = (bf16[256,2048]{1,0:T(8,128)(2,1)}, f32[8,1,1024]{2,1,0:T(1,128)}, bf16[2048,1024]{1,0:T(8,128)(2,1)}) custom-call(bf16[768,2048]{1,0:T(8,128)(2,1)} %get-tuple-element.74.q_ref.k_ref.v_ref, bf16[768,2048]{1,0:T(8,128)(2,1)} %get-tuple-element.74.q_ref.k_ref.v_ref, bf16[768,2048]{1,0:T(8,128)(2,1)} %get-tuple-element.74.q_ref.k_ref.v_ref, ...), custom_call_target="tpu_custom_call" | custom-call | flops 4294967296 | bytes 16777216 | tf_op jit(solution)/shard_map/pallas_call | solution.py:197
  49.9 0.0 collective-permute-done.far_gate
  49.9 0.0 copy-start.5
  50.0 76.5 %shard_map.215 = (bf16[4,512,1024]{2,1,0:T(8,128)(2,1)}, f32[512,1024]{1,0:T(8,128)}, f32[512,1]{1,0:T(8,128)}, bf16[2048,1024]{1,0:T(8,128)(2,1)}, bf16[1280,10...) custom-call(bf16[4,512,1024]{2,1,0:T(8,128)(2,1)} %bitcast.26, ...), custom_call_target="tpu_custom_call" | custom-call | flops 41943040 | bytes 209715200 | tf_op jit(solution)/shard_map/pallas_call | solution.py:583
  126.5 0.0 copy-done.5
  126.5 11.9 %shard_map.216 = (bf16[1280,1024]{1,0:T(8,128)(2,1)}, bf16[1280,1024]{1,0:T(8,128)(2,1)}, f32[1280,1]{1,0:T(8,128)}, f32[2,2048]{1,0:T(2,128)}) custom-call(s32[2,2048]{1,0:T(2,128)} %get-tuple-element.78.code_ref, s32[2,2048]{1,0:T(2,128)} %bitcast.29, bf16[16,1024]{1,0:T(8,128)(2,1)} %bitcast.31, bf16[2048,1024]{1,0:T(8,128)(2,1)} %bitcast.24, ...), custom_call_target="tpu_custom_call" | custom-call | flops 5368709120 | bytes 12058624 | tf_op jit(solution)/shard_map/pallas_call | solution.py:886
  138.3 277.3 %shard_map.217 = (bf16[1280,1024]{1,0:T(8,128)(2,1)}, bf16[1280,1024]{1,0:T(8,128)(2,1)}, f32[704,1024]{1,0:T(8,128)}, f32[704,1024]{1,0:T(8,128)}, f32[704,1024...) custom-call(bf16[1280,1024]{1,0:T(8,128)(2,1)} %get-tuple-element.81.rows_in, ...), custom_call_target="tpu_custom_call" | custom-call | flops 66437775360 | bytes 42598400 | tf_op jit(solution)/shard_map/pallas_call | solution.py:1104
  415.7 80.3 %shard_map.218 = (bf16[4,512,1024]{2,1,0:T(8,128)(2,1)}, f32[512,1024]{1,0:T(8,128)}, f32[1,1024]{1,0:T(1,128)}, f32[16,1024]{1,0:T(8,128)}, bf16[2048,1024]{1,0:T(8,128)(2,1)}) custom-call(bf16[1280,1024]{1,0:T(8,128)(2,1)} %get-tuple-element.84.ret_in, bf16[1280,1024]{1,0:T(8,128)(2,1)} %get-tuple-element.85.back_ref, ...), custom_call_target="tpu_custom_call" | custom-call | flops 41943040 | bytes 209715200 | tf_op jit(solution)/shard_map/pallas_call | solution.py:583
  495.9 36.6 %shard_map.219 = (bf16[256,2048]{1,0:T(8,128)(2,1)}, bf16[256,2048]{1,0:T(8,128)(2,1)}, bf16[256,2048]{1,0:T(8,128)(2,1)}, f32[8,3,256,256]{3,2,1,0:T(8,128)}, f...) custom-call(bf16[768,2048]{1,0:T(8,128)(2,1)} %get-tuple-element.74.q_ref.k_ref.v_ref, ...), custom_call_target="tpu_custom_call" | custom-call | flops 10737418240 | bytes 33554432 | tf_op jit(solution)/shard_map/pallas_call | solution.py:334
  532.6 1.5 collective-permute-start.2
  534.1 0.6 collective-permute-start.1
  534.7 20.4 %shard_map.220 = (bf16[1024,1024]{1,0:T(8,128)(2,1)}, bf16[2048,1024]{1,0:T(8,128)(2,1)}, f32[1,1024]{1,0:T(1,128)}, f32[2,704,1024]{2,1,0:T(8,128)}, f32[2,704,1024]{2,1,0:T(8,128)}) custom-call(s32[2]{0:T(128)} %pad_add_fusion.place_ref, bf16[1024,2048]{1,0:T(8,128)(2,1)} %x_ref.5, f32[1024,1]{1,0:T(8,128)} %copy.30.gain_ref, f32[1,1024]{1,0:T(1,128)} %bitcast.35, ...), custom_call_target="tpu_custom_call" | custom-call | flops 8053063680 | bytes 22675456 | tf_op jit(solution)/shard_map/pallas_call | solution.py:419
  555.1 0.0 all-reduce.2.cloned.1.call-update
  555.1 0.0 collective-permute-done.2.y_along
  555.1 0.0 copy-start
  555.1 0.5 collective-permute-done.1.y_across
  555.6 0.0 copy-start.1
  555.6 0.5 copy-done
  556.1 0.5 copy-done.1
  556.6 104.2 %shard_map.221 = (bf16[4,512,1024]{2,1,0:T(8,128)(2,1)}, bf16[4,512,1024]{2,1,0:T(8,128)(2,1)}, f32[32,1024]{1,0:T(8,128)}) custom-call(bf16[4,512,1024]{2,1,0:T(8,128)(2,1)} %bitcast.27, bf16[512,1024]{1,0:T(8,128)(2,1)} %get-tuple-element.108.x_in, f32[1,2048]{1,0:T(1,128)} %get-tuple-element.73.scale_ref, f32[512,1024]{1,0:T(8,128)} %get-tuple-element.109.grad_in, ...), custom_call_target="tpu_custom_call" | custom-call | flops 41943040 | bytes 209715200 | tf_op jit(solution)/shard_map/pallas_call | solution.py:583
  660.8 0.0 all-reduce.2.cloned.1.call-done.summed_ref
  660.8 15.7 %shard_map.222 = (bf16[1024,2048]{1,0:T(8,128)(2,1)}, f32[1024,2048]{1,0:T(8,128)}, f32[2,704,1024]{2,1,0:T(8,128)}, f32[768,1024]{1,0:T(8,128)}, f32[256,1024]{...) custom-call(s32[2]{0:T(128)} %pad_add_fusion.place_ref, ...), custom_call_target="tpu_custom_call" | custom-call | bytes 37355520 | tf_op jit(solution)/shard_map/pallas_call | solution.py:1161
  (1 shorter events, 0.0 us)
Async XLA Ops:
  7.2 4.6 copy-start.4
  7.2 5.3 copy-start.2
  7.2 653.6 %all-reduce.2.cloned.1.call-start = ((), (), s32[]{:S(2)}) async-start(), calls=%async_computation | async-start | bytes 4194304 | tf_op jit(solution)/shard_map/psum | solution.py:1279
  7.3 10.0 %copy-start.3 = (s32[2,2]{1,0:T(2,128)S(1)}, s32[2,2]{1,0:T(2,128)}, u32[]{:S(2)}) copy-start(s32[2,2]{1,0:T(2,128)} %param.24) | copy-start | bytes 52
  8.8 41.2 %collective-permute-start = (bf16[704,1024]{1,0:T(8,128)(2,1)S(1)}, bf16[704,1024]{1,0:T(8,128)(2,1)S(1)}, u32[]{:S(2)}, u32[]{:S(2)}) collective-permute-start(bf16[704,1024]{1,0:T(8,128)(2,1)S(1)} %dynamic-slice_bitcast_fusion), channel_id=1, source_target_pairs={{0,1},{1,0},{2,3},{3,2},{4,5},{5,4},{6,7},{7,6},{8,9},{9,8},{10,11... | collective-permute-start | bytes 4325384 | tf_op jit(solution)/shard_map/ppermute | solution.py:1213
  49.9 76.5 %copy-start.5 = (bf16[704,1024]{1,0:T(8,128)(2,1)}, bf16[704,1024]{1,0:T(8,128)(2,1)S(1)}, u32[]{:S(2)}) copy-start(bf16[704,1024]{1,0:T(8,128)(2,1)S(1)} %collective-permute-done.far_gate) | copy-start | bytes 4325380
  532.6 22.6 %collective-permute-start.2 = (bf16[512,1024]{1,0:T(8,128)(2,1)}, bf16[512,1024]{1,0:T(8,128)(2,1)S(1)}, u32[]{:S(2)}, u32[]{:S(2)}) collective-permute-start(bf16[512,1024]{1,0:T(8,128)(2,1)} %get-tuple-element.106.y_own), channel_id=1, source_target_pairs={{0,2},{1,3},{2,0},{3,1},{4,6},{5,7},{6,4},{7,5},{8,10},{9,11},{10,... | collective-permute-start | bytes 3145736 | tf_op jit(solution)/shard_map/ppermute | solution.py:1273
  534.1 21.5 %collective-permute-start.1 = (bf16[512,1024]{1,0:T(8,128)(2,1)}, bf16[512,1024]{1,0:T(8,128)(2,1)S(1)}, u32[]{:S(2)}, u32[]{:S(2)}) collective-permute-start(bf16[512,1024]{1,0:T(8,128)(2,1)} %get-tuple-element.106.y_own), channel_id=1, source_target_pairs={{0,1},{1,0},{2,3},{3,2},{4,5},{5,4},{6,7},{7,6},{8,9},{9,8},{10,11... | collective-permute-start | bytes 3145736 | tf_op jit(solution)/shard_map/ppermute | solution.py:1272
  555.1 1.0 copy-start
  555.6 1.0 copy-start.1
Sparse Core Ops, SparseCore 0:
  555.2 74.2 all-reduce.1

commit v9 on v8

--- a/solution.py
+++ b/solution.py
@@ -383,7 +383,7 @@
 ):
     step = pl.program_id(0)
     own_refs, got_refs, (weight_ref, out_ref, gain_grad_ref), placed_refs, total = (
-        refs[:2], refs[2:4], refs[4:7], refs[7:9], refs[9]
+        refs[:3], refs[3:6], refs[6:9], refs[9:12], refs[12]
     )
     for own_ref, got_ref, placed_ref in zip(own_refs, got_refs, placed_refs):
         placed_ref[place_ref[0]] = own_ref[...]
@@ -430,19 +430,19 @@
             pl.BlockSpec((tile, width), lambda i: (i, 0)),
         ]
         + [column(rows // 3)] * 3
-        + [pl.BlockSpec((part, width), lambda i: (i, 0))] * 4,
+        + [pl.BlockSpec((part, width), lambda i: (i, 0))] * 6,
         out_specs=[
             pl.BlockSpec((rows + heads_width, width), lambda i: (0, 0)),
             pl.BlockSpec((tile, width), lambda i: (i, 0)),
             pl.BlockSpec((1, width), lambda i: (0, 0)),
         ]
-        + [pl.BlockSpec((2, part, width), lambda i: (0, i, 0))] * 2,
+        + [pl.BlockSpec((2, part, width), lambda i: (0, i, 0))] * 3,
         out_shape=[
             jax.ShapeDtypeStruct((rows + heads_width, width), BF16),
             jax.ShapeDtypeStruct((tokens, width), BF16),
             jax.ShapeDtypeStruct((1, width), F32),
         ]
-        + [jax.ShapeDtypeStruct((2, units, width), F32)] * 2,
+        + [jax.ShapeDtypeStruct((2, units, width), F32)] * 3,
         scratch_shapes=[pltpu.VMEM((rows + heads_width, width), F32)],
         compiler_params=params(),
         cost_estimate=cost(5 * width * tokens * rows, 6 * width * tokens + 14 * units * width),
@@ -1127,14 +1127,12 @@
 
 
 def finish_kernel(
-    place_ref, rows_ref, y_ref, own_ref, got_ref, summed_ref, small_ref,
-    output_ref, grad_ref, placed_ref, in_ref, out_ref, one_ref, two_ref, router_ref, bias_ref,
+    rows_ref, y_ref, summed_ref, small_ref,
+    output_ref, grad_ref, in_ref, out_ref, one_ref, two_ref, router_ref, bias_ref,
 ):
     step = pl.program_id(0)
     output_ref[...] = y_ref[...].astype(F32).T.astype(BF16)
     grad_ref[...] = rows_ref[...].astype(F32).T
-    placed_ref[place_ref[0]] = own_ref[...]
-    placed_ref[1 - place_ref[0]] = got_ref[...].astype(F32)
 
     @pl.when(step < 3)
     def _():
@@ -1149,12 +1147,10 @@
         bias_ref[...] = small_ref[EXPERTS + 2 : EXPERTS + 2 + bias_ref.shape[0], :BUCKETS]
 
 
-def finish_outputs(place, rows, y_rows, own, got, summed, small, heads):
+def finish_outputs(rows, y_rows, summed, small, heads):
     tokens, width = rows.shape
-    units = own.shape[0]
     steps = 4
-    tile, part, block = tokens // steps, units // steps, summed.shape[0] // steps
-    quarter = pl.BlockSpec((part, width), lambda i: (i, 0))
+    tile, block = tokens // steps, summed.shape[0] // steps
     token_spec = pl.BlockSpec((tile, width), lambda i: (i, 0))
     feature_spec = pl.BlockSpec((width, tile), lambda i: (0, i))
     whole = lambda *shape: pl.BlockSpec(shape, lambda i: (0, 0))
@@ -1162,18 +1158,14 @@
         finish_kernel,
         grid=(steps,),
         in_specs=[
-            pl.BlockSpec(memory_space=pltpu.SMEM),
             token_spec,
             token_spec,
-            quarter,
-            quarter,
             pl.BlockSpec((block, width), lambda i: (i, 0)),
             whole(*small.shape),
         ],
         out_specs=[
             feature_spec,
             feature_spec,
-            pl.BlockSpec((2, part, width), lambda i: (0, i, 0)),
             pl.BlockSpec((block, width), lambda i: (jnp.minimum(i, 2), 0)),
             whole(block, width),
             whole(1, width),
@@ -1184,7 +1176,6 @@
         out_shape=[
             jax.ShapeDtypeStruct((width, tokens), BF16),
             jax.ShapeDtypeStruct((width, tokens), F32),
-            jax.ShapeDtypeStruct((2, units, width), F32),
             jax.ShapeDtypeStruct((3 * block, width), F32),
             jax.ShapeDtypeStruct((block, width), F32),
             jax.ShapeDtypeStruct((1, width), F32),
@@ -1193,8 +1184,8 @@
             jax.ShapeDtypeStruct((heads, BUCKETS), F32),
         ],
         compiler_params=params(),
-        cost_estimate=cost(0, 10 * rows.size + 14 * own.size + 6 * summed.size),
-    )(place, rows, y_rows, own, got, summed, small)
+        cost_estimate=cost(0, 10 * rows.size + 6 * summed.size),
+    )(rows, y_rows, summed, small)
 
 
 def on_device(
@@ -1271,9 +1262,9 @@
     dq, y_own = lax.optimization_barrier((dq, y_own))
     y_across = lax.ppermute(y_own, "tensor", [(r, r ^ 1) for r in range(ranks)])
     y_along = lax.ppermute(y_own, "tensor", [(r, r ^ 2) for r in range(ranks)])
-    weight_rows, sent, grad_gain_one, grad_gate, grad_up = project_back(
+    weight_rows, sent, grad_gain_one, grad_gate, grad_up, grad_down = project_back(
         place, layer_input, gain_col, gain_one[None], scale_one, w_in, mixed, grad_attn, (dq, dk, dv),
-        weight_grads[:2], weight_grads[3:5],
+        weight_grads[:3], weight_grads[3:],
     )
     sent, y_across, y_along = lax.optimization_barrier((sent, y_across, y_along))
     summed = lax.psum(weight_rows, "expert")
@@ -1288,12 +1279,12 @@
         + [pltpu.SemaphoreType.DMA((3,))]
         + [pltpu.SemaphoreType.DMA((2,))] * 2
         + [pltpu.SemaphoreType.DMA((groups,))] * 2,
-        (1, 3, 5, 6, 7, 11),
+        (1, 3, 11),
         (0,),
     )
     summed, grad_rows = lax.optimization_barrier((summed, grad_rows))
-    layer_output, grad_input, grad_down, grad_in, grad_attn_out, grad_one, grad_two, grad_router, grad_bias = finish_outputs(
-        place, grad_rows, y_full.reshape(tokens, width), weight_grads[2], weight_grads[5], summed, small, rel_bias.shape[1]
+    layer_output, grad_input, grad_in, grad_attn_out, grad_one, grad_two, grad_router, grad_bias = finish_outputs(
+        grad_rows, y_full.reshape(tokens, width), summed, small, rel_bias.shape[1]
     )
     return (
         layer_output,

time: 693 us -> 679 us (0.980)
  Pallas kernels: 658 us -> 643 us
    pallas_call x3, Pallas kernels: 261 us -> 248 us  [exchange_call(): pl.pallas_call(kernel, in_specs=[pl.BlockSpec(memory_space=pl.ANY) if k i...]
  transfers between devices with their start and end apart: 4 -> 4, of which waited for: 1 -> 0; matrix products, arithmetic and copies ran while one was open for 0% -> 0% of each run, Pallas kernels for 23% -> 22%
where the time goes in v9:
time: 679 us; the launch traced here: 669 us
  Pallas kernels  643 us (95%)
  between operations  14.6 us (2%)
    pallas_call x1, Pallas kernels, run_experts(): pl.pallas_call(expert_kernel, in_specs=[anywhere] * 6, out_specs=[anywher...  277 us
    pallas_call x3, Pallas kernels, exchange_call(): pl.pallas_call(kernel, in_specs=[pl.BlockSpec(memory_space=pl.ANY) if k i...  248 us
    pallas_call x1, Pallas kernels, attend_back(): pl.pallas_call(attend_back_kernel, grid=(seqs, heads), in_specs=[pl.Block...  36.6 us
    pallas_call x1, Pallas kernels, attend(): pl.pallas_call(attend_kernel, grid=(seqs, heads), in_specs=[pl.BlockSpec(...  23.6 us
    pallas_call x1, Pallas kernels, project_back(): pl.pallas_call(project_back_kernel, grid=(steps,), in_specs=[pl.BlockSpec...  22.6 us
  transfers between devices with their start and end apart: 4, of which 0 were waited for; matrix products, arithmetic and copies ran while one was open for 0% of the time, Pallas kernels for 22%

profile of v9, /device:TPU:0, one launch (start us, length us, event | category | flops | bytes accessed | tf_op | source)
XLA Modules:
  0.0 669.0 jit_solution(4236740050269281056)
XLA Ops:
  7.2 0.0 copy-start.2
  7.2 0.0 copy-start.4
  7.2 0.0 all-reduce.2.cloned.1.call-start
  7.3 0.0 copy-start.3
  7.3 1.5 dynamic-slice_bitcast_fusion
  8.8 3.0 collective-permute-start
  11.8 0.0 copy-done.2
  11.8 1.1 copy.30.gain_ref
  12.8 0.0 copy-done.4
  12.8 0.7 copy.29.table_ref
  13.5 3.2 shard_map.213.tiles_ref
  16.7 0.6 pad_add_fusion.place_ref
  17.3 0.0 copy-done.3
  17.3 0.1 fusion
  17.4 0.6 iota_maximum_fusion.limit_ref
  18.0 8.3 %shard_map.212 = (bf16[768,2048]{1,0:T(8,128)(2,1)}, f32[1,2048]{1,0:T(1,128)}) custom-call(bf16[1024,2048]{1,0:T(8,128)(2,1)} %x_ref.5, f32[1024,1]{1,0:T(8,128)} %copy.30.gain_ref, bf16[768,1024]{1,0:T(8,128)(2,1)} %bitcast.42), custom_call_target="tpu_custom_call" | custom-call | flops 3221225472 | bytes 8388608 | tf_op jit(solution)/shard_map/pallas_call | solution.py:64
  26.4 23.6 %shard_map.214 = (bf16[256,2048]{1,0:T(8,128)(2,1)}, f32[8,1,1024]{2,1,0:T(1,128)}, bf16[2048,1024]{1,0:T(8,128)(2,1)}) custom-call(bf16[768,2048]{1,0:T(8,128)(2,1)} %get-tuple-element.74.q_ref.k_ref.v_ref, bf16[768,2048]{1,0:T(8,128)(2,1)} %get-tuple-element.74.q_ref.k_ref.v_ref, bf16[768,2048]{1,0:T(8,128)(2,1)} %get-tuple-element.74.q_ref.k_ref.v_ref, ...), custom_call_target="tpu_custom_call" | custom-call | flops 4294967296 | bytes 16777216 | tf_op jit(solution)/shard_map/pallas_call | solution.py:197
  50.0 0.0 collective-permute-done.far_gate
  50.0 0.0 copy-start.5
  50.0 76.4 %shard_map.215 = (bf16[4,512,1024]{2,1,0:T(8,128)(2,1)}, f32[512,1024]{1,0:T(8,128)}, f32[512,1]{1,0:T(8,128)}, bf16[2048,1024]{1,0:T(8,128)(2,1)}, bf16[1280,10...) custom-call(bf16[4,512,1024]{2,1,0:T(8,128)(2,1)} %bitcast.24, ...), custom_call_target="tpu_custom_call" | custom-call | flops 41943040 | bytes 209715200 | tf_op jit(solution)/shard_map/pallas_call | solution.py:583
  126.4 0.0 copy-done.5
  126.4 11.9 %shard_map.216 = (bf16[1280,1024]{1,0:T(8,128)(2,1)}, bf16[1280,1024]{1,0:T(8,128)(2,1)}, f32[1280,1]{1,0:T(8,128)}, f32[2,2048]{1,0:T(2,128)}) custom-call(s32[2,2048]{1,0:T(2,128)} %get-tuple-element.78.code_ref, s32[2,2048]{1,0:T(2,128)} %bitcast.29, bf16[16,1024]{1,0:T(8,128)(2,1)} %bitcast.31, bf16[2048,1024]{1,0:T(8,128)(2,1)} %bitcast.22, ...), custom_call_target="tpu_custom_call" | custom-call | flops 5368709120 | bytes 12058624 | tf_op jit(solution)/shard_map/pallas_call | solution.py:886
  138.3 277.3 %shard_map.217 = (bf16[1280,1024]{1,0:T(8,128)(2,1)}, bf16[1280,1024]{1,0:T(8,128)(2,1)}, f32[704,1024]{1,0:T(8,128)}, f32[704,1024]{1,0:T(8,128)}, f32[704,1024...) custom-call(bf16[1280,1024]{1,0:T(8,128)(2,1)} %get-tuple-element.81.rows_in, ...), custom_call_target="tpu_custom_call" | custom-call | flops 66437775360 | bytes 42598400 | tf_op jit(solution)/shard_map/pallas_call | solution.py:1104
  415.6 80.2 %shard_map.218 = (bf16[4,512,1024]{2,1,0:T(8,128)(2,1)}, f32[512,1024]{1,0:T(8,128)}, f32[1,1024]{1,0:T(1,128)}, f32[16,1024]{1,0:T(8,128)}, bf16[2048,1024]{1,0:T(8,128)(2,1)}) custom-call(bf16[1280,1024]{1,0:T(8,128)(2,1)} %get-tuple-element.84.ret_in, bf16[1280,1024]{1,0:T(8,128)(2,1)} %get-tuple-element.85.back_ref, ...), custom_call_target="tpu_custom_call" | custom-call | flops 41943040 | bytes 209715200 | tf_op jit(solution)/shard_map/pallas_call | solution.py:583
  495.9 36.6 %shard_map.219 = (bf16[256,2048]{1,0:T(8,128)(2,1)}, bf16[256,2048]{1,0:T(8,128)(2,1)}, bf16[256,2048]{1,0:T(8,128)(2,1)}, f32[8,3,256,256]{3,2,1,0:T(8,128)}, f...) custom-call(bf16[768,2048]{1,0:T(8,128)(2,1)} %get-tuple-element.74.q_ref.k_ref.v_ref, ...), custom_call_target="tpu_custom_call" | custom-call | flops 10737418240 | bytes 33554432 | tf_op jit(solution)/shard_map/pallas_call | solution.py:334
  532.5 1.5 collective-permute-start.1
  534.0 0.6 collective-permute-start.2
  534.6 22.6 %shard_map.220 = (bf16[1024,1024]{1,0:T(8,128)(2,1)}, bf16[2048,1024]{1,0:T(8,128)(2,1)}, f32[1,1024]{1,0:T(1,128)}, f32[2,704,1024]{2,1,0:T(8,128)}, f32[2,704,1024]{2,1,0:T(8,128)}, /*index=5*/f32[2,704,1024]{2,1,0:T(8,128)}) custom-call(s32[2]{0:T(128)} %pad_add_fusion.place_ref, bf16[1024,2048]{1,0:T(8,128)(2,1)} %x_ref.5, f32[1024,1]{1,0:T(8,128)} %copy.30.gain_ref, ...), custom_call_target="tpu_custom_call" | custom-call | flops 8053063680 | bytes 22675456 | tf_op jit(solution)/shard_map/pallas_call | solution.py:419
  557.2 0.0 all-reduce.2.cloned.1.call-update
  557.2 0.0 collective-permute-done.1.y_across
  557.2 0.0 copy-start
  557.2 0.0 collective-permute-done.2.y_along
  557.2 0.0 copy-start.1
  557.3 0.9 copy-done
  558.2 0.3 copy-done.1
  558.5 91.6 %shard_map.221 = (bf16[4,512,1024]{2,1,0:T(8,128)(2,1)}, bf16[4,512,1024]{2,1,0:T(8,128)(2,1)}, f32[32,1024]{1,0:T(8,128)}) custom-call(bf16[4,512,1024]{2,1,0:T(8,128)(2,1)} %bitcast.25, bf16[512,1024]{1,0:T(8,128)(2,1)} %get-tuple-element.110.x_in, f32[1,2048]{1,0:T(1,128)} %get-tuple-element.73.scale_ref, f32[512,1024]{1,0:T(8,128)} %get-tuple-element.111.grad_in, ...), custom_call_target="tpu_custom_call" | custom-call | flops 41943040 | bytes 209715200 | tf_op jit(solution)/shard_map/pallas_call | solution.py:583
  650.1 0.0 all-reduce.2.cloned.1.call-done.summed_ref
  650.2 11.6 %shard_map.222 = (bf16[1024,2048]{1,0:T(8,128)(2,1)}, f32[1024,2048]{1,0:T(8,128)}, f32[768,1024]{1,0:T(8,128)}, f32[256,1024]{1,0:T(8,128)}, f32[1,1024]{1,0:T(...) custom-call(bf16[2048,1024]{1,0:T(8,128)(2,1)} %bitcast.26, bf16[2048,1024]{1,0:T(8,128)(2,1)} %bitcast.27, ...), custom_call_target="tpu_custom_call" | custom-call | bytes 27262976 | tf_op jit(solution)/shard_map/pallas_call | solution.py:1157
  (1 shorter events, 0.0 us)
Async XLA Ops:
  7.2 4.6 copy-start.2
  7.2 5.6 copy-start.4
  7.2 643.0 %all-reduce.2.cloned.1.call-start = ((), (), s32[]{:S(2)}) async-start(), calls=%async_computation | async-start | bytes 4194304 | tf_op jit(solution)/shard_map/psum | solution.py:1270
  7.3 10.0 %copy-start.3 = (s32[2,2]{1,0:T(2,128)S(1)}, s32[2,2]{1,0:T(2,128)}, u32[]{:S(2)}) copy-start(s32[2,2]{1,0:T(2,128)} %param.24) | copy-start | bytes 52
  8.8 41.2 %collective-permute-start = (bf16[704,1024]{1,0:T(8,128)(2,1)S(1)}, bf16[704,1024]{1,0:T(8,128)(2,1)S(1)}, u32[]{:S(2)}, u32[]{:S(2)}) collective-permute-start(bf16[704,1024]{1,0:T(8,128)(2,1)S(1)} %dynamic-slice_bitcast_fusion), channel_id=1, source_target_pairs={{0,1},{1,0},{2,3},{3,2},{4,5},{5,4},{6,7},{7,6},{8,9},{9,8},{10,11... | collective-permute-start | bytes 4325384 | tf_op jit(solution)/shard_map/ppermute | solution.py:1204
  50.0 76.4 %copy-start.5 = (bf16[704,1024]{1,0:T(8,128)(2,1)}, bf16[704,1024]{1,0:T(8,128)(2,1)S(1)}, u32[]{:S(2)}) copy-start(bf16[704,1024]{1,0:T(8,128)(2,1)S(1)} %collective-permute-done.far_gate) | copy-start | bytes 4325380
  532.5 24.7 %collective-permute-start.1 = (bf16[512,1024]{1,0:T(8,128)(2,1)}, bf16[512,1024]{1,0:T(8,128)(2,1)S(1)}, u32[]{:S(2)}, u32[]{:S(2)}) collective-permute-start(bf16[512,1024]{1,0:T(8,128)(2,1)} %get-tuple-element.108.y_own), channel_id=1, source_target_pairs={{0,1},{1,0},{2,3},{3,2},{4,5},{5,4},{6,7},{7,6},{8,9},{9,8},{10,11... | collective-permute-start | bytes 3145736 | tf_op jit(solution)/shard_map/ppermute | solution.py:1263
  534.0 23.3 %collective-permute-start.2 = (bf16[512,1024]{1,0:T(8,128)(2,1)}, bf16[512,1024]{1,0:T(8,128)(2,1)S(1)}, u32[]{:S(2)}, u32[]{:S(2)}) collective-permute-start(bf16[512,1024]{1,0:T(8,128)(2,1)} %get-tuple-element.108.y_own), channel_id=1, source_target_pairs={{0,2},{1,3},{2,0},{3,1},{4,6},{5,7},{6,4},{7,5},{8,10},{9,11},{10,... | collective-permute-start | bytes 3145736 | tf_op jit(solution)/shard_map/ppermute | solution.py:1264
  557.2 1.0 copy-start
  557.2 1.3 copy-start.1
Sparse Core Ops, SparseCore 0:
  557.3 74.4 all-reduce.1

commit v10 on v9

--- a/solution.py
+++ b/solution.py
@@ -151,7 +151,7 @@
     return 2 * BLK if query_block < 2 else 4 * BLK
 
 
-def block_scores(keys, queries, tiles_ref, limit, block):
+def block_scores(keys, queries, tile_of, limit, block):
     count = key_count(block)
     parts = []
     whole = mm(keys[:, :count], queries, TN)
@@ -159,7 +159,7 @@
         part = whole[key_block * BLK : (key_block + 1) * BLK]
         shift = key_block - block
         if -1 <= shift <= 1:
-            part = part + tiles_ref[0, shift + 1]
+            part = part + tile_of(shift)
         if shift >= 0:
             key_at = lax.broadcasted_iota(jnp.int32, (BLK, BLK), 0) + key_block * BLK
             part = jnp.where(key_at <= limit, part, NEG)
@@ -167,58 +167,30 @@
     return jnp.concatenate(parts, axis=0)
 
 
-def attend_kernel(q_ref, k_ref, v_ref, tiles_ref, limit_ref, w_ref, out_ref, lse_ref, sent_ref, held):
-    head = pl.program_id(1)
-    width = q_ref.shape[0]
-    queries = q_ref[...] * BF16(0.125)
-    keys, values = k_ref[...], v_ref[...]
-    for block in range(SEQ // BLK):
-        cols = slice(block * BLK, (block + 1) * BLK)
-        scores = block_scores(keys, queries[:, cols], tiles_ref, limit_ref[0, :, cols], block)
-        top = jnp.max(scores, axis=0, keepdims=True)
-        exponent = jnp.exp(scores - top)
-        total = jnp.sum(exponent, axis=0, keepdims=True)
-        mixed = mm(values[:, : key_count(block)], exponent.astype(BF16)) / total
-        mixed = mixed.astype(BF16)
-        out_ref[:, cols] = mixed
-        held[pl.ds(pl.multiple_of(head * width, width), width), cols] = mixed
-        lse_ref[0, :, cols] = top + jnp.log(total)
-
-    @pl.when(head == pl.num_programs(1) - 1)
-    def _():
-        sent_ref[...] = mm(held[...], w_ref[...], TN).astype(BF16)
-
-
-def attend(qkv, tiles, limits, attn_out):
-    heads = tiles.shape[0]
-    seqs = limits.shape[0]
-    width = qkv.shape[0] // (3 * heads)
-    model_width = attn_out.shape[1]
-    return pl.pallas_call(
-        attend_kernel,
-        grid=(seqs, heads),
-        in_specs=[
-            pl.BlockSpec((width, SEQ), lambda s, h: (h, s)),
-            pl.BlockSpec((width, SEQ), lambda s, h: (heads + h, s)),
-            pl.BlockSpec((width, SEQ), lambda s, h: (2 * heads + h, s)),
-            pl.BlockSpec((1, 3, BLK, BLK), lambda s, h: (h, 0, 0, 0)),
-            pl.BlockSpec((1, 1, SEQ), lambda s, h: (s, 0, 0)),
-            pl.BlockSpec((heads * width, model_width), lambda s, h: (0, 0)),
-        ],
-        out_specs=[
-            pl.BlockSpec((width, SEQ), lambda s, h: (h, s)),
-            pl.BlockSpec((1, 1, SEQ), lambda s, h: (s * heads + h, 0, 0)),
-            pl.BlockSpec((SEQ, model_width), lambda s, h: (s, 0)),
-        ],
-        out_shape=[
-            jax.ShapeDtypeStruct((heads * width, seqs * SEQ), BF16),
-            jax.ShapeDtypeStruct((seqs * heads, 1, SEQ), F32),
-            jax.ShapeDtypeStruct((seqs * SEQ, model_width), BF16),
-        ],
-        scratch_shapes=[pltpu.VMEM((heads * width, SEQ), BF16)],
-        compiler_params=params(),
-        cost_estimate=cost(seqs * heads * SEQ * SEQ * 512, seqs * heads * SEQ * 2048, seqs * heads * SEQ * SEQ),
-    )(qkv, qkv, qkv, tiles, limits, attn_out)
+def attend_half(qkv_ref, tiles_ref, limit_ref, mixed_ref, lse_ref, seq, half):
+    heads = tiles_ref.shape[0]
+    width = mixed_ref.shape[0] // heads
+    base = pl.multiple_of(seq * SEQ, SEQ)
+
+    def one_head(head, carry):
+        at = lambda kind: pl.ds(pl.multiple_of((kind * heads + head) * width, width), width)
+        keys, values = qkv_ref[at(1), pl.ds(base, SEQ)], qkv_ref[at(2), pl.ds(base, SEQ)]
+        for block in (2 * half, 2 * half + 1):
+            cols = pl.ds(pl.multiple_of(base + block * BLK, BLK), BLK)
+            span = slice(block * BLK, (block + 1) * BLK)
+            queries = qkv_ref[at(0), cols] * BF16(0.125)
+            scores = block_scores(
+                keys, queries, lambda shift: tiles_ref[head, shift + 1], limit_ref[seq, :, span], block
+            )
+            top = jnp.max(scores, axis=0, keepdims=True)
+            exponent = jnp.exp(scores - top)
+            total = jnp.sum(exponent, axis=0, keepdims=True)
+            mixed = mm(values[:, : key_count(block)], exponent.astype(BF16)) / total
+            mixed_ref[at(0), cols] = mixed.astype(BF16)
+            lse_ref[seq * heads + head, :, span] = top + jnp.log(total)
+        return carry
+
+    lax.fori_loop(0, heads, one_head, 0)
 
 
 def attend_back_kernel(
@@ -288,7 +260,9 @@
     for block in range(SEQ // BLK):
         count = key_count(block)
         cols = slice(block * BLK, (block + 1) * BLK)
-        scores = block_scores(keys, queries[:, cols], tiles_ref, limit_ref[0, :, cols], block)
+        scores = block_scores(
+            keys, queries[:, cols], lambda shift: tiles_ref[0, shift + 1], limit_ref[0, :, cols], block
+        )
         probs = jnp.exp(scores - lse_ref[0, :, cols])
         grad_probs = mm(values[:, :count], grads[:, cols], TN)
         inner = jnp.sum(probs * grad_probs, axis=0, keepdims=True)
@@ -601,10 +575,10 @@
 
 
 def norm_two_kernel(
-    source, x_ref, gain_ref, grad_out_ref, routes_ref,
-    full, resid_ref, scale_ref, dy_out, dy_rows_out, code_ref, codes_ref, own_ref, *rest,
+    qkv_ref, tiles_ref, limit_ref, w_ref, x_ref, gain_ref, grad_out_ref, routes_ref, gate_ref,
+    full, resid_ref, scale_ref, dy_out, dy_rows_out, code_ref, codes_ref, own_ref, mixed_ref, lse_ref, got_gate, *rest,
 ):
-    held, grad_out, dy_ref, dy_rows_ref, load = rest[-5:]
+    source, held, grad_out, dy_ref, dy_rows_ref, load, send, recv = rest[-8:]
     rank = lax.axis_index("tensor")
     ranks, rows, width = source.shape
     loading = pltpu.make_async_copy(grad_out_ref, grad_out, load.at[1])
@@ -613,9 +587,32 @@
         pltpu.make_async_copy(dy_rows_ref, dy_rows_out, load.at[3]),
     ]
 
+    pair_class = rank % 2
+    part = got_gate.shape[0] // 2
+    swaps = [
+        pltpu.make_async_remote_copy(
+            src_ref=gate_ref.at[1 - pair_class, pl.ds((2 + piece) * part, part)],
+            dst_ref=got_gate.at[pl.ds(piece * part, part)],
+            send_sem=send.at[piece],
+            recv_sem=recv.at[piece],
+            device_id={"tensor": rank + 1 - 2 * pair_class},
+            device_id_type=pl.DeviceIdType.MESH,
+        )
+        for piece in range(2)
+    ]
+
     def start():
         own.start()
         loading.start()
+        swaps[0].start()
+
+    def fill(shard):
+        for half in range(2):
+            pl.when(shard % 2 == half)(
+                partial(attend_half, qkv_ref, tiles_ref, limit_ref, mixed_ref, lse_ref, shard // 2, half)
+            )
+        columns = pl.ds(pl.multiple_of(shard * rows, rows), rows)
+        source[shard] = mm(mixed_ref[:, columns], w_ref[...], TN).astype(BF16)
 
     slots = dy_rows_ref.shape[0] // ranks
     own = pltpu.make_async_copy(x_ref.at[:, pl.ds(pl.multiple_of(rank * rows, rows), rows)], held, load.at[0])
@@ -627,30 +624,33 @@
         scale_ref[span, :] = scale
         return resid * scale * gain_ref[...]
 
+    def later(others):
+        own.wait()
+        own_ref[...] = held[...].astype(F32).T.astype(BF16)
+        local_codes(routes_ref, code_ref, pair_class, rank // 2, CAP // 2)
+        codes_ref[...] = jnp.concatenate([code_ref[...].astype(F32)] * 4, axis=0).T[:, :TOP].astype(jnp.int32)
+        loading.wait()
+        for number in range(ranks):
+            span = slice(number * rows, (number + 1) * rows)
+            dy_ref[span, :] = grad_out[:, span].astype(F32).T.astype(BF16)
+        storing[0].start()
+
     def side(number):
         if number == 0:
-            own.wait()
-            own_ref[...] = held[...].astype(F32).T.astype(BF16)
-            local_codes(routes_ref, code_ref, rank % 2, rank // 2, CAP // 2)
-            codes_ref[...] = jnp.concatenate([code_ref[...].astype(F32)] * 4, axis=0).T[:, :TOP].astype(jnp.int32)
-            loading.wait()
-        if number < ranks:
-            span = slice(number * rows, (number + 1) * rows)
-            dy_ref[span, :] = grad_out[:, span].astype(F32).T.astype(BF16)
-        elif number < 2 * ranks:
-            start = (number - ranks) * slots
-            slot = lax.broadcasted_iota(jnp.int32, (slots, dy_ref.shape[0]), 0) + start
+            swaps[1].start()
+        elif ranks <= number < 2 * ranks:
+            begin = (number - ranks) * slots
+            slot = lax.broadcasted_iota(jnp.int32, (slots, dy_ref.shape[0]), 0) + begin
             take = jnp.where((slot == code_ref[0:1]) | (slot == code_ref[1:2]), 1.0, 0.0).astype(BF16)
-            dy_rows_ref[start : start + slots, :] = mm(take, dy_ref[...]).astype(BF16)
-        if number == ranks - 1:
-            storing[0].start()
-        elif number == 2 * ranks - 1:
+            dy_rows_ref[begin : begin + slots, :] = mm(take, dy_ref[...]).astype(BF16)
+        elif number == 2 * ranks:
             storing[1].start()
-        elif number == 2 * ranks:
-            for copy in storing:
+            for copy in swaps + storing:
                 copy.wait()
 
-    exchange(math, rank, source, full, *rest[:-5], side=side, start=start)
+    exchange(
+        math, rank, source, full, *rest[:-8], side=side, start=start, fill=fill, later=later, cut=3 * width // 8
+    )
 
 
 def norm_back(grad, value, scale, gain):
@@ -913,7 +913,7 @@
 
 
 def expert_kernel(
-    rows_in, grads_in, gate_in, up_in, down_in, far_gate,
+    rows_in, grads_in, gate_in, up_in, down_in, far_gate, far_gate_too,
     ret_out, back_out, own_gate, own_up, own_down, got_gate, got_up, got_down,
     rows, grads, weights, sums, parts, z_send, z_recv, y_send, y_recv, p_send, p_recv, r_send, r_recv, w_send, w_recv, g_send, g_recv, local,
 ):
@@ -979,7 +979,10 @@
         pltpu.make_async_copy(ref.at[pair_class], weights.at[number, 0], local.at[2 + number])
         for number, ref in enumerate((gate_in, up_in, down_in))
     ]
-    kept.append(pltpu.make_async_copy(far_gate, weights.at[0, 1], local.at[5]))
+    some = far_gate.shape[0]
+    for number, ref in enumerate((far_gate, far_gate_too)):
+        target = weights.at[0, 1, pl.ds(number * some, some)]
+        kept.append(pltpu.make_async_copy(ref, target, local.at[5 + number]))
     kept += [
         remote(ref.at[1 - pair_class], weights.at[number, 1], w_send.at[number - 1], w_recv.at[number - 1], across)
         for number, ref in ((1, up_in), (2, down_in))
@@ -1094,7 +1097,7 @@
             result(kind, step).wait()
 
 
-def run_experts(rows, grads, w_gate, w_up, w_down, far_gate):
+def run_experts(rows, grads, w_gate, w_up, w_down, far_gate, far_gate_too):
     slots, width = rows.shape
     half = CAP // 2
     groups = slots // half
@@ -1103,7 +1106,7 @@
     pair = pltpu.SemaphoreType.DMA((2, groups))
     return pl.pallas_call(
         expert_kernel,
-        in_specs=[anywhere] * 6,
+        in_specs=[anywhere] * 7,
         out_specs=[anywhere] * 8,
         out_shape=[jax.ShapeDtypeStruct((slots, width), BF16)] * 2
         + [jax.ShapeDtypeStruct((units, width), F32)] * 3
@@ -1118,12 +1121,12 @@
         + [pair] * 8
         + [pltpu.SemaphoreType.DMA((2,))] * 2
         + [pltpu.SemaphoreType.DMA((3,))] * 2
-        + [pltpu.SemaphoreType.DMA((6,))],
+        + [pltpu.SemaphoreType.DMA((7,))],
         compiler_params=pltpu.CompilerParams(
             vmem_limit_bytes=60 * MIB, collective_id=1, has_side_effects=True
         ),
         cost_estimate=cost(72 * slots * units * width, 16 * slots * width + 30 * units * width),
-    )(rows, grads, w_gate, w_up, w_down, far_gate)
+    )(rows, grads, w_gate, w_up, w_down, far_gate, far_gate_too)
 
 
 def finish_kernel(
@@ -1199,11 +1202,9 @@
     pair_class, half_index = rank % 2, rank // 2
     half = CAP // 2
 
-    def trade(weights):
-        other = lax.dynamic_index_in_dim(weights, 1 - pair_class, 0, keepdims=False)
-        return lax.ppermute(other, "tensor", [(r, r ^ 1) for r in range(ranks)])
-
-    traded = trade(expert_gate)
+    units = expert_gate.shape[1]
+    other = lax.dynamic_slice(expert_gate, (1 - pair_class, 0, 0), (1, units // 2, width))[0]
+    traded = lax.ppermute(other, "tensor", [(r, r ^ 1) for r in range(ranks)])
     gain_col = gain_one[:, None]
     w_in = attn_in.reshape(-1, width)
     qkv, scale_one = project(layer_input, gain_col, w_in)
@@ -1221,21 +1222,24 @@
     def by_rank(rows):
         return rows.reshape(ranks, share, width)
 
-    mixed, lse, sent = attend(qkv, tiles, limits, attn_out)
-    sent, traded = lax.optimization_barrier((sent, traded))
+    qkv, traded = lax.optimization_barrier((qkv, traded))
     slots = groups * half
-    h2, resid, scale_two, dy, dy_rows, code, code_cols, own_x = exchange_call(
-        norm_two_kernel, 2, sent.shape, [by_rank(sent), layer_input, gain_two[None], grad_out, routes_t],
+    heads = rel_bias.shape[1]
+    h2, resid, scale_two, dy, dy_rows, code, code_cols, own_x, mixed, lse, traded_too = exchange_call(
+        norm_two_kernel, 2, (tokens, width),
+        [qkv, tiles, limits, attn_out, layer_input, gain_two[None], grad_out, routes_t, expert_gate],
         [((share, width), F32), ((share, 1), F32), ((tokens, width), BF16), ((slots, width), BF16)]
-        + [((TOP, tokens), jnp.int32), ((tokens, TOP), jnp.int32), ((share, width), BF16)],
-        [pltpu.VMEM((width, share), BF16), pltpu.VMEM((width, tokens), BF16), pltpu.VMEM((tokens, width), BF16)]
-        + [pltpu.VMEM((slots, width), BF16), pltpu.SemaphoreType.DMA((4,))],
-        (1, 3),
-        (2, 3),
+        + [((TOP, tokens), jnp.int32), ((tokens, TOP), jnp.int32), ((share, width), BF16)]
+        + [(attn_out.shape[:1] + (tokens,), BF16), ((heads * tokens // SEQ, 1, SEQ), F32), (traded.shape, BF16)],
+        [pltpu.VMEM((ranks, share, width), BF16), pltpu.VMEM((width, share), BF16), pltpu.VMEM((width, tokens), BF16)]
+        + [pltpu.VMEM((tokens, width), BF16), pltpu.VMEM((slots, width), BF16), pltpu.SemaphoreType.DMA((4,))]
+        + [pltpu.SemaphoreType.DMA((2,))] * 2,
+        (4, 6, 8),
+        (2, 3, 9),
     )
     rows, row_grads, gate_rows, gates = dispatch(code, routes_t, router.T, h2, dy_rows)
     ret, back, *weight_grads = run_experts(
-        rows, row_grads, expert_gate, expert_up, expert_down, traded
+        rows, row_grads, expert_gate, expert_up, expert_down, traded, traded_too
     )
     grad_attn, grad_resid, grad_gain_two, grad_router, partial_y = exchange_call(
         norm_two_back_kernel, 3, (tokens, width),

time: 679 us -> 670 us (0.987)
  Pallas kernels: 643 us -> 635 us
    pallas_call x2 -> x1, Pallas kernels: 301 us -> 277 us  [run_experts(): pl.pallas_call(expert_kernel, in_specs=[anywhere] * 7, out_specs=[anywher...]
    pallas_call x3, Pallas kernels: 248 us -> 263 us  [exchange_call(): pl.pallas_call(kernel, in_specs=[pl.BlockSpec(memory_space=pl.ANY) if k i...]
  transfers between devices with their start and end apart: 4 -> 4, of which waited for: 0 -> 1; matrix products, arithmetic and copies ran while one was open for 0% -> 1% of each run, Pallas kernels for 22% -> 19%
where the time goes in v10:
time: 670 us; the launch traced here: 662 us
  Pallas kernels  635 us (95%)
  between operations  14.6 us (2%)
    pallas_call x1, Pallas kernels, run_experts(): pl.pallas_call(expert_kernel, in_specs=[anywhere] * 7, out_specs=[anywher...  277 us
    pallas_call x3, Pallas kernels, exchange_call(): pl.pallas_call(kernel, in_specs=[pl.BlockSpec(memory_space=pl.ANY) if k i...  263 us
    pallas_call x1, Pallas kernels, attend_back(): pl.pallas_call(attend_back_kernel, grid=(seqs, heads), in_specs=[pl.Block...  37.5 us
    pallas_call x1, Pallas kernels, project_back(): pl.pallas_call(project_back_kernel, grid=(steps,), in_specs=[pl.BlockSpec...  22.6 us
  transfers between devices with their start and end apart: 4, of which 1 were waited for; matrix products, arithmetic and copies ran while one was open for 1% of the time, Pallas kernels for 19%

profile of v10, /device:TPU:0, one launch (start us, length us, event | category | flops | bytes accessed | tf_op | source)
XLA Modules:
  0.0 661.6 jit_solution(14106050956392105406)
XLA Ops:
  7.2 0.0 copy-start.2
  7.2 0.0 all-reduce.2.cloned.1.call-start
  7.3 1.2 dynamic-slice_bitcast_fusion
  8.4 3.0 collective-permute-start
  11.4 1.7 copy.30.gain_ref
  13.1 1.4 copy.29.table_ref
  14.5 3.2 shard_map.213.tiles_ref
  17.7 0.6 pad_add_fusion.place_ref
  18.3 0.0 copy-done.2
  18.3 0.1 fusion
  18.4 0.6 iota_maximum_fusion.limit_ref
  19.0 8.3 %shard_map.212 = (bf16[768,2048]{1,0:T(8,128)(2,1)}, f32[1,2048]{1,0:T(1,128)}) custom-call(bf16[1024,2048]{1,0:T(8,128)(2,1)} %x_ref.5, f32[1024,1]{1,0:T(8,128)} %copy.30.gain_ref, bf16[768,1024]{1,0:T(8,128)(2,1)} %bitcast.40), custom_call_target="tpu_custom_call" | custom-call | flops 3221225472 | bytes 8388608 | tf_op jit(solution)/shard_map/pallas_call | solution.py:64
  27.3 0.2 collective-permute-done.far_gate
  27.6 0.0 copy-start.3
  27.6 90.8 %shard_map.214 = (bf16[4,512,1024]{2,1,0:T(8,128)(2,1)}, f32[512,1024]{1,0:T(8,128)}, f32[512,1]{1,0:T(8,128)}, bf16[2048,1024]{1,0:T(8,128)(2,1)}, bf16[1280,10...) custom-call(bf16[768,2048]{1,0:T(8,128)(2,1)} %get-tuple-element.75., ...), custom_call_target="tpu_custom_call" | custom-call | flops 41943040 | bytes 209715200 | tf_op jit(solution)/shard_map/pallas_call | solution.py:557
  118.4 0.0 copy-done.3
  118.4 11.5 %shard_map.215 = (bf16[1280,1024]{1,0:T(8,128)(2,1)}, bf16[1280,1024]{1,0:T(8,128)(2,1)}, f32[1280,1]{1,0:T(8,128)}, f32[2,2048]{1,0:T(2,128)}) custom-call(s32[2,2048]{1,0:T(2,128)} %get-tuple-element.77.code_ref, s32[2,2048]{1,0:T(2,128)} %bitcast.27, bf16[16,1024]{1,0:T(8,128)(2,1)} %bitcast.29, bf16[2048,1024]{1,0:T(8,128)(2,1)} %bitcast.21, ...), custom_call_target="tpu_custom_call" | custom-call | flops 5368709120 | bytes 12058624 | tf_op jit(solution)/shard_map/pallas_call | solution.py:886
  129.9 276.8 %shard_map.216 = (bf16[1280,1024]{1,0:T(8,128)(2,1)}, bf16[1280,1024]{1,0:T(8,128)(2,1)}, f32[704,1024]{1,0:T(8,128)}, f32[704,1024]{1,0:T(8,128)}, f32[704,1024...) custom-call(bf16[1280,1024]{1,0:T(8,128)(2,1)} %get-tuple-element.80.rows_in, ...), custom_call_target="tpu_custom_call" | custom-call | flops 66437775360 | bytes 42598400 | tf_op jit(solution)/shard_map/pallas_call | solution.py:1107
  406.7 80.7 %shard_map.217 = (bf16[4,512,1024]{2,1,0:T(8,128)(2,1)}, f32[512,1024]{1,0:T(8,128)}, f32[1,1024]{1,0:T(1,128)}, f32[16,1024]{1,0:T(8,128)}, bf16[2048,1024]{1,0:T(8,128)(2,1)}) custom-call(bf16[1280,1024]{1,0:T(8,128)(2,1)} %get-tuple-element.84.ret_in, bf16[1280,1024]{1,0:T(8,128)(2,1)} %get-tuple-element.85.back_ref, ...), custom_call_target="tpu_custom_call" | custom-call | flops 41943040 | bytes 209715200 | tf_op jit(solution)/shard_map/pallas_call | solution.py:557
  487.4 37.5 %shard_map.218 = (bf16[256,2048]{1,0:T(8,128)(2,1)}, bf16[256,2048]{1,0:T(8,128)(2,1)}, bf16[256,2048]{1,0:T(8,128)(2,1)}, f32[8,3,256,256]{3,2,1,0:T(8,128)}, f...) custom-call(bf16[768,2048]{1,0:T(8,128)(2,1)} %get-tuple-element.75.qkv_ref.q_ref.k_ref.v_ref, ...), custom_call_target="tpu_custom_call" | custom-call | flops 10737418240 | bytes 33554432 | tf_op jit(solution)/shard_map/pallas_call | solution.py:308
  524.9 0.7 collective-permute-start.1
  525.6 1.4 collective-permute-start.2
  527.0 22.6 %shard_map.219 = (bf16[1024,1024]{1,0:T(8,128)(2,1)}, bf16[2048,1024]{1,0:T(8,128)(2,1)}, f32[1,1024]{1,0:T(1,128)}, f32[2,704,1024]{2,1,0:T(8,128)}, f32[2,704,1024]{2,1,0:T(8,128)}, /*index=5*/f32[2,704,1024]{2,1,0:T(8,128)}) custom-call(s32[2]{0:T(128)} %pad_add_fusion.place_ref, bf16[1024,2048]{1,0:T(8,128)(2,1)} %x_ref.5, f32[1024,1]{1,0:T(8,128)} %copy.30.gain_ref, ...), custom_call_target="tpu_custom_call" | custom-call | flops 8053063680 | bytes 22675456 | tf_op jit(solution)/shard_map/pallas_call | solution.py:393
  549.7 0.0 all-reduce.2.cloned.1.call-update
  549.7 0.0 collective-permute-done.1.y_across
  549.7 0.0 copy-start
  549.7 0.0 collective-permute-done.2.y_along
  549.7 0.0 copy-start.1
  549.7 0.9 copy-done
  550.7 0.3 copy-done.1
  551.0 91.7 %shard_map.220 = (bf16[4,512,1024]{2,1,0:T(8,128)(2,1)}, bf16[4,512,1024]{2,1,0:T(8,128)(2,1)}, f32[32,1024]{1,0:T(8,128)}) custom-call(bf16[4,512,1024]{2,1,0:T(8,128)(2,1)} %bitcast.23, bf16[512,1024]{1,0:T(8,128)(2,1)} %get-tuple-element.110.x_in, f32[1,2048]{1,0:T(1,128)} %get-tuple-element.73.scale_ref, f32[512,1024]{1,0:T(8,128)} %get-tuple-element.111.grad_in, ...), custom_call_target="tpu_custom_call" | custom-call | flops 41943040 | bytes 209715200 | tf_op jit(solution)/shard_map/pallas_call | solution.py:557
  642.7 0.0 all-reduce.2.cloned.1.call-done.summed_ref
  642.7 11.6 %shard_map.221 = (bf16[1024,2048]{1,0:T(8,128)(2,1)}, f32[1024,2048]{1,0:T(8,128)}, f32[768,1024]{1,0:T(8,128)}, f32[256,1024]{1,0:T(8,128)}, f32[1,1024]{1,0:T(...) custom-call(bf16[2048,1024]{1,0:T(8,128)(2,1)} %bitcast.24, bf16[2048,1024]{1,0:T(8,128)(2,1)} %bitcast.25, ...), custom_call_target="tpu_custom_call" | custom-call | bytes 27262976 | tf_op jit(solution)/shard_map/pallas_call | solution.py:1160
  (1 shorter events, 0.0 us)
Async XLA Ops:
  7.2 11.1 %copy-start.2 = (s32[2,2]{1,0:T(2,128)S(1)}, s32[2,2]{1,0:T(2,128)}, u32[]{:S(2)}) copy-start(s32[2,2]{1,0:T(2,128)} %param.24) | copy-start | bytes 52
  7.2 635.5 %all-reduce.2.cloned.1.call-start = ((), (), s32[]{:S(2)}) async-start(), calls=%async_computation | async-start | bytes 4194304 | tf_op jit(solution)/shard_map/psum | solution.py:1274
  8.4 19.1 %collective-permute-start = (bf16[352,1024]{1,0:T(8,128)(2,1)S(1)}, bf16[352,1024]{1,0:T(8,128)(2,1)S(1)}, u32[]{:S(2)}, u32[]{:S(2)}) collective-permute-start(bf16[352,1024]{1,0:T(8,128)(2,1)S(1)} %dynamic-slice_bitcast_fusion), channel_id=1, source_target_pairs={{0,1},{1,0},{2,3},{3,2},{4,5},{5,4},{6,7},{7,6},{8,9},{9,8},{10,11... | collective-permute-start | bytes 2162696 | tf_op jit(solution)/shard_map/ppermute | solution.py:1207
  27.6 90.8 %copy-start.3 = (bf16[352,1024]{1,0:T(8,128)(2,1)}, bf16[352,1024]{1,0:T(8,128)(2,1)S(1)}, u32[]{:S(2)}) copy-start(bf16[352,1024]{1,0:T(8,128)(2,1)S(1)} %collective-permute-done.far_gate) | copy-start | bytes 2162692
  524.9 24.7 %collective-permute-start.1 = (bf16[512,1024]{1,0:T(8,128)(2,1)}, bf16[512,1024]{1,0:T(8,128)(2,1)S(1)}, u32[]{:S(2)}, u32[]{:S(2)}) collective-permute-start(bf16[512,1024]{1,0:T(8,128)(2,1)} %get-tuple-element.108.y_own), channel_id=1, source_target_pairs={{0,1},{1,0},{2,3},{3,2},{4,5},{5,4},{6,7},{7,6},{8,9},{9,8},{10,11... | collective-permute-start | bytes 3145736 | tf_op jit(solution)/shard_map/ppermute | solution.py:1267
  525.6 24.1 %collective-permute-start.2 = (bf16[512,1024]{1,0:T(8,128)(2,1)}, bf16[512,1024]{1,0:T(8,128)(2,1)S(1)}, u32[]{:S(2)}, u32[]{:S(2)}) collective-permute-start(bf16[512,1024]{1,0:T(8,128)(2,1)} %get-tuple-element.108.y_own), channel_id=1, source_target_pairs={{0,2},{1,3},{2,0},{3,1},{4,6},{5,7},{6,4},{7,5},{8,10},{9,11},{10,... | collective-permute-start | bytes 3145736 | tf_op jit(solution)/shard_map/ppermute | solution.py:1268
  549.7 1.0 copy-start
  549.7 1.3 copy-start.1
Sparse Core Ops, SparseCore 0:
  549.8 73.2 all-reduce.1

commit v11 on v10

--- a/solution.py
+++ b/solution.py
@@ -915,7 +915,7 @@
 def expert_kernel(
     rows_in, grads_in, gate_in, up_in, down_in, far_gate, far_gate_too,
     ret_out, back_out, own_gate, own_up, own_down, got_gate, got_up, got_down,
-    rows, grads, weights, sums, parts, z_send, z_recv, y_send, y_recv, p_send, p_recv, r_send, r_recv, w_send, w_recv, g_send, g_recv, local,
+    rows, grads, weights, sums, parts, opened, z_send, z_recv, y_send, y_recv, p_send, p_recv, r_send, r_recv, w_send, w_recv, g_send, g_recv, local,
 ):
     groups, half, width = rows.shape[1:]
     group, rank = lax.axis_index("expert"), lax.axis_index("tensor")
@@ -1023,19 +1023,22 @@
         for action, step in plan:
             action(step)
 
-    order = (0, 1, 4, 5, 2, 6, 3, 7)
+    order = ((0, 0, 0), (1, 0, 1), (2, 0, 2), (3, 0, 3), (2, 1, 2), (4, 0, 2), (4, 1, 2), (5, 0, 2), (5, 1, 2), (3, 1, 3), (1, 1, 1), (0, 1, 0), (6, 0, 0), (6, 1, 0), (7, 0, 0), (7, 1, 0))
     before = {
-        0: [(arrive, 1), (arrive, 2), (arrive, 3), (arrive, 4)],
-        1: [(give, 0)],
-        2: [(arrive, 5)],
-        3: [(give, 4), (finish, 0)],
-        4: [(arrive, 6)],
-        5: [(give, 5), (finish, 4)],
-        6: [(arrive, 7)],
-        7: [(give, 6), (finish, 5)],
+        0: [(arrive, 1), (arrive, 2)],
+        1: [(arrive, 3)],
+        2: [(arrive, 4)],
+        3: [(arrive, 5)],
+        5: [(give, 2)],
+        7: [(give, 4)],
+        8: [(arrive, 6)],
+        10: [(finish, 2)],
+        12: [(arrive, 7), (finish, 4), (give, 5)],
+        14: [(give, 6)],
     }
     ahead = [(give, 7)]
-    last = [(give, 2), (finish, 6), (give, 3), (finish, 7), (give, 1), (finish, 2), (finish, 3), (finish, 1)]
+    last = [(finish, 5), (give, 3), (finish, 6), (give, 1), (finish, 7), (give, 0), (finish, 3), (finish, 1), (finish, 0)]
+    first_far = [part for _, part, _ in order].index(1)
     for copy in own:
         copy.wait()
     for kind in range(2):
@@ -1047,39 +1050,55 @@
 
         @pl.when(turn == 0)
         def _():
-            for copy in kept:
+            for copy in kept[:3]:
                 copy.wait()
 
-        step = sum((turn == number).astype(jnp.int32) * which for number, which in enumerate(order))
-        for kind in range(2):
-            forward(kind, step).wait()
+        @pl.when(turn == first_far)
+        def _():
+            for copy in kept[3:]:
+                copy.wait()
+
+        step, part, place = (
+            sum((turn == number).astype(jnp.int32) * unit[k] for number, unit in enumerate(order)) for k in range(3)
+        )
         other = partner_of(group, step)
+
+        @pl.when(part == 0)
+        def _():
+            for kind in range(2):
+                forward(kind, step).wait()
+
         tile = jnp.concatenate([rows[0, other], rows[1, other]], axis=0)
         grad = jnp.concatenate([grads[0, other], grads[1, other]], axis=0)
-        ret = jnp.zeros(tile.shape, F32)
-        back = jnp.zeros(tile.shape, F32)
-        for part in range(2):
-            w_gate, w_up, w_down = weights[0, part], weights[1, part], weights[2, part]
-            gate_part = mm(tile, w_gate, NT)
-            up_part = mm(tile, w_up, NT)
-            grad_hidden = mm(grad, w_down, NT)
-            bent, slope = gelu_parts(gate_part)
-            hidden = (bent * up_part).astype(BF16)
-            grad_gate = (grad_hidden * up_part * slope).astype(BF16)
-            grad_up = (grad_hidden * bent).astype(BF16)
-            ret = ret + mm(hidden, w_down)
-            back = back + mm(grad_gate, w_gate) + mm(grad_up, w_up)
-            sums[0, part] += mm(grad_gate, tile, TN)
-            sums[1, part] += mm(grad_up, tile, TN)
-            sums[2, part] += mm(hidden, grad, TN)
-        for kind, value in enumerate((ret, back)):
-            held = moved[kind][1]
-            held[0, other] = value[:half].astype(BF16)
-            held[1, other] = value[half:].astype(BF16)
+        w_gate, w_up, w_down = weights[0, part], weights[1, part], weights[2, part]
+        gate_part = mm(tile, w_gate, NT)
+        up_part = mm(tile, w_up, NT)
+        grad_hidden = mm(grad, w_down, NT)
+        bent, slope = gelu_parts(gate_part)
+        hidden = (bent * up_part).astype(BF16)
+        grad_gate = (grad_hidden * up_part * slope).astype(BF16)
+        grad_up = (grad_hidden * bent).astype(BF16)
+        results = mm(hidden, w_down), mm(grad_gate, w_gate) + mm(grad_up, w_up)
+        sums[0, part] += mm(grad_gate, tile, TN)
+        sums[1, part] += mm(grad_up, tile, TN)
+        sums[2, part] += mm(hidden, grad, TN)
+
+        @pl.when(part == 0)
+        def _():
+            for kind, value in enumerate(results):
+                opened[place, kind] = value.astype(BF16)
+
+        @pl.when(part == 1)
+        def _():
+            for kind, value in enumerate(results):
+                held = moved[kind][1]
+                value = value + opened[place, kind].astype(F32)
+                held[0, other] = value[:half].astype(BF16)
+                held[1, other] = value[half:].astype(BF16)
 
         return carry
 
-    lax.fori_loop(0, groups, body, 0)
+    lax.fori_loop(0, len(order), body, 0)
     act(ahead)
     copies = []
     for number, (own_ref, got_ref) in enumerate(((own_gate, got_gate), (own_up, got_up), (own_down, got_down))):
@@ -1117,6 +1136,7 @@
             pltpu.VMEM((3, 2, units, width), BF16),
             pltpu.VMEM((3, 2, units, width), F32),
             pltpu.VMEM((2, groups, half, width), BF16),
+            pltpu.VMEM((4, 2, 2 * half, width), BF16),
         ]
         + [pair] * 8
         + [pltpu.SemaphoreType.DMA((2,))] * 2

time: 670 us -> 657 us (0.981)
  Pallas kernels: 635 us -> 622 us
    pallas_call x1, Pallas kernels: 277 us -> 249 us  [run_experts(): pl.pallas_call(expert_kernel, in_specs=[anywhere] * 7, out_specs=[anywher...]
    pallas_call x3, Pallas kernels: 263 us -> 276 us  [exchange_call(): pl.pallas_call(kernel, in_specs=[pl.BlockSpec(memory_space=pl.ANY) if k i...]
  transfers between devices with their start and end apart: 4 -> 4, of which waited for: 1 -> 1; matrix products, arithmetic and copies ran while one was open for 1% -> 1% of each run, Pallas kernels for 19% -> 22%
where the time goes in v11:
time: 657 us; the launch traced here: 648 us
  Pallas kernels  622 us (95%)
  between operations  14.6 us (2%)
    pallas_call x3, Pallas kernels, exchange_call(): pl.pallas_call(kernel, in_specs=[pl.BlockSpec(memory_space=pl.ANY) if k i...  276 us
    pallas_call x1, Pallas kernels, run_experts(): pl.pallas_call(expert_kernel, in_specs=[anywhere] * 7, out_specs=[anywher...  249 us
    pallas_call x1, Pallas kernels, attend_back(): pl.pallas_call(attend_back_kernel, grid=(seqs, heads), in_specs=[pl.Block...  38.5 us
    pallas_call x1, Pallas kernels, project_back(): pl.pallas_call(project_back_kernel, grid=(steps,), in_specs=[pl.BlockSpec...  22.6 us
  transfers between devices with their start and end apart: 4, of which 1 were waited for; matrix products, arithmetic and copies ran while one was open for 1% of the time, Pallas kernels for 22%

profile of v11, /device:TPU:0, one launch (start us, length us, event | category | flops | bytes accessed | tf_op | source)
XLA Modules:
  0.0 648.5 jit_solution(867400011900718129)
XLA Ops:
  7.2 0.0 copy-start.2
  7.2 0.0 all-reduce.2.cloned.1.call-start
  7.3 1.2 dynamic-slice_bitcast_fusion
  8.4 3.0 collective-permute-start
  11.4 1.7 copy.30.gain_ref
  13.1 1.4 copy.29.table_ref
  14.5 3.2 shard_map.213.tiles_ref
  17.7 0.6 pad_add_fusion.place_ref
  18.3 0.0 copy-done.2
  18.3 0.1 fusion
  18.4 0.6 iota_maximum_fusion.limit_ref
  19.0 8.3 %shard_map.212 = (bf16[768,2048]{1,0:T(8,128)(2,1)}, f32[1,2048]{1,0:T(1,128)}) custom-call(bf16[1024,2048]{1,0:T(8,128)(2,1)} %x_ref.5, f32[1024,1]{1,0:T(8,128)} %copy.30.gain_ref, bf16[768,1024]{1,0:T(8,128)(2,1)} %bitcast.40), custom_call_target="tpu_custom_call" | custom-call | flops 3221225472 | bytes 8388608 | tf_op jit(solution)/shard_map/pallas_call | solution.py:64
  27.3 0.2 collective-permute-done.far_gate
  27.6 0.0 copy-start.3
  27.6 90.8 %shard_map.214 = (bf16[4,512,1024]{2,1,0:T(8,128)(2,1)}, f32[512,1024]{1,0:T(8,128)}, f32[512,1]{1,0:T(8,128)}, bf16[2048,1024]{1,0:T(8,128)(2,1)}, bf16[1280,10...) custom-call(bf16[768,2048]{1,0:T(8,128)(2,1)} %get-tuple-element.75., ...), custom_call_target="tpu_custom_call" | custom-call | flops 41943040 | bytes 209715200 | tf_op jit(solution)/shard_map/pallas_call | solution.py:557
  118.4 0.0 copy-done.3
  118.4 11.9 %shard_map.215 = (bf16[1280,1024]{1,0:T(8,128)(2,1)}, bf16[1280,1024]{1,0:T(8,128)(2,1)}, f32[1280,1]{1,0:T(8,128)}, f32[2,2048]{1,0:T(2,128)}) custom-call(s32[2,2048]{1,0:T(2,128)} %get-tuple-element.77.code_ref, s32[2,2048]{1,0:T(2,128)} %bitcast.27, bf16[16,1024]{1,0:T(8,128)(2,1)} %bitcast.29, bf16[2048,1024]{1,0:T(8,128)(2,1)} %bitcast.21, ...), custom_call_target="tpu_custom_call" | custom-call | flops 5368709120 | bytes 12058624 | tf_op jit(solution)/shard_map/pallas_call | solution.py:886
  130.3 249.2 %shard_map.216 = (bf16[1280,1024]{1,0:T(8,128)(2,1)}, bf16[1280,1024]{1,0:T(8,128)(2,1)}, f32[704,1024]{1,0:T(8,128)}, f32[704,1024]{1,0:T(8,128)}, f32[704,1024...) custom-call(bf16[1280,1024]{1,0:T(8,128)(2,1)} %get-tuple-element.80.rows_in, ...), custom_call_target="tpu_custom_call" | custom-call | flops 66437775360 | bytes 42598400 | tf_op jit(solution)/shard_map/pallas_call | solution.py:1126
  379.6 77.7 %shard_map.217 = (bf16[4,512,1024]{2,1,0:T(8,128)(2,1)}, f32[512,1024]{1,0:T(8,128)}, f32[1,1024]{1,0:T(1,128)}, f32[16,1024]{1,0:T(8,128)}, bf16[2048,1024]{1,0:T(8,128)(2,1)}) custom-call(bf16[1280,1024]{1,0:T(8,128)(2,1)} %get-tuple-element.84.ret_in, bf16[1280,1024]{1,0:T(8,128)(2,1)} %get-tuple-element.85.back_ref, ...), custom_call_target="tpu_custom_call" | custom-call | flops 41943040 | bytes 209715200 | tf_op jit(solution)/shard_map/pallas_call | solution.py:557
  457.2 38.5 %shard_map.218 = (bf16[256,2048]{1,0:T(8,128)(2,1)}, bf16[256,2048]{1,0:T(8,128)(2,1)}, bf16[256,2048]{1,0:T(8,128)(2,1)}, f32[8,3,256,256]{3,2,1,0:T(8,128)}, f...) custom-call(bf16[768,2048]{1,0:T(8,128)(2,1)} %get-tuple-element.75.qkv_ref.q_ref.k_ref.v_ref, ...), custom_call_target="tpu_custom_call" | custom-call | flops 10737418240 | bytes 33554432 | tf_op jit(solution)/shard_map/pallas_call | solution.py:308
  495.7 0.5 collective-permute-start.1
  496.2 1.6 collective-permute-start.2
  497.8 22.6 %shard_map.219 = (bf16[1024,1024]{1,0:T(8,128)(2,1)}, bf16[2048,1024]{1,0:T(8,128)(2,1)}, f32[1,1024]{1,0:T(1,128)}, f32[2,704,1024]{2,1,0:T(8,128)}, f32[2,704,1024]{2,1,0:T(8,128)}, /*index=5*/f32[2,704,1024]{2,1,0:T(8,128)}) custom-call(s32[2]{0:T(128)} %pad_add_fusion.place_ref, bf16[1024,2048]{1,0:T(8,128)(2,1)} %x_ref.5, f32[1024,1]{1,0:T(8,128)} %copy.30.gain_ref, ...), custom_call_target="tpu_custom_call" | custom-call | flops 8053063680 | bytes 22675456 | tf_op jit(solution)/shard_map/pallas_call | solution.py:393
  520.4 0.0 all-reduce.2.cloned.1.call-update
  520.5 0.0 collective-permute-done.1.y_across
  520.5 0.0 copy-start
  520.5 0.0 collective-permute-done.2.y_along
  520.5 0.0 copy-start.1
  520.5 0.9 copy-done
  521.4 0.3 copy-done.1
  521.8 107.8 %shard_map.220 = (bf16[4,512,1024]{2,1,0:T(8,128)(2,1)}, bf16[4,512,1024]{2,1,0:T(8,128)(2,1)}, f32[32,1024]{1,0:T(8,128)}) custom-call(bf16[4,512,1024]{2,1,0:T(8,128)(2,1)} %bitcast.23, bf16[512,1024]{1,0:T(8,128)(2,1)} %get-tuple-element.110.x_in, f32[1,2048]{1,0:T(1,128)} %get-tuple-element.73.scale_ref, f32[512,1024]{1,0:T(8,128)} %get-tuple-element.111.grad_in, ...), custom_call_target="tpu_custom_call" | custom-call | flops 41943040 | bytes 209715200 | tf_op jit(solution)/shard_map/pallas_call | solution.py:557
  629.6 0.0 all-reduce.2.cloned.1.call-done.summed_ref
  629.6 11.6 %shard_map.221 = (bf16[1024,2048]{1,0:T(8,128)(2,1)}, f32[1024,2048]{1,0:T(8,128)}, f32[768,1024]{1,0:T(8,128)}, f32[256,1024]{1,0:T(8,128)}, f32[1,1024]{1,0:T(...) custom-call(bf16[2048,1024]{1,0:T(8,128)(2,1)} %bitcast.24, bf16[2048,1024]{1,0:T(8,128)(2,1)} %bitcast.25, ...), custom_call_target="tpu_custom_call" | custom-call | bytes 27262976 | tf_op jit(solution)/shard_map/pallas_call | solution.py:1180
  (1 shorter events, 0.0 us)
Async XLA Ops:
  7.2 11.1 %copy-start.2 = (s32[2,2]{1,0:T(2,128)S(1)}, s32[2,2]{1,0:T(2,128)}, u32[]{:S(2)}) copy-start(s32[2,2]{1,0:T(2,128)} %param.24) | copy-start | bytes 52
  7.2 622.4 %all-reduce.2.cloned.1.call-start = ((), (), s32[]{:S(2)}) async-start(), calls=%async_computation | async-start | bytes 4194304 | tf_op jit(solution)/shard_map/psum | solution.py:1294
  8.4 19.1 %collective-permute-start = (bf16[352,1024]{1,0:T(8,128)(2,1)S(1)}, bf16[352,1024]{1,0:T(8,128)(2,1)S(1)}, u32[]{:S(2)}, u32[]{:S(2)}) collective-permute-start(bf16[352,1024]{1,0:T(8,128)(2,1)S(1)} %dynamic-slice_bitcast_fusion), channel_id=1, source_target_pairs={{0,1},{1,0},{2,3},{3,2},{4,5},{5,4},{6,7},{7,6},{8,9},{9,8},{10,11... | collective-permute-start | bytes 2162696 | tf_op jit(solution)/shard_map/ppermute | solution.py:1227
  27.6 90.8 %copy-start.3 = (bf16[352,1024]{1,0:T(8,128)(2,1)}, bf16[352,1024]{1,0:T(8,128)(2,1)S(1)}, u32[]{:S(2)}) copy-start(bf16[352,1024]{1,0:T(8,128)(2,1)S(1)} %collective-permute-done.far_gate) | copy-start | bytes 2162692
  495.7 24.7 %collective-permute-start.1 = (bf16[512,1024]{1,0:T(8,128)(2,1)}, bf16[512,1024]{1,0:T(8,128)(2,1)S(1)}, u32[]{:S(2)}, u32[]{:S(2)}) collective-permute-start(bf16[512,1024]{1,0:T(8,128)(2,1)} %get-tuple-element.108.y_own), channel_id=1, source_target_pairs={{0,1},{1,0},{2,3},{3,2},{4,5},{5,4},{6,7},{7,6},{8,9},{9,8},{10,11... | collective-permute-start | bytes 3145736 | tf_op jit(solution)/shard_map/ppermute | solution.py:1287
  496.2 24.3 %collective-permute-start.2 = (bf16[512,1024]{1,0:T(8,128)(2,1)}, bf16[512,1024]{1,0:T(8,128)(2,1)S(1)}, u32[]{:S(2)}, u32[]{:S(2)}) collective-permute-start(bf16[512,1024]{1,0:T(8,128)(2,1)} %get-tuple-element.108.y_own), channel_id=1, source_target_pairs={{0,2},{1,3},{2,0},{3,1},{4,6},{5,7},{6,4},{7,5},{8,10},{9,11},{10,... | collective-permute-start | bytes 3145736 | tf_op jit(solution)/shard_map/ppermute | solution.py:1288
  520.5 1.0 copy-start
  520.5 1.3 copy-start.1
Sparse Core Ops, SparseCore 0:
  520.6 89.7 all-reduce.1

commit v12 on v11

--- a/solution.py
+++ b/solution.py
@@ -49,37 +49,46 @@
     return lower_part + 16 * (offset > 0).astype(jnp.int32)
 
 
-def project_kernel(x_ref, gain_ref, w_ref, out_ref, scale_ref):
+def as_column(line):
+    return jnp.broadcast_to(line, (8, line.shape[1])).T[:, :1]
+
+
+def project_kernel(x_ref, gain_ref, w_ref, table_ref, out_ref, scale_ref, tiles_ref):
     x = x_ref[...].astype(F32)
     scale = lax.rsqrt(jnp.sum(x * x, axis=0, keepdims=True) / x.shape[0] + EPS)
-    normed = (x * scale * gain_ref[...]).astype(BF16)
+    normed = (x * scale * as_column(gain_ref[...])).astype(BF16)
     out_ref[...] = mm(w_ref[...], normed).astype(BF16)
     scale_ref[...] = scale
-
-
-def project(x, gain, weights):
+    bias_tiles(table_ref, pl.program_id(0), tiles_ref)
+
+
+def project(x, gain, weights, table):
     width, tokens = x.shape
     rows = weights.shape[0]
-    tile = 512
+    heads = table.shape[0]
+    tile = tokens // heads
     return pl.pallas_call(
         project_kernel,
-        grid=(tokens // tile,),
+        grid=(heads,),
         in_specs=[
             pl.BlockSpec((width, tile), lambda i: (0, i)),
-            pl.BlockSpec((width, 1), lambda i: (0, 0)),
+            pl.BlockSpec((1, width), lambda i: (0, 0)),
             pl.BlockSpec((rows, width), lambda i: (0, 0)),
+            pl.BlockSpec(memory_space=pltpu.SMEM),
         ],
         out_specs=[
             pl.BlockSpec((rows, tile), lambda i: (0, i)),
             pl.BlockSpec((1, tile), lambda i: (0, i)),
+            pl.BlockSpec((1, 3, BLK, BLK), lambda i: (i, 0, 0, 0)),
         ],
         out_shape=[
             jax.ShapeDtypeStruct((rows, tokens), BF16),
             jax.ShapeDtypeStruct((1, tokens), F32),
+            jax.ShapeDtypeStruct((heads, 3, BLK, BLK), F32),
         ],
         compiler_params=params(),
         cost_estimate=cost(2 * width * tokens * rows, 2 * width * tokens * 2),
-    )(x, gain, weights)
+    )(x, gain, weights, table)
 
 
 def line_offsets(number):
@@ -87,33 +96,20 @@
     return (number - 1) * BLK - column
 
 
-def bias_tiles_kernel(table_ref, tiles_ref):
+def bias_tiles(table_ref, head, tiles_ref):
     row = lax.broadcasted_iota(jnp.int32, (BLK, BLK), 0)
     column = lax.broadcasted_iota(jnp.int32, (BLK, BLK), 1)
-    buckets = [bucket_of(line_offsets(number)) for number in range(4)]
-    for head in range(tiles_ref.shape[0]):
-        far = table_ref[15, head]
-        rolled = []
-        for number, bucket in enumerate(buckets):
-            value = jnp.zeros((8, BLK), F32)
-            for index in range(BUCKETS):
-                value = jnp.where(bucket == index, table_ref[index, head] - far, value)
-            whole = jnp.broadcast_to(value[0:1], (BLK, BLK))
-            rolled.append(pltpu.roll(whole, 0, 1, stride=1, stride_axis=0))
-        for number in range(3):
-            tiles_ref[head, number] = jnp.where(column >= row, rolled[number], rolled[number + 1])
-
-
-def bias_tiles(table):
-    heads = table.shape[1]
-    return pl.pallas_call(
-        bias_tiles_kernel,
-        in_specs=[pl.BlockSpec(memory_space=pltpu.SMEM)],
-        out_specs=pl.BlockSpec(memory_space=pltpu.VMEM),
-        out_shape=jax.ShapeDtypeStruct((heads, 3, BLK, BLK), F32),
-        compiler_params=params(),
-        cost_estimate=cost(heads * 3 * BLK * BLK * 60, heads * 3 * BLK * BLK * 4),
-    )(table)
+    far = table_ref[head, 15]
+    rolled = []
+    for number in range(4):
+        bucket = bucket_of(line_offsets(number))
+        value = jnp.zeros((8, BLK), F32)
+        for index in range(BUCKETS):
+            value = jnp.where(bucket == index, table_ref[head, index] - far, value)
+        whole = jnp.broadcast_to(value[0:1], (BLK, BLK))
+        rolled.append(pltpu.roll(whole, 0, 1, stride=1, stride_axis=0))
+    for number in range(3):
+        tiles_ref[0, number] = jnp.where(column >= row, rolled[number], rolled[number + 1])
 
 
 def bias_fold(near_ref, far_ref):
@@ -353,7 +349,7 @@
 
 
 def project_back_kernel(
-    place_ref, x_ref, gain_ref, gain_row_ref, scale_ref, w_ref, mixed_ref, attn_ref, dq_ref, dk_ref, dv_ref, *refs
+    place_ref, x_ref, gain_ref, scale_ref, w_ref, mixed_ref, attn_ref, dq_ref, dk_ref, dv_ref, *refs
 ):
     step = pl.program_id(0)
     own_refs, got_refs, (weight_ref, out_ref, gain_grad_ref), placed_refs, total = (
@@ -364,7 +360,7 @@
         placed_ref[1 - place_ref[0]] = got_ref[...].astype(F32)
     grads = jnp.concatenate([dq_ref[...], dk_ref[...], dv_ref[...]], axis=0)
     rows = grads.shape[0]
-    normed = (x_ref[...].astype(F32) * scale_ref[...] * gain_ref[...]).astype(BF16)
+    normed = (x_ref[...].astype(F32) * scale_ref[...] * as_column(gain_ref[...])).astype(BF16)
 
     @pl.when(step == 0)
     def _():
@@ -378,10 +374,10 @@
     def _():
         weight_ref[...] = total[...].astype(BF16)
         through = jnp.sum(total[:rows] * w_ref[...].astype(F32), axis=0, keepdims=True)
-        gain_grad_ref[...] = through / gain_row_ref[...]
-
-
-def project_back(place, x, gain, gain_row, scale, weights, mixed, grad_attn, grads, owns, gots):
+        gain_grad_ref[...] = through / gain_ref[...]
+
+
+def project_back(place, x, gain, scale, weights, mixed, grad_attn, grads, owns, gots):
     width, tokens = x.shape
     rows = weights.shape[0]
     heads_width = mixed.shape[0]
@@ -396,7 +392,6 @@
         in_specs=[
             pl.BlockSpec(memory_space=pltpu.SMEM),
             column(width),
-            pl.BlockSpec((width, 1), lambda i: (0, 0)),
             pl.BlockSpec((1, width), lambda i: (0, 0)),
             column(1),
             pl.BlockSpec((rows, width), lambda i: (0, 0)),
@@ -420,7 +415,7 @@
         scratch_shapes=[pltpu.VMEM((rows + heads_width, width), F32)],
         compiler_params=params(),
         cost_estimate=cost(5 * width * tokens * rows, 6 * width * tokens + 14 * units * width),
-    )(place, x, gain, gain_row, scale, weights, mixed, grad_attn, *grads, *owns, *gots)
+    )(place, x, gain, scale, weights, mixed, grad_attn, *grads, *owns, *gots)
 
 
 def exchange(
@@ -1225,10 +1220,8 @@
     units = expert_gate.shape[1]
     other = lax.dynamic_slice(expert_gate, (1 - pair_class, 0, 0), (1, units // 2, width))[0]
     traded = lax.ppermute(other, "tensor", [(r, r ^ 1) for r in range(ranks)])
-    gain_col = gain_one[:, None]
     w_in = attn_in.reshape(-1, width)
-    qkv, scale_one = project(layer_input, gain_col, w_in)
-    tiles = bias_tiles(rel_bias)
+    qkv, scale_one, tiles = project(layer_input, gain_one[None], w_in, rel_bias.T)
     position = jnp.arange(SEQ, dtype=jnp.int32)[None, None, :]
     starts = piece_starts[:, :, None]
     inside = (position >= starts) & (position < starts + PIECE)
@@ -1287,7 +1280,7 @@
     y_across = lax.ppermute(y_own, "tensor", [(r, r ^ 1) for r in range(ranks)])
     y_along = lax.ppermute(y_own, "tensor", [(r, r ^ 2) for r in range(ranks)])
     weight_rows, sent, grad_gain_one, grad_gate, grad_up, grad_down = project_back(
-        place, layer_input, gain_col, gain_one[None], scale_one, w_in, mixed, grad_attn, (dq, dk, dv),
+        place, layer_input, gain_one[None], scale_one, w_in, mixed, grad_attn, (dq, dk, dv),
         weight_grads[:3], weight_grads[3:],
     )
     sent, y_across, y_along = lax.optimization_barrier((sent, y_across, y_along))

time: 657 us -> 657 us (level)
  transfers between devices with their start and end apart: 4 -> 4, of which waited for: 1 -> 1; matrix products, arithmetic and copies ran while one was open for 1% -> 0% of each run, Pallas kernels for 22% -> 21%
where the time goes in v12:
time: 657 us; the launch traced here: 649 us
  Pallas kernels  619 us (94%)
  between operations  14.6 us (2%)
    pallas_call x3, Pallas kernels, exchange_call(): pl.pallas_call(kernel, in_specs=[pl.BlockSpec(memory_space=pl.ANY) if k i...  276 us
    pallas_call x1, Pallas kernels, run_experts(): pl.pallas_call(expert_kernel, in_specs=[anywhere] * 7, out_specs=[anywher...  249 us
    pallas_call x1, Pallas kernels, attend_back(): pl.pallas_call(attend_back_kernel, grid=(seqs, heads), in_specs=[pl.Block...  38.5 us
    pallas_call x1, Pallas kernels, project_back(): pl.pallas_call(project_back_kernel, grid=(steps,), in_specs=[pl.BlockSpec...  23 us
  transfers between devices with their start and end apart: 4, of which 1 were waited for; matrix products, arithmetic and copies ran while one was open for 0% of the time, Pallas kernels for 21%

profile of v12, /device:TPU:0, one launch (start us, length us, event | category | flops | bytes accessed | tf_op | source)
XLA Modules:
  0.0 648.9 jit_solution(13816242999152254059)
XLA Ops:
  7.2 0.0 all-reduce.2.cloned.1.call-start
  7.2 1.2 dynamic-slice_bitcast_fusion
  8.4 3.0 collective-permute-start
  11.4 0.6 pad_add_fusion.place_ref
  12.0 0.7 broadcast_add_fusion.1
  12.7 0.8 fusion
  13.5 0.6 iota_maximum_fusion.limit_ref
  14.1 8.6 %shard_map.212 = (bf16[768,2048]{1,0:T(8,128)(2,1)}, f32[1,2048]{1,0:T(1,128)}, f32[4,3,256,256]{3,2,1,0:T(8,128)}) custom-call(bf16[1024,2048]{1,0:T(8,128)(2,1)} %x_ref.5, f32[1,1024]{1,0:T(1,128)} %bitcast.33, bf16[768,1024]{1,0:T(8,128)(2,1)} %bitcast.40, f32[4,32]{1,0:T(4,128)} %bitcast.45), custom_call_target="tpu_custom_call" | custom-call | flops 3221225472 | bytes 8388608 | tf_op jit(solution)/shard_map/pallas_call | solution.py:70
  22.7 4.9 collective-permute-done.far_gate
  27.5 0.0 copy-start.2
  27.5 90.8 %shard_map.213 = (bf16[4,512,1024]{2,1,0:T(8,128)(2,1)}, f32[512,1024]{1,0:T(8,128)}, f32[512,1]{1,0:T(8,128)}, bf16[2048,1024]{1,0:T(8,128)(2,1)}, bf16[1280,10...) custom-call(bf16[768,2048]{1,0:T(8,128)(2,1)} %get-tuple-element.76., ...), custom_call_target="tpu_custom_call" | custom-call | flops 41943040 | bytes 209715200 | tf_op jit(solution)/shard_map/pallas_call | solution.py:552
  118.4 0.0 copy-done.2
  118.4 11.9 %shard_map.214 = (bf16[1280,1024]{1,0:T(8,128)(2,1)}, bf16[1280,1024]{1,0:T(8,128)(2,1)}, f32[1280,1]{1,0:T(8,128)}, f32[2,2048]{1,0:T(2,128)}) custom-call(s32[2,2048]{1,0:T(2,128)} %get-tuple-element.79.code_ref, s32[2,2048]{1,0:T(2,128)} %bitcast.27, bf16[16,1024]{1,0:T(8,128)(2,1)} %bitcast.29, bf16[2048,1024]{1,0:T(8,128)(2,1)} %bitcast.21, ...), custom_call_target="tpu_custom_call" | custom-call | flops 5368709120 | bytes 12058624 | tf_op jit(solution)/shard_map/pallas_call | solution.py:881
  130.3 249.3 %shard_map.215 = (bf16[1280,1024]{1,0:T(8,128)(2,1)}, bf16[1280,1024]{1,0:T(8,128)(2,1)}, f32[704,1024]{1,0:T(8,128)}, f32[704,1024]{1,0:T(8,128)}, f32[704,1024...) custom-call(bf16[1280,1024]{1,0:T(8,128)(2,1)} %get-tuple-element.82.rows_in, ...), custom_call_target="tpu_custom_call" | custom-call | flops 66437775360 | bytes 42598400 | tf_op jit(solution)/shard_map/pallas_call | solution.py:1121
  379.6 77.7 %shard_map.216 = (bf16[4,512,1024]{2,1,0:T(8,128)(2,1)}, f32[512,1024]{1,0:T(8,128)}, f32[1,1024]{1,0:T(1,128)}, f32[16,1024]{1,0:T(8,128)}, bf16[2048,1024]{1,0:T(8,128)(2,1)}) custom-call(bf16[1280,1024]{1,0:T(8,128)(2,1)} %get-tuple-element.86.ret_in, bf16[1280,1024]{1,0:T(8,128)(2,1)} %get-tuple-element.87.back_ref, ...), custom_call_target="tpu_custom_call" | custom-call | flops 41943040 | bytes 209715200 | tf_op jit(solution)/shard_map/pallas_call | solution.py:552
  457.3 38.5 %shard_map.217 = (bf16[256,2048]{1,0:T(8,128)(2,1)}, bf16[256,2048]{1,0:T(8,128)(2,1)}, bf16[256,2048]{1,0:T(8,128)(2,1)}, f32[8,3,256,256]{3,2,1,0:T(8,128)}, f...) custom-call(bf16[768,2048]{1,0:T(8,128)(2,1)} %get-tuple-element.76.qkv_ref.q_ref.k_ref.v_ref, ...), custom_call_target="tpu_custom_call" | custom-call | flops 10737418240 | bytes 33554432 | tf_op jit(solution)/shard_map/pallas_call | solution.py:304
  495.8 0.4 collective-permute-start.1
  496.2 1.7 collective-permute-start.2
  497.8 23.0 %shard_map.218 = (bf16[1024,1024]{1,0:T(8,128)(2,1)}, bf16[2048,1024]{1,0:T(8,128)(2,1)}, f32[1,1024]{1,0:T(1,128)}, f32[2,704,1024]{2,1,0:T(8,128)}, f32[2,704,1024]{2,1,0:T(8,128)}, /*index=5*/f32[2,704,1024]{2,1,0:T(8,128)}) custom-call(s32[2]{0:T(128)} %pad_add_fusion.place_ref, bf16[1024,2048]{1,0:T(8,128)(2,1)} %x_ref.5, f32[1,1024]{1,0:T(1,128)} %bitcast.34, ...), custom_call_target="tpu_custom_call" | custom-call | flops 8053063680 | bytes 22675456 | tf_op jit(solution)/shard_map/pallas_call | solution.py:389
  520.9 0.0 all-reduce.2.cloned.1.call-update
  520.9 0.0 collective-permute-done.1.y_across
  520.9 0.0 copy-start
  520.9 0.0 collective-permute-done.2.y_along
  520.9 0.0 copy-start.1
  520.9 0.9 copy-done
  521.9 0.3 copy-done.1
  522.2 107.7 %shard_map.219 = (bf16[4,512,1024]{2,1,0:T(8,128)(2,1)}, bf16[4,512,1024]{2,1,0:T(8,128)(2,1)}, f32[32,1024]{1,0:T(8,128)}) custom-call(bf16[4,512,1024]{2,1,0:T(8,128)(2,1)} %bitcast.23, bf16[512,1024]{1,0:T(8,128)(2,1)} %get-tuple-element.112.x_in, f32[1,2048]{1,0:T(1,128)} %get-tuple-element.74.scale_ref, f32[512,1024]{1,0:T(8,128)} %get-tuple-element.113.grad_in, ...), custom_call_target="tpu_custom_call" | custom-call | flops 41943040 | bytes 209715200 | tf_op jit(solution)/shard_map/pallas_call | solution.py:552
  630.0 0.0 all-reduce.2.cloned.1.call-done.summed_ref
  630.0 11.6 %shard_map.220 = (bf16[1024,2048]{1,0:T(8,128)(2,1)}, f32[1024,2048]{1,0:T(8,128)}, f32[768,1024]{1,0:T(8,128)}, f32[256,1024]{1,0:T(8,128)}, f32[1,1024]{1,0:T(...) custom-call(bf16[2048,1024]{1,0:T(8,128)(2,1)} %bitcast.24, bf16[2048,1024]{1,0:T(8,128)(2,1)} %bitcast.25, ...), custom_call_target="tpu_custom_call" | custom-call | bytes 27262976 | tf_op jit(solution)/shard_map/pallas_call | solution.py:1175
Async XLA Ops:
  7.2 622.8 %all-reduce.2.cloned.1.call-start = ((), (), s32[]{:S(2)}) async-start(), calls=%async_computation | async-start | bytes 4194304 | tf_op jit(solution)/shard_map/psum | solution.py:1287
  8.4 19.1 %collective-permute-start = (bf16[352,1024]{1,0:T(8,128)(2,1)S(1)}, bf16[352,1024]{1,0:T(8,128)(2,1)S(1)}, u32[]{:S(2)}, u32[]{:S(2)}) collective-permute-start(bf16[352,1024]{1,0:T(8,128)(2,1)S(1)} %dynamic-slice_bitcast_fusion), channel_id=1, source_target_pairs={{0,1},{1,0},{2,3},{3,2},{4,5},{5,4},{6,7},{7,6},{8,9},{9,8},{10,11... | collective-permute-start | bytes 2162696 | tf_op jit(solution)/shard_map/ppermute | solution.py:1222
  27.5 90.8 %copy-start.2 = (bf16[352,1024]{1,0:T(8,128)(2,1)}, bf16[352,1024]{1,0:T(8,128)(2,1)S(1)}, u32[]{:S(2)}) copy-start(bf16[352,1024]{1,0:T(8,128)(2,1)S(1)} %collective-permute-done.far_gate) | copy-start | bytes 2162692
  495.8 25.2 %collective-permute-start.1 = (bf16[512,1024]{1,0:T(8,128)(2,1)}, bf16[512,1024]{1,0:T(8,128)(2,1)S(1)}, u32[]{:S(2)}, u32[]{:S(2)}) collective-permute-start(bf16[512,1024]{1,0:T(8,128)(2,1)} %get-tuple-element.110.y_own), channel_id=1, source_target_pairs={{0,1},{1,0},{2,3},{3,2},{4,5},{5,4},{6,7},{7,6},{8,9},{9,8},{10,11... | collective-permute-start | bytes 3145736 | tf_op jit(solution)/shard_map/ppermute | solution.py:1280
  496.2 24.7 %collective-permute-start.2 = (bf16[512,1024]{1,0:T(8,128)(2,1)}, bf16[512,1024]{1,0:T(8,128)(2,1)S(1)}, u32[]{:S(2)}, u32[]{:S(2)}) collective-permute-start(bf16[512,1024]{1,0:T(8,128)(2,1)} %get-tuple-element.110.y_own), channel_id=1, source_target_pairs={{0,2},{1,3},{2,0},{3,1},{4,6},{5,7},{6,4},{7,5},{8,10},{9,11},{10,... | collective-permute-start | bytes 3145736 | tf_op jit(solution)/shard_map/ppermute | solution.py:1281
  520.9 1.0 copy-start
  520.9 1.3 copy-start.1
Sparse Core Ops, SparseCore 0:
  521.0 89.7 all-reduce.1

commit v13 on v12

--- a/solution.py
+++ b/solution.py
@@ -586,7 +586,7 @@
     part = got_gate.shape[0] // 2
     swaps = [
         pltpu.make_async_remote_copy(
-            src_ref=gate_ref.at[1 - pair_class, pl.ds((2 + piece) * part, part)],
+            src_ref=gate_ref.at[1 - pair_class, pl.ds(gate_ref.shape[1] - (2 - piece) * part, part)],
             dst_ref=got_gate.at[pl.ds(piece * part, part)],
             send_sem=send.at[piece],
             recv_sem=recv.at[piece],
@@ -644,7 +644,7 @@
                 copy.wait()
 
     exchange(
-        math, rank, source, full, *rest[:-8], side=side, start=start, fill=fill, later=later, cut=3 * width // 8
+        math, rank, source, full, *rest[:-8], side=side, start=start, fill=fill, later=later, cut=width // 4
     )
 
 
@@ -974,9 +974,8 @@
         pltpu.make_async_copy(ref.at[pair_class], weights.at[number, 0], local.at[2 + number])
         for number, ref in enumerate((gate_in, up_in, down_in))
     ]
-    some = far_gate.shape[0]
     for number, ref in enumerate((far_gate, far_gate_too)):
-        target = weights.at[0, 1, pl.ds(number * some, some)]
+        target = weights.at[0, 1, pl.ds(number * far_gate.shape[0], ref.shape[0])]
         kept.append(pltpu.make_async_copy(ref, target, local.at[5 + number]))
     kept += [
         remote(ref.at[1 - pair_class], weights.at[number, 1], w_send.at[number - 1], w_recv.at[number - 1], across)
@@ -1218,7 +1217,7 @@
     half = CAP // 2
 
     units = expert_gate.shape[1]
-    other = lax.dynamic_slice(expert_gate, (1 - pair_class, 0, 0), (1, units // 2, width))[0]
+    other = lax.dynamic_slice(expert_gate, (1 - pair_class, 0, 0), (1, units // 11 * 4, width))[0]
     traded = lax.ppermute(other, "tensor", [(r, r ^ 1) for r in range(ranks)])
     w_in = attn_in.reshape(-1, width)
     qkv, scale_one, tiles = project(layer_input, gain_one[None], w_in, rel_bias.T)
@@ -1243,7 +1242,7 @@
         [qkv, tiles, limits, attn_out, layer_input, gain_two[None], grad_out, routes_t, expert_gate],
         [((share, width), F32), ((share, 1), F32), ((tokens, width), BF16), ((slots, width), BF16)]
         + [((TOP, tokens), jnp.int32), ((tokens, TOP), jnp.int32), ((share, width), BF16)]
-        + [(attn_out.shape[:1] + (tokens,), BF16), ((heads * tokens // SEQ, 1, SEQ), F32), (traded.shape, BF16)],
+        + [(attn_out.shape[:1] + (tokens,), BF16), ((heads * tokens // SEQ, 1, SEQ), F32), ((units - traded.shape[0], width), BF16)],
         [pltpu.VMEM((ranks, share, width), BF16), pltpu.VMEM((width, share), BF16), pltpu.VMEM((width, tokens), BF16)]
         + [pltpu.VMEM((tokens, width), BF16), pltpu.VMEM((slots, width), BF16), pltpu.SemaphoreType.DMA((4,))]
         + [pltpu.SemaphoreType.DMA((2,))] * 2,

time: 657 us -> 656 us (level)
  transfers between devices with their start and end apart: 4 -> 4, of which waited for: 1 -> 2; matrix products, arithmetic and copies ran while one was open for 0% -> 0% of each run, Pallas kernels for 21% -> 21%
where the time goes in v13:
time: 656 us; the launch traced here: 649 us
  Pallas kernels  623 us (95%)
  between operations  14.6 us (2%)
    pallas_call x3, Pallas kernels, exchange_call(): pl.pallas_call(kernel, in_specs=[pl.BlockSpec(memory_space=pl.ANY) if k i...  282 us
    pallas_call x1, Pallas kernels, run_experts(): pl.pallas_call(expert_kernel, in_specs=[anywhere] * 7, out_specs=[anywher...  248 us
    pallas_call x1, Pallas kernels, attend_back(): pl.pallas_call(attend_back_kernel, grid=(seqs, heads), in_specs=[pl.Block...  38.1 us
    pallas_call x1, Pallas kernels, project_back(): pl.pallas_call(project_back_kernel, grid=(steps,), in_specs=[pl.BlockSpec...  23 us
  transfers between devices with their start and end apart: 4, of which 2 were waited for; matrix products, arithmetic and copies ran while one was open for 0% of the time, Pallas kernels for 21%

profile of v13, /device:TPU:0, one launch (start us, length us, event | category | flops | bytes accessed | tf_op | source)
XLA Modules:
  0.0 648.8 jit_solution(14369423961780277668)
XLA Ops:
  7.2 0.0 all-reduce.2.cloned.1.call-start
  7.2 1.1 dynamic-slice_bitcast_fusion
  8.3 3.0 collective-permute-start
  11.3 0.7 broadcast_add_fusion.1
  12.0 0.8 fusion
  12.8 0.6 pad_add_fusion.place_ref
  13.4 0.6 iota_maximum_fusion.limit_ref
  14.0 8.6 %shard_map.212 = (bf16[768,2048]{1,0:T(8,128)(2,1)}, f32[1,2048]{1,0:T(1,128)}, f32[4,3,256,256]{3,2,1,0:T(8,128)}) custom-call(bf16[1024,2048]{1,0:T(8,128)(2,1)} %x_ref.5, f32[1,1024]{1,0:T(1,128)} %bitcast.33, bf16[768,1024]{1,0:T(8,128)(2,1)} %bitcast.40, f32[4,32]{1,0:T(4,128)} %bitcast.45), custom_call_target="tpu_custom_call" | custom-call | flops 3221225472 | bytes 8388608 | tf_op jit(solution)/shard_map/pallas_call | solution.py:70
  22.6 0.6 collective-permute-done.far_gate
  23.3 0.0 copy-start.2
  23.3 95.3 %shard_map.213 = (bf16[4,512,1024]{2,1,0:T(8,128)(2,1)}, f32[512,1024]{1,0:T(8,128)}, f32[512,1]{1,0:T(8,128)}, bf16[2048,1024]{1,0:T(8,128)(2,1)}, bf16[1280,10...) custom-call(bf16[768,2048]{1,0:T(8,128)(2,1)} %get-tuple-element.76., ...), custom_call_target="tpu_custom_call" | custom-call | flops 41943040 | bytes 209715200 | tf_op jit(solution)/shard_map/pallas_call | solution.py:552
  118.5 0.0 copy-done.2
  118.6 11.9 %shard_map.214 = (bf16[1280,1024]{1,0:T(8,128)(2,1)}, bf16[1280,1024]{1,0:T(8,128)(2,1)}, f32[1280,1]{1,0:T(8,128)}, f32[2,2048]{1,0:T(2,128)}) custom-call(s32[2,2048]{1,0:T(2,128)} %get-tuple-element.79.code_ref, s32[2,2048]{1,0:T(2,128)} %bitcast.27, bf16[16,1024]{1,0:T(8,128)(2,1)} %bitcast.29, bf16[2048,1024]{1,0:T(8,128)(2,1)} %bitcast.21, ...), custom_call_target="tpu_custom_call" | custom-call | flops 5368709120 | bytes 12058624 | tf_op jit(solution)/shard_map/pallas_call | solution.py:881
  130.5 247.6 %shard_map.215 = (bf16[1280,1024]{1,0:T(8,128)(2,1)}, bf16[1280,1024]{1,0:T(8,128)(2,1)}, f32[704,1024]{1,0:T(8,128)}, f32[704,1024]{1,0:T(8,128)}, f32[704,1024...) custom-call(bf16[1280,1024]{1,0:T(8,128)(2,1)} %get-tuple-element.82.rows_in, ...), custom_call_target="tpu_custom_call" | custom-call | flops 66437775360 | bytes 42598400 | tf_op jit(solution)/shard_map/pallas_call | solution.py:1120
  378.1 79.3 %shard_map.216 = (bf16[4,512,1024]{2,1,0:T(8,128)(2,1)}, f32[512,1024]{1,0:T(8,128)}, f32[1,1024]{1,0:T(1,128)}, f32[16,1024]{1,0:T(8,128)}, bf16[2048,1024]{1,0:T(8,128)(2,1)}) custom-call(bf16[1280,1024]{1,0:T(8,128)(2,1)} %get-tuple-element.86.ret_in, bf16[1280,1024]{1,0:T(8,128)(2,1)} %get-tuple-element.87.back_ref, ...), custom_call_target="tpu_custom_call" | custom-call | flops 41943040 | bytes 209715200 | tf_op jit(solution)/shard_map/pallas_call | solution.py:552
  457.4 38.1 %shard_map.217 = (bf16[256,2048]{1,0:T(8,128)(2,1)}, bf16[256,2048]{1,0:T(8,128)(2,1)}, bf16[256,2048]{1,0:T(8,128)(2,1)}, f32[8,3,256,256]{3,2,1,0:T(8,128)}, f...) custom-call(bf16[768,2048]{1,0:T(8,128)(2,1)} %get-tuple-element.76.qkv_ref.q_ref.k_ref.v_ref, ...), custom_call_target="tpu_custom_call" | custom-call | flops 10737418240 | bytes 33554432 | tf_op jit(solution)/shard_map/pallas_call | solution.py:304
  495.6 1.8 collective-permute-start.1
  497.3 0.3 collective-permute-start.2
  497.7 23.0 %shard_map.218 = (bf16[1024,1024]{1,0:T(8,128)(2,1)}, bf16[2048,1024]{1,0:T(8,128)(2,1)}, f32[1,1024]{1,0:T(1,128)}, f32[2,704,1024]{2,1,0:T(8,128)}, f32[2,704,1024]{2,1,0:T(8,128)}, /*index=5*/f32[2,704,1024]{2,1,0:T(8,128)}) custom-call(s32[2]{0:T(128)} %pad_add_fusion.place_ref, bf16[1024,2048]{1,0:T(8,128)(2,1)} %x_ref.5, f32[1,1024]{1,0:T(1,128)} %bitcast.34, ...), custom_call_target="tpu_custom_call" | custom-call | flops 8053063680 | bytes 22675456 | tf_op jit(solution)/shard_map/pallas_call | solution.py:389
  520.7 0.0 all-reduce.2.cloned.1.call-update
  520.7 0.0 collective-permute-done.1.y_across
  520.7 0.0 copy-start
  520.8 0.9 collective-permute-done.2.y_along
  521.7 0.0 copy-start.1
  521.7 0.1 copy-done
  521.7 0.9 copy-done.1
  522.6 107.2 %shard_map.219 = (bf16[4,512,1024]{2,1,0:T(8,128)(2,1)}, bf16[4,512,1024]{2,1,0:T(8,128)(2,1)}, f32[32,1024]{1,0:T(8,128)}) custom-call(bf16[4,512,1024]{2,1,0:T(8,128)(2,1)} %bitcast.23, bf16[512,1024]{1,0:T(8,128)(2,1)} %get-tuple-element.112.x_in, f32[1,2048]{1,0:T(1,128)} %get-tuple-element.74.scale_ref, f32[512,1024]{1,0:T(8,128)} %get-tuple-element.113.grad_in, ...), custom_call_target="tpu_custom_call" | custom-call | flops 41943040 | bytes 209715200 | tf_op jit(solution)/shard_map/pallas_call | solution.py:552
  629.9 0.0 all-reduce.2.cloned.1.call-done.summed_ref
  629.9 11.6 %shard_map.220 = (bf16[1024,2048]{1,0:T(8,128)(2,1)}, f32[1024,2048]{1,0:T(8,128)}, f32[768,1024]{1,0:T(8,128)}, f32[256,1024]{1,0:T(8,128)}, f32[1,1024]{1,0:T(...) custom-call(bf16[2048,1024]{1,0:T(8,128)(2,1)} %bitcast.24, bf16[2048,1024]{1,0:T(8,128)(2,1)} %bitcast.25, ...), custom_call_target="tpu_custom_call" | custom-call | bytes 27262976 | tf_op jit(solution)/shard_map/pallas_call | solution.py:1174
Async XLA Ops:
  7.2 622.7 %all-reduce.2.cloned.1.call-start = ((), (), s32[]{:S(2)}) async-start(), calls=%async_computation | async-start | bytes 4194304 | tf_op jit(solution)/shard_map/psum | solution.py:1286
  8.3 14.9 %collective-permute-start = (bf16[256,1024]{1,0:T(8,128)(2,1)S(1)}, bf16[256,1024]{1,0:T(8,128)(2,1)S(1)}, u32[]{:S(2)}, u32[]{:S(2)}) collective-permute-start(bf16[256,1024]{1,0:T(8,128)(2,1)S(1)} %dynamic-slice_bitcast_fusion), channel_id=1, source_target_pairs={{0,1},{1,0},{2,3},{3,2},{4,5},{5,4},{6,7},{7,6},{8,9},{9,8},{10,11... | collective-permute-start | bytes 1572872 | tf_op jit(solution)/shard_map/ppermute | solution.py:1221
  23.3 95.3 %copy-start.2 = (bf16[256,1024]{1,0:T(8,128)(2,1)}, bf16[256,1024]{1,0:T(8,128)(2,1)S(1)}, u32[]{:S(2)}) copy-start(bf16[256,1024]{1,0:T(8,128)(2,1)S(1)} %collective-permute-done.far_gate) | copy-start | bytes 1572868
  495.6 25.2 %collective-permute-start.1 = (bf16[512,1024]{1,0:T(8,128)(2,1)}, bf16[512,1024]{1,0:T(8,128)(2,1)S(1)}, u32[]{:S(2)}, u32[]{:S(2)}) collective-permute-start(bf16[512,1024]{1,0:T(8,128)(2,1)} %get-tuple-element.110.y_own), channel_id=1, source_target_pairs={{0,1},{1,0},{2,3},{3,2},{4,5},{5,4},{6,7},{7,6},{8,9},{9,8},{10,11... | collective-permute-start | bytes 3145736 | tf_op jit(solution)/shard_map/ppermute | solution.py:1279
  497.3 24.3 %collective-permute-start.2 = (bf16[512,1024]{1,0:T(8,128)(2,1)}, bf16[512,1024]{1,0:T(8,128)(2,1)S(1)}, u32[]{:S(2)}, u32[]{:S(2)}) collective-permute-start(bf16[512,1024]{1,0:T(8,128)(2,1)} %get-tuple-element.110.y_own), channel_id=1, source_target_pairs={{0,2},{1,3},{2,0},{3,1},{4,6},{5,7},{6,4},{7,5},{8,10},{9,11},{10,... | collective-permute-start | bytes 3145736 | tf_op jit(solution)/shard_map/ppermute | solution.py:1280
  520.7 1.0 copy-start
  521.7 1.0 copy-start.1
Sparse Core Ops, SparseCore 0:
  520.9 90.3 all-reduce.1
